TPU v7x, 32 devices: a whole 2x2x4 slice. The times are simulated.
32 devices in a mesh: regions: 2 (over y), gz: 8 (over z, x), gy: 2 (over core).
Axes of the slice: x: 2, y: 2, z: 4, core: 2. Of those that a mesh axis runs over, the one named last changes fastest.
Arguments:
- iterate: float32 [16, 32, 128, 256], P(None, ('regions', 'gz'), 'gy'), parts along dimension 1, may hold values from -6 to 6
- residual: float32 [16, 32, 128, 256], P(None, ('regions', 'gz'), 'gy'), parts along dimension 1, may hold values from -16 to 16
- labels: int32 [32, 128, 256], P(('regions', 'gz'), 'gy'), parts along dimension 0, may hold values from 0 to 7
- boundary: int32 [32, 128, 256], P(('regions', 'gz'), 'gy'), parts along dimension 0, may hold values 0 or 1
Outputs:
- iterate_out: float32 [16, 32, 128, 256], P(None, ('regions', 'gz'), 'gy'), parts along dimension 1
- residual_out: float32 [16, 32, 128, 256], P(None, ('regions', 'gz'), 'gy'), parts along dimension 1
There are 2 independent parts, one for each index of `regions`. A program takes and returns all parts, laid end to end along the dimension named above; each array names one. Nothing has to cross between parts.
All inputs are finite; a program needn't handle non-finite values. No bound on the sum of `boundary` on one device may be relied on, other than what follows from the above.
Results may differ from a plain program's by a relative error of at most 0.0003.
Values sent between devices are 32-bit elements; how exact they have to be, the bound alone decides.
No kernel may reach another device: no remote copies, remote signals or barrier semaphores. Data moves between devices by JAX's collectives and lax.ppermute only.
A program may use at most 128 MiB of HBM per device.

v0:
```python
import math

import jax
import jax.numpy as jnp
from jax import lax
from jax.sharding import PartitionSpec as P

NCLASS = 8
ITERS = 3


contrast_log = 4.0 * math.log(10.0)
highest = lax.Precision.HIGHEST


def extended_2(cells, sides, width):
    for axis, dim in sides:
        count = lax.axis_size(axis)
        ends = count - 1
        head = lax.slice_in_dim(cells, 0, width, axis=dim)
        tail = lax.slice_in_dim(cells, cells.shape[dim] - width, cells.shape[dim], axis=dim)
        cells = jnp.concatenate(
            [
                lax.ppermute(tail, axis, [(i, (i + 1) % count) for i in range(ends)]),
                cells,
                lax.ppermute(head, axis, [((i + 1) % count, i) for i in range(ends)]),
            ],
            axis=dim,
        )
    return cells


def shift_cells(block, forward):
    widths = [(0, 0)] * (block.ndim - 1)
    if forward:
        return jnp.pad(block[..., 1:], widths + [(0, 1)])
    return jnp.pad(block[..., :-1], widths + [(1, 0)])


def neighbors(extended):
    center = extended[..., 1:-1, 1:-1, :]
    beside = [
        extended[..., 2:, 1:-1, :],
        extended[..., :-2, 1:-1, :],
        extended[..., 1:-1, 2:, :],
        extended[..., 1:-1, :-2, :],
        shift_cells(center, True),
        shift_cells(center, False),
    ]
    return (center, beside)


def couplings_of(extended):
    coef_center, coef_beside = neighbors(extended[0])
    inner_center, inner_beside = neighbors(extended[1])
    diagonal = jnp.zeros_like(coef_center)
    offsets = []
    for neighbor_coef, neighbor_inner in zip(coef_beside, inner_beside):
        face_coef = jnp.where(
            neighbor_coef > 0.0,
            2.0 * coef_center * neighbor_coef / (coef_center + neighbor_coef),
            coef_center,
        )
        diagonal = diagonal + face_coef
        offsets.append(inner_center * face_coef * neighbor_inner)
    diagonal = inner_center * diagonal + (1.0 - inner_center)
    return (diagonal, offsets)


def apply_operator(diagonal, offsets, extended):
    center, beside = neighbors(extended)
    coupled = offsets[0] * beside[0]
    for weight, values in zip(offsets[1:], beside[1:]):
        coupled = coupled + weight * values
    return diagonal * center - coupled


def cell_fields(labels, boundary):
    coef = jnp.exp(labels.astype(jnp.float32) * (contrast_log / (NCLASS - 1)))
    interior = (1 - boundary).astype(jnp.float32)
    return jnp.stack([coef, interior])


def gram(left_block, right_block):
    left_flat = left_block.reshape(left_block.shape[0], -1)
    right_flat = right_block.reshape(right_block.shape[0], -1)
    return lax.dot_general(left_flat, right_flat, (((1,), (1,)), ((), ())), precision=highest)


def combine(block, weights):
    flat = block.reshape(block.shape[0], -1)
    mixed = lax.dot_general(weights, flat, (((0,), (0,)), ((), ())), precision=highest)
    return mixed.reshape(block.shape)


def spd_solve(matrix, right):
    factor = jnp.linalg.cholesky(matrix)
    return jax.scipy.linalg.cho_solve((factor, True), right)


def direction_cells(field):
    return extended_2(field, (("gz", 1), ("gy", 2)), 1)


def on_device(iterate, residual, labels, boundary):
    fields = cell_fields(labels, boundary)
    extended = extended_2(fields, (("gz", 1), ("gy", 2)), 1)
    diagonal, offsets = couplings_of(extended)
    inverse_diag = 1.0 / diagonal
    scaled = inverse_diag * residual
    direction = scaled
    for iteration in range(ITERS):
        direction_ext = direction_cells(direction)
        image = apply_operator(diagonal, offsets, direction_ext)
        weighted = inverse_diag * image
        summed_rho, curvature, cross_gram, image_gram = lax.psum(
            (
                gram(residual, scaled),
                gram(direction, image),
                gram(scaled, image),
                gram(image, weighted),
            ),
            ("gz", "gy"),
        )
        step_size = spd_solve(curvature, summed_rho)
        iterate = iterate + combine(direction, step_size)
        residual = residual - combine(image, step_size)
        if iteration + 1 < ITERS:
            scaled = inverse_diag * residual
            moved = jnp.dot(cross_gram, step_size, precision=highest)
            quadratic = jnp.dot(
                step_size.T, jnp.dot(image_gram, step_size, precision=highest), precision=highest
            )
            next_rho = summed_rho - moved - moved.T + quadratic
            momentum = spd_solve(summed_rho, next_rho)
            direction = scaled + combine(direction, momentum)
            summed_rho = next_rho
    return (iterate, residual)


def solution(mesh):
    placed = (
        P(None, ("regions", "gz"), "gy", None),
        P(None, ("regions", "gz"), "gy", None),
        P(("regions", "gz"), "gy", None),
        P(("regions", "gz"), "gy", None),
    )
    return jax.shard_map(
        on_device,
        mesh=mesh,
        in_specs=placed,
        out_specs=(P(None, ("regions", "gz"), "gy", None), P(None, ("regions", "gz"), "gy", None)),
        check_vma=False,
    )
```

profile of v0, /device:TPU:0, one launch (start us, length us, event | category | flops | bytes accessed | tf_op | source)
XLA Modules:
  0.0 462.9 jit_solution(4175048000201397154)
XLA Ops:
  2.5 1.3 collective-permute-start.1
  3.8 5.5 %collective-permute-start = (f32[2,1,64,256]{3,2,1,0:T(8,128)S(1)}, f32[2,1,64,256]{3,2,1,0:T(8,128)S(1)}, u32[]{:S(2)}, u32[]{:S(2)}) collective-permute-start(f32[2,1,64,256]{3,2,1,0:T(8,128)S(1)} %get-tuple-element.51), channel_id=1, source_target_pairs={{0,2},{2,4},{4,6},{6,8},{8,10},{10,12},{12,14},{1,3},{3,5},{5,7},{... | collective-permute-start | bytes 393224 | tf_op jit(solution)/shard_map/ppermute | solution.py:24
  9.3 1.5 collective-permute-done.1
  10.8 3.0 collective-permute-done
  13.8 1.3 collective-permute-start.3
  15.1 3.0 collective-permute-start.2
  22.0 1.3 collective-permute-start.4
  23.3 5.1 %collective-permute-start.5 = (f32[16,1,64,256]{3,0,2,1:T(8,128)S(1)}, f32[16,1,64,256]{3,0,2,1:T(8,128)S(1)}, u32[]{:S(2)}, u32[]{:S(2)}) collective-permute-start(f32[16,1,64,256]{3,0,2,1:T(8,128)S(1)} %get-tuple-element.35), channel_id=1, source_target_pairs={{0,2},{2,4},{4,6},{6,8},{8,10},{10,12},{12,14},{1,3},{3,5},{5,7},{... | collective-permute-start | bytes 3145736 | tf_op jit(solution)/shard_map/ppermute | solution.py:24
  28.4 3.5 fusion.74
  32.6 17.4 %collective-permute-done.4 = f32[16,1,64,256]{3,0,2,1:T(8,128)S(1)} collective-permute-done((f32[16,1,64,256]{3,0,2,1:T(8,128)S(1)}, f32[16,1,64,256]{3,0,2,1:T(8,128)S(1)}, u32[]{:S(2)}, u32[]{:S(2)}) %collective-permute-start.4) | collective-permute-done | bytes 1048608 | tf_op jit(solution)/shard_map/ppermute | solution.py:26
  50.1 22.6 %collective-permute-done.5 = f32[16,1,64,256]{3,0,2,1:T(8,128)S(1)} collective-permute-done((f32[16,1,64,256]{3,0,2,1:T(8,128)S(1)}, f32[16,1,64,256]{3,0,2,1:T(8,128)S(1)}, u32[]{:S(2)}, u32[]{:S(2)}) %collective-permute-start.5) | collective-permute-done | bytes 1048608 | tf_op jit(solution)/shard_map/ppermute | solution.py:24
  72.7 1.9 collective-permute-start.7
  74.7 1.5 collective-permute-start.6
  76.4 2.5 copy.93
  78.9 3.2 fusion.34
  82.2 3.8 convolution_bitcast_fusion.5
  86.0 2.8 fusion.86
  88.8 2.6 copy.95
  91.4 60.9 %all-reduce.12 = (f32[16,16]{0,1:T(8,128)S(1)}, f32[16,16]{0,1:T(8,128)S(1)}, f32[16,16]{1,0:T(8,128)S(1)}) all-reduce(f32[16,16]{0,1:T(8,128)S(1)} %fusion.74, f32[16,16]{0,1:T(8,128)S(1)} %convolution_bitcast_fusion.5, f32[16,16]{1,0:T(8,128)S(1)} %fusion.86), channel_id=1, replica_groups=mesh['regions'=2,'gz'=8,'gy'=2] {'gz','gy'}, use_global_device_ids=true, to_apply=%region_3.5 | all-reduce | flops 768 | bytes 6144 | tf_op jit(solution)/shard_map/psum | solution.py:116
  152.4 1.5 cholesky.89
  155.2 1.2 custom-call.11
  157.0 6.3 %copy_subtract_fusion = f32[16,2,64,256]{3,0,2,1:T(8,128)S(1)} fusion(f32[16,2,64,256]{3,2,1,0:T(8,128)} %param.8, f32[2,64,256,16]{2,1,0,3:T(8,128)} %bitcast.241, f32[16,16]{1,0:T(8,128)S(1)} %fusion.124), kind=kOutput, calls=%fused_computation.85 | convolution fusion | flops 101187584 | bytes 6292480 | tf_op jit(solution)/shard_map/dot_general | solution.py:92
  163.5 1.5 cholesky.100
  166.3 1.2 custom-call.12
  168.1 4.5 multiply_add_fusion.1
  172.8 1.3 collective-permute-start.8
  174.1 4.6 collective-permute-start.9
  179.5 15.8 %collective-permute-done.8 = f32[16,1,64,256]{3,0,2,1:T(8,128)S(1)} collective-permute-done((f32[16,1,64,256]{3,0,2,1:T(8,128)S(1)}, f32[16,1,64,256]{3,0,2,1:T(8,128)S(1)}, u32[]{:S(2)}, u32[]{:S(2)}) %collective-permute-start.8) | collective-permute-done | bytes 1048608 | tf_op jit(solution)/shard_map/ppermute | solution.py:26
  195.3 18.0 %collective-permute-done.9 = f32[16,1,64,256]{3,0,2,1:T(8,128)S(1)} collective-permute-done((f32[16,1,64,256]{3,0,2,1:T(8,128)S(1)}, f32[16,1,64,256]{3,0,2,1:T(8,128)S(1)}, u32[]{:S(2)}, u32[]{:S(2)}) %collective-permute-start.9) | collective-permute-done | bytes 1048608 | tf_op jit(solution)/shard_map/ppermute | solution.py:24
  213.3 1.9 collective-permute-start.11
  215.2 1.8 collective-permute-start.10
  217.0 2.8 fusion.77
  219.7 2.6 copy.97
  222.3 3.2 fusion.24
  225.6 2.9 convolution_bitcast_fusion.3
  228.4 2.7 fusion.89
  231.2 2.8 fusion.80
  234.0 2.6 copy.99
  236.5 62.7 %all-reduce.11 = (f32[16,16]{0,1:T(8,128)S(1)}, f32[16,16]{0,1:T(8,128)S(1)}, f32[16,16]{1,0:T(8,128)S(1)}, f32[16,16]{1,0:T(8,128)S(1)}) all-reduce(f32[16,16]{0,1:T(8,128)S(1)} %fusion.77, f32[16,16]{0,1:T(8,128)S(1)} %convolution_bitcast_fusion.3, f32[16,16]{1,0:T(8,128)S(1)} %fusion.89, ...), channel_id=1, replica_groups=mesh['regions'=2,'gz'=8,'gy'=2] {'gz','gy'}, use_global_device_ids=true, to_apply=%region_6.9 | all-reduce | flops 1024 | bytes 8192 | tf_op jit(solution)/shard_map/psum | solution.py:116
  299.3 1.5 cholesky.111
  301.9 1.2 custom-call.13
  303.6 5.7 %fusion.68 = f32[16,2,64,256]{3,0,2,1:T(8,128)} fusion(f32[16,2,64,256]{3,0,2,1:T(8,128)S(1)} %copy_subtract_fusion, f32[2,64,256,16]{2,1,0,3:T(8,128)} %bitcast.240, f32[16,16]{1,0:T(8,128)S(1)} %fusion.113), kind=kOutput, calls=%fused_computation.89 | convolution fusion | flops 101187584 | bytes 6292480 | tf_op jit(solution)/shard_map/dot_general | solution.py:92
  309.6 1.5 cholesky.122
  312.4 1.2 custom-call.14
  314.2 5.2 %multiply_add_fusion = f32[16,2,64,256]{3,0,2,1:T(8,128)S(1)} fusion(f32[16,2,64,256]{3,0,2,1:T(8,128)} %fusion.68, f32[16,16,1,1]{0,1,3,2:T(8,128)S(1)} %convolution_bitcast_fusion.2, f32[2,64,256,16]{2,1,0,3:T(8,128)} %bitcast.234, f32[2,64,256]{2,1,0:T(8,128)S(1)} %get-tuple-element.17), kind=kOutput, calls=%fused_computation.6 | convolution fusion | flops 101711872 | bytes 6423552 | tf_op jit(solution)/shard_map/dot_general | solution.py:92
  319.6 1.4 collective-permute-start.12
  321.0 4.6 collective-permute-start.13
  325.6 4.2 fusion.52
  330.6 11.6 %collective-permute-done.12 = f32[16,1,64,256]{3,0,2,1:T(8,128)S(1)} collective-permute-done((f32[16,1,64,256]{3,0,2,1:T(8,128)S(1)}, f32[16,1,64,256]{3,0,2,1:T(8,128)S(1)}, u32[]{:S(2)}, u32[]{:S(2)}) %collective-permute-start.12) | collective-permute-done | bytes 1048608 | tf_op jit(solution)/shard_map/ppermute | solution.py:26
  342.1 18.0 %collective-permute-done.13 = f32[16,1,64,256]{3,0,2,1:T(8,128)S(1)} collective-permute-done((f32[16,1,64,256]{3,0,2,1:T(8,128)S(1)}, f32[16,1,64,256]{3,0,2,1:T(8,128)S(1)}, u32[]{:S(2)}, u32[]{:S(2)}) %collective-permute-start.13) | collective-permute-done | bytes 1048608 | tf_op jit(solution)/shard_map/ppermute | solution.py:24
  360.1 1.9 collective-permute-start.15
  362.0 1.3 collective-permute-start.14
  363.3 2.7 fusion.83
  366.1 2.6 copy.101
  368.6 3.2 fusion.14
  371.9 1.3 copy-done.4
  373.2 2.9 convolution_bitcast_fusion.1
  376.0 62.6 %all-reduce.10 = (f32[16,16]{1,0:T(8,128)S(1)}, f32[16,16]{0,1:T(8,128)S(1)}) all-reduce(f32[16,16]{1,0:T(8,128)S(1)} %fusion.83, f32[16,16]{0,1:T(8,128)S(1)} %convolution_bitcast_fusion.1), channel_id=1, replica_groups=mesh['regions'=2,'gz'=8,'gy'=2] {'gz','gy'}, use_global_device_ids=true, to_apply=%region_10.13 | all-reduce | flops 512 | bytes 4096 | tf_op jit(solution)/shard_map/psum | solution.py:116
  438.8 1.5 cholesky.133
  443.1 4.5 fusion.42
  447.7 5.7 %fusion.49 = f32[16,2,64,256]{3,0,2,1:T(8,128)S(1)} fusion(f32[16,2,64,256]{3,0,2,1:T(8,128)S(1)} %fusion.42, f32[16,2,64,256]{3,0,2,1:T(8,128)S(1)} %copy-done.6, f32[16,2,64,256]{3,2,1,0:T(8,128)} %param.7, f32[2,64,256,16]{2,1,0,3:T(8,128)S(1)} %bitcast.237, f32[16,16]{1,0:T(8,128)S(1)} %fusion.124), kind=kOutput, calls=%fused_computation.76 | convolution fusion | flops 102236160 | bytes 10486784 | tf_op jit(solution)/shard_map/dot_general | solution.py:92
  453.4 2.5 copy.64
  457.1 2.9 fusion.71
  460.0 2.5 copy.65
  (85 shorter events, 20.9 us)
Async XLA Ops:
  2.5 8.3 %collective-permute-start.1 = (f32[2,1,64,256]{3,2,1,0:T(8,128)S(1)}, f32[2,1,64,256]{3,2,1,0:T(8,128)S(1)}, u32[]{:S(2)}, u32[]{:S(2)}) collective-permute-start(f32[2,1,64,256]{3,2,1,0:T(8,128)S(1)} %get-tuple-element.52), channel_id=1, source_target_pairs={{2,0},{4,2},{6,4},{8,6},{10,8},{12,10},{14,12},{3,1},{5,3},{7,5},{... | collective-permute-start | bytes 393224 | tf_op jit(solution)/shard_map/ppermute | solution.py:26
  3.8 10.0 %collective-permute-start = (f32[2,1,64,256]{3,2,1,0:T(8,128)S(1)}, f32[2,1,64,256]{3,2,1,0:T(8,128)S(1)}, u32[]{:S(2)}, u32[]{:S(2)}) collective-permute-start(f32[2,1,64,256]{3,2,1,0:T(8,128)S(1)} %get-tuple-element.51), channel_id=1, source_target_pairs={{0,2},{2,4},{4,6},{6,8},{8,10},{10,12},{12,14},{1,3},{3,5},{5,7},{... | collective-permute-start | bytes 393224 | tf_op jit(solution)/shard_map/ppermute | solution.py:24
  13.8 4.3 collective-permute-start.3
  15.1 3.8 collective-permute-start.2
  19.0 1.6 copy-start
  22.0 28.1 %collective-permute-start.4 = (f32[16,1,64,256]{3,0,2,1:T(8,128)S(1)}, f32[16,1,64,256]{3,0,2,1:T(8,128)S(1)}, u32[]{:S(2)}, u32[]{:S(2)}) collective-permute-start(f32[16,1,64,256]{3,0,2,1:T(8,128)S(1)} %get-tuple-element.36), channel_id=1, source_target_pairs={{2,0},{4,2},{6,4},{8,6},{10,8},{12,10},{14,12},{3,1},{5,3},{7,5},{... | collective-permute-start | bytes 3145736 | tf_op jit(solution)/shard_map/ppermute | solution.py:26
  23.3 49.4 %collective-permute-start.5 = (f32[16,1,64,256]{3,0,2,1:T(8,128)S(1)}, f32[16,1,64,256]{3,0,2,1:T(8,128)S(1)}, u32[]{:S(2)}, u32[]{:S(2)}) collective-permute-start(f32[16,1,64,256]{3,0,2,1:T(8,128)S(1)} %get-tuple-element.35), channel_id=1, source_target_pairs={{0,2},{2,4},{4,6},{6,8},{8,10},{10,12},{12,14},{1,3},{3,5},{5,7},{... | collective-permute-start | bytes 3145736 | tf_op jit(solution)/shard_map/ppermute | solution.py:24
  72.7 6.2 %collective-permute-start.7 = (f32[16,4,1,256]{3,0,2,1:T(8,128)S(1)}, f32[16,4,1,256]{3,0,2,1:T(8,128)S(1)}, u32[]{:S(2)}, u32[]{:S(2)}) collective-permute-start(f32[16,4,1,256]{3,0,2,1:T(8,128)S(1)} %get-tuple-element.24), channel_id=1, source_target_pairs={{0,1},{2,3},{4,5},{6,7},{8,9},{10,11},{12,13},{14,15},{16,17},{18,... | collective-permute-start | bytes 196616 | tf_op jit(solution)/shard_map/ppermute | solution.py:24
  74.7 4.3 collective-permute-start.6
  172.8 22.4 %collective-permute-start.8 = (f32[16,1,64,256]{3,0,2,1:T(8,128)S(1)}, f32[16,1,64,256]{3,0,2,1:T(8,128)S(1)}, u32[]{:S(2)}, u32[]{:S(2)}) collective-permute-start(f32[16,1,64,256]{3,0,2,1:T(8,128)S(1)} %get-tuple-element.32), channel_id=1, source_target_pairs={{2,0},{4,2},{6,4},{8,6},{10,8},{12,10},{14,12},{3,1},{5,3},{7,5},{... | collective-permute-start | bytes 3145736 | tf_op jit(solution)/shard_map/ppermute | solution.py:26
  174.1 39.1 %collective-permute-start.9 = (f32[16,1,64,256]{3,0,2,1:T(8,128)S(1)}, f32[16,1,64,256]{3,0,2,1:T(8,128)S(1)}, u32[]{:S(2)}, u32[]{:S(2)}) collective-permute-start(f32[16,1,64,256]{3,0,2,1:T(8,128)S(1)} %get-tuple-element.31), channel_id=1, source_target_pairs={{0,2},{2,4},{4,6},{6,8},{8,10},{10,12},{12,14},{1,3},{3,5},{5,7},{... | collective-permute-start | bytes 3145736 | tf_op jit(solution)/shard_map/ppermute | solution.py:24
  213.3 9.0 %collective-permute-start.11 = (f32[16,4,1,256]{3,0,2,1:T(8,128)S(1)}, f32[16,4,1,256]{3,0,2,1:T(8,128)S(1)}, u32[]{:S(2)}, u32[]{:S(2)}) collective-permute-start(f32[16,4,1,256]{3,0,2,1:T(8,128)S(1)} %get-tuple-element.22), channel_id=1, source_target_pairs={{0,1},{2,3},{4,5},{6,7},{8,9},{10,11},{12,13},{14,15},{16,17},{18,... | collective-permute-start | bytes 196616 | tf_op jit(solution)/shard_map/ppermute | solution.py:24
  215.2 7.1 %collective-permute-start.10 = (f32[16,4,1,256]{3,0,2,1:T(8,128)S(1)}, f32[16,4,1,256]{3,0,2,1:T(8,128)S(1)}, u32[]{:S(2)}, u32[]{:S(2)}) collective-permute-start(f32[16,4,1,256]{3,0,2,1:T(8,128)S(1)} %get-tuple-element.21), channel_id=1, source_target_pairs={{1,0},{3,2},{5,4},{7,6},{9,8},{11,10},{13,12},{15,14},{17,16},{19,... | collective-permute-start | bytes 196616 | tf_op jit(solution)/shard_map/ppermute | solution.py:26
  319.4 6.2 %copy-start.2 = (f32[2,8,128,256]{3,2,1,0:T(8,128)S(1)}, f32[2,8,128,256]{3,2,1,0:T(8,128)}, u32[]{:S(2)}) copy-start(f32[2,8,128,256]{3,2,1,0:T(8,128)} %copy.97) | copy-start | bytes 6291460
  319.6 22.6 %collective-permute-start.12 = (f32[16,1,64,256]{3,0,2,1:T(8,128)S(1)}, f32[16,1,64,256]{3,0,2,1:T(8,128)S(1)}, u32[]{:S(2)}, u32[]{:S(2)}) collective-permute-start(f32[16,1,64,256]{3,0,2,1:T(8,128)S(1)} %get-tuple-element.28), channel_id=1, source_target_pairs={{2,0},{4,2},{6,4},{8,6},{10,8},{12,10},{14,12},{3,1},{5,3},{7,5},{... | collective-permute-start | bytes 3145736 | tf_op jit(solution)/shard_map/ppermute | solution.py:26
  321.0 39.1 %collective-permute-start.13 = (f32[16,1,64,256]{3,0,2,1:T(8,128)S(1)}, f32[16,1,64,256]{3,0,2,1:T(8,128)S(1)}, u32[]{:S(2)}, u32[]{:S(2)}) collective-permute-start(f32[16,1,64,256]{3,0,2,1:T(8,128)S(1)} %get-tuple-element.27), channel_id=1, source_target_pairs={{0,2},{2,4},{4,6},{6,8},{8,10},{10,12},{12,14},{1,3},{3,5},{5,7},{... | collective-permute-start | bytes 3145736 | tf_op jit(solution)/shard_map/ppermute | solution.py:24
  330.6 32.8 %copy-start.1 = (f32[16,2,64,256]{3,0,2,1:T(8,128)S(1)}, f32[16,2,64,256]{3,0,2,1:T(8,128)}, u32[]{:S(2)}) copy-start(f32[16,2,64,256]{3,0,2,1:T(8,128)} %fusion.68) | copy-start | bytes 6291460
  360.1 8.5 %collective-permute-start.15 = (f32[16,4,1,256]{3,0,2,1:T(8,128)S(1)}, f32[16,4,1,256]{3,0,2,1:T(8,128)S(1)}, u32[]{:S(2)}, u32[]{:S(2)}) collective-permute-start(f32[16,4,1,256]{3,0,2,1:T(8,128)S(1)} %get-tuple-element.20), channel_id=1, source_target_pairs={{0,1},{2,3},{4,5},{6,7},{8,9},{10,11},{12,13},{14,15},{16,17},{18,... | collective-permute-start | bytes 196616 | tf_op jit(solution)/shard_map/ppermute | solution.py:24
  362.0 6.6 %collective-permute-start.14 = (f32[16,4,1,256]{3,0,2,1:T(8,128)S(1)}, f32[16,4,1,256]{3,0,2,1:T(8,128)S(1)}, u32[]{:S(2)}, u32[]{:S(2)}) collective-permute-start(f32[16,4,1,256]{3,0,2,1:T(8,128)S(1)} %get-tuple-element.19), channel_id=1, source_target_pairs={{1,0},{3,2},{5,4},{7,6},{9,8},{11,10},{13,12},{15,14},{17,16},{19,... | collective-permute-start | bytes 196616 | tf_op jit(solution)/shard_map/ppermute | solution.py:26
  371.9 1.3 copy-start.4
  443.1 4.6 copy-start.3
  443.1 4.6 copy-start.6
  453.4 2.5 copy-start.5
where the time goes:
time: 469 us; the launch traced here: 463 us
  blocking collectives  186 us (40%)
  waiting for transfers between devices  109 us (23%)
  matrix products  68.6 us (15%)
  starting transfers between devices  39.7 us (8%)
  other arithmetic  33.3 us (7%)
  local copies, waits for them, and re-layouts  24.9 us (5%)
    psum x3, blocking collectives, on_device(): lax.psum((gram(residual, scaled), gram(direction, image), gram(scaled, im...  186 us
    ppermute x8, waiting for transfers between devices, extended_2(): lax.ppermute(tail, axis, [(i, (i + 1) % count) for i in range(ends)])  62.3 us
    ppermute x8, waiting for transfers between devices, extended_2(): lax.ppermute(head, axis, [((i + 1) % count, i) for i in range(ends)])  46.3 us
    dot_general x8, matrix products, combine(): lax.dot_general(weights, flat, (((0,), (0,)), ((), ())), precision=highest)  38.8 us
    ppermute x8, starting transfers between devices, extended_2(): lax.ppermute(tail, axis, [(i, (i + 1) % count) for i in range(ends)])  28.6 us
    dot_general x9, matrix products, gram(): lax.dot_general(left_flat, right_flat, (((1,), (1,)), ((), ())), precisio...  26.8 us
    unnamed x22, local copies, waits for them, and re-layouts  21.5 us
    ppermute x8, starting transfers between devices, extended_2(): lax.ppermute(head, axis, [((i + 1) % count, i) for i in range(ends)])  11.1 us
  transfers between devices with their start and end apart: 16, of which 9 were waited for; matrix products, arithmetic and copies ran while one was open for 5% of the time, Pallas kernels for 0%

commit v1 on v0

v1 whole, which is shorter than its diff:
```python
import math
from functools import partial

import jax
import jax.numpy as jnp
from jax import lax
from jax.experimental import pallas as pl
from jax.experimental.pallas import tpu as pltpu
from jax.sharding import PartitionSpec as P

NCLASS = 8
ITERS = 3
REACH = ITERS

contrast_log = 4.0 * math.log(10.0)
highest = lax.Precision.HIGHEST
f32 = jnp.float32
bf16 = jnp.bfloat16


def shifted(block, axis, step):
    count = lax.axis_size(axis)
    pairs = [(i, i + step) for i in range(count) if 0 <= i + step < count]
    return lax.ppermute(block, axis, pairs)


def with_rows(block, dim, width):
    size = block.shape[dim]
    head = lax.slice_in_dim(block, 0, width, axis=dim)
    tail = lax.slice_in_dim(block, size - width, size, axis=dim)
    return jnp.concatenate(
        [shifted(tail, "gy", 1), block, shifted(head, "gy", -1)], axis=dim
    )


def all_sum(values, axes):
    for axis in axes:
        count = lax.axis_size(axis)
        if count & (count - 1):
            values = lax.psum(values, axis)
            continue
        step = 1
        while step < count:
            values = values + lax.ppermute(values, axis, [(i, i ^ step) for i in range(count)])
            step *= 2
    return values


def face_of(center, beside):
    return jnp.where(beside > 0.0, 2.0 * center * beside / (center + beside), center)


def symmetric_operator(coef, inner):
    def pad_x(a, forward):
        return jnp.pad(a[..., 1:], ((0, 0), (0, 0), (0, 1))) if forward else jnp.pad(a[..., :-1], ((0, 0), (0, 0), (1, 0)))

    center = coef[1:-1, 1:-1]
    here = inner[1:-1, 1:-1]
    total = jnp.zeros_like(center)
    for beside in (
        coef[2:, 1:-1], coef[:-2, 1:-1], coef[1:-1, 2:], coef[1:-1, :-2], pad_x(center, True), pad_x(center, False)
    ):
        total = total + face_of(center, beside)
    diagonal = here * total + (1.0 - here)
    root = jnp.sqrt(diagonal)
    inverse = 1.0 / root
    masked = here * inverse

    def coupling(a, b, ma, mb):
        return ma * face_of(a, b) * mb

    along_x = coupling(center, pad_x(center, True), masked, pad_x(masked, True))
    along_y = coupling(center[:, :-1], center[:, 1:], masked[:, :-1], masked[:, 1:])
    along_z = coupling(center[:-1], center[1:], masked[:-1], masked[1:])
    return root, inverse, along_x, along_y, along_z


def powers_kernel(
    rows, lo2, lo1, own, hi1, hi2, inverse, sx, sy, sz, moments, split, u0, u1, u2, u3
):
    first = REACH
    scaled = (u0, u1, u2, u3)
    pieces = [(lo2, 0), (lo1, 0), (lo1, 1), (own, 0), (own, 1), (hi1, 0), (hi1, 1), (hi2, 0)]
    depth = own.shape[0]
    planes = len(pieces)

    def distance(plane):
        return max(first - plane, plane - (first + depth - 1), 0)

    for plane, (piece, index) in enumerate(pieces):
        reach = REACH - distance(plane)

        def scale_row(y, carry, plane=plane, piece=piece, index=index):
            u0[plane, y] = piece[index, y] * inverse[plane, pl.ds(y, 1), :]
            return carry

        lax.fori_loop(first - reach, first + rows + reach, scale_row, 0, unroll=2)

    for power in range(1, REACH + 1):
        src, dst = scaled[power - 1], scaled[power]
        for plane in range(planes):
            reach = REACH - power - distance(plane)
            if reach < 0:
                continue

            def apply_row(y, carry, plane=plane, src=src, dst=dst):
                here = src[plane, y]
                ahead = sx[plane, pl.ds(y, 1), :]
                width = here.shape[-1]
                total = ahead * pltpu.roll(here, width - 1, 1) + pltpu.roll(ahead * here, 1, 1)
                total += sy[plane, pl.ds(y, 1), :] * src[plane, y + 1]
                total += sy[plane, pl.ds(y - 1, 1), :] * src[plane, y - 1]
                total += sz[plane, pl.ds(y, 1), :] * src[plane + 1, y]
                total += sz[plane - 1, pl.ds(y, 1), :] * src[plane - 1, y]
                dst[plane, y] = total
                return carry

            lax.fori_loop(first - reach, first + rows + reach, apply_row, 0, unroll=2)

    rhs = own.shape[2]
    height = rhs * (REACH + 1)

    def gram_rows(block, total):
        plane = block // (rows // 4)
        start = (block % (rows // 4)) * 4
        parts = []
        for j in range(4):
            stack = jnp.concatenate([u[plane + first, start + j + first] for u in scaled], axis=0)
            high = stack.astype(bf16)
            low = (stack - high.astype(f32)).astype(bf16)
            both = jnp.concatenate([high, low], axis=0)
            split[plane, start + j] = both
            parts.append(both)
        wide = jnp.concatenate(parts, axis=1)
        return total + lax.dot_general(wide, wide, (((1,), (1,)), ((), ())), preferred_element_type=f32)

    gram = lax.fori_loop(0, depth * rows // 4, gram_rows, jnp.zeros((2 * height, 2 * height), f32))
    gram = gram[:height] + gram[height:]
    gram = gram[:, :height] + gram[:, height:]
    blocks = []
    for power in range(2 * REACH):
        i = power // 2
        j = power - i
        blocks.append(gram[i * rhs : (i + 1) * rhs, j * rhs : (j + 1) * rhs])
    blocks.append(jnp.zeros((rhs, moments.shape[1] - rhs * len(blocks)), f32))
    moments[...] = jnp.concatenate(blocks, axis=1)


def eliminate(stacked, size):
    lane = lax.broadcasted_iota(jnp.int32, (1, size), 1)
    for k in range(size):
        row = stacked[k : k + 1, :]
        column = stacked[:, k : k + 1] * (1.0 / stacked[k : k + 1, k : k + 1])
        stacked = jnp.where(lane == k, column, stacked - column * row)
    return stacked[size:]


def mixing(moments, rhs):
    width = moments.shape[1]
    lane = lax.broadcasted_iota(jnp.int32, (rhs, width), 1)

    def hankel(first, degree):
        rows = []
        for i in range(degree):
            shifted_by = (i + first) * rhs
            rows.append(pltpu.roll(moments, width - shifted_by, 1) if shifted_by else moments)
        rows.append(jnp.zeros((width - degree * rhs, width), f32))
        return jnp.concatenate(rows, axis=0)

    def product(a, b):
        return jnp.dot(a, b, precision=highest, preferred_element_type=f32)

    def quadratic(coefs, matrix):
        return lax.dot_general(
            product(coefs, matrix), coefs, (((1,), (1,)), ((), ())), precision=highest, preferred_element_type=f32
        )

    plain = hankel(0, REACH)
    energy = plain - hankel(1, REACH)
    eye = (lax.broadcasted_iota(jnp.int32, (rhs, rhs), 0) == lax.broadcasted_iota(jnp.int32, (rhs, rhs), 1)).astype(f32)
    direction = (lax.broadcasted_iota(jnp.int32, (rhs, width), 0) == lane).astype(f32)
    residual = direction
    solution_part = jnp.zeros((rhs, width), f32)
    rho = moments[:, :rhs]
    for iteration in range(ITERS):
        curvature = rho - moments[:, rhs : 2 * rhs] if iteration == 0 else quadratic(direction, energy)
        step = eliminate(jnp.concatenate([curvature, rho], axis=0), rhs)
        solution_part = solution_part + product(step, direction)
        image = direction - pltpu.roll(direction, rhs, 1)
        residual = residual - product(step, image)
        if iteration + 1 < ITERS:
            following = quadratic(residual, plain)
            inverse = eliminate(jnp.concatenate([rho, eye], axis=0), rhs)
            direction = residual + product(product(following, inverse), direction)
            rho = following
    return solution_part, residual


def outputs_kernel(moments, split, inverse, root, iterate, iterate_out, residual_out, coefs):
    rhs = iterate.shape[0]
    height = rhs * (REACH + 1)
    rows = split.shape[1]

    @pl.when((pl.program_id(0) == 0) & (pl.program_id(1) == 0))
    def _():
        solution_part, residual = mixing(moments[...], rhs)
        both = jnp.concatenate([solution_part[:, :height], residual[:, :height]], axis=0)
        high = both.astype(bf16).astype(f32)
        stacked = jnp.concatenate([high, both - high], axis=0)
        coefs[...] = jnp.concatenate([stacked, stacked], axis=1).astype(bf16)

    wide = jnp.concatenate([split[0, j] for j in range(rows)], axis=1)
    mixed = jnp.dot(coefs[...], wide, preferred_element_type=f32)
    mixed = mixed[: 2 * rhs] + mixed[2 * rhs :]
    nx = split.shape[-1]
    by_row = jnp.stack([mixed[:, j * nx : (j + 1) * nx] for j in range(rows)], axis=0)
    by_rhs = pltpu.einshape("abc->bac", by_row)
    iterate_out[:, 0] = iterate[:, 0] + by_rhs[:rhs] * inverse[...]
    residual_out[:, 0] = by_rhs[rhs:] * root[...]


def on_device(iterate, residual, labels, boundary):
    rhs, depth, rows, nx = residual.shape
    assert depth == 2 and REACH == 3
    coef = jnp.exp(labels.astype(f32) * (contrast_log / (NCLASS - 1)))
    inner = (1 - boundary).astype(f32)

    fields = with_rows(jnp.stack([coef, inner]), 2, REACH + 1)
    own = with_rows(jnp.transpose(residual, (1, 2, 0, 3)), 1, REACH)

    field_lo1 = shifted(fields, "gz", 1)
    field_hi1 = shifted(fields, "gz", -1)
    field_lo2 = shifted(fields, "gz", 2)
    field_hi2 = shifted(fields, "gz", -2)
    lo1 = shifted(own, "gz", 1)
    hi1 = shifted(own, "gz", -1)
    lo2 = shifted(own[1:], "gz", 2)
    hi2 = shifted(own[:1], "gz", -2)

    fields = jnp.concatenate([field_lo2, field_lo1, fields, field_hi1, field_hi2], axis=1)
    root, inverse, sx, sy, sz = symmetric_operator(fields[0], fields[1])

    planes = depth + 2 * REACH
    extended = rows + 2 * REACH
    vmem = pl.BlockSpec(memory_space=pltpu.VMEM)
    moments, split = pl.pallas_call(
        partial(powers_kernel, rows),
        out_shape=(
            jax.ShapeDtypeStruct((rhs, 128), f32),
            jax.ShapeDtypeStruct((depth, rows, 2 * rhs * (REACH + 1), nx), bf16),
        ),
        in_specs=[vmem] * 9,
        out_specs=(vmem, vmem),
        scratch_shapes=[pltpu.VMEM((planes, extended, rhs, nx), f32)] * 3
        + [pltpu.VMEM((planes, extended, rhs, nx), f32)],
        compiler_params=pltpu.CompilerParams(vmem_limit_bytes=62 * 2**20),
    )(lo2, lo1, own, hi1, hi2, inverse, sx, sy, sz)

    moments = all_sum(moments, ("gy", "gz"))

    inverse = inverse[REACH : REACH + depth, REACH : REACH + rows]
    root = root[REACH : REACH + depth, REACH : REACH + rows]
    tile = 8
    plane_rows = pl.BlockSpec((rhs, 1, tile, nx), lambda z, y: (0, z, y, 0))
    cell_rows = pl.BlockSpec((None, tile, nx), lambda z, y: (z, y, 0))
    return pl.pallas_call(
        outputs_kernel,
        grid=(depth, rows // tile),
        out_shape=(jax.ShapeDtypeStruct(iterate.shape, f32), jax.ShapeDtypeStruct(residual.shape, f32)),
        in_specs=[
            pl.BlockSpec((rhs, 128), lambda z, y: (0, 0)),
            pl.BlockSpec((1, tile) + split.shape[2:], lambda z, y: (z, y, 0, 0)),
            cell_rows,
            cell_rows,
            plane_rows,
        ],
        out_specs=(plane_rows, plane_rows),
        scratch_shapes=[pltpu.VMEM((4 * rhs, 2 * rhs * (REACH + 1)), bf16)],
        compiler_params=pltpu.CompilerParams(vmem_limit_bytes=32 * 2**20),
    )(moments, split, inverse, root, iterate)


def solution(mesh):
    placed = (
        P(None, ("regions", "gz"), "gy", None),
        P(None, ("regions", "gz"), "gy", None),
        P(("regions", "gz"), "gy", None),
        P(("regions", "gz"), "gy", None),
    )
    return jax.shard_map(
        on_device,
        mesh=mesh,
        in_specs=placed,
        out_specs=(P(None, ("regions", "gz"), "gy", None), P(None, ("regions", "gz"), "gy", None)),
        check_vma=False,
    )
```

time: 469 us -> 223 us (0.48); the launches traced: 463 us -> 222 us
  blocking collectives: 186 us -> 0 us
  matrix products: 68.6 us -> 0 us
  Pallas kernels: 0 us -> 67.6 us
  other arithmetic: 33.3 us -> 7.44 us
  waiting for transfers between devices: 109 us -> 91.4 us
  local copies, waits for them, and re-layouts: 24.9 us -> 11.1 us
    psum x3 -> x0, blocking collectives: 186 us -> none  [on_device(): lax.psum((gram(residual, scaled), gram(direction, image), gram(scaled, im...]
    pallas_call x0 -> x2, Pallas kernels: none -> 67.6 us  [the longest x1 52.8 us: on_device(): pl.pallas_call(partial(powers_kernel, rows), out_shape=(jax.ShapeDtypeStr...]
    dot_general x23 -> x0, matrix products: 66.7 us -> none  [the longest x8 38.8 us: combine(): lax.dot_general(weights, flat, (((0,), (0,)), ((), ())), precision=highest)]
    another operation x28 -> x4, other arithmetic: 21.8 us -> 1.88 us  [on_device(): fields = with_rows(jnp.stack([coef, inner]), 2, REACH + 1)]
    ppermute x16, waiting for transfers between devices: 109 us -> 91.4 us  [the longest x12 86.4 us: shifted(): return lax.ppermute(block, axis, pairs)]
    unnamed x22 -> x18, local copies, waits for them, and re-layouts: 21.5 us -> 9.34 us
    sub x3 -> x0, other arithmetic: 9.72 us -> none  [apply_operator(): return diagonal * center - coupled]
  transfers between devices with their start and end apart: 16 -> 16, of which waited for: 9 -> 9; matrix products, arithmetic and copies ran while one was open for 5% -> 4% of each run, Pallas kernels for 0% -> 0%
where the time goes in v1:
time: 223 us; the launch traced here: 222 us
  waiting for transfers between devices  91.4 us (41%)
  Pallas kernels  67.6 us (30%)
  starting transfers between devices  43.9 us (20%)
  local copies, waits for them, and re-layouts  11.1 us (5%)
  other arithmetic  7.44 us (3%)
    ppermute x12, waiting for transfers between devices, shifted(): return lax.ppermute(block, axis, pairs)  86.4 us
    pallas_call x1, Pallas kernels, on_device(): pl.pallas_call(partial(powers_kernel, rows), out_shape=(jax.ShapeDtypeStr...  52.8 us
    ppermute x12, starting transfers between devices, shifted(): return lax.ppermute(block, axis, pairs)  35.1 us
    pallas_call x1, Pallas kernels, on_device(): pl.pallas_call(outputs_kernel, grid=(depth, rows // tile), out_shape=(jax...  14.9 us
    unnamed x18, local copies, waits for them, and re-layouts  9.34 us
    ppermute x4, starting transfers between devices, all_sum(): lax.ppermute(values, axis, [(i, i ^ step) for i in range(count)])  8.78 us
    ppermute x4, waiting for transfers between devices, all_sum(): lax.ppermute(values, axis, [(i, i ^ step) for i in range(count)])  4.98 us
  transfers between devices with their start and end apart: 16, of which 9 were waited for; matrix products, arithmetic and copies ran while one was open for 4% of the time, Pallas kernels for 0%

profile of v1, /device:TPU:0, one launch (start us, length us, event | category | flops | bytes accessed | tf_op | source)
XLA Modules:
  0.0 222.3 jit_solution(8866079740640946571)
XLA Ops:
  0.6 0.9 exponential_bitcast_fusion
  1.6 0.9 convert_bitcast_fusion
  2.5 2.4 %collective-permute-start.6 = (f32[2,2,4,256]{3,2,1,0:T(4,128)S(1)}, f32[2,2,4,256]{3,2,1,0:T(4,128)S(1)}, u32[]{:S(2)}, u32[]{:S(2)}) collective-permute-start(f32[2,2,4,256]{3,2,1,0:T(4,128)S(1)} %get-tuple-element.16), channel_id=1, source_target_pairs={{0,1},{2,3},{4,5},{6,7},{8,9},{10,11},{12,13},{14,15},{16,17},{18,... | collective-permute-start | bytes 49160 | tf_op jit(solution)/shard_map/ppermute | solution.py:24
  4.9 1.3 collective-permute-start.7
  6.2 2.8 %copy.8 = f32[16,2,64,256]{3,0,2,1:T(8,128)S(1)} copy(f32[16,2,64,256]{3,2,1,0:T(8,128)} %param.5) | data formatting | bytes 4194304 | tf_op args[1]
  9.0 3.0 %collective-permute-start = (f32[2,3,16,256]{3,2,1,0:T(8,128)S(1)}, f32[2,3,16,256]{3,2,1,0:T(8,128)S(1)}, u32[]{:S(2)}, u32[]{:S(2)}) collective-permute-start(f32[2,3,16,256]{3,2,1,0:T(8,128)S(1)} %get-tuple-element.10), channel_id=1, source_target_pairs={{0,1},{2,3},{4,5},{6,7},{8,9},{10,11},{12,13},{14,15},{16,17},{18,... | collective-permute-start | bytes 294920 | tf_op jit(solution)/shard_map/ppermute | solution.py:24
  12.0 1.3 collective-permute-start.1
  13.4 0.0 collective-permute-done.6
  13.4 0.0 collective-permute-done.7
  13.4 1.3 collective-permute-start.11
  14.7 1.3 collective-permute-start.10
  16.0 4.9 %collective-permute-start.9 = (f32[2,2,72,256]{3,2,1,0:T(8,128)S(1)}, f32[2,2,72,256]{3,2,1,0:T(8,128)S(1)}, u32[]{:S(2)}, u32[]{:S(2)}) collective-permute-start(f32[2,2,72,256]{3,2,1,0:T(8,128)S(1)} %pad_maximum_fusion.2), channel_id=1, source_target_pairs={{0,2},{2,4},{4,6},{6,8},{8,10},{10,12},{12,14},{1,3},{3,5},{5,7},{... | collective-permute-start | bytes 884744 | tf_op jit(solution)/shard_map/ppermute | solution.py:24
  20.9 0.0 collective-permute-done
  20.9 4.6 %collective-permute-start.8 = (f32[2,2,72,256]{3,2,1,0:T(8,128)S(1)}, f32[2,2,72,256]{3,2,1,0:T(8,128)S(1)}, u32[]{:S(2)}, u32[]{:S(2)}) collective-permute-start(f32[2,2,72,256]{3,2,1,0:T(8,128)S(1)} %pad_maximum_fusion.2), channel_id=1, source_target_pairs={{0,4},{2,6},{4,8},{6,10},{8,12},{10,14},{1,5},{3,7},{5,9},{7,11},{... | collective-permute-start | bytes 884744 | tf_op jit(solution)/shard_map/ppermute | solution.py:24
  25.6 0.0 collective-permute-done.1
  25.6 0.2 pad_maximum_fusion.own
  25.8 0.0 copy-start.2
  25.8 1.3 collective-permute-start.4
  27.1 0.2 fusion.11
  27.3 5.2 %collective-permute-done.8 = f32[2,2,72,256]{3,2,1,0:T(8,128)S(1)} collective-permute-done((f32[2,2,72,256]{3,2,1,0:T(8,128)S(1)}, f32[2,2,72,256]{3,2,1,0:T(8,128)S(1)}, u32[]{:S(2)}, u32[]{:S(2)}) %collective-permute-start.8) | collective-permute-done | bytes 294944 | tf_op jit(solution)/shard_map/ppermute | solution.py:24
  32.5 0.0 copy-done.2
  32.5 6.9 %collective-permute-start.3 = (f32[2,70,16,256]{3,2,1,0:T(8,128)S(1)}, f32[2,70,16,256]{3,2,1,0:T(8,128)S(1)}, u32[]{:S(2)}, u32[]{:S(2)}) collective-permute-start(f32[2,70,16,256]{3,2,1,0:T(8,128)S(1)} %pad_maximum_fusion.own), channel_id=1, source_target_pairs={{0,2},{2,4},{4,6},{6,8},{8,10},{10,12},{12,14},{1,3},{3,5},{5,7},{... | collective-permute-start | bytes 6881288 | tf_op jit(solution)/shard_map/ppermute | solution.py:24
  39.5 44.1 %collective-permute-done.9 = f32[2,2,72,256]{3,2,1,0:T(8,128)S(1)} collective-permute-done((f32[2,2,72,256]{3,2,1,0:T(8,128)S(1)}, f32[2,2,72,256]{3,2,1,0:T(8,128)S(1)}, u32[]{:S(2)}, u32[]{:S(2)}) %collective-permute-start.9) | collective-permute-done | bytes 294944 | tf_op jit(solution)/shard_map/ppermute | solution.py:24
  83.6 1.3 collective-permute-start.5
  84.9 0.0 collective-permute-done.10
  85.0 5.5 %collective-permute-start.2 = (f32[1,70,16,256]{3,2,1,0:T(8,128)S(1)}, f32[1,70,16,256]{3,2,1,0:T(8,128)S(1)}, u32[]{:S(2)}, u32[]{:S(2)}) collective-permute-start(f32[1,70,16,256]{3,2,1,0:T(8,128)S(1)} %get-tuple-element.9), channel_id=1, source_target_pairs={{0,4},{2,6},{4,8},{6,10},{8,12},{10,14},{1,5},{3,7},{5,9},{7,11},{... | collective-permute-start | bytes 3440648 | tf_op jit(solution)/shard_map/ppermute | solution.py:24
  90.5 0.0 collective-permute-done.11
  90.5 0.1 slice_bitcast_fusion
  90.6 0.2 fusion.13
  90.9 1.2 slice_multiply_fusion.2
  92.0 0.2 slice.133
  92.3 1.0 slice_multiply_fusion.3.sz
  93.3 1.1 slice_multiply_fusion.sy
  94.4 1.3 pad_multiply_fusion
  95.7 18.0 %collective-permute-done.5.hi2 = f32[1,70,16,256]{3,2,1,0:T(8,128)S(1)} collective-permute-done((f32[1,70,16,256]{3,2,1,0:T(8,128)S(1)}, f32[1,70,16,256]{3,2,1,0:T(8,128)S(1)}, u32[]{:S(2)}, u32[]{:S(2)}) %collective-permute-start.5) | collective-permute-done | bytes 1146912 | tf_op jit(solution)/shard_map/ppermute | solution.py:24
  113.7 0.0 copy-start.5
  113.7 1.3 collective-permute-done.2.lo2
  114.9 0.0 copy-start.6
  114.9 0.0 collective-permute-done.4.hi1
  114.9 0.0 copy-start.3
  114.9 17.8 %collective-permute-done.3.lo1 = f32[2,70,16,256]{3,2,1,0:T(8,128)S(1)} collective-permute-done((f32[2,70,16,256]{3,2,1,0:T(8,128)S(1)}, f32[2,70,16,256]{3,2,1,0:T(8,128)S(1)}, u32[]{:S(2)}, u32[]{:S(2)}) %collective-permute-start.3) | collective-permute-done | bytes 2293792 | tf_op jit(solution)/shard_map/ppermute | solution.py:24
  132.7 0.0 copy-done.3
  132.7 0.0 copy-start.4
  132.8 0.0 copy-done.6
  132.8 1.5 copy-done.4
  134.2 0.0 copy-done.5
  134.2 52.8 %shard_map.59 = (f32[16,128]{1,0:T(8,128)}, bf16[2,64,128,256]{3,2,1,0:T(8,128)(2,1)}) custom-call(f32[1,70,16,256]{3,2,1,0:T(8,128)} %copy-done.6, f32[2,70,16,256]{3,2,1,0:T(8,128)} %copy-done.4, f32[2,70,16,256]{3,2,1,0:T(8,128)} %copy-done.2, f32[2,70,16,256]{3,2,1,0:T(8,128)} %copy-done.3, f32[1,70,16,256]{3,2,1,0:T(8,128)} %copy-done.5, ...), custom_call_target="tpu_custom_call" | custom-call | tf_op jit(solution)/shard_map/pallas_call | solution.py:246
  187.0 0.3 collective-permute-start.12
  187.3 1.0 collective-permute-done.12
  188.4 0.7 add.75
  189.1 2.5 %collective-permute-start.13 = (f32[16,128]{1,0:T(8,128)S(1)}, f32[16,128]{1,0:T(8,128)S(1)}, u32[]{:S(2)}, u32[]{:S(2)}) collective-permute-start(f32[16,128]{1,0:T(8,128)S(1)} %add.75), channel_id=1, source_target_pairs={{0,2},{2,0},{4,6},{6,4},{8,10},{10,8},{12,14},{14,12},{1,3},{3,1},... | collective-permute-start | bytes 24584 | tf_op jit(solution)/shard_map/ppermute | solution.py:44
  191.6 1.6 collective-permute-done.13
  193.2 2.8 %collective-permute-start.14 = (f32[16,128]{1,0:T(8,128)S(1)}, f32[16,128]{1,0:T(8,128)S(1)}, u32[]{:S(2)}, u32[]{:S(2)}) collective-permute-start(f32[16,128]{1,0:T(8,128)S(1)} %add.76), channel_id=1, source_target_pairs={{0,4},{2,6},{4,0},{6,2},{8,12},{10,14},{12,8},{14,10},{1,5},{3,7},... | collective-permute-start | bytes 24584 | tf_op jit(solution)/shard_map/ppermute | solution.py:44
  195.9 1.6 collective-permute-done.14
  197.6 3.2 %collective-permute-start.15 = (f32[16,128]{1,0:T(8,128)S(1)}, f32[16,128]{1,0:T(8,128)S(1)}, u32[]{:S(2)}, u32[]{:S(2)}) collective-permute-start(f32[16,128]{1,0:T(8,128)S(1)} %add.77), channel_id=1, source_target_pairs={{0,8},{2,10},{4,12},{6,14},{8,0},{10,2},{12,4},{14,6},{1,9},{3,11}... | collective-permute-start | bytes 24584 | tf_op jit(solution)/shard_map/ppermute | solution.py:44
  200.8 0.9 slice.142.inverse
  201.7 0.7 collective-permute-done.15
  202.4 0.0 copy-start
  202.4 3.4 %copy-done = bf16[2,64,128,256]{3,2,1,0:T(8,128)(2,1)S(1)} copy-done((bf16[2,64,128,256]{3,2,1,0:T(8,128)(2,1)S(1)}, bf16[2,64,128,256]{3,2,1,0:T(8,128)(2,1)}, u32[]{:S(2)}) %copy-start) | copy-done | bytes 8388632
  205.8 0.0 copy-start.1
  205.8 1.6 copy-done.1
  207.4 14.9 %shard_map.60 = (f32[16,2,64,256]{3,2,1,0:T(8,128)}, f32[16,2,64,256]{3,2,1,0:T(8,128)}) custom-call(f32[16,128]{1,0:T(8,128)S(1)} %add.78.moments, bf16[2,64,128,256]{3,2,1,0:T(8,128)(2,1)S(1)} %copy-done, f32[2,64,256]{2,1,0:T(8,128)S(1)} %slice.142.inverse, f32[2,64,256]{2,1,0:T(8,128)S(1)} %slice.143.root, f32[16,2,64,256]{3,2,1,0:T(8,128)S(1)} %copy-done.1), custom_call_target="tpu_custom_call" | custom-call | tf_op jit(solution)/shard_map/pallas_call | solution.py:266
  (13 shorter events, 0.2 us)
Async XLA Ops:
  2.5 10.9 %collective-permute-start.6 = (f32[2,2,4,256]{3,2,1,0:T(4,128)S(1)}, f32[2,2,4,256]{3,2,1,0:T(4,128)S(1)}, u32[]{:S(2)}, u32[]{:S(2)}) collective-permute-start(f32[2,2,4,256]{3,2,1,0:T(4,128)S(1)} %get-tuple-element.16), channel_id=1, source_target_pairs={{0,1},{2,3},{4,5},{6,7},{8,9},{10,11},{12,13},{14,15},{16,17},{18,... | collective-permute-start | bytes 49160 | tf_op jit(solution)/shard_map/ppermute | solution.py:24
  4.9 8.5 %collective-permute-start.7 = (f32[2,2,4,256]{3,2,1,0:T(4,128)S(1)}, f32[2,2,4,256]{3,2,1,0:T(4,128)S(1)}, u32[]{:S(2)}, u32[]{:S(2)}) collective-permute-start(f32[2,2,4,256]{3,2,1,0:T(4,128)S(1)} %get-tuple-element.17), channel_id=1, source_target_pairs={{1,0},{3,2},{5,4},{7,6},{9,8},{11,10},{13,12},{15,14},{17,16},{19,... | collective-permute-start | bytes 49160 | tf_op jit(solution)/shard_map/ppermute | solution.py:24
  9.0 11.9 %collective-permute-start = (f32[2,3,16,256]{3,2,1,0:T(8,128)S(1)}, f32[2,3,16,256]{3,2,1,0:T(8,128)S(1)}, u32[]{:S(2)}, u32[]{:S(2)}) collective-permute-start(f32[2,3,16,256]{3,2,1,0:T(8,128)S(1)} %get-tuple-element.10), channel_id=1, source_target_pairs={{0,1},{2,3},{4,5},{6,7},{8,9},{10,11},{12,13},{14,15},{16,17},{18,... | collective-permute-start | bytes 294920 | tf_op jit(solution)/shard_map/ppermute | solution.py:24
  12.0 13.5 %collective-permute-start.1 = (f32[2,3,16,256]{3,2,1,0:T(8,128)S(1)}, f32[2,3,16,256]{3,2,1,0:T(8,128)S(1)}, u32[]{:S(2)}, u32[]{:S(2)}) collective-permute-start(f32[2,3,16,256]{3,2,1,0:T(8,128)S(1)} %get-tuple-element.11), channel_id=1, source_target_pairs={{1,0},{3,2},{5,4},{7,6},{9,8},{11,10},{13,12},{15,14},{17,16},{19,... | collective-permute-start | bytes 294920 | tf_op jit(solution)/shard_map/ppermute | solution.py:24
  13.4 77.1 %collective-permute-start.11 = (f32[2,2,72,256]{3,2,1,0:T(8,128)S(1)}, f32[2,2,72,256]{3,2,1,0:T(8,128)S(1)}, u32[]{:S(2)}, u32[]{:S(2)}) collective-permute-start(f32[2,2,72,256]{3,2,1,0:T(8,128)S(1)} %pad_maximum_fusion.2), channel_id=1, source_target_pairs={{4,0},{6,2},{8,4},{10,6},{12,8},{14,10},{5,1},{7,3},{9,5},{11,7},{... | collective-permute-start | bytes 884744 | tf_op jit(solution)/shard_map/ppermute | solution.py:24
  14.7 70.2 %collective-permute-start.10 = (f32[2,2,72,256]{3,2,1,0:T(8,128)S(1)}, f32[2,2,72,256]{3,2,1,0:T(8,128)S(1)}, u32[]{:S(2)}, u32[]{:S(2)}) collective-permute-start(f32[2,2,72,256]{3,2,1,0:T(8,128)S(1)} %pad_maximum_fusion.2), channel_id=1, source_target_pairs={{2,0},{4,2},{6,4},{8,6},{10,8},{12,10},{14,12},{3,1},{5,3},{7,5},{... | collective-permute-start | bytes 884744 | tf_op jit(solution)/shard_map/ppermute | solution.py:24
  16.0 67.6 %collective-permute-start.9 = (f32[2,2,72,256]{3,2,1,0:T(8,128)S(1)}, f32[2,2,72,256]{3,2,1,0:T(8,128)S(1)}, u32[]{:S(2)}, u32[]{:S(2)}) collective-permute-start(f32[2,2,72,256]{3,2,1,0:T(8,128)S(1)} %pad_maximum_fusion.2), channel_id=1, source_target_pairs={{0,2},{2,4},{4,6},{6,8},{8,10},{10,12},{12,14},{1,3},{3,5},{5,7},{... | collective-permute-start | bytes 884744 | tf_op jit(solution)/shard_map/ppermute | solution.py:24
  20.9 11.6 %collective-permute-start.8 = (f32[2,2,72,256]{3,2,1,0:T(8,128)S(1)}, f32[2,2,72,256]{3,2,1,0:T(8,128)S(1)}, u32[]{:S(2)}, u32[]{:S(2)}) collective-permute-start(f32[2,2,72,256]{3,2,1,0:T(8,128)S(1)} %pad_maximum_fusion.2), channel_id=1, source_target_pairs={{0,4},{2,6},{4,8},{6,10},{8,12},{10,14},{1,5},{3,7},{5,9},{7,11},{... | collective-permute-start | bytes 884744 | tf_op jit(solution)/shard_map/ppermute | solution.py:24
  25.8 6.7 %copy-start.2 = (f32[2,70,16,256]{3,2,1,0:T(8,128)}, f32[2,70,16,256]{3,2,1,0:T(8,128)S(1)}, u32[]{:S(2)}) copy-start(f32[2,70,16,256]{3,2,1,0:T(8,128)S(1)} %pad_maximum_fusion.own) | copy-start | bytes 6881284
  25.8 89.1 %collective-permute-start.4 = (f32[2,70,16,256]{3,2,1,0:T(8,128)S(1)}, f32[2,70,16,256]{3,2,1,0:T(8,128)S(1)}, u32[]{:S(2)}, u32[]{:S(2)}) collective-permute-start(f32[2,70,16,256]{3,2,1,0:T(8,128)S(1)} %pad_maximum_fusion.own), channel_id=1, source_target_pairs={{2,0},{4,2},{6,4},{8,6},{10,8},{12,10},{14,12},{3,1},{5,3},{7,5},{... | collective-permute-start | bytes 6881288 | tf_op jit(solution)/shard_map/ppermute | solution.py:24
  32.5 100.2 %collective-permute-start.3 = (f32[2,70,16,256]{3,2,1,0:T(8,128)S(1)}, f32[2,70,16,256]{3,2,1,0:T(8,128)S(1)}, u32[]{:S(2)}, u32[]{:S(2)}) collective-permute-start(f32[2,70,16,256]{3,2,1,0:T(8,128)S(1)} %pad_maximum_fusion.own), channel_id=1, source_target_pairs={{0,2},{2,4},{4,6},{6,8},{8,10},{10,12},{12,14},{1,3},{3,5},{5,7},{... | collective-permute-start | bytes 6881288 | tf_op jit(solution)/shard_map/ppermute | solution.py:24
  83.6 30.1 %collective-permute-start.5 = (f32[1,70,16,256]{3,2,1,0:T(8,128)S(1)}, f32[1,70,16,256]{3,2,1,0:T(8,128)S(1)}, u32[]{:S(2)}, u32[]{:S(2)}) collective-permute-start(f32[1,70,16,256]{3,2,1,0:T(8,128)S(1)} %get-tuple-element.8), channel_id=1, source_target_pairs={{4,0},{6,2},{8,4},{10,6},{12,8},{14,10},{5,1},{7,3},{9,5},{11,7},{... | collective-permute-start | bytes 3440648 | tf_op jit(solution)/shard_map/ppermute | solution.py:24
  85.0 30.0 %collective-permute-start.2 = (f32[1,70,16,256]{3,2,1,0:T(8,128)S(1)}, f32[1,70,16,256]{3,2,1,0:T(8,128)S(1)}, u32[]{:S(2)}, u32[]{:S(2)}) collective-permute-start(f32[1,70,16,256]{3,2,1,0:T(8,128)S(1)} %get-tuple-element.9), channel_id=1, source_target_pairs={{0,4},{2,6},{4,8},{6,10},{8,12},{10,14},{1,5},{3,7},{5,9},{7,11},{... | collective-permute-start | bytes 3440648 | tf_op jit(solution)/shard_map/ppermute | solution.py:24
  113.7 20.6 %copy-start.5 = (f32[1,70,16,256]{3,2,1,0:T(8,128)}, f32[1,70,16,256]{3,2,1,0:T(8,128)S(1)}, u32[]{:S(2)}) copy-start(f32[1,70,16,256]{3,2,1,0:T(8,128)S(1)} %collective-permute-done.5.hi2) | copy-start | bytes 3440644
  114.9 17.8 %copy-start.6 = (f32[1,70,16,256]{3,2,1,0:T(8,128)}, f32[1,70,16,256]{3,2,1,0:T(8,128)S(1)}, u32[]{:S(2)}) copy-start(f32[1,70,16,256]{3,2,1,0:T(8,128)S(1)} %collective-permute-done.2.lo2) | copy-start | bytes 3440644
  114.9 17.8 %copy-start.3 = (f32[2,70,16,256]{3,2,1,0:T(8,128)}, f32[2,70,16,256]{3,2,1,0:T(8,128)S(1)}, u32[]{:S(2)}) copy-start(f32[2,70,16,256]{3,2,1,0:T(8,128)S(1)} %collective-permute-done.4.hi1) | copy-start | bytes 6881284
  132.7 1.5 copy-start.4
  187.0 1.4 collective-permute-start.12
  189.1 4.1 %collective-permute-start.13 = (f32[16,128]{1,0:T(8,128)S(1)}, f32[16,128]{1,0:T(8,128)S(1)}, u32[]{:S(2)}, u32[]{:S(2)}) collective-permute-start(f32[16,128]{1,0:T(8,128)S(1)} %add.75), channel_id=1, source_target_pairs={{0,2},{2,0},{4,6},{6,4},{8,10},{10,8},{12,14},{14,12},{1,3},{3,1},... | collective-permute-start | bytes 24584 | tf_op jit(solution)/shard_map/ppermute | solution.py:44
  193.2 4.4 %collective-permute-start.14 = (f32[16,128]{1,0:T(8,128)S(1)}, f32[16,128]{1,0:T(8,128)S(1)}, u32[]{:S(2)}, u32[]{:S(2)}) collective-permute-start(f32[16,128]{1,0:T(8,128)S(1)} %add.76), channel_id=1, source_target_pairs={{0,4},{2,6},{4,0},{6,2},{8,12},{10,14},{12,8},{14,10},{1,5},{3,7},... | collective-permute-start | bytes 24584 | tf_op jit(solution)/shard_map/ppermute | solution.py:44
  197.6 4.8 %collective-permute-start.15 = (f32[16,128]{1,0:T(8,128)S(1)}, f32[16,128]{1,0:T(8,128)S(1)}, u32[]{:S(2)}, u32[]{:S(2)}) collective-permute-start(f32[16,128]{1,0:T(8,128)S(1)} %add.77), channel_id=1, source_target_pairs={{0,8},{2,10},{4,12},{6,14},{8,0},{10,2},{12,4},{14,6},{1,9},{3,11}... | collective-permute-start | bytes 24584 | tf_op jit(solution)/shard_map/ppermute | solution.py:44
  202.4 3.4 %copy-start = (bf16[2,64,128,256]{3,2,1,0:T(8,128)(2,1)S(1)}, bf16[2,64,128,256]{3,2,1,0:T(8,128)(2,1)}, u32[]{:S(2)}) copy-start(bf16[2,64,128,256]{3,2,1,0:T(8,128)(2,1)} %get-tuple-element.5.split) | copy-start | bytes 25165828
  205.8 1.6 copy-start.1

commit v2 on v1

--- a/solution.py
+++ b/solution.py
@@ -18,19 +18,33 @@
 bf16 = jnp.bfloat16
 
 
+def moved(block, axis, pairs):
+    return lax.ppermute(block, axis, pairs)
+
+
 def shifted(block, axis, step):
     count = lax.axis_size(axis)
-    pairs = [(i, i + step) for i in range(count) if 0 <= i + step < count]
-    return lax.ppermute(block, axis, pairs)
-
-
-def with_rows(block, dim, width):
-    size = block.shape[dim]
-    head = lax.slice_in_dim(block, 0, width, axis=dim)
-    tail = lax.slice_in_dim(block, size - width, size, axis=dim)
-    return jnp.concatenate(
-        [shifted(tail, "gy", 1), block, shifted(head, "gy", -1)], axis=dim
-    )
+    return moved(block, axis, [(i, i + step) for i in range(count) if 0 <= i + step < count])
+
+
+def swapped(block):
+    return moved(block, "gz", [(i, i ^ 1) for i in range(lax.axis_size("gz"))])
+
+
+def relayed(block):
+    count = lax.axis_size("gz")
+    steps = [(i, i + 2 - 4 * (i % 2)) for i in range(count)]
+    return moved(block, "gz", [(i, j) for i, j in steps if 0 <= j < count])
+
+
+def rows_beside(before, after):
+    count = lax.axis_size("gy")
+    if count != 2:
+        return shifted(after, "gy", 1), shifted(before, "gy", -1)
+    second = lax.axis_index("gy") == 1
+    other = moved(jnp.where(second, before, after), "gy", [(0, 1), (1, 0)])
+    zero = jnp.zeros_like(other)
+    return jnp.where(second, other, zero), jnp.where(second, zero, other)
 
 
 def all_sum(values, axes):
@@ -75,12 +89,22 @@
     return root, inverse, along_x, along_y, along_z
 
 
+def row_blocks(start, stop, body, size=8):
+    blocks = -(-(stop - start) // size)
+
+    def step(block, carry):
+        body(jnp.minimum(start + block * size, stop - size))
+        return carry
+
+    lax.fori_loop(0, blocks, step, 0)
+
+
 def powers_kernel(
-    rows, lo2, lo1, own, hi1, hi2, inverse, sx, sy, sz, moments, split, u0, u1, u2, u3
+    rows, lo3, lo2, lo1, own, hi1, hi2, hi3, inverse, sx, sy, sz, moments, split, u0, u1, u2, u3
 ):
     first = REACH
     scaled = (u0, u1, u2, u3)
-    pieces = [(lo2, 0), (lo1, 0), (lo1, 1), (own, 0), (own, 1), (hi1, 0), (hi1, 1), (hi2, 0)]
+    pieces = [(lo3, 0), (lo2, 0), (lo1, 0), (own, 0), (own, 1), (hi1, 0), (hi2, 0), (hi3, 0)]
     depth = own.shape[0]
     planes = len(pieces)
 
@@ -89,12 +113,13 @@
 
     for plane, (piece, index) in enumerate(pieces):
         reach = REACH - distance(plane)
-
-        def scale_row(y, carry, plane=plane, piece=piece, index=index):
-            u0[plane, y] = piece[index, y] * inverse[plane, pl.ds(y, 1), :]
-            return carry
-
-        lax.fori_loop(first - reach, first + rows + reach, scale_row, 0, unroll=2)
+        margin = (piece.shape[1] - rows) // 2
+
+        def scale_rows(y, plane=plane, piece=piece, index=index, margin=margin):
+            for j in range(8):
+                u0[plane, y + j] = piece[index, y + (j + margin - first)] * inverse[plane, pl.ds(y + j, 1), :]
+
+        row_blocks(first - reach, first + rows + reach, scale_rows)
 
     for power in range(1, REACH + 1):
         src, dst = scaled[power - 1], scaled[power]
@@ -103,19 +128,20 @@
             if reach < 0:
                 continue
 
-            def apply_row(y, carry, plane=plane, src=src, dst=dst):
-                here = src[plane, y]
-                ahead = sx[plane, pl.ds(y, 1), :]
-                width = here.shape[-1]
-                total = ahead * pltpu.roll(here, width - 1, 1) + pltpu.roll(ahead * here, 1, 1)
-                total += sy[plane, pl.ds(y, 1), :] * src[plane, y + 1]
-                total += sy[plane, pl.ds(y - 1, 1), :] * src[plane, y - 1]
-                total += sz[plane, pl.ds(y, 1), :] * src[plane + 1, y]
-                total += sz[plane - 1, pl.ds(y, 1), :] * src[plane - 1, y]
-                dst[plane, y] = total
-                return carry
-
-            lax.fori_loop(first - reach, first + rows + reach, apply_row, 0, unroll=2)
+            def apply_rows(start, plane=plane, src=src, dst=dst):
+                for j in range(8):
+                    y = start + j
+                    here = src[plane, y]
+                    ahead = sx[plane, pl.ds(y, 1), :]
+                    width = here.shape[-1]
+                    total = ahead * pltpu.roll(here, width - 1, 1) + pltpu.roll(ahead * here, 1, 1)
+                    total += sy[plane, pl.ds(y, 1), :] * src[plane, y + 1]
+                    total += sy[plane, pl.ds(y - 1, 1), :] * src[plane, y - 1]
+                    total += sz[plane, pl.ds(y, 1), :] * src[plane + 1, y]
+                    total += sz[plane - 1, pl.ds(y, 1), :] * src[plane - 1, y]
+                    dst[plane, y] = total
+
+            row_blocks(first - reach, first + rows + reach, apply_rows)
 
     rhs = own.shape[2]
     height = rhs * (REACH + 1)
@@ -225,17 +251,42 @@
     coef = jnp.exp(labels.astype(f32) * (contrast_log / (NCLASS - 1)))
     inner = (1 - boundary).astype(f32)
 
-    fields = with_rows(jnp.stack([coef, inner]), 2, REACH + 1)
-    own = with_rows(jnp.transpose(residual, (1, 2, 0, 3)), 1, REACH)
-
-    field_lo1 = shifted(fields, "gz", 1)
-    field_hi1 = shifted(fields, "gz", -1)
+    fields = jnp.stack([coef, inner])
+    own = jnp.transpose(residual, (1, 2, 0, 3))
+    odd = lax.axis_index("gz") % 2 == 1
+
+    wide = REACH + 1
+
+    ends = [
+        jnp.concatenate([own[:, a:b].reshape(-1, nx), fields[:, :, c:d].reshape(-1, nx)], axis=0)
+        for a, b, c, d in ((0, REACH, 0, wide), (rows - REACH, rows, rows - wide, rows))
+    ]
+    cut = depth * REACH * rhs
+    sides = [
+        (side[:cut].reshape(depth, REACH, rhs, nx), side[cut:].reshape(2, depth, wide, nx))
+        for side in rows_beside(*ends)
+    ]
+    fields = jnp.concatenate([sides[0][1], fields, sides[1][1]], axis=2)
+    core = own
+    own = jnp.concatenate([sides[0][0], own, sides[1][0]], axis=1)
+    sent = own[:, 1:-1]
+
+    field_pair = swapped(fields)
     field_lo2 = shifted(fields, "gz", 2)
     field_hi2 = shifted(fields, "gz", -2)
-    lo1 = shifted(own, "gz", 1)
-    hi1 = shifted(own, "gz", -1)
-    lo2 = shifted(own[1:], "gz", 2)
-    hi2 = shifted(own[:1], "gz", -2)
+    lo3 = shifted(core[1:], "gz", 2)
+    hi3 = shifted(core[:1], "gz", -2)
+    pair2 = swapped(jnp.where(odd, sent[1:], sent[:1]))
+    pair1 = swapped(jnp.where(odd, sent[:1], sent[1:]))
+    field_far = relayed(field_pair)
+    far1 = relayed(pair2)
+    far2 = relayed(pair1)
+    field_lo1 = jnp.where(odd, field_pair, field_far)
+    field_hi1 = jnp.where(odd, field_far, field_pair)
+    lo1 = jnp.where(odd, pair1, far1)
+    lo2 = jnp.where(odd, pair2, far2)
+    hi1 = jnp.where(odd, far1, pair1)
+    hi2 = jnp.where(odd, far2, pair2)
 
     fields = jnp.concatenate([field_lo2, field_lo1, fields, field_hi1, field_hi2], axis=1)
     root, inverse, sx, sy, sz = symmetric_operator(fields[0], fields[1])
@@ -249,12 +300,12 @@
             jax.ShapeDtypeStruct((rhs, 128), f32),
             jax.ShapeDtypeStruct((depth, rows, 2 * rhs * (REACH + 1), nx), bf16),
         ),
-        in_specs=[vmem] * 9,
+        in_specs=[vmem] * 11,
         out_specs=(vmem, vmem),
         scratch_shapes=[pltpu.VMEM((planes, extended, rhs, nx), f32)] * 3
         + [pltpu.VMEM((planes, extended, rhs, nx), f32)],
         compiler_params=pltpu.CompilerParams(vmem_limit_bytes=62 * 2**20),
-    )(lo2, lo1, own, hi1, hi2, inverse, sx, sy, sz)
+    )(lo3, lo2, lo1, own, hi1, hi2, hi3, inverse, sx, sy, sz)
 
     moments = all_sum(moments, ("gy", "gz"))
 

time: 223 us -> 188 us (0.84)
  Pallas kernels: 67.6 us -> 46 us
  waiting for transfers between devices: 91.4 us -> 81.7 us
  starting transfers between devices: 43.9 us -> 36.1 us
  other arithmetic: 7.44 us -> 11.9 us
    pallas_call x1, Pallas kernels: 52.8 us -> 31.1 us  [on_device(): pl.pallas_call(partial(powers_kernel, rows), out_shape=(jax.ShapeDtypeStr...]
    ppermute x12 -> x11, waiting for transfers between devices: 86.4 us -> 76.3 us  [moved(): return lax.ppermute(block, axis, pairs)]
    ppermute x12 -> x11, starting transfers between devices: 35.1 us -> 28 us  [moved(): return lax.ppermute(block, axis, pairs)]
    select_n x0 -> x5, other arithmetic: none -> 3.6 us  [the longest x1 1.71 us: on_device(): hi1 = jnp.where(odd, far1, pair1)]
    unnamed x18 -> x8, local copies, waits for them, and re-layouts: 9.34 us -> 7.81 us
  transfers between devices with their start and end apart: 16 -> 15, of which waited for: 9 -> 10; matrix products, arithmetic and copies ran while one was open for 4% -> 7% of each run, Pallas kernels for 0% -> 0%
where the time goes in v2:
time: 188 us; the launch traced here: 187 us
  waiting for transfers between devices  81.7 us (43%)
  Pallas kernels  46 us (24%)
  starting transfers between devices  36.1 us (19%)
  other arithmetic  11.9 us (6%)
  local copies, waits for them, and re-layouts  10.9 us (6%)
    ppermute x11, waiting for transfers between devices, moved(): return lax.ppermute(block, axis, pairs)  76.3 us
    pallas_call x1, Pallas kernels, on_device(): pl.pallas_call(partial(powers_kernel, rows), out_shape=(jax.ShapeDtypeStr...  31.1 us
    ppermute x11, starting transfers between devices, moved(): return lax.ppermute(block, axis, pairs)  28 us
    pallas_call x1, Pallas kernels, on_device(): pl.pallas_call(outputs_kernel, grid=(depth, rows // tile), out_shape=(jax...  14.9 us
    ppermute x4, starting transfers between devices, all_sum(): lax.ppermute(values, axis, [(i, i ^ step) for i in range(count)])  8.06 us
    unnamed x8, local copies, waits for them, and re-layouts  7.81 us
    ppermute x4, waiting for transfers between devices, all_sum(): lax.ppermute(values, axis, [(i, i ^ step) for i in range(count)])  5.32 us
  transfers between devices with their start and end apart: 15, of which 10 were waited for; matrix products, arithmetic and copies ran while one was open for 7% of the time, Pallas kernels for 0%

profile of v2, /device:TPU:0, one launch (start us, length us, event | category | flops | bytes accessed | tf_op | source)
XLA Modules:
  0.0 187.4 jit_solution(9666906112551685466)
XLA Ops:
  0.6 0.9 exponential_bitcast_fusion
  1.6 0.9 convert_bitcast_fusion
  2.5 2.8 %copy.8 = f32[16,2,64,256]{3,0,2,1:T(8,128)S(1)} copy(f32[16,2,64,256]{3,2,1,0:T(8,128)} %param.5) | data formatting | bytes 4194304 | tf_op args[1]
  5.4 0.5 collective-permute-start.1
  5.9 1.0 collective-permute-done.1
  7.0 2.9 %collective-permute-start.8 = (f32[2,2,72,256]{3,2,1,0:T(8,128)S(1)}, f32[2,2,72,256]{3,2,1,0:T(8,128)S(1)}, u32[]{:S(2)}, u32[]{:S(2)}) collective-permute-start(f32[2,2,72,256]{3,2,1,0:T(8,128)S(1)} %pad_maximum_fusion.2), channel_id=1, source_target_pairs={{0,2},{2,0},{4,6},{6,4},{8,10},{10,8},{12,14},{14,12},{1,3},{3,1},... | collective-permute-start | bytes 884744 | tf_op jit(solution)/shard_map/ppermute | solution.py:22
  9.9 1.5 fusion.11
  11.4 1.3 collective-permute-start.6
  12.7 5.5 %collective-permute-start = (f32[1,64,16,256]{3,2,1,0:T(8,128)}, f32[1,64,16,256]{3,2,1,0:T(8,128)}, u32[]{:S(2)}, u32[]{:S(2)}) collective-permute-start(f32[1,64,16,256]{3,2,1,0:T(8,128)} %get-tuple-element.15), channel_id=1, source_target_pairs={{0,4},{2,6},{4,8},{6,10},{8,12},{10,14},{1,5},{3,7},{5,9},{7,11},{... | collective-permute-start | bytes 3145736 | tf_op jit(solution)/shard_map/ppermute | solution.py:22
  18.3 1.3 collective-permute-start.10
  19.6 4.6 %collective-permute-start.7 = (f32[2,2,72,256]{3,2,1,0:T(8,128)S(1)}, f32[2,2,72,256]{3,2,1,0:T(8,128)S(1)}, u32[]{:S(2)}, u32[]{:S(2)}) collective-permute-start(f32[2,2,72,256]{3,2,1,0:T(8,128)S(1)} %pad_maximum_fusion.2), channel_id=1, source_target_pairs={{0,4},{2,6},{4,8},{6,10},{8,12},{10,14},{1,5},{3,7},{5,9},{7,11},{... | collective-permute-start | bytes 884744 | tf_op jit(solution)/shard_map/ppermute | solution.py:22
  24.2 0.2 pad_maximum_fusion.own
  24.4 0.0 copy-start.2
  24.4 0.0 collective-permute-done.8
  24.4 3.1 %collective-permute-start.9 = (f32[2,2,72,256]{3,2,1,0:T(8,128)S(1)}, f32[2,2,72,256]{3,2,1,0:T(8,128)S(1)}, u32[]{:S(2)}, u32[]{:S(2)}) collective-permute-start(f32[2,2,72,256]{3,2,1,0:T(8,128)S(1)} %collective-permute-done.8), channel_id=1, source_target_pairs={{0,4},{4,8},{6,2},{8,12},{10,6},{14,10},{1,5},{5,9},{7,3},{9,13},{... | collective-permute-start | bytes 884744 | tf_op jit(solution)/shard_map/ppermute | solution.py:22
  27.5 0.2 slice_select_fusion
  27.7 0.0 copy-done.2
  27.7 19.7 %collective-permute-done.7 = f32[2,2,72,256]{3,2,1,0:T(8,128)S(1)} collective-permute-done((f32[2,2,72,256]{3,2,1,0:T(8,128)S(1)}, f32[2,2,72,256]{3,2,1,0:T(8,128)S(1)}, u32[]{:S(2)}, u32[]{:S(2)}) %collective-permute-start.7) | collective-permute-done | bytes 294944 | tf_op jit(solution)/shard_map/ppermute | solution.py:22
  47.4 0.0 collective-permute-start.3
  47.4 4.9 %collective-permute-done.9 = f32[2,2,72,256]{3,2,1,0:T(8,128)S(1)} collective-permute-done((f32[2,2,72,256]{3,2,1,0:T(8,128)S(1)}, f32[2,2,72,256]{3,2,1,0:T(8,128)S(1)}, u32[]{:S(2)}, u32[]{:S(2)}) %collective-permute-start.9) | collective-permute-done | bytes 294944 | tf_op jit(solution)/shard_map/ppermute | solution.py:22
  52.3 0.0 collective-permute-start.2
  52.4 0.0 collective-permute-done.10
  52.4 0.1 slice_bitcast_fusion
  52.6 0.2 fusion.13
  52.8 22.1 %collective-permute-done.3 = f32[1,68,16,256]{3,2,1,0:T(8,128)S(1)} collective-permute-done((f32[1,68,16,256]{3,2,1,0:T(8,128)S(1)}, f32[1,68,16,256]{3,2,1,0:T(8,128)S(1)}, u32[]{:S(2)}, u32[]{:S(2)}) %collective-permute-start.3) | collective-permute-done | bytes 1114144 | tf_op jit(solution)/shard_map/ppermute | solution.py:22
  74.9 4.4 %collective-permute-start.4 = (f32[1,68,16,256]{3,2,1,0:T(8,128)S(1)}, f32[1,68,16,256]{3,2,1,0:T(8,128)S(1)}, u32[]{:S(2)}, u32[]{:S(2)}) collective-permute-start(f32[1,68,16,256]{3,2,1,0:T(8,128)S(1)} %collective-permute-done.3), channel_id=1, source_target_pairs={{0,4},{4,8},{6,2},{8,12},{10,6},{14,10},{1,5},{5,9},{7,3},{9,13},{... | collective-permute-start | bytes 3342344 | tf_op jit(solution)/shard_map/ppermute | solution.py:22
  79.3 1.2 slice_multiply_fusion.2
  80.5 1.1 slice_multiply_fusion.sy
  81.6 13.4 %collective-permute-done.2 = f32[1,68,16,256]{3,2,1,0:T(8,128)S(1)} collective-permute-done((f32[1,68,16,256]{3,2,1,0:T(8,128)S(1)}, f32[1,68,16,256]{3,2,1,0:T(8,128)S(1)}, u32[]{:S(2)}, u32[]{:S(2)}) %collective-permute-start.2) | collective-permute-done | bytes 1114144 | tf_op jit(solution)/shard_map/ppermute | solution.py:22
  95.0 4.4 %collective-permute-start.5 = (f32[1,68,16,256]{3,2,1,0:T(8,128)S(1)}, f32[1,68,16,256]{3,2,1,0:T(8,128)S(1)}, u32[]{:S(2)}, u32[]{:S(2)}) collective-permute-start(f32[1,68,16,256]{3,2,1,0:T(8,128)S(1)} %collective-permute-done.2), channel_id=1, source_target_pairs={{0,4},{4,8},{6,2},{8,12},{10,6},{14,10},{1,5},{5,9},{7,3},{9,13},{... | collective-permute-start | bytes 3342344 | tf_op jit(solution)/shard_map/ppermute | solution.py:22
  99.4 1.0 slice_multiply_fusion.3.sz
  100.4 0.9 broadcast_divide_fusion.inverse
  101.4 0.2 slice.168
  101.6 1.1 pad_multiply_fusion.sx
  102.7 0.0 collective-permute-done.4
  102.7 1.6 broadcast_select_fusion
  104.3 15.4 %collective-permute-done.5 = f32[1,68,16,256]{3,2,1,0:T(8,128)S(1)} collective-permute-done((f32[1,68,16,256]{3,2,1,0:T(8,128)S(1)}, f32[1,68,16,256]{3,2,1,0:T(8,128)S(1)}, u32[]{:S(2)}, u32[]{:S(2)}) %collective-permute-start.5) | collective-permute-done | bytes 1114144 | tf_op jit(solution)/shard_map/ppermute | solution.py:22
  119.7 1.7 broadcast_select_fusion.1
  121.4 0.0 collective-permute-done.6.hi3
  121.4 0.0 collective-permute-done.lo3
  121.4 31.1 %shard_map.59 = (f32[16,128]{1,0:T(8,128)}, bf16[2,64,128,256]{3,2,1,0:T(8,128)(2,1)}) custom-call(f32[1,64,16,256]{3,2,1,0:T(8,128)} %collective-permute-done.lo3, f32[1,68,16,256]{3,2,1,0:T(8,128)} %get-tuple-element.11.lo2, f32[1,68,16,256]{3,2,1,0:T(8,128)} %get-tuple-element.13.lo1, f32[2,70,16,256]{3,2,1,0:T(8,128)} %copy-done.2, ...), custom_call_target="tpu_custom_call" | custom-call | tf_op jit(solution)/shard_map/pallas_call | solution.py:297
  152.5 0.0 collective-permute-start.11
  152.5 1.4 collective-permute-done.11
  153.9 0.7 add.80
  154.6 2.1 %collective-permute-start.12 = (f32[16,128]{1,0:T(8,128)S(1)}, f32[16,128]{1,0:T(8,128)S(1)}, u32[]{:S(2)}, u32[]{:S(2)}) collective-permute-start(f32[16,128]{1,0:T(8,128)S(1)} %add.80), channel_id=1, source_target_pairs={{0,2},{2,0},{4,6},{6,4},{8,10},{10,8},{12,14},{14,12},{1,3},{3,1},... | collective-permute-start | bytes 24584 | tf_op jit(solution)/shard_map/ppermute | solution.py:58
  156.8 1.6 collective-permute-done.12
  158.4 2.4 %collective-permute-start.13 = (f32[16,128]{1,0:T(8,128)S(1)}, f32[16,128]{1,0:T(8,128)S(1)}, u32[]{:S(2)}, u32[]{:S(2)}) collective-permute-start(f32[16,128]{1,0:T(8,128)S(1)} %add.81), channel_id=1, source_target_pairs={{0,4},{2,6},{4,0},{6,2},{8,12},{10,14},{12,8},{14,10},{1,5},{3,7},... | collective-permute-start | bytes 24584 | tf_op jit(solution)/shard_map/ppermute | solution.py:58
  160.8 1.6 collective-permute-done.13
  162.4 3.6 %collective-permute-start.14 = (f32[16,128]{1,0:T(8,128)S(1)}, f32[16,128]{1,0:T(8,128)S(1)}, u32[]{:S(2)}, u32[]{:S(2)}) collective-permute-start(f32[16,128]{1,0:T(8,128)S(1)} %add.82), channel_id=1, source_target_pairs={{0,8},{2,10},{4,12},{6,14},{8,0},{10,2},{12,4},{14,6},{1,9},{3,11}... | collective-permute-start | bytes 24584 | tf_op jit(solution)/shard_map/ppermute | solution.py:58
  166.0 0.9 slice.177.inverse
  166.9 0.7 collective-permute-done.14
  167.6 0.0 copy-start
  167.6 3.4 %copy-done = bf16[2,64,128,256]{3,2,1,0:T(8,128)(2,1)S(1)} copy-done((bf16[2,64,128,256]{3,2,1,0:T(8,128)(2,1)S(1)}, bf16[2,64,128,256]{3,2,1,0:T(8,128)(2,1)}, u32[]{:S(2)}) %copy-start) | copy-done | bytes 8388632
  171.0 0.0 copy-start.1
  171.0 1.6 copy-done.1
  172.5 14.9 %shard_map.60 = (f32[16,2,64,256]{3,2,1,0:T(8,128)}, f32[16,2,64,256]{3,2,1,0:T(8,128)}) custom-call(f32[16,128]{1,0:T(8,128)S(1)} %add.83.moments, bf16[2,64,128,256]{3,2,1,0:T(8,128)(2,1)S(1)} %copy-done, f32[2,64,256]{2,1,0:T(8,128)S(1)} %slice.177.inverse, f32[2,64,256]{2,1,0:T(8,128)S(1)} %slice.178.root, f32[16,2,64,256]{3,2,1,0:T(8,128)S(1)} %copy-done.1), custom_call_target="tpu_custom_call" | custom-call | tf_op jit(solution)/shard_map/pallas_call | solution.py:317
  (23 shorter events, 0.4 us)
Async XLA Ops:
  5.4 1.5 collective-permute-start.1
  7.0 17.4 %collective-permute-start.8 = (f32[2,2,72,256]{3,2,1,0:T(8,128)S(1)}, f32[2,2,72,256]{3,2,1,0:T(8,128)S(1)}, u32[]{:S(2)}, u32[]{:S(2)}) collective-permute-start(f32[2,2,72,256]{3,2,1,0:T(8,128)S(1)} %pad_maximum_fusion.2), channel_id=1, source_target_pairs={{0,2},{2,0},{4,6},{6,4},{8,10},{10,8},{12,14},{14,12},{1,3},{3,1},... | collective-permute-start | bytes 884744 | tf_op jit(solution)/shard_map/ppermute | solution.py:22
  11.4 110.0 %collective-permute-start.6 = (f32[1,64,16,256]{3,2,1,0:T(8,128)}, f32[1,64,16,256]{3,2,1,0:T(8,128)}, u32[]{:S(2)}, u32[]{:S(2)}) collective-permute-start(f32[1,64,16,256]{3,2,1,0:T(8,128)} %get-tuple-element.14), channel_id=1, source_target_pairs={{4,0},{6,2},{8,4},{10,6},{12,8},{14,10},{5,1},{7,3},{9,5},{11,7},{... | collective-permute-start | bytes 3145736 | tf_op jit(solution)/shard_map/ppermute | solution.py:22
  12.7 108.7 %collective-permute-start = (f32[1,64,16,256]{3,2,1,0:T(8,128)}, f32[1,64,16,256]{3,2,1,0:T(8,128)}, u32[]{:S(2)}, u32[]{:S(2)}) collective-permute-start(f32[1,64,16,256]{3,2,1,0:T(8,128)} %get-tuple-element.15), channel_id=1, source_target_pairs={{0,4},{2,6},{4,8},{6,10},{8,12},{10,14},{1,5},{3,7},{5,9},{7,11},{... | collective-permute-start | bytes 3145736 | tf_op jit(solution)/shard_map/ppermute | solution.py:22
  18.3 34.1 %collective-permute-start.10 = (f32[2,2,72,256]{3,2,1,0:T(8,128)S(1)}, f32[2,2,72,256]{3,2,1,0:T(8,128)S(1)}, u32[]{:S(2)}, u32[]{:S(2)}) collective-permute-start(f32[2,2,72,256]{3,2,1,0:T(8,128)S(1)} %pad_maximum_fusion.2), channel_id=1, source_target_pairs={{4,0},{6,2},{8,4},{10,6},{12,8},{14,10},{5,1},{7,3},{9,5},{11,7},{... | collective-permute-start | bytes 884744 | tf_op jit(solution)/shard_map/ppermute | solution.py:22
  19.6 27.8 %collective-permute-start.7 = (f32[2,2,72,256]{3,2,1,0:T(8,128)S(1)}, f32[2,2,72,256]{3,2,1,0:T(8,128)S(1)}, u32[]{:S(2)}, u32[]{:S(2)}) collective-permute-start(f32[2,2,72,256]{3,2,1,0:T(8,128)S(1)} %pad_maximum_fusion.2), channel_id=1, source_target_pairs={{0,4},{2,6},{4,8},{6,10},{8,12},{10,14},{1,5},{3,7},{5,9},{7,11},{... | collective-permute-start | bytes 884744 | tf_op jit(solution)/shard_map/ppermute | solution.py:22
  24.4 3.3 %copy-start.2 = (f32[2,70,16,256]{3,2,1,0:T(8,128)}, f32[2,70,16,256]{3,2,1,0:T(8,128)S(1)}, u32[]{:S(2)}) copy-start(f32[2,70,16,256]{3,2,1,0:T(8,128)S(1)} %pad_maximum_fusion.own) | copy-start | bytes 6881284
  24.4 27.9 %collective-permute-start.9 = (f32[2,2,72,256]{3,2,1,0:T(8,128)S(1)}, f32[2,2,72,256]{3,2,1,0:T(8,128)S(1)}, u32[]{:S(2)}, u32[]{:S(2)}) collective-permute-start(f32[2,2,72,256]{3,2,1,0:T(8,128)S(1)} %collective-permute-done.8), channel_id=1, source_target_pairs={{0,4},{4,8},{6,2},{8,12},{10,6},{14,10},{1,5},{5,9},{7,3},{9,13},{... | collective-permute-start | bytes 884744 | tf_op jit(solution)/shard_map/ppermute | solution.py:22
  47.4 27.5 %collective-permute-start.3 = (f32[1,68,16,256]{3,2,1,0:T(8,128)S(1)}, f32[1,68,16,256]{3,2,1,0:T(8,128)S(1)}, u32[]{:S(2)}, u32[]{:S(2)}) collective-permute-start(f32[1,68,16,256]{3,2,1,0:T(8,128)S(1)} %get-tuple-element.8), channel_id=1, source_target_pairs={{0,2},{2,0},{4,6},{6,4},{8,10},{10,8},{12,14},{14,12},{1,3},{3,1},... | collective-permute-start | bytes 3342344 | tf_op jit(solution)/shard_map/ppermute | solution.py:22
  52.3 42.7 %collective-permute-start.2 = (f32[1,68,16,256]{3,2,1,0:T(8,128)S(1)}, f32[1,68,16,256]{3,2,1,0:T(8,128)S(1)}, u32[]{:S(2)}, u32[]{:S(2)}) collective-permute-start(f32[1,68,16,256]{3,2,1,0:T(8,128)S(1)} %get-tuple-element.9), channel_id=1, source_target_pairs={{0,2},{2,0},{4,6},{6,4},{8,10},{10,8},{12,14},{14,12},{1,3},{3,1},... | collective-permute-start | bytes 3342344 | tf_op jit(solution)/shard_map/ppermute | solution.py:22
  74.9 27.8 %collective-permute-start.4 = (f32[1,68,16,256]{3,2,1,0:T(8,128)S(1)}, f32[1,68,16,256]{3,2,1,0:T(8,128)S(1)}, u32[]{:S(2)}, u32[]{:S(2)}) collective-permute-start(f32[1,68,16,256]{3,2,1,0:T(8,128)S(1)} %collective-permute-done.3), channel_id=1, source_target_pairs={{0,4},{4,8},{6,2},{8,12},{10,6},{14,10},{1,5},{5,9},{7,3},{9,13},{... | collective-permute-start | bytes 3342344 | tf_op jit(solution)/shard_map/ppermute | solution.py:22
  95.0 24.7 %collective-permute-start.5 = (f32[1,68,16,256]{3,2,1,0:T(8,128)S(1)}, f32[1,68,16,256]{3,2,1,0:T(8,128)S(1)}, u32[]{:S(2)}, u32[]{:S(2)}) collective-permute-start(f32[1,68,16,256]{3,2,1,0:T(8,128)S(1)} %collective-permute-done.2), channel_id=1, source_target_pairs={{0,4},{4,8},{6,2},{8,12},{10,6},{14,10},{1,5},{5,9},{7,3},{9,13},{... | collective-permute-start | bytes 3342344 | tf_op jit(solution)/shard_map/ppermute | solution.py:22
  152.5 1.4 collective-permute-start.11
  154.6 3.8 %collective-permute-start.12 = (f32[16,128]{1,0:T(8,128)S(1)}, f32[16,128]{1,0:T(8,128)S(1)}, u32[]{:S(2)}, u32[]{:S(2)}) collective-permute-start(f32[16,128]{1,0:T(8,128)S(1)} %add.80), channel_id=1, source_target_pairs={{0,2},{2,0},{4,6},{6,4},{8,10},{10,8},{12,14},{14,12},{1,3},{3,1},... | collective-permute-start | bytes 24584 | tf_op jit(solution)/shard_map/ppermute | solution.py:58
  158.4 4.0 %collective-permute-start.13 = (f32[16,128]{1,0:T(8,128)S(1)}, f32[16,128]{1,0:T(8,128)S(1)}, u32[]{:S(2)}, u32[]{:S(2)}) collective-permute-start(f32[16,128]{1,0:T(8,128)S(1)} %add.81), channel_id=1, source_target_pairs={{0,4},{2,6},{4,0},{6,2},{8,12},{10,14},{12,8},{14,10},{1,5},{3,7},... | collective-permute-start | bytes 24584 | tf_op jit(solution)/shard_map/ppermute | solution.py:58
  162.4 5.2 %collective-permute-start.14 = (f32[16,128]{1,0:T(8,128)S(1)}, f32[16,128]{1,0:T(8,128)S(1)}, u32[]{:S(2)}, u32[]{:S(2)}) collective-permute-start(f32[16,128]{1,0:T(8,128)S(1)} %add.82), channel_id=1, source_target_pairs={{0,8},{2,10},{4,12},{6,14},{8,0},{10,2},{12,4},{14,6},{1,9},{3,11}... | collective-permute-start | bytes 24584 | tf_op jit(solution)/shard_map/ppermute | solution.py:58
  167.6 3.4 %copy-start = (bf16[2,64,128,256]{3,2,1,0:T(8,128)(2,1)S(1)}, bf16[2,64,128,256]{3,2,1,0:T(8,128)(2,1)}, u32[]{:S(2)}) copy-start(bf16[2,64,128,256]{3,2,1,0:T(8,128)(2,1)} %get-tuple-element.5.split) | copy-start | bytes 25165828
  171.0 1.6 copy-start.1

commit v3 on v2

--- a/solution.py
+++ b/solution.py
@@ -31,10 +31,15 @@
     return moved(block, "gz", [(i, i ^ 1) for i in range(lax.axis_size("gz"))])
 
 
-def relayed(block):
+def relayed(block, back=False):
     count = lax.axis_size("gz")
     steps = [(i, i + 2 - 4 * (i % 2)) for i in range(count)]
-    return moved(block, "gz", [(i, j) for i, j in steps if 0 <= j < count])
+    pairs = [(i, j) for i, j in steps if 0 <= j < count]
+    return moved(block, "gz", [(j, i) for i, j in pairs] if back else pairs)
+
+
+def after(value, *earlier):
+    return lax.optimization_barrier((value,) + earlier)[0]
 
 
 def rows_beside(before, after):
@@ -99,68 +104,113 @@
     lax.fori_loop(0, blocks, step, 0)
 
 
-def powers_kernel(
-    rows, lo3, lo2, lo1, own, hi1, hi2, hi3, inverse, sx, sy, sz, moments, split, u0, u1, u2, u3
-):
-    first = REACH
-    scaled = (u0, u1, u2, u3)
-    pieces = [(lo3, 0), (lo2, 0), (lo1, 0), (own, 0), (own, 1), (hi1, 0), (hi2, 0), (hi3, 0)]
-    depth = own.shape[0]
-    planes = len(pieces)
-
-    def distance(plane):
-        return max(first - plane, plane - (first + depth - 1), 0)
-
-    for plane, (piece, index) in enumerate(pieces):
-        reach = REACH - distance(plane)
-        margin = (piece.shape[1] - rows) // 2
-
-        def scale_rows(y, plane=plane, piece=piece, index=index, margin=margin):
+def apply_rows(operator, plane, start, before, here, after, size=8):
+    sx, sy, sz = operator
+    out = []
+    for j in range(size):
+        y = start + j
+        ref, index = here
+        center = ref[index, y]
+        ahead = sx[plane, pl.ds(y, 1), :]
+        width = center.shape[-1]
+        total = ahead * pltpu.roll(center, width - 1, 1) + pltpu.roll(ahead * center, 1, 1)
+        total += sy[plane, pl.ds(y, 1), :] * ref[index, y + 1]
+        total += sy[plane, pl.ds(y - 1, 1), :] * ref[index, y - 1]
+        total += sz[plane, pl.ds(y, 1), :] * after[0][after[1], y]
+        total += sz[plane - 1, pl.ds(y, 1), :] * before[0][before[1], y]
+        out.append(total)
+    return out
+
+
+def spread(plane, depth=2):
+    return max(REACH - plane, plane - (REACH + depth - 1), 0)
+
+
+def scale_plane(rows, plane, piece, inverse, dst):
+    reach = REACH - spread(plane)
+    ref, index = piece
+    out, place = dst
+    shift = (ref.shape[1] - rows) // 2 - REACH
+
+    def body(y):
+        for j in range(8):
+            out[place, y + j] = ref[index, y + (j + shift)] * inverse[plane, pl.ds(y + j, 1), :]
+
+    row_blocks(REACH - reach, REACH + rows + reach, body)
+
+
+def apply_plane(rows, power, plane, operator, fields):
+    reach = REACH - power - spread(plane)
+    src = [fields[power - 1, plane + offset] for offset in (-1, 0, 1)]
+    out, place = fields[power, plane]
+
+    def body(y):
+        for j, values in enumerate(apply_rows(operator, plane, y, *src)):
+            out[place, y + j] = values
+
+    row_blocks(REACH - reach, REACH + rows + reach, body)
+
+
+LATE = 1
+
+
+def early_kernel(rows, far3, far1, own, near1, near2, near3, inverse, sx, sy, sz, u0_out, u1_out, u2_out, u0, u1):
+    operator = (sx, sy, sz)
+    fields = {(0, plane): (u0_out, plane) for plane in range(5)}
+    fields.update({(0, plane): (u0, plane - 5) for plane in range(5, 8)})
+    fields.update({(1, 3): (u1_out, 0), (1, 4): (u1_out, 1), (1, 5): (u1, 0), (1, 6): (u1, 1)})
+    fields.update({(2, 4): (u2_out, 0), (2, 5): (u2_out, 1)})
+    pieces = {0: (far3, 0), 2: (far1, 0), 3: (own, 0), 4: (own, 1), 5: (near1, 0), 6: (near2, 0), 7: (near3, 0)}
+    for plane, piece in pieces.items():
+        scale_plane(rows, plane, piece, inverse, fields[0, plane])
+    for power, plane in ((1, 3), (1, 4), (1, 5), (1, 6), (2, 4), (2, 5)):
+        apply_plane(rows, power, plane, operator, fields)
+
+
+def late_kernel(rows, far2a, far2b, u0_in, u1_in, u2_in, inverse, sx, sy, sz, moments, split, u0, u1, u2):
+    operator = (sx, sy, sz)
+    fields = {(0, plane): (u0_in, plane) for plane in range(5)}
+    fields[0, LATE] = (u0, 0)
+    fields.update({(1, 1): (u1, 0), (1, 2): (u1, 1), (1, 3): (u1_in, 0), (1, 4): (u1_in, 1)})
+    fields.update({(2, 2): (u2, 0), (2, 3): (u2, 1), (2, 4): (u2_in, 0), (2, 5): (u2_in, 1)})
+
+    reach = REACH - spread(LATE)
+    shift = (far2a.shape[1] - rows) // 2 - REACH
+    part = far2a.shape[2]
+
+    def scale(y):
+        for j in range(8):
+            factor = inverse[LATE, pl.ds(y + j, 1), :]
+            u0[0, y + j, :part] = far2a[0, y + (j + shift)] * factor
+            u0[0, y + j, part:] = far2b[0, y + (j + shift)] * factor
+
+    row_blocks(REACH - reach, REACH + rows + reach, scale)
+    for power, plane in ((1, 1), (1, 2), (2, 2), (2, 3)):
+        apply_plane(rows, power, plane, operator, fields)
+
+    rhs = u0.shape[2]
+    height = rhs * (REACH + 1)
+    gram = jnp.zeros((2 * height, 2 * height), f32)
+    for plane in range(2):
+        level = plane + REACH
+
+        def gram_rows(block, total, plane=plane, level=level):
+            start = block * 8
+            y = start + REACH
+            last = apply_rows(operator, level, y, *[fields[2, level + offset] for offset in (-1, 0, 1)])
+            parts = []
             for j in range(8):
-                u0[plane, y + j] = piece[index, y + (j + margin - first)] * inverse[plane, pl.ds(y + j, 1), :]
-
-        row_blocks(first - reach, first + rows + reach, scale_rows)
-
-    for power in range(1, REACH + 1):
-        src, dst = scaled[power - 1], scaled[power]
-        for plane in range(planes):
-            reach = REACH - power - distance(plane)
-            if reach < 0:
-                continue
-
-            def apply_rows(start, plane=plane, src=src, dst=dst):
-                for j in range(8):
-                    y = start + j
-                    here = src[plane, y]
-                    ahead = sx[plane, pl.ds(y, 1), :]
-                    width = here.shape[-1]
-                    total = ahead * pltpu.roll(here, width - 1, 1) + pltpu.roll(ahead * here, 1, 1)
-                    total += sy[plane, pl.ds(y, 1), :] * src[plane, y + 1]
-                    total += sy[plane, pl.ds(y - 1, 1), :] * src[plane, y - 1]
-                    total += sz[plane, pl.ds(y, 1), :] * src[plane + 1, y]
-                    total += sz[plane - 1, pl.ds(y, 1), :] * src[plane - 1, y]
-                    dst[plane, y] = total
-
-            row_blocks(first - reach, first + rows + reach, apply_rows)
-
-    rhs = own.shape[2]
-    height = rhs * (REACH + 1)
-
-    def gram_rows(block, total):
-        plane = block // (rows // 4)
-        start = (block % (rows // 4)) * 4
-        parts = []
-        for j in range(4):
-            stack = jnp.concatenate([u[plane + first, start + j + first] for u in scaled], axis=0)
-            high = stack.astype(bf16)
-            low = (stack - high.astype(f32)).astype(bf16)
-            both = jnp.concatenate([high, low], axis=0)
-            split[plane, start + j] = both
-            parts.append(both)
-        wide = jnp.concatenate(parts, axis=1)
-        return total + lax.dot_general(wide, wide, (((1,), (1,)), ((), ())), preferred_element_type=f32)
-
-    gram = lax.fori_loop(0, depth * rows // 4, gram_rows, jnp.zeros((2 * height, 2 * height), f32))
+                lower = [fields[power, level] for power in range(REACH)]
+                stack = jnp.concatenate([ref[index, y + j] for ref, index in lower] + [last[j]], axis=0)
+                high = stack.astype(bf16)
+                low = (stack - high.astype(f32)).astype(bf16)
+                both = jnp.concatenate([high, low], axis=0)
+                split[plane, start + j] = both
+                parts.append(both)
+            wide = jnp.concatenate(parts, axis=1)
+            return total + lax.dot_general(wide, wide, (((1,), (1,)), ((), ())), preferred_element_type=f32)
+
+        gram = lax.fori_loop(0, rows // 8, gram_rows, gram)
     gram = gram[:height] + gram[height:]
     gram = gram[:, :height] + gram[:, height:]
     blocks = []
@@ -222,7 +272,7 @@
     return solution_part, residual
 
 
-def outputs_kernel(moments, split, inverse, root, iterate, iterate_out, residual_out, coefs):
+def outputs_kernel(odd, moments, split, inverse, root, iterate, iterate_out, residual_out, coefs):
     rhs = iterate.shape[0]
     height = rhs * (REACH + 1)
     rows = split.shape[1]
@@ -247,88 +297,114 @@
 
 def on_device(iterate, residual, labels, boundary):
     rhs, depth, rows, nx = residual.shape
-    assert depth == 2 and REACH == 3
-    coef = jnp.exp(labels.astype(f32) * (contrast_log / (NCLASS - 1)))
-    inner = (1 - boundary).astype(f32)
-
+    assert depth == 2 and REACH == 3 and lax.axis_size("gz") % 2 == 0
+    half = rhs // 2
+    odd = lax.axis_index("gz") % 2 == 1
+
+    def mirrored(block, dim):
+        return jnp.where(odd, jnp.flip(block, dim), block)
+
+    cells = jnp.stack([labels, boundary])
+    cells = mirrored(cells, 1)
+    coef = jnp.exp(cells[0].astype(f32) * (contrast_log / (NCLASS - 1)))
+    inner = (1 - cells[1]).astype(f32)
     fields = jnp.stack([coef, inner])
-    own = jnp.transpose(residual, (1, 2, 0, 3))
-    odd = lax.axis_index("gz") % 2 == 1
-
+    field_pair = swapped(fields)
+    field_far = relayed(jnp.concatenate([coef, inner[1:]], axis=0))
+    field_near = relayed(jnp.concatenate([coef, inner[:1]], axis=0), back=True)
+
+    own = mirrored(jnp.transpose(residual, (1, 2, 0, 3)), 0)
+    core = after(own, field_far, field_near)
+    far3 = relayed(core[1:])
+    near3 = relayed(core[:1], back=True)
+    before, behind = rows_beside(own[:, :REACH], own[:, -REACH:])
+    own = jnp.concatenate([before, own, behind], axis=1)
+    sent = after(own, field_pair)[:, 1:-1]
+    near2 = swapped(sent[:1])
+    field_relay = relayed(field_pair)
+    sent = after(sent, field_relay)
+    near1a = swapped(sent[1:, :, :half])
+    near1b = swapped(sent[1:, :, half:])
+    far1 = relayed(near2)
+    far2a = relayed(near1a)
+    far2b = relayed(near1b)
+    near1 = jnp.concatenate([near1a, near1b], axis=2)
+
+    none = jnp.zeros_like(coef[:1])
+    coef = jnp.concatenate(
+        [
+            field_far[:2], field_relay[0, 1:], field_relay[0, :1], coef,
+            field_pair[0, 1:], field_pair[0, :1], field_near[:2],
+        ],
+        axis=0,
+    )
+    inner = jnp.concatenate(
+        [
+            none, field_far[2:], field_relay[1, 1:], field_relay[1, :1], inner,
+            field_pair[1, 1:], field_pair[1, :1], field_near[2:], none,
+        ],
+        axis=0,
+    )
+    fields = jnp.stack([coef, inner])
     wide = REACH + 1
-
-    ends = [
-        jnp.concatenate([own[:, a:b].reshape(-1, nx), fields[:, :, c:d].reshape(-1, nx)], axis=0)
-        for a, b, c, d in ((0, REACH, 0, wide), (rows - REACH, rows, rows - wide, rows))
-    ]
-    cut = depth * REACH * rhs
-    sides = [
-        (side[:cut].reshape(depth, REACH, rhs, nx), side[cut:].reshape(2, depth, wide, nx))
-        for side in rows_beside(*ends)
-    ]
-    fields = jnp.concatenate([sides[0][1], fields, sides[1][1]], axis=2)
-    core = own
-    own = jnp.concatenate([sides[0][0], own, sides[1][0]], axis=1)
-    sent = own[:, 1:-1]
-
-    field_pair = swapped(fields)
-    field_lo2 = shifted(fields, "gz", 2)
-    field_hi2 = shifted(fields, "gz", -2)
-    lo3 = shifted(core[1:], "gz", 2)
-    hi3 = shifted(core[:1], "gz", -2)
-    pair2 = swapped(jnp.where(odd, sent[1:], sent[:1]))
-    pair1 = swapped(jnp.where(odd, sent[:1], sent[1:]))
-    field_far = relayed(field_pair)
-    far1 = relayed(pair2)
-    far2 = relayed(pair1)
-    field_lo1 = jnp.where(odd, field_pair, field_far)
-    field_hi1 = jnp.where(odd, field_far, field_pair)
-    lo1 = jnp.where(odd, pair1, far1)
-    lo2 = jnp.where(odd, pair2, far2)
-    hi1 = jnp.where(odd, far1, pair1)
-    hi2 = jnp.where(odd, far2, pair2)
-
-    fields = jnp.concatenate([field_lo2, field_lo1, fields, field_hi1, field_hi2], axis=1)
+    before, behind = rows_beside(fields[:, :, :wide], fields[:, :, -wide:])
+    fields = jnp.concatenate([before, fields, behind], axis=2)
     root, inverse, sx, sy, sz = symmetric_operator(fields[0], fields[1])
 
-    planes = depth + 2 * REACH
     extended = rows + 2 * REACH
     vmem = pl.BlockSpec(memory_space=pltpu.VMEM)
+
+    def planes(count):
+        return (count, extended, rhs, nx)
+
+    u0, u1, u2 = pl.pallas_call(
+        partial(early_kernel, rows),
+        out_shape=tuple(jax.ShapeDtypeStruct(planes(count), f32) for count in (5, 2, 2)),
+        in_specs=[vmem] * 10,
+        out_specs=(vmem,) * 3,
+        scratch_shapes=[pltpu.VMEM(planes(count), f32) for count in (3, 2)],
+        compiler_params=pltpu.CompilerParams(vmem_limit_bytes=40 * 2**20),
+        cost_estimate=pl.CostEstimate(flops=0, bytes_accessed=50 * 2**20, transcendentals=0),
+    )(far3, far1, own, near1, near2, near3, inverse, sx, sy, sz)
+
     moments, split = pl.pallas_call(
-        partial(powers_kernel, rows),
+        partial(late_kernel, rows),
         out_shape=(
             jax.ShapeDtypeStruct((rhs, 128), f32),
             jax.ShapeDtypeStruct((depth, rows, 2 * rhs * (REACH + 1), nx), bf16),
         ),
-        in_specs=[vmem] * 11,
+        in_specs=[vmem] * 9,
         out_specs=(vmem, vmem),
-        scratch_shapes=[pltpu.VMEM((planes, extended, rhs, nx), f32)] * 3
-        + [pltpu.VMEM((planes, extended, rhs, nx), f32)],
-        compiler_params=pltpu.CompilerParams(vmem_limit_bytes=62 * 2**20),
-    )(lo3, lo2, lo1, own, hi1, hi2, hi3, inverse, sx, sy, sz)
+        scratch_shapes=[pltpu.VMEM(planes(count), f32) for count in (1, 2, 2)],
+        compiler_params=pltpu.CompilerParams(vmem_limit_bytes=40 * 2**20),
+        cost_estimate=pl.CostEstimate(flops=0, bytes_accessed=50 * 2**20, transcendentals=0),
+    )(far2a, far2b, u0, u1, u2, inverse, sx, sy, sz)
 
     moments = all_sum(moments, ("gy", "gz"))
 
     inverse = inverse[REACH : REACH + depth, REACH : REACH + rows]
     root = root[REACH : REACH + depth, REACH : REACH + rows]
     tile = 8
-    plane_rows = pl.BlockSpec((rhs, 1, tile, nx), lambda z, y: (0, z, y, 0))
-    cell_rows = pl.BlockSpec((None, tile, nx), lambda z, y: (z, y, 0))
+    plane_rows = pl.BlockSpec((rhs, 1, tile, nx), lambda z, y, odd: (0, jnp.bitwise_xor(z, odd[0]), y, 0))
+    cell_rows = pl.BlockSpec((None, tile, nx), lambda z, y, odd: (z, y, 0))
     return pl.pallas_call(
         outputs_kernel,
-        grid=(depth, rows // tile),
         out_shape=(jax.ShapeDtypeStruct(iterate.shape, f32), jax.ShapeDtypeStruct(residual.shape, f32)),
-        in_specs=[
-            pl.BlockSpec((rhs, 128), lambda z, y: (0, 0)),
-            pl.BlockSpec((1, tile) + split.shape[2:], lambda z, y: (z, y, 0, 0)),
-            cell_rows,
-            cell_rows,
-            plane_rows,
-        ],
-        out_specs=(plane_rows, plane_rows),
-        scratch_shapes=[pltpu.VMEM((4 * rhs, 2 * rhs * (REACH + 1)), bf16)],
+        grid_spec=pltpu.PrefetchScalarGridSpec(
+            num_scalar_prefetch=1,
+            grid=(depth, rows // tile),
+            in_specs=[
+                pl.BlockSpec((rhs, 128), lambda z, y, odd: (0, 0)),
+                pl.BlockSpec((1, tile) + split.shape[2:], lambda z, y, odd: (z, y, 0, 0)),
+                cell_rows,
+                cell_rows,
+                plane_rows,
+            ],
+            out_specs=(plane_rows, plane_rows),
+            scratch_shapes=[pltpu.VMEM((4 * rhs, 2 * rhs * (REACH + 1)), bf16)],
+        ),
         compiler_params=pltpu.CompilerParams(vmem_limit_bytes=32 * 2**20),
-    )(moments, split, inverse, root, iterate)
+    )(odd.astype(jnp.int32).reshape(1), moments, split, inverse, root, iterate)
 
 
 def solution(mesh):

time: 188 us -> 156 us (0.83)
  waiting for transfers between devices: 81.7 us -> 60.9 us
  other arithmetic: 11.9 us -> 4.76 us
  Pallas kernels: 46 us -> 41.1 us
  starting transfers between devices: 36.1 us -> 39.6 us
  local copies, waits for them, and re-layouts: 10.9 us -> 8.27 us
    ppermute x11 -> x14, waiting for transfers between devices: 76.3 us -> 53.8 us  [moved(): return lax.ppermute(block, axis, pairs)]
    ppermute x11 -> x14, starting transfers between devices: 28 us -> 33.3 us  [moved(): return lax.ppermute(block, axis, pairs)]
    pallas_call x2 -> x3, Pallas kernels: 46 us -> 41.1 us  [the longest x1 14.9 us: on_device(): pl.pallas_call(partial(late_kernel, rows), out_shape=(jax.ShapeDtypeStruc...]
    select_n x3 -> x2, other arithmetic: 3.57 us -> 0.26 us  [mirrored(): return jnp.where(odd, jnp.flip(block, dim), block)]
    mul x3, other arithmetic: 3.21 us -> 0.73 us  [coupling(): return ma * face_of(a, b) * mb]
    unnamed x8 -> x21, local copies, waits for them, and re-layouts: 7.81 us -> 7.32 us
  transfers between devices with their start and end apart: 15 -> 18, of which waited for: 10 -> 12; matrix products, arithmetic and copies ran while one was open for 7% -> 3% of each run, Pallas kernels for 0% -> 7%
where the time goes in v3:
time: 156 us
  waiting for transfers between devices  60.9 us (39%)
  Pallas kernels  41.1 us (26%)
  starting transfers between devices  39.6 us (25%)
  local copies, waits for them, and re-layouts  8.27 us (5%)
  other arithmetic  4.76 us (3%)
    ppermute x14, waiting for transfers between devices, moved(): return lax.ppermute(block, axis, pairs)  53.8 us
    ppermute x14, starting transfers between devices, moved(): return lax.ppermute(block, axis, pairs)  33.3 us
    pallas_call x1, Pallas kernels, on_device(): pl.pallas_call(partial(late_kernel, rows), out_shape=(jax.ShapeDtypeStruc...  14.9 us
    pallas_call x1, Pallas kernels, on_device(): pl.pallas_call(outputs_kernel, out_shape=(jax.ShapeDtypeStruct(iterate.sh...  14.9 us
    pallas_call x1, Pallas kernels, on_device(): pl.pallas_call(partial(early_kernel, rows), out_shape=tuple((jax.ShapeDty...  11.3 us
    unnamed x21, local copies, waits for them, and re-layouts  7.32 us
    ppermute x4, waiting for transfers between devices, all_sum(): lax.ppermute(values, axis, [(i, i ^ step) for i in range(count)])  7.12 us
    ppermute x4, starting transfers between devices, all_sum(): lax.ppermute(values, axis, [(i, i ^ step) for i in range(count)])  6.32 us
  transfers between devices with their start and end apart: 18, of which 12 were waited for; matrix products, arithmetic and copies ran while one was open for 3% of the time, Pallas kernels for 7%

profile of v3, /device:TPU:0, one launch (start us, length us, event | category | flops | bytes accessed | tf_op | source)
XLA Modules:
  0.0 155.8 jit_solution(12286956140036003182)
XLA Ops:
  0.6 0.0 copy-start.5
  0.7 1.1 pad_add_fusion
  1.9 0.7 pad_maximum_fusion.4
  2.6 1.3 collective-permute-start.8
  3.9 5.6 %collective-permute-start.7 = (f32[3,64,256]{2,1,0:T(8,128)S(1)}, f32[3,64,256]{2,1,0:T(8,128)S(1)}, u32[]{:S(2)}, u32[]{:S(2)}) collective-permute-start(f32[3,64,256]{2,1,0:T(8,128)S(1)} %get-tuple-element.41), channel_id=1, source_target_pairs={{0,4},{4,8},{6,2},{8,12},{10,6},{14,10},{1,5},{5,9},{7,3},{9,13},{... | collective-permute-start | bytes 589832 | tf_op jit(solution)/shard_map/ppermute | solution.py:22
  9.5 0.9 collective-permute-start.1
  10.4 0.0 copy-done.5
  10.4 1.2 copy.8
  11.6 0.2 reverse_select_fusion
  11.9 0.1 collective-permute-start
  12.0 1.3 collective-permute-done
  13.3 0.2 pad_maximum_fusion.own
  13.5 0.0 collective-permute-done.8
  13.5 0.1 collective-permute-done.7
  13.6 0.2 fusion.22
  13.8 1.3 collective-permute-start.12
  15.1 5.2 %collective-permute-start.9 = (f32[1,64,16,256]{3,2,1,0:T(8,128)S(1)}, f32[1,64,16,256]{3,2,1,0:T(8,128)S(1)}, u32[]{:S(2)}, u32[]{:S(2)}) collective-permute-start(f32[1,64,16,256]{3,2,1,0:T(8,128)S(1)} %get-tuple-element.23), channel_id=1, source_target_pairs={{0,4},{4,8},{6,2},{8,12},{10,6},{14,10},{1,5},{5,9},{7,3},{9,13},{... | collective-permute-start | bytes 3145736 | tf_op jit(solution)/shard_map/ppermute | solution.py:22
  20.3 0.0 collective-permute-done.1
  20.3 3.9 %collective-permute-start.2 = (f32[2,2,64,256]{3,2,1,0:T(8,128)S(1)}, f32[2,2,64,256]{3,2,1,0:T(8,128)S(1)}, u32[]{:S(2)}, u32[]{:S(2)}) collective-permute-start(f32[2,2,64,256]{3,2,1,0:T(8,128)S(1)} %collective-permute-done.1), channel_id=1, source_target_pairs={{0,4},{4,8},{6,2},{8,12},{10,6},{14,10},{1,5},{5,9},{7,3},{9,13},{... | collective-permute-start | bytes 786440 | tf_op jit(solution)/shard_map/ppermute | solution.py:22
  24.2 0.1 slice.167
  24.3 0.0 slice-start
  24.3 0.1 collective-permute-start.10
  24.4 24.2 %collective-permute-done.2 = f32[2,2,64,256]{3,2,1,0:T(8,128)S(1)} collective-permute-done((f32[2,2,64,256]{3,2,1,0:T(8,128)S(1)}, f32[2,2,64,256]{3,2,1,0:T(8,128)S(1)}, u32[]{:S(2)}, u32[]{:S(2)}) %collective-permute-start.2) | collective-permute-done | bytes 262176 | tf_op jit(solution)/shard_map/ppermute | solution.py:22
  48.7 0.1 collective-permute-start.13
  48.8 0.0 slice-done
  48.8 0.1 fusion.21
  48.9 3.5 %collective-permute-start.5 = (f32[1,68,8,256]{3,2,1,0:T(8,128)S(1)}, f32[1,68,8,256]{3,2,1,0:T(8,128)S(1)}, u32[]{:S(2)}, u32[]{:S(2)}) collective-permute-start(f32[1,68,8,256]{3,2,1,0:T(8,128)S(1)} %get-tuple-element.20), channel_id=1, source_target_pairs={{0,2},{2,0},{4,6},{6,4},{8,10},{10,8},{12,14},{14,12},{1,3},{3,1},... | collective-permute-start | bytes 1671176 | tf_op jit(solution)/shard_map/ppermute | solution.py:22
  52.4 0.0 collective-permute-done.13
  52.4 1.1 collective-permute-start.3
  53.5 0.2 pad_maximum_fusion.1
  53.7 0.1 slice_bitcast_fusion
  53.9 0.2 fusion.23
  54.1 1.2 slice_multiply_fusion.2
  55.3 0.0 collective-permute-done.10.near2
  55.3 3.5 %collective-permute-start.11 = (f32[1,68,16,256]{3,2,1,0:T(8,128)S(1)}, f32[1,68,16,256]{3,2,1,0:T(8,128)S(1)}, u32[]{:S(2)}, u32[]{:S(2)}) collective-permute-start(f32[1,68,16,256]{3,2,1,0:T(8,128)S(1)} %collective-permute-done.10.near2), channel_id=1, source_target_pairs={{0,4},{4,8},{6,2},{8,12},{10,6},{14,10},{1,5},{5,9},{7,3},{9,13},{... | collective-permute-start | bytes 3342344 | tf_op jit(solution)/shard_map/ppermute | solution.py:22
  58.8 0.2 slice_multiply_fusion.3.sz
  59.0 0.2 slice.232
  59.2 0.3 slice_multiply_fusion.sy
  59.5 6.4 %collective-permute-done.5 = f32[1,68,8,256]{3,2,1,0:T(8,128)S(1)} collective-permute-done((f32[1,68,8,256]{3,2,1,0:T(8,128)S(1)}, f32[1,68,8,256]{3,2,1,0:T(8,128)S(1)}, u32[]{:S(2)}, u32[]{:S(2)}) %collective-permute-start.5) | collective-permute-done | bytes 557088 | tf_op jit(solution)/shard_map/ppermute | solution.py:22
  65.9 3.4 %collective-permute-start.6 = (f32[1,68,8,256]{3,2,1,0:T(8,128)S(1)}, f32[1,68,8,256]{3,2,1,0:T(8,128)S(1)}, u32[]{:S(2)}, u32[]{:S(2)}) collective-permute-start(f32[1,68,8,256]{3,2,1,0:T(8,128)S(1)} %collective-permute-done.5), channel_id=1, source_target_pairs={{0,4},{4,8},{6,2},{8,12},{10,6},{14,10},{1,5},{5,9},{7,3},{9,13},{... | collective-permute-start | bytes 1671176 | tf_op jit(solution)/shard_map/ppermute | solution.py:22
  69.3 8.3 %collective-permute-done.3 = f32[1,68,8,256]{3,2,1,0:T(8,128)S(1)} collective-permute-done((f32[1,68,8,256]{3,2,1,0:T(8,128)S(1)}, f32[1,68,8,256]{3,2,1,0:T(8,128)S(1)}, u32[]{:S(2)}, u32[]{:S(2)}) %collective-permute-start.3) | collective-permute-done | bytes 557088 | tf_op jit(solution)/shard_map/ppermute | solution.py:22
  77.6 3.4 %collective-permute-start.4 = (f32[1,68,8,256]{3,2,1,0:T(8,128)S(1)}, f32[1,68,8,256]{3,2,1,0:T(8,128)S(1)}, u32[]{:S(2)}, u32[]{:S(2)}) collective-permute-start(f32[1,68,8,256]{3,2,1,0:T(8,128)S(1)} %collective-permute-done.3), channel_id=1, source_target_pairs={{0,4},{4,8},{6,2},{8,12},{10,6},{14,10},{1,5},{5,9},{7,3},{9,13},{... | collective-permute-start | bytes 1671176 | tf_op jit(solution)/shard_map/ppermute | solution.py:22
  81.1 0.1 broadcast_divide_fusion.inverse
  81.2 0.0 copy-start.1
  81.2 0.2 pad_multiply_fusion.sx
  81.4 0.1 pad_maximum_fusion.2.near1
  81.5 0.0 collective-permute-done.12.near3
  81.5 0.0 collective-permute-done.9.far3
  81.5 2.1 %collective-permute-done.11.far1 = f32[1,68,16,256]{3,2,1,0:T(8,128)S(1)} collective-permute-done((f32[1,68,16,256]{3,2,1,0:T(8,128)S(1)}, f32[1,68,16,256]{3,2,1,0:T(8,128)S(1)}, u32[]{:S(2)}, u32[]{:S(2)}) %collective-permute-start.11) | collective-permute-done | bytes 1114144 | tf_op jit(solution)/shard_map/ppermute | solution.py:22
  83.7 11.3 %shard_map.59 = (f32[5,70,16,256]{3,2,1,0:T(8,128)}, f32[2,70,16,256]{3,2,1,0:T(8,128)S(1)}, f32[2,70,16,256]{3,2,1,0:T(8,128)S(1)}) custom-call(f32[1,64,16,256]{3,2,1,0:T(8,128)S(1)} %collective-permute-done.9.far3, f32[1,68,16,256]{3,2,1,0:T(8,128)S(1)} %collective-permute-done.11.far1, f32[2,70,16,256]{3,2,1,0:T(8,128)S(1)} %copy-done.1, ...), custom_call_target="tpu_custom_call" | custom-call | bytes 52428800 | tf_op jit(solution)/shard_map/pallas_call | solution.py:360
  94.9 0.7 collective-permute-done.6.far2b
  95.6 10.8 %collective-permute-done.4.far2a = f32[1,68,8,256]{3,2,1,0:T(8,128)S(1)} collective-permute-done((f32[1,68,8,256]{3,2,1,0:T(8,128)S(1)}, f32[1,68,8,256]{3,2,1,0:T(8,128)S(1)}, u32[]{:S(2)}, u32[]{:S(2)}) %collective-permute-start.4) | collective-permute-done | bytes 557088 | tf_op jit(solution)/shard_map/ppermute | solution.py:22
  106.4 2.6 %copy-done.3 = f32[5,70,16,256]{3,2,1,0:T(8,128)S(1)} copy-done((f32[5,70,16,256]{3,2,1,0:T(8,128)S(1)}, f32[5,70,16,256]{3,2,1,0:T(8,128)}, u32[]{:S(2)}) %copy-start.3) | copy-done | bytes 5734424
  109.1 14.9 %shard_map.60 = (f32[16,128]{1,0:T(8,128)S(1)}, bf16[2,64,128,256]{3,2,1,0:T(8,128)(2,1)}) custom-call(f32[1,68,8,256]{3,2,1,0:T(8,128)S(1)} %collective-permute-done.4.far2a, f32[1,68,8,256]{3,2,1,0:T(8,128)S(1)} %collective-permute-done.6.far2b, f32[5,70,16,256]{3,2,1,0:T(8,128)S(1)} %copy-done.3, f32[2,70,16,256]{3,2,1,0:T(8,128)S(1)} %get-tuple-element.14.u1_in, ...), custom_call_target="tpu_custom_call" | custom-call | bytes 52428800 | tf_op jit(solution)/shard_map/pallas_call | solution.py:370
  124.0 0.0 collective-permute-start.14
  124.0 1.2 collective-permute-done.14
  125.2 1.9 %collective-permute-start.15 = (f32[16,128]{1,0:T(8,128)S(1)}, f32[16,128]{1,0:T(8,128)S(1)}, u32[]{:S(2)}, u32[]{:S(2)}) collective-permute-start(f32[16,128]{1,0:T(8,128)S(1)} %add.80), channel_id=1, source_target_pairs={{0,2},{2,0},{4,6},{6,4},{8,10},{10,8},{12,14},{14,12},{1,3},{3,1},... | collective-permute-start | bytes 24584 | tf_op jit(solution)/shard_map/ppermute | solution.py:63
  127.1 1.7 %collective-permute-done.15 = f32[16,128]{1,0:T(8,128)S(1)} collective-permute-done((f32[16,128]{1,0:T(8,128)S(1)}, f32[16,128]{1,0:T(8,128)S(1)}, u32[]{:S(2)}, u32[]{:S(2)}) %collective-permute-start.15) | collective-permute-done | bytes 8224 | tf_op jit(solution)/shard_map/ppermute | solution.py:63
  128.8 2.5 %collective-permute-start.16 = (f32[16,128]{1,0:T(8,128)S(1)}, f32[16,128]{1,0:T(8,128)S(1)}, u32[]{:S(2)}, u32[]{:S(2)}) collective-permute-start(f32[16,128]{1,0:T(8,128)S(1)} %add.81), channel_id=1, source_target_pairs={{0,4},{2,6},{4,0},{6,2},{8,12},{10,14},{12,8},{14,10},{1,5},{3,7},... | collective-permute-start | bytes 24584 | tf_op jit(solution)/shard_map/ppermute | solution.py:63
  131.3 1.6 %collective-permute-done.16 = f32[16,128]{1,0:T(8,128)S(1)} collective-permute-done((f32[16,128]{1,0:T(8,128)S(1)}, f32[16,128]{1,0:T(8,128)S(1)}, u32[]{:S(2)}, u32[]{:S(2)}) %collective-permute-start.16) | collective-permute-done | bytes 8224 | tf_op jit(solution)/shard_map/ppermute | solution.py:63
  132.9 1.9 %collective-permute-start.17 = (f32[16,128]{1,0:T(8,128)S(1)}, f32[16,128]{1,0:T(8,128)S(1)}, u32[]{:S(2)}, u32[]{:S(2)}) collective-permute-start(f32[16,128]{1,0:T(8,128)S(1)} %add.82), channel_id=1, source_target_pairs={{0,8},{2,10},{4,12},{6,14},{8,0},{10,2},{12,4},{14,6},{1,9},{3,11}... | collective-permute-start | bytes 24584 | tf_op jit(solution)/shard_map/ppermute | solution.py:63
  134.9 2.6 %collective-permute-done.17 = f32[16,128]{1,0:T(8,128)S(1)} collective-permute-done((f32[16,128]{1,0:T(8,128)S(1)}, f32[16,128]{1,0:T(8,128)S(1)}, u32[]{:S(2)}, u32[]{:S(2)}) %collective-permute-start.17) | collective-permute-done | bytes 8224 | tf_op jit(solution)/shard_map/ppermute | solution.py:63
  137.5 3.4 %copy-done.2 = bf16[2,64,128,256]{3,2,1,0:T(8,128)(2,1)S(1)} copy-done((bf16[2,64,128,256]{3,2,1,0:T(8,128)(2,1)S(1)}, bf16[2,64,128,256]{3,2,1,0:T(8,128)(2,1)}, u32[]{:S(2)}) %copy-start.2) | copy-done | bytes 8388632
  140.9 14.9 %shard_map.61 = (f32[16,2,64,256]{3,2,1,0:T(8,128)}, f32[16,2,64,256]{3,2,1,0:T(8,128)}) custom-call(s32[1]{0:T(128)} %bitcast.odd, f32[16,128]{1,0:T(8,128)S(1)} %add.83.moments, bf16[2,64,128,256]{3,2,1,0:T(8,128)(2,1)S(1)} %copy-done.2, f32[2,64,256]{2,1,0:T(8,128)S(1)} %slice.241.inverse, f32[2,64,256]{2,1,0:T(8,128)S(1)} %slice.242.root, ...), custom_call_target="tpu_custom_call" | custom-call | tf_op jit(solution)/shard_map/pallas_call | solution.py:390
  (33 shorter events, 0.4 us)
Async XLA Ops:
  0.6 9.8 %copy-start.5 = (f32[16,2,64,256]{3,2,1,0:T(8,128)S(1)}, f32[16,2,64,256]{3,2,1,0:T(8,128)}, u32[]{:S(2)}) copy-start(f32[16,2,64,256]{3,2,1,0:T(8,128)} %param.5) | copy-start | bytes 6291460
  2.6 10.9 %collective-permute-start.8 = (f32[3,64,256]{2,1,0:T(8,128)}, f32[3,64,256]{2,1,0:T(8,128)S(1)}, u32[]{:S(2)}, u32[]{:S(2)}) collective-permute-start(f32[3,64,256]{2,1,0:T(8,128)} %get-tuple-element.40), channel_id=1, source_target_pairs={{4,0},{8,4},{2,6},{12,8},{6,10},{10,14},{5,1},{9,5},{3,7},{13,9},{... | collective-permute-start | bytes 589832 | tf_op jit(solution)/shard_map/ppermute | solution.py:22
  3.9 9.7 %collective-permute-start.7 = (f32[3,64,256]{2,1,0:T(8,128)S(1)}, f32[3,64,256]{2,1,0:T(8,128)S(1)}, u32[]{:S(2)}, u32[]{:S(2)}) collective-permute-start(f32[3,64,256]{2,1,0:T(8,128)S(1)} %get-tuple-element.41), channel_id=1, source_target_pairs={{0,4},{4,8},{6,2},{8,12},{10,6},{14,10},{1,5},{5,9},{7,3},{9,13},{... | collective-permute-start | bytes 589832 | tf_op jit(solution)/shard_map/ppermute | solution.py:22
  9.5 10.8 %collective-permute-start.1 = (f32[2,2,64,256]{3,2,1,0:T(8,128)S(1)}, f32[2,2,64,256]{3,2,1,0:T(8,128)S(1)}, u32[]{:S(2)}, u32[]{:S(2)}) collective-permute-start(f32[2,2,64,256]{3,2,1,0:T(8,128)S(1)} %pad_maximum_fusion.3), channel_id=1, source_target_pairs={{0,2},{2,0},{4,6},{6,4},{8,10},{10,8},{12,14},{14,12},{1,3},{3,1},... | collective-permute-start | bytes 786440 | tf_op jit(solution)/shard_map/ppermute | solution.py:22
  11.9 1.4 collective-permute-start
  13.5 10.8 %copy-start = (f32[2,70,16,256]{3,2,1,0:T(8,128)}, f32[2,70,16,256]{3,2,1,0:T(8,128)S(1)}, u32[]{:S(2)}) copy-start(f32[2,70,16,256]{3,2,1,0:T(8,128)S(1)} %pad_maximum_fusion.own) | copy-start | bytes 6881284
  13.8 67.7 %collective-permute-start.12 = (f32[1,64,16,256]{3,2,1,0:T(8,128)S(1)}, f32[1,64,16,256]{3,2,1,0:T(8,128)S(1)}, u32[]{:S(2)}, u32[]{:S(2)}) collective-permute-start(f32[1,64,16,256]{3,2,1,0:T(8,128)S(1)} %get-tuple-element.22), channel_id=1, source_target_pairs={{4,0},{8,4},{2,6},{12,8},{6,10},{10,14},{5,1},{9,5},{3,7},{13,9},{... | collective-permute-start | bytes 3145736 | tf_op jit(solution)/shard_map/ppermute | solution.py:22
  15.1 66.4 %collective-permute-start.9 = (f32[1,64,16,256]{3,2,1,0:T(8,128)S(1)}, f32[1,64,16,256]{3,2,1,0:T(8,128)S(1)}, u32[]{:S(2)}, u32[]{:S(2)}) collective-permute-start(f32[1,64,16,256]{3,2,1,0:T(8,128)S(1)} %get-tuple-element.23), channel_id=1, source_target_pairs={{0,4},{4,8},{6,2},{8,12},{10,6},{14,10},{1,5},{5,9},{7,3},{9,13},{... | collective-permute-start | bytes 3145736 | tf_op jit(solution)/shard_map/ppermute | solution.py:22
  20.3 28.3 %collective-permute-start.2 = (f32[2,2,64,256]{3,2,1,0:T(8,128)S(1)}, f32[2,2,64,256]{3,2,1,0:T(8,128)S(1)}, u32[]{:S(2)}, u32[]{:S(2)}) collective-permute-start(f32[2,2,64,256]{3,2,1,0:T(8,128)S(1)} %collective-permute-done.1), channel_id=1, source_target_pairs={{0,4},{4,8},{6,2},{8,12},{10,6},{14,10},{1,5},{5,9},{7,3},{9,13},{... | collective-permute-start | bytes 786440 | tf_op jit(solution)/shard_map/ppermute | solution.py:22
  24.3 24.5 %slice-start = ((f32[2,70,16,256]{3,2,1,0:T(8,128)}), f32[2,68,16,256]{3,2,1,0:T(8,128)S(1)}, s32[]{:S(2)}) async-start(f32[2,70,16,256]{3,2,1,0:T(8,128)} %copy-done), calls=%async_computation | async-start | bytes 4456448 | tf_op jit(solution)/shard_map/slice | solution.py:322
  24.3 31.0 %collective-permute-start.10 = (f32[1,68,16,256]{3,2,1,0:T(8,128)S(1)}, f32[1,68,16,256]{3,2,1,0:T(8,128)S(1)}, u32[]{:S(2)}, u32[]{:S(2)}) collective-permute-start(f32[1,68,16,256]{3,2,1,0:T(8,128)S(1)} %slice.167), channel_id=1, source_target_pairs={{0,2},{2,0},{4,6},{6,4},{8,10},{10,8},{12,14},{14,12},{1,3},{3,1},... | collective-permute-start | bytes 3342344 | tf_op jit(solution)/shard_map/ppermute | solution.py:22
  48.7 3.7 %collective-permute-start.13 = (f32[2,10,4,256]{3,2,1,0:T(4,128)S(1)}, f32[2,10,4,256]{3,2,1,0:T(4,128)S(1)}, u32[]{:S(2)}, u32[]{:S(2)}) collective-permute-start(f32[2,10,4,256]{3,2,1,0:T(4,128)S(1)} %fusion.11), channel_id=1, source_target_pairs={{0,1},{1,0},{2,3},{3,2},{4,5},{5,4},{6,7},{7,6},{8,9},{9,8},{10,11... | collective-permute-start | bytes 245768 | tf_op jit(solution)/shard_map/ppermute | solution.py:22
  48.9 17.0 %collective-permute-start.5 = (f32[1,68,8,256]{3,2,1,0:T(8,128)S(1)}, f32[1,68,8,256]{3,2,1,0:T(8,128)S(1)}, u32[]{:S(2)}, u32[]{:S(2)}) collective-permute-start(f32[1,68,8,256]{3,2,1,0:T(8,128)S(1)} %get-tuple-element.20), channel_id=1, source_target_pairs={{0,2},{2,0},{4,6},{6,4},{8,10},{10,8},{12,14},{14,12},{1,3},{3,1},... | collective-permute-start | bytes 1671176 | tf_op jit(solution)/shard_map/ppermute | solution.py:22
  52.4 25.2 %collective-permute-start.3 = (f32[1,68,8,256]{3,2,1,0:T(8,128)S(1)}, f32[1,68,8,256]{3,2,1,0:T(8,128)S(1)}, u32[]{:S(2)}, u32[]{:S(2)}) collective-permute-start(f32[1,68,8,256]{3,2,1,0:T(8,128)S(1)} %get-tuple-element.21), channel_id=1, source_target_pairs={{0,2},{2,0},{4,6},{6,4},{8,10},{10,8},{12,14},{14,12},{1,3},{3,1},... | collective-permute-start | bytes 1671176 | tf_op jit(solution)/shard_map/ppermute | solution.py:22
  55.3 28.4 %collective-permute-start.11 = (f32[1,68,16,256]{3,2,1,0:T(8,128)S(1)}, f32[1,68,16,256]{3,2,1,0:T(8,128)S(1)}, u32[]{:S(2)}, u32[]{:S(2)}) collective-permute-start(f32[1,68,16,256]{3,2,1,0:T(8,128)S(1)} %collective-permute-done.10.near2), channel_id=1, source_target_pairs={{0,4},{4,8},{6,2},{8,12},{10,6},{14,10},{1,5},{5,9},{7,3},{9,13},{... | collective-permute-start | bytes 3342344 | tf_op jit(solution)/shard_map/ppermute | solution.py:22
  65.9 29.7 %collective-permute-start.6 = (f32[1,68,8,256]{3,2,1,0:T(8,128)S(1)}, f32[1,68,8,256]{3,2,1,0:T(8,128)S(1)}, u32[]{:S(2)}, u32[]{:S(2)}) collective-permute-start(f32[1,68,8,256]{3,2,1,0:T(8,128)S(1)} %collective-permute-done.5), channel_id=1, source_target_pairs={{0,4},{4,8},{6,2},{8,12},{10,6},{14,10},{1,5},{5,9},{7,3},{9,13},{... | collective-permute-start | bytes 1671176 | tf_op jit(solution)/shard_map/ppermute | solution.py:22
  77.6 28.8 %collective-permute-start.4 = (f32[1,68,8,256]{3,2,1,0:T(8,128)S(1)}, f32[1,68,8,256]{3,2,1,0:T(8,128)S(1)}, u32[]{:S(2)}, u32[]{:S(2)}) collective-permute-start(f32[1,68,8,256]{3,2,1,0:T(8,128)S(1)} %collective-permute-done.3), channel_id=1, source_target_pairs={{0,4},{4,8},{6,2},{8,12},{10,6},{14,10},{1,5},{5,9},{7,3},{9,13},{... | collective-permute-start | bytes 1671176 | tf_op jit(solution)/shard_map/ppermute | solution.py:22
  81.2 2.5 %copy-start.1 = (f32[2,70,16,256]{3,2,1,0:T(8,128)S(1)}, f32[2,70,16,256]{3,2,1,0:T(8,128)}, u32[]{:S(2)}) copy-start(f32[2,70,16,256]{3,2,1,0:T(8,128)} %copy-done) | copy-start | bytes 6881284
  106.4 2.6 %copy-start.3 = (f32[5,70,16,256]{3,2,1,0:T(8,128)S(1)}, f32[5,70,16,256]{3,2,1,0:T(8,128)}, u32[]{:S(2)}) copy-start(f32[5,70,16,256]{3,2,1,0:T(8,128)} %get-tuple-element.13.u0_in) | copy-start | bytes 17203204
  109.0 28.4 %copy-start.4 = (f32[16,2,64,256]{3,2,1,0:T(8,128)S(1)}, f32[16,2,64,256]{3,2,1,0:T(8,128)}, u32[]{:S(2)}) copy-start(f32[16,2,64,256]{3,2,1,0:T(8,128)} %iterate.1) | copy-start | bytes 6291460
  124.0 1.2 collective-permute-start.14
  125.2 3.7 %collective-permute-start.15 = (f32[16,128]{1,0:T(8,128)S(1)}, f32[16,128]{1,0:T(8,128)S(1)}, u32[]{:S(2)}, u32[]{:S(2)}) collective-permute-start(f32[16,128]{1,0:T(8,128)S(1)} %add.80), channel_id=1, source_target_pairs={{0,2},{2,0},{4,6},{6,4},{8,10},{10,8},{12,14},{14,12},{1,3},{3,1},... | collective-permute-start | bytes 24584 | tf_op jit(solution)/shard_map/ppermute | solution.py:63
  128.8 4.1 %collective-permute-start.16 = (f32[16,128]{1,0:T(8,128)S(1)}, f32[16,128]{1,0:T(8,128)S(1)}, u32[]{:S(2)}, u32[]{:S(2)}) collective-permute-start(f32[16,128]{1,0:T(8,128)S(1)} %add.81), channel_id=1, source_target_pairs={{0,4},{2,6},{4,0},{6,2},{8,12},{10,14},{12,8},{14,10},{1,5},{3,7},... | collective-permute-start | bytes 24584 | tf_op jit(solution)/shard_map/ppermute | solution.py:63
  132.9 4.5 %collective-permute-start.17 = (f32[16,128]{1,0:T(8,128)S(1)}, f32[16,128]{1,0:T(8,128)S(1)}, u32[]{:S(2)}, u32[]{:S(2)}) collective-permute-start(f32[16,128]{1,0:T(8,128)S(1)} %add.82), channel_id=1, source_target_pairs={{0,8},{2,10},{4,12},{6,14},{8,0},{10,2},{12,4},{14,6},{1,9},{3,11}... | collective-permute-start | bytes 24584 | tf_op jit(solution)/shard_map/ppermute | solution.py:63
  137.5 3.4 %copy-start.2 = (bf16[2,64,128,256]{3,2,1,0:T(8,128)(2,1)S(1)}, bf16[2,64,128,256]{3,2,1,0:T(8,128)(2,1)}, u32[]{:S(2)}) copy-start(bf16[2,64,128,256]{3,2,1,0:T(8,128)(2,1)} %get-tuple-element.17.split) | copy-start | bytes 25165828

commit v4 on v3

--- a/solution.py
+++ b/solution.py
@@ -31,6 +31,12 @@
     return moved(block, "gz", [(i, i ^ 1) for i in range(lax.axis_size("gz"))])
 
 
+def swapped_far(block):
+    count = lax.axis_size("gz")
+    steps = [(i, i - 1 + 2 * (i % 2)) for i in range(count)]
+    return moved(block, "gz", [(i, j) for i, j in steps if 0 <= j < count])
+
+
 def relayed(block, back=False):
     count = lax.axis_size("gz")
     steps = [(i, i + 2 - 4 * (i % 2)) for i in range(count)]
@@ -39,7 +45,10 @@
 
 
 def after(value, *earlier):
-    return lax.optimization_barrier((value,) + earlier)[0]
+    here = True
+    for block in earlier:
+        here = here & (block[(0,) * block.ndim] >= jnp.finfo(f32).min)
+    return jnp.where(here, value, 0.0)
 
 
 def rows_beside(before, after):
@@ -106,19 +115,22 @@
 
 def apply_rows(operator, plane, start, before, here, after, size=8):
     sx, sy, sz = operator
+    ref, index = here
     out = []
+    last, center = ref[index, start - 1], ref[index, start]
+    below = sy[plane, pl.ds(start - 1, 1), :]
+    width = center.shape[-1]
     for j in range(size):
         y = start + j
-        ref, index = here
-        center = ref[index, y]
+        following = ref[index, y + 1]
+        above = sy[plane, pl.ds(y, 1), :]
         ahead = sx[plane, pl.ds(y, 1), :]
-        width = center.shape[-1]
         total = ahead * pltpu.roll(center, width - 1, 1) + pltpu.roll(ahead * center, 1, 1)
-        total += sy[plane, pl.ds(y, 1), :] * ref[index, y + 1]
-        total += sy[plane, pl.ds(y - 1, 1), :] * ref[index, y - 1]
+        total += above * following + below * last
         total += sz[plane, pl.ds(y, 1), :] * after[0][after[1], y]
         total += sz[plane - 1, pl.ds(y, 1), :] * before[0][before[1], y]
         out.append(total)
+        last, center, below = center, following, above
     return out
 
 
@@ -154,7 +166,26 @@
 LATE = 1
 
 
-def early_kernel(rows, far3, far1, own, near1, near2, near3, inverse, sx, sy, sz, u0_out, u1_out, u2_out, u0, u1):
+def halves(blocks):
+    stack = jnp.concatenate(blocks, axis=0)
+    high = stack.astype(bf16)
+    low = (stack - high.astype(f32)).astype(bf16)
+    return jnp.concatenate([high, low], axis=0)
+
+
+def inner_products(left, right):
+    return lax.dot_general(left, right, (((1,), (1,)), ((), ())), preferred_element_type=f32)
+
+
+def whole(gram, left, right):
+    gram = gram[:left] + gram[left : 2 * left]
+    return gram[:, :right] + gram[:, right : 2 * right]
+
+
+def early_kernel(
+    rows, far3, far1, own, near1, near2, near3, inverse, sx, sy, sz,
+    u0_out, u1_out, u2_out, split, moments, u0, u1,
+):
     operator = (sx, sy, sz)
     fields = {(0, plane): (u0_out, plane) for plane in range(5)}
     fields.update({(0, plane): (u0, plane - 5) for plane in range(5, 8)})
@@ -166,8 +197,30 @@
     for power, plane in ((1, 3), (1, 4), (1, 5), (1, 6), (2, 4), (2, 5)):
         apply_plane(rows, power, plane, operator, fields)
 
-
-def late_kernel(rows, far2a, far2b, u0_in, u1_in, u2_in, inverse, sx, sy, sz, moments, split, u0, u1, u2):
+    rhs = u0.shape[2]
+    gram = jnp.zeros((4 * rhs, 4 * rhs), f32)
+    for plane in range(2):
+
+        def gram_rows(block, total, plane=plane):
+            parts = []
+            for j in range(8):
+                y = block * 8 + j
+                sources = [fields[power, plane + REACH] for power in range(2)]
+                both = halves([ref[index, y + REACH] for ref, index in sources])
+                split[plane, y] = both
+                parts.append(both)
+            wide = jnp.concatenate(parts, axis=1)
+            return total + inner_products(wide, wide)
+
+        gram = lax.fori_loop(0, rows // 8, gram_rows, gram)
+    gram = whole(gram, 2 * rhs, 2 * rhs)
+    moments[:, : 2 * rhs] = gram[:rhs]
+    moments[:, 2 * rhs : 3 * rhs] = gram[rhs:, rhs:]
+
+
+def late_kernel(
+    rows, far2a, far2b, u0_in, u1_in, u2_in, split_in, moments_in, inverse, sx, sy, sz, moments, split, u0, u1, u2
+):
     operator = (sx, sy, sz)
     fields = {(0, plane): (u0_in, plane) for plane in range(5)}
     fields[0, LATE] = (u0, 0)
@@ -189,8 +242,7 @@
         apply_plane(rows, power, plane, operator, fields)
 
     rhs = u0.shape[2]
-    height = rhs * (REACH + 1)
-    gram = jnp.zeros((2 * height, 2 * height), f32)
+    gram = jnp.zeros((6 * rhs, 2 * rhs), f32)
     for plane in range(2):
         level = plane + REACH
 
@@ -198,97 +250,77 @@
             start = block * 8
             y = start + REACH
             last = apply_rows(operator, level, y, *[fields[2, level + offset] for offset in (-1, 0, 1)])
-            parts = []
+            left, right = [], []
             for j in range(8):
-                lower = [fields[power, level] for power in range(REACH)]
-                stack = jnp.concatenate([ref[index, y + j] for ref, index in lower] + [last[j]], axis=0)
-                high = stack.astype(bf16)
-                low = (stack - high.astype(f32)).astype(bf16)
-                both = jnp.concatenate([high, low], axis=0)
+                ref, index = fields[2, level]
+                both = halves([ref[index, y + j], last[j]])
                 split[plane, start + j] = both
-                parts.append(both)
-            wide = jnp.concatenate(parts, axis=1)
-            return total + lax.dot_general(wide, wide, (((1,), (1,)), ((), ())), preferred_element_type=f32)
+                first = [split_in[plane, start + j, part * rhs : (part + 1) * rhs] for part in (1, 3)]
+                left.append(jnp.concatenate(first + [both], axis=0))
+                right.append(jnp.concatenate([both[:rhs], both[2 * rhs : 3 * rhs]], axis=0))
+            return total + inner_products(jnp.concatenate(left, axis=1), jnp.concatenate(right, axis=1))
 
         gram = lax.fori_loop(0, rows // 8, gram_rows, gram)
-    gram = gram[:height] + gram[height:]
-    gram = gram[:, :height] + gram[:, height:]
-    blocks = []
-    for power in range(2 * REACH):
-        i = power // 2
-        j = power - i
-        blocks.append(gram[i * rhs : (i + 1) * rhs, j * rhs : (j + 1) * rhs])
-    blocks.append(jnp.zeros((rhs, moments.shape[1] - rhs * len(blocks)), f32))
-    moments[...] = jnp.concatenate(blocks, axis=1)
+    gram = gram[:, :rhs] + gram[:, rhs:]
+    blocks = [gram[part * rhs : (part + 1) * rhs] for part in range(6)]
+    moments[:, : 3 * rhs] = moments_in[:, : 3 * rhs]
+    moments[:, 3 * rhs : 4 * rhs] = blocks[0] + blocks[1]
+    moments[:, 4 * rhs : 5 * rhs] = blocks[2] + blocks[4]
+    moments[:, 5 * rhs : 6 * rhs] = blocks[3] + blocks[5]
+    moments[:, 6 * rhs :] = jnp.zeros((rhs, moments.shape[1] - 6 * rhs), f32)
 
 
 def eliminate(stacked, size):
-    lane = lax.broadcasted_iota(jnp.int32, (1, size), 1)
-    for k in range(size):
-        row = stacked[k : k + 1, :]
-        column = stacked[:, k : k + 1] * (1.0 / stacked[k : k + 1, k : k + 1])
-        stacked = jnp.where(lane == k, column, stacked - column * row)
-    return stacked[size:]
+    lane = lax.broadcasted_iota(jnp.int32, (1, stacked.shape[1]), 1)
+    done = 0
+    for k in range(0, size, 2):
+        if k - done == 8:
+            stacked, done = stacked[8:], k
+        at = k - done
+        row0, row1 = stacked[at : at + 1, :], stacked[at + 1 : at + 2, :]
+        col0, col1 = stacked[:, k : k + 1], stacked[:, k + 1 : k + 2]
+        a, b = row0[:, k : k + 1], row0[:, k + 1 : k + 2]
+        c, d = row1[:, k : k + 1], row1[:, k + 1 : k + 2]
+        scale = 1.0 / (a * d - b * c)
+        new0 = col0 * (d * scale) - col1 * (c * scale)
+        new1 = col1 * (a * scale) - col0 * (b * scale)
+        rest = stacked - new0 * row0 - new1 * row1
+        stacked = jnp.where(lane == k, new0, jnp.where(lane == k + 1, new1, rest))
+    return stacked[size - done :]
 
 
 def mixing(moments, rhs):
     width = moments.shape[1]
     lane = lax.broadcasted_iota(jnp.int32, (rhs, width), 1)
-
-    def hankel(first, degree):
-        rows = []
-        for i in range(degree):
-            shifted_by = (i + first) * rhs
-            rows.append(pltpu.roll(moments, width - shifted_by, 1) if shifted_by else moments)
-        rows.append(jnp.zeros((width - degree * rhs, width), f32))
-        return jnp.concatenate(rows, axis=0)
-
-    def product(a, b):
-        return jnp.dot(a, b, precision=highest, preferred_element_type=f32)
-
-    def quadratic(coefs, matrix):
-        return lax.dot_general(
-            product(coefs, matrix), coefs, (((1,), (1,)), ((), ())), precision=highest, preferred_element_type=f32
-        )
-
-    plain = hankel(0, REACH)
-    energy = plain - hankel(1, REACH)
-    eye = (lax.broadcasted_iota(jnp.int32, (rhs, rhs), 0) == lax.broadcasted_iota(jnp.int32, (rhs, rhs), 1)).astype(f32)
-    direction = (lax.broadcasted_iota(jnp.int32, (rhs, width), 0) == lane).astype(f32)
-    residual = direction
-    solution_part = jnp.zeros((rhs, width), f32)
-    rho = moments[:, :rhs]
-    for iteration in range(ITERS):
-        curvature = rho - moments[:, rhs : 2 * rhs] if iteration == 0 else quadratic(direction, energy)
-        step = eliminate(jnp.concatenate([curvature, rho], axis=0), rhs)
-        solution_part = solution_part + product(step, direction)
-        image = direction - pltpu.roll(direction, rhs, 1)
-        residual = residual - product(step, image)
-        if iteration + 1 < ITERS:
-            following = quadratic(residual, plain)
-            inverse = eliminate(jnp.concatenate([rho, eye], axis=0), rhs)
-            direction = residual + product(product(following, inverse), direction)
-            rho = following
-    return solution_part, residual
-
-
-def outputs_kernel(odd, moments, split, inverse, root, iterate, iterate_out, residual_out, coefs):
+    row = lax.broadcasted_iota(jnp.int32, (rhs, width), 0)
+    size = REACH * rhs
+    rolled = [moments] + [pltpu.roll(moments, width - i * rhs, 1) for i in range(1, REACH + 1)]
+    energy = [rolled[i] - rolled[i + 1] for i in range(REACH)]
+    solved = eliminate(jnp.concatenate(energy + [moments], axis=0), size)
+    solved = jnp.where(lane < size, solved, 0.0)
+    residual = (row == lane).astype(f32) - (solved - pltpu.roll(solved, rhs, 1))
+    return solved, residual
+
+
+def outputs_kernel(odd, moments, split01, split23, inverse, root, iterate, iterate_out, residual_out, coefs):
     rhs = iterate.shape[0]
-    height = rhs * (REACH + 1)
-    rows = split.shape[1]
+    rows = split01.shape[1]
 
     @pl.when((pl.program_id(0) == 0) & (pl.program_id(1) == 0))
     def _():
-        solution_part, residual = mixing(moments[...], rhs)
-        both = jnp.concatenate([solution_part[:, :height], residual[:, :height]], axis=0)
+        solved, residual = mixing(moments[...], rhs)
+        both = jnp.concatenate([solved[:, : 4 * rhs], residual[:, : 4 * rhs]], axis=0)
         high = both.astype(bf16).astype(f32)
         stacked = jnp.concatenate([high, both - high], axis=0)
-        coefs[...] = jnp.concatenate([stacked, stacked], axis=1).astype(bf16)
-
-    wide = jnp.concatenate([split[0, j] for j in range(rows)], axis=1)
+        pair01, pair23 = stacked[:, : 2 * rhs], stacked[:, 2 * rhs :]
+        coefs[...] = jnp.concatenate([pair01, pair01, pair23, pair23], axis=1).astype(bf16)
+
+    wide = jnp.concatenate(
+        [jnp.concatenate([split01[0, j], split23[0, j]], axis=0) for j in range(rows)], axis=1
+    )
     mixed = jnp.dot(coefs[...], wide, preferred_element_type=f32)
     mixed = mixed[: 2 * rhs] + mixed[2 * rhs :]
-    nx = split.shape[-1]
+    nx = split01.shape[-1]
     by_row = jnp.stack([mixed[:, j * nx : (j + 1) * nx] for j in range(rows)], axis=0)
     by_rhs = pltpu.einshape("abc->bac", by_row)
     iterate_out[:, 0] = iterate[:, 0] + by_rhs[:rhs] * inverse[...]
@@ -310,21 +342,24 @@
     inner = (1 - cells[1]).astype(f32)
     fields = jnp.stack([coef, inner])
     field_pair = swapped(fields)
-    field_far = relayed(jnp.concatenate([coef, inner[1:]], axis=0))
-    field_near = relayed(jnp.concatenate([coef, inner[:1]], axis=0), back=True)
+    field_beyond = swapped_far(fields)
 
     own = mirrored(jnp.transpose(residual, (1, 2, 0, 3)), 0)
-    core = after(own, field_far, field_near)
-    far3 = relayed(core[1:])
-    near3 = relayed(core[:1], back=True)
     before, behind = rows_beside(own[:, :REACH], own[:, -REACH:])
+    def with_fields(plane, *cells):
+        return jnp.concatenate([plane] + [block.reshape(-1, rhs, nx) for block in cells], axis=0)
+
+    def without_fields(message):
+        return message[None, :rows], message[rows:].reshape(-1, rows, nx)
+
+    far3, field_far = without_fields(relayed(with_fields(own[1], coef, inner[1:])))
+    near3, field_near = without_fields(relayed(with_fields(own[0], coef, inner[:1]), back=True))
     own = jnp.concatenate([before, own, behind], axis=1)
-    sent = after(own, field_pair)[:, 1:-1]
+    sent = after(own, field_pair, field_beyond)[:, 1:-1]
     near2 = swapped(sent[:1])
-    field_relay = relayed(field_pair)
-    sent = after(sent, field_relay)
-    near1a = swapped(sent[1:, :, :half])
-    near1b = swapped(sent[1:, :, half:])
+    last = after(sent[1:], near2)
+    near1a = swapped(last[:, :, :half])
+    near1b = swapped(last[:, :, half:])
     far1 = relayed(near2)
     far2a = relayed(near1a)
     far2b = relayed(near1b)
@@ -333,14 +368,14 @@
     none = jnp.zeros_like(coef[:1])
     coef = jnp.concatenate(
         [
-            field_far[:2], field_relay[0, 1:], field_relay[0, :1], coef,
+            field_far[:2], field_beyond[0, 1:], field_beyond[0, :1], coef,
             field_pair[0, 1:], field_pair[0, :1], field_near[:2],
         ],
         axis=0,
     )
     inner = jnp.concatenate(
         [
-            none, field_far[2:], field_relay[1, 1:], field_relay[1, :1], inner,
+            none, field_far[2:], field_beyond[1, 1:], field_beyond[1, :1], inner,
             field_pair[1, 1:], field_pair[1, :1], field_near[2:], none,
         ],
         axis=0,
@@ -357,28 +392,27 @@
     def planes(count):
         return (count, extended, rhs, nx)
 
-    u0, u1, u2 = pl.pallas_call(
+    spl = jax.ShapeDtypeStruct((depth, rows, 4 * rhs, nx), bf16)
+    sums = jax.ShapeDtypeStruct((rhs, 128), f32)
+    u0, u1, u2, split01, moments = pl.pallas_call(
         partial(early_kernel, rows),
-        out_shape=tuple(jax.ShapeDtypeStruct(planes(count), f32) for count in (5, 2, 2)),
+        out_shape=tuple(jax.ShapeDtypeStruct(planes(count), f32) for count in (5, 2, 2)) + (spl, sums),
         in_specs=[vmem] * 10,
-        out_specs=(vmem,) * 3,
+        out_specs=(vmem,) * 5,
         scratch_shapes=[pltpu.VMEM(planes(count), f32) for count in (3, 2)],
-        compiler_params=pltpu.CompilerParams(vmem_limit_bytes=40 * 2**20),
+        compiler_params=pltpu.CompilerParams(vmem_limit_bytes=32 * 2**20),
         cost_estimate=pl.CostEstimate(flops=0, bytes_accessed=50 * 2**20, transcendentals=0),
     )(far3, far1, own, near1, near2, near3, inverse, sx, sy, sz)
 
-    moments, split = pl.pallas_call(
+    moments, split23 = pl.pallas_call(
         partial(late_kernel, rows),
-        out_shape=(
-            jax.ShapeDtypeStruct((rhs, 128), f32),
-            jax.ShapeDtypeStruct((depth, rows, 2 * rhs * (REACH + 1), nx), bf16),
-        ),
-        in_specs=[vmem] * 9,
+        out_shape=(sums, spl),
+        in_specs=[vmem] * 11,
         out_specs=(vmem, vmem),
         scratch_shapes=[pltpu.VMEM(planes(count), f32) for count in (1, 2, 2)],
-        compiler_params=pltpu.CompilerParams(vmem_limit_bytes=40 * 2**20),
+        compiler_params=pltpu.CompilerParams(vmem_limit_bytes=32 * 2**20),
         cost_estimate=pl.CostEstimate(flops=0, bytes_accessed=50 * 2**20, transcendentals=0),
-    )(far2a, far2b, u0, u1, u2, inverse, sx, sy, sz)
+    )(far2a, far2b, u0, u1, u2, split01, moments, inverse, sx, sy, sz)
 
     moments = all_sum(moments, ("gy", "gz"))
 
@@ -395,16 +429,16 @@
             grid=(depth, rows // tile),
             in_specs=[
                 pl.BlockSpec((rhs, 128), lambda z, y, odd: (0, 0)),
-                pl.BlockSpec((1, tile) + split.shape[2:], lambda z, y, odd: (z, y, 0, 0)),
+                *[pl.BlockSpec((1, tile) + spl.shape[2:], lambda z, y, odd: (z, y, 0, 0))] * 2,
                 cell_rows,
                 cell_rows,
                 plane_rows,
             ],
             out_specs=(plane_rows, plane_rows),
-            scratch_shapes=[pltpu.VMEM((4 * rhs, 2 * rhs * (REACH + 1)), bf16)],
+            scratch_shapes=[pltpu.VMEM((4 * rhs, 8 * rhs), bf16)],
         ),
-        compiler_params=pltpu.CompilerParams(vmem_limit_bytes=32 * 2**20),
-    )(odd.astype(jnp.int32).reshape(1), moments, split, inverse, root, iterate)
+        compiler_params=pltpu.CompilerParams(vmem_limit_bytes=16 * 2**20),
+    )(odd.astype(jnp.int32).reshape(1), moments, split01, split23, inverse, root, iterate)
 
 
 def solution(mesh):

time: 156 us -> 162 us (1.038)
  local copies, waits for them, and re-layouts: 8.27 us -> 17.6 us
  waiting for transfers between devices: 60.9 us -> 55.5 us
  starting transfers between devices: 39.6 us -> 35.8 us
  Pallas kernels: 41.1 us -> 43.3 us
  between operations: 1.09 us -> 3.06 us
    ppermute x14 -> x12, waiting for transfers between devices: 53.8 us -> 47.6 us  [moved(): return lax.ppermute(block, axis, pairs)]
    unnamed x21, local copies, waits for them, and re-layouts: 7.32 us -> 11.9 us
    pallas_call x1, Pallas kernels: 14.9 us -> 10.6 us  [on_device(): pl.pallas_call(partial(late_kernel, rows), out_shape=(sums, spl), in_spec...]
    pallas_call x1, Pallas kernels: 14.9 us -> 18.3 us  [on_device(): pl.pallas_call(outputs_kernel, out_shape=(jax.ShapeDtypeStruct(iterate.sh...]
    slice x5 -> x9, local copies, waits for them, and re-layouts: 0.27 us -> 3.54 us  [the longest x3 1.67 us: after(): here = here & (block[(0,) * block.ndim] >= jnp.finfo(f32).min)]
    pallas_call x1, Pallas kernels: 11.3 us -> 14.4 us  [on_device(): pl.pallas_call(partial(early_kernel, rows), out_shape=tuple((jax.ShapeDty...]
    ppermute x14 -> x12, starting transfers between devices: 33.3 us -> 30.3 us  [moved(): return lax.ppermute(block, axis, pairs)]
  transfers between devices with their start and end apart: 18 -> 16, of which waited for: 12 -> 12; matrix products, arithmetic and copies ran while one was open for 3% -> 5% of each run, Pallas kernels for 7% -> 9%
where the time goes in v4:
time: 162 us; the launch traced here: 161 us
  waiting for transfers between devices  55.5 us (34%)
  Pallas kernels  43.3 us (27%)
  starting transfers between devices  35.8 us (22%)
  local copies, waits for them, and re-layouts  17.6 us (11%)
  other arithmetic  6.12 us (4%)
  between operations  3.06 us (2%)
    ppermute x12, waiting for transfers between devices, moved(): return lax.ppermute(block, axis, pairs)  47.6 us
    ppermute x12, starting transfers between devices, moved(): return lax.ppermute(block, axis, pairs)  30.3 us
    pallas_call x1, Pallas kernels, on_device(): pl.pallas_call(outputs_kernel, out_shape=(jax.ShapeDtypeStruct(iterate.sh...  18.3 us
    pallas_call x1, Pallas kernels, on_device(): pl.pallas_call(partial(early_kernel, rows), out_shape=tuple((jax.ShapeDty...  14.4 us
    unnamed x21, local copies, waits for them, and re-layouts  11.9 us
    pallas_call x1, Pallas kernels, on_device(): pl.pallas_call(partial(late_kernel, rows), out_shape=(sums, spl), in_spec...  10.6 us
    ppermute x4, waiting for transfers between devices, all_sum(): lax.ppermute(values, axis, [(i, i ^ step) for i in range(count)])  7.89 us
    ppermute x4, starting transfers between devices, all_sum(): lax.ppermute(values, axis, [(i, i ^ step) for i in range(count)])  5.56 us
  transfers between devices with their start and end apart: 16, of which 12 were waited for; matrix products, arithmetic and copies ran while one was open for 5% of the time, Pallas kernels for 9%

profile of v4, /device:TPU:0, one launch (start us, length us, event | category | flops | bytes accessed | tf_op | source)
XLA Modules:
  0.0 161.4 jit_solution(1923278480273998580)
XLA Ops:
  0.6 1.0 pad_add_fusion
  1.7 2.8 %copy.8 = f32[16,2,64,256]{3,0,2,1:T(8,128)S(1)} copy(f32[16,2,64,256]{3,2,1,0:T(8,128)} %param.5) | data formatting | bytes 4194304 | tf_op args[1]
  4.5 0.2 reverse_select_fusion
  4.8 0.2 slice_bitcast_fusion.1
  5.0 1.7 %fusion.1 = (f32[76,16,256]{2,1,0:T(8,128)}, f32[76,16,256]{2,1,0:T(8,128)}) fusion(f32[8,16,256]{2,1,0:T(8,128)S(1)} %bitcast.78, f32[4,16,256]{2,1,0:T(8,128)S(1)} %bitcast.81, f32[64,16,256]{2,1,0:T(8,128)S(1)} %get-tuple-element.20, f32[4,16,256]{2,1,0:T(8,128)S(1)} %bitcast.82, f32[64,16,256]{2,1,0:T(8,128)S(1)} %get-tuple-element.21), kind=kLoop, calls=%fused_computation.7 | loop fusion | flops 1245184 | bytes 4849664 | tf_op jit(solution)/shard_map/concatenate | solution.py:350
  6.7 6.0 %collective-permute-start.8 = (f32[76,16,256]{2,1,0:T(8,128)}, f32[76,16,256]{2,1,0:T(8,128)}, u32[]{:S(2)}, u32[]{:S(2)}) collective-permute-start(f32[76,16,256]{2,1,0:T(8,128)} %get-tuple-element.39), channel_id=1, source_target_pairs={{0,4},{4,8},{6,2},{8,12},{10,6},{14,10},{1,5},{5,9},{7,3},{9,13},{... | collective-permute-start | bytes 3735560 | tf_op jit(solution)/shard_map/ppermute | solution.py:22
  12.7 0.7 collective-permute-start.1
  13.3 3.3 %collective-permute-start = (f32[2,2,64,256]{3,2,1,0:T(8,128)S(1)}, f32[2,2,64,256]{3,2,1,0:T(8,128)S(1)}, u32[]{:S(2)}, u32[]{:S(2)}) collective-permute-start(f32[2,2,64,256]{3,2,1,0:T(8,128)S(1)} %pad_maximum_fusion.5), channel_id=1, source_target_pairs={{0,2},{2,0},{4,6},{6,4},{8,10},{10,8},{12,14},{14,12},{1,3},{3,1},... | collective-permute-start | bytes 786440 | tf_op jit(solution)/shard_map/ppermute | solution.py:22
  16.6 0.1 collective-permute-start.2
  16.7 1.3 collective-permute-start.10
  18.0 0.0 collective-permute-done.2
  18.1 0.0 collective-permute-done.1
  18.1 0.6 slice.245
  19.4 6.4 %collective-permute-done = f32[2,2,64,256]{3,2,1,0:T(8,128)S(1)} collective-permute-done((f32[2,2,64,256]{3,2,1,0:T(8,128)S(1)}, f32[2,2,64,256]{3,2,1,0:T(8,128)S(1)}, u32[]{:S(2)}, u32[]{:S(2)}) %collective-permute-start) | collective-permute-done | bytes 262176 | tf_op jit(solution)/shard_map/ppermute | solution.py:22
  25.7 0.6 slice.244
  27.0 0.7 pad_maximum_fusion
  27.7 0.1 slice.248
  27.8 2.5 %collective-permute-start.3 = (f32[1,68,16,256]{3,2,1,0:T(8,128)S(1)}, f32[1,68,16,256]{3,2,1,0:T(8,128)S(1)}, u32[]{:S(2)}, u32[]{:S(2)}) collective-permute-start(f32[1,68,16,256]{3,2,1,0:T(8,128)S(1)} %slice.248), channel_id=1, source_target_pairs={{0,2},{2,0},{4,6},{6,4},{8,10},{10,8},{12,14},{14,12},{1,3},{3,1},... | collective-permute-start | bytes 3342344 | tf_op jit(solution)/shard_map/ppermute | solution.py:22
  30.3 8.2 %collective-permute-done.8 = f32[76,16,256]{2,1,0:T(8,128)} collective-permute-done((f32[76,16,256]{2,1,0:T(8,128)}, f32[76,16,256]{2,1,0:T(8,128)}, u32[]{:S(2)}, u32[]{:S(2)}) %collective-permute-start.8) | collective-permute-done | bytes 1245216 | tf_op jit(solution)/shard_map/ppermute | solution.py:22
  38.5 0.8 slice.265
  39.4 0.9 slice.259
  40.4 8.2 %collective-permute-done.10 = f32[76,16,256]{2,1,0:T(8,128)S(1)} collective-permute-done((f32[76,16,256]{2,1,0:T(8,128)}, f32[76,16,256]{2,1,0:T(8,128)S(1)}, u32[]{:S(2)}, u32[]{:S(2)}) %collective-permute-start.10) | collective-permute-done | bytes 1245216 | tf_op jit(solution)/shard_map/ppermute | solution.py:22
  48.7 0.1 collective-permute-start.11
  48.8 0.1 slice_bitcast_fusion.near3
  48.9 1.3 slice_bitcast_fusion.2.far3
  50.2 0.0 collective-permute-done.11
  50.2 0.2 pad_maximum_fusion.3
  50.4 0.1 slice_bitcast_fusion.4
  50.5 0.2 fusion.23
  50.8 4.4 %collective-permute-done.3.near2 = f32[1,68,16,256]{3,2,1,0:T(8,128)S(1)} collective-permute-done((f32[1,68,16,256]{3,2,1,0:T(8,128)S(1)}, f32[1,68,16,256]{3,2,1,0:T(8,128)S(1)}, u32[]{:S(2)}, u32[]{:S(2)}) %collective-permute-start.3) | collective-permute-done | bytes 1114144 | tf_op jit(solution)/shard_map/ppermute | solution.py:22
  55.2 0.5 slice.249
  56.3 0.1 slice_select_fusion
  56.4 0.1 fusion.22
  56.5 1.8 %collective-permute-start.6 = (f32[1,68,8,256]{3,2,1,0:T(8,128)S(1)}, f32[1,68,8,256]{3,2,1,0:T(8,128)S(1)}, u32[]{:S(2)}, u32[]{:S(2)}) collective-permute-start(f32[1,68,8,256]{3,2,1,0:T(8,128)S(1)} %get-tuple-element.24), channel_id=1, source_target_pairs={{0,2},{2,0},{4,6},{6,4},{8,10},{10,8},{12,14},{14,12},{1,3},{3,1},... | collective-permute-start | bytes 1671176 | tf_op jit(solution)/shard_map/ppermute | solution.py:22
  58.3 0.3 collective-permute-start.4
  58.6 4.9 %collective-permute-start.9 = (f32[1,68,16,256]{3,2,1,0:T(8,128)S(1)}, f32[1,68,16,256]{3,2,1,0:T(8,128)S(1)}, u32[]{:S(2)}, u32[]{:S(2)}) collective-permute-start(f32[1,68,16,256]{3,2,1,0:T(8,128)S(1)} %collective-permute-done.3.near2), channel_id=1, source_target_pairs={{0,4},{4,8},{6,2},{8,12},{10,6},{14,10},{1,5},{5,9},{7,3},{9,13},{... | collective-permute-start | bytes 3342344 | tf_op jit(solution)/shard_map/ppermute | solution.py:22
  63.5 1.2 slice_multiply_fusion.2
  64.7 0.3 slice_multiply_fusion.sy
  65.0 7.1 %collective-permute-done.6 = f32[1,68,8,256]{3,2,1,0:T(8,128)S(1)} collective-permute-done((f32[1,68,8,256]{3,2,1,0:T(8,128)S(1)}, f32[1,68,8,256]{3,2,1,0:T(8,128)S(1)}, u32[]{:S(2)}, u32[]{:S(2)}) %collective-permute-start.6) | collective-permute-done | bytes 557088 | tf_op jit(solution)/shard_map/ppermute | solution.py:22
  72.1 4.9 %collective-permute-start.7 = (f32[1,68,8,256]{3,2,1,0:T(8,128)S(1)}, f32[1,68,8,256]{3,2,1,0:T(8,128)S(1)}, u32[]{:S(2)}, u32[]{:S(2)}) collective-permute-start(f32[1,68,8,256]{3,2,1,0:T(8,128)S(1)} %collective-permute-done.6), channel_id=1, source_target_pairs={{0,4},{4,8},{6,2},{8,12},{10,6},{14,10},{1,5},{5,9},{7,3},{9,13},{... | collective-permute-start | bytes 1671176 | tf_op jit(solution)/shard_map/ppermute | solution.py:22
  77.0 5.7 %collective-permute-done.4 = f32[1,68,8,256]{3,2,1,0:T(8,128)S(1)} collective-permute-done((f32[1,68,8,256]{3,2,1,0:T(8,128)S(1)}, f32[1,68,8,256]{3,2,1,0:T(8,128)S(1)}, u32[]{:S(2)}, u32[]{:S(2)}) %collective-permute-start.4) | collective-permute-done | bytes 557088 | tf_op jit(solution)/shard_map/ppermute | solution.py:22
  82.7 4.5 %collective-permute-start.5 = (f32[1,68,8,256]{3,2,1,0:T(8,128)S(1)}, f32[1,68,8,256]{3,2,1,0:T(8,128)S(1)}, u32[]{:S(2)}, u32[]{:S(2)}) collective-permute-start(f32[1,68,8,256]{3,2,1,0:T(8,128)S(1)} %collective-permute-done.4), channel_id=1, source_target_pairs={{0,4},{4,8},{6,2},{8,12},{10,6},{14,10},{1,5},{5,9},{7,3},{9,13},{... | collective-permute-start | bytes 1671176 | tf_op jit(solution)/shard_map/ppermute | solution.py:22
  87.2 0.2 slice_multiply_fusion.3.sz
  87.4 0.2 slice.281
  87.6 0.3 pad_multiply_fusion
  87.9 0.1 pad_maximum_fusion.4.near1
  88.0 0.5 collective-permute-done.9.far1
  88.4 14.4 %shard_map.59 = (f32[5,70,16,256]{3,2,1,0:T(8,128)}, f32[2,70,16,256]{3,2,1,0:T(8,128)S(1)}, f32[2,70,16,256]{3,2,1,0:T(8,128)S(1)}, bf16[2,64,64,256]{3,2,1,0:T(8,128)(2,1)S(1)}, f32[16,128]{1,0:T(8,128)S(1)}) custom-call(f32[1,64,16,256]{3,2,1,0:T(8,128)S(1)} %slice_bitcast_fusion.2.far3, f32[1,68,16,256]{3,2,1,0:T(8,128)S(1)} %collective-permute-done.9.far1, ...), custom_call_target="tpu_custom_call" | custom-call | bytes 52428800 | tf_op jit(solution)/shard_map/pallas_call | solution.py:397
  102.9 0.0 collective-permute-done.7.far2b
  102.9 7.1 %collective-permute-done.5.far2a = f32[1,68,8,256]{3,2,1,0:T(8,128)S(1)} collective-permute-done((f32[1,68,8,256]{3,2,1,0:T(8,128)S(1)}, f32[1,68,8,256]{3,2,1,0:T(8,128)S(1)}, u32[]{:S(2)}, u32[]{:S(2)}) %collective-permute-start.5) | collective-permute-done | bytes 557088 | tf_op jit(solution)/shard_map/ppermute | solution.py:22
  110.0 2.6 %copy-done.2 = f32[5,70,16,256]{3,2,1,0:T(8,128)S(1)} copy-done((f32[5,70,16,256]{3,2,1,0:T(8,128)S(1)}, f32[5,70,16,256]{3,2,1,0:T(8,128)}, u32[]{:S(2)}) %copy-start.2) | copy-done | bytes 5734424
  112.6 10.6 %shard_map.60 = (f32[16,128]{1,0:T(8,128)S(1)}, bf16[2,64,64,256]{3,2,1,0:T(8,128)(2,1)S(1)}) custom-call(f32[1,68,8,256]{3,2,1,0:T(8,128)S(1)} %collective-permute-done.5.far2a, f32[1,68,8,256]{3,2,1,0:T(8,128)S(1)} %collective-permute-done.7.far2b, f32[5,70,16,256]{3,2,1,0:T(8,128)S(1)} %copy-done.2, f32[2,70,16,256]{3,2,1,0:T(8,128)S(1)} %get-tuple-element.10.u1_in, ...), custom_call_target="tpu_custom_call" | custom-call | bytes 52428800 | tf_op jit(solution)/shard_map/pallas_call | solution.py:407
  123.2 2.0 %copy-done.3 = bf16[2,64,64,256]{3,2,1,0:T(8,128)(2,1)} copy-done((bf16[2,64,64,256]{3,2,1,0:T(8,128)(2,1)}, bf16[2,64,64,256]{3,2,1,0:T(8,128)(2,1)S(1)}, u32[]{:S(2)}) %copy-start.3) | copy-done | bytes 4194328
  125.2 0.0 collective-permute-start.12
  125.2 1.2 collective-permute-done.12
  126.4 1.3 collective-permute-start.13
  127.7 2.3 %collective-permute-done.13 = f32[16,128]{1,0:T(8,128)S(1)} collective-permute-done((f32[16,128]{1,0:T(8,128)S(1)}, f32[16,128]{1,0:T(8,128)S(1)}, u32[]{:S(2)}, u32[]{:S(2)}) %collective-permute-start.13) | collective-permute-done | bytes 8224 | tf_op jit(solution)/shard_map/ppermute | solution.py:72
  130.0 2.5 %collective-permute-start.14 = (f32[16,128]{1,0:T(8,128)S(1)}, f32[16,128]{1,0:T(8,128)S(1)}, u32[]{:S(2)}, u32[]{:S(2)}) collective-permute-start(f32[16,128]{1,0:T(8,128)S(1)} %add.81), channel_id=1, source_target_pairs={{0,4},{2,6},{4,0},{6,2},{8,12},{10,14},{12,8},{14,10},{1,5},{3,7},... | collective-permute-start | bytes 24584 | tf_op jit(solution)/shard_map/ppermute | solution.py:72
  132.5 1.6 %collective-permute-done.14 = f32[16,128]{1,0:T(8,128)S(1)} collective-permute-done((f32[16,128]{1,0:T(8,128)S(1)}, f32[16,128]{1,0:T(8,128)S(1)}, u32[]{:S(2)}, u32[]{:S(2)}) %collective-permute-start.14) | collective-permute-done | bytes 8224 | tf_op jit(solution)/shard_map/ppermute | solution.py:72
  134.1 1.7 %collective-permute-start.15 = (f32[16,128]{1,0:T(8,128)S(1)}, f32[16,128]{1,0:T(8,128)S(1)}, u32[]{:S(2)}, u32[]{:S(2)}) collective-permute-start(f32[16,128]{1,0:T(8,128)S(1)} %add.82), channel_id=1, source_target_pairs={{0,8},{2,10},{4,12},{6,14},{8,0},{10,2},{12,4},{14,6},{1,9},{3,11}... | collective-permute-start | bytes 24584 | tf_op jit(solution)/shard_map/ppermute | solution.py:72
  135.9 2.8 %collective-permute-done.15 = f32[16,128]{1,0:T(8,128)S(1)} collective-permute-done((f32[16,128]{1,0:T(8,128)S(1)}, f32[16,128]{1,0:T(8,128)S(1)}, u32[]{:S(2)}, u32[]{:S(2)}) %collective-permute-start.15) | collective-permute-done | bytes 8224 | tf_op jit(solution)/shard_map/ppermute | solution.py:72
  138.7 2.2 %copy-done.1 = bf16[2,64,64,256]{3,2,1,0:T(8,128)(2,1)S(1)} copy-done((bf16[2,64,64,256]{3,2,1,0:T(8,128)(2,1)S(1)}, bf16[2,64,64,256]{3,2,1,0:T(8,128)(2,1)}, u32[]{:S(2)}) %copy-start.1) | copy-done | bytes 4194328
  140.9 2.2 %copy-done.4 = bf16[2,64,64,256]{3,2,1,0:T(8,128)(2,1)S(1)} copy-done((bf16[2,64,64,256]{3,2,1,0:T(8,128)(2,1)S(1)}, bf16[2,64,64,256]{3,2,1,0:T(8,128)(2,1)}, u32[]{:S(2)}) %copy-start.4) | copy-done | bytes 4194328
  143.1 18.3 %shard_map.61 = (f32[16,2,64,256]{3,2,1,0:T(8,128)}, f32[16,2,64,256]{3,2,1,0:T(8,128)}) custom-call(s32[1]{0:T(128)} %bitcast.odd, f32[16,128]{1,0:T(8,128)S(1)} %add.83.moments, bf16[2,64,64,256]{3,2,1,0:T(8,128)(2,1)S(1)} %copy-done.1, bf16[2,64,64,256]{3,2,1,0:T(8,128)(2,1)S(1)} %copy-done.4, f32[2,64,256]{2,1,0:T(8,128)S(1)} %slice.290.inverse, ...), custom_call_target="tpu_custom_call" | custom-call | tf_op jit(solution)/shard_map/pallas_call | solution.py:424
  (36 shorter events, 0.4 us)
Async XLA Ops:
  6.7 31.9 %collective-permute-start.8 = (f32[76,16,256]{2,1,0:T(8,128)}, f32[76,16,256]{2,1,0:T(8,128)}, u32[]{:S(2)}, u32[]{:S(2)}) collective-permute-start(f32[76,16,256]{2,1,0:T(8,128)} %get-tuple-element.39), channel_id=1, source_target_pairs={{0,4},{4,8},{6,2},{8,12},{10,6},{14,10},{1,5},{5,9},{7,3},{9,13},{... | collective-permute-start | bytes 3735560 | tf_op jit(solution)/shard_map/ppermute | solution.py:22
  12.7 5.4 %collective-permute-start.1 = (f32[2,2,64,256]{3,2,1,0:T(8,128)S(1)}, f32[2,2,64,256]{3,2,1,0:T(8,128)S(1)}, u32[]{:S(2)}, u32[]{:S(2)}) collective-permute-start(f32[2,2,64,256]{3,2,1,0:T(8,128)S(1)} %pad_maximum_fusion.5), channel_id=1, source_target_pairs={{2,4},{4,2},{6,8},{8,6},{10,12},{12,10},{3,5},{5,3},{7,9},{9,7},{1... | collective-permute-start | bytes 786440 | tf_op jit(solution)/shard_map/ppermute | solution.py:22
  13.3 12.4 %collective-permute-start = (f32[2,2,64,256]{3,2,1,0:T(8,128)S(1)}, f32[2,2,64,256]{3,2,1,0:T(8,128)S(1)}, u32[]{:S(2)}, u32[]{:S(2)}) collective-permute-start(f32[2,2,64,256]{3,2,1,0:T(8,128)S(1)} %pad_maximum_fusion.5), channel_id=1, source_target_pairs={{0,2},{2,0},{4,6},{6,4},{8,10},{10,8},{12,14},{14,12},{1,3},{3,1},... | collective-permute-start | bytes 786440 | tf_op jit(solution)/shard_map/ppermute | solution.py:22
  16.6 1.4 collective-permute-start.2
  16.7 31.9 %collective-permute-start.10 = (f32[76,16,256]{2,1,0:T(8,128)}, f32[76,16,256]{2,1,0:T(8,128)S(1)}, u32[]{:S(2)}, u32[]{:S(2)}) collective-permute-start(f32[76,16,256]{2,1,0:T(8,128)} %get-tuple-element.38), channel_id=1, source_target_pairs={{4,0},{8,4},{2,6},{12,8},{6,10},{10,14},{5,1},{9,5},{3,7},{13,9},{... | collective-permute-start | bytes 3735560 | tf_op jit(solution)/shard_map/ppermute | solution.py:22
  27.8 27.4 %collective-permute-start.3 = (f32[1,68,16,256]{3,2,1,0:T(8,128)S(1)}, f32[1,68,16,256]{3,2,1,0:T(8,128)S(1)}, u32[]{:S(2)}, u32[]{:S(2)}) collective-permute-start(f32[1,68,16,256]{3,2,1,0:T(8,128)S(1)} %slice.248), channel_id=1, source_target_pairs={{0,2},{2,0},{4,6},{6,4},{8,10},{10,8},{12,14},{14,12},{1,3},{3,1},... | collective-permute-start | bytes 3342344 | tf_op jit(solution)/shard_map/ppermute | solution.py:22
  48.7 1.5 collective-permute-start.11
  56.5 15.6 %collective-permute-start.6 = (f32[1,68,8,256]{3,2,1,0:T(8,128)S(1)}, f32[1,68,8,256]{3,2,1,0:T(8,128)S(1)}, u32[]{:S(2)}, u32[]{:S(2)}) collective-permute-start(f32[1,68,8,256]{3,2,1,0:T(8,128)S(1)} %get-tuple-element.24), channel_id=1, source_target_pairs={{0,2},{2,0},{4,6},{6,4},{8,10},{10,8},{12,14},{14,12},{1,3},{3,1},... | collective-permute-start | bytes 1671176 | tf_op jit(solution)/shard_map/ppermute | solution.py:22
  58.3 24.3 %collective-permute-start.4 = (f32[1,68,8,256]{3,2,1,0:T(8,128)S(1)}, f32[1,68,8,256]{3,2,1,0:T(8,128)S(1)}, u32[]{:S(2)}, u32[]{:S(2)}) collective-permute-start(f32[1,68,8,256]{3,2,1,0:T(8,128)S(1)} %get-tuple-element.25), channel_id=1, source_target_pairs={{0,2},{2,0},{4,6},{6,4},{8,10},{10,8},{12,14},{14,12},{1,3},{3,1},... | collective-permute-start | bytes 1671176 | tf_op jit(solution)/shard_map/ppermute | solution.py:22
  58.6 29.8 %collective-permute-start.9 = (f32[1,68,16,256]{3,2,1,0:T(8,128)S(1)}, f32[1,68,16,256]{3,2,1,0:T(8,128)S(1)}, u32[]{:S(2)}, u32[]{:S(2)}) collective-permute-start(f32[1,68,16,256]{3,2,1,0:T(8,128)S(1)} %collective-permute-done.3.near2), channel_id=1, source_target_pairs={{0,4},{4,8},{6,2},{8,12},{10,6},{14,10},{1,5},{5,9},{7,3},{9,13},{... | collective-permute-start | bytes 3342344 | tf_op jit(solution)/shard_map/ppermute | solution.py:22
  72.1 30.7 %collective-permute-start.7 = (f32[1,68,8,256]{3,2,1,0:T(8,128)S(1)}, f32[1,68,8,256]{3,2,1,0:T(8,128)S(1)}, u32[]{:S(2)}, u32[]{:S(2)}) collective-permute-start(f32[1,68,8,256]{3,2,1,0:T(8,128)S(1)} %collective-permute-done.6), channel_id=1, source_target_pairs={{0,4},{4,8},{6,2},{8,12},{10,6},{14,10},{1,5},{5,9},{7,3},{9,13},{... | collective-permute-start | bytes 1671176 | tf_op jit(solution)/shard_map/ppermute | solution.py:22
  82.7 27.3 %collective-permute-start.5 = (f32[1,68,8,256]{3,2,1,0:T(8,128)S(1)}, f32[1,68,8,256]{3,2,1,0:T(8,128)S(1)}, u32[]{:S(2)}, u32[]{:S(2)}) collective-permute-start(f32[1,68,8,256]{3,2,1,0:T(8,128)S(1)} %collective-permute-done.4), channel_id=1, source_target_pairs={{0,4},{4,8},{6,2},{8,12},{10,6},{14,10},{1,5},{5,9},{7,3},{9,13},{... | collective-permute-start | bytes 1671176 | tf_op jit(solution)/shard_map/ppermute | solution.py:22
  102.9 20.3 %copy-start = (bf16[2,64,64,256]{3,2,1,0:T(8,128)(2,1)}, bf16[2,64,64,256]{3,2,1,0:T(8,128)(2,1)S(1)}, u32[]{:S(2)}) copy-start(bf16[2,64,64,256]{3,2,1,0:T(8,128)(2,1)S(1)} %get-tuple-element.12.split_in.split01) | copy-start | bytes 12582916
  110.0 2.6 %copy-start.2 = (f32[5,70,16,256]{3,2,1,0:T(8,128)S(1)}, f32[5,70,16,256]{3,2,1,0:T(8,128)}, u32[]{:S(2)}) copy-start(f32[5,70,16,256]{3,2,1,0:T(8,128)} %get-tuple-element.9.u0_in) | copy-start | bytes 17203204
  112.6 26.1 %copy-start.5 = (f32[16,2,64,256]{3,2,1,0:T(8,128)S(1)}, f32[16,2,64,256]{3,2,1,0:T(8,128)}, u32[]{:S(2)}) copy-start(f32[16,2,64,256]{3,2,1,0:T(8,128)} %iterate.1) | copy-start | bytes 6291460
  123.2 2.0 %copy-start.3 = (bf16[2,64,64,256]{3,2,1,0:T(8,128)(2,1)}, bf16[2,64,64,256]{3,2,1,0:T(8,128)(2,1)S(1)}, u32[]{:S(2)}) copy-start(bf16[2,64,64,256]{3,2,1,0:T(8,128)(2,1)S(1)} %get-tuple-element.15.split23) | copy-start | bytes 12582916
  125.2 1.2 collective-permute-start.12
  126.4 3.7 %collective-permute-start.13 = (f32[16,128]{1,0:T(8,128)S(1)}, f32[16,128]{1,0:T(8,128)S(1)}, u32[]{:S(2)}, u32[]{:S(2)}) collective-permute-start(f32[16,128]{1,0:T(8,128)S(1)} %add.80), channel_id=1, source_target_pairs={{0,2},{2,0},{4,6},{6,4},{8,10},{10,8},{12,14},{14,12},{1,3},{3,1},... | collective-permute-start | bytes 24584 | tf_op jit(solution)/shard_map/ppermute | solution.py:72
  130.0 4.1 %collective-permute-start.14 = (f32[16,128]{1,0:T(8,128)S(1)}, f32[16,128]{1,0:T(8,128)S(1)}, u32[]{:S(2)}, u32[]{:S(2)}) collective-permute-start(f32[16,128]{1,0:T(8,128)S(1)} %add.81), channel_id=1, source_target_pairs={{0,4},{2,6},{4,0},{6,2},{8,12},{10,14},{12,8},{14,10},{1,5},{3,7},... | collective-permute-start | bytes 24584 | tf_op jit(solution)/shard_map/ppermute | solution.py:72
  134.1 4.5 %collective-permute-start.15 = (f32[16,128]{1,0:T(8,128)S(1)}, f32[16,128]{1,0:T(8,128)S(1)}, u32[]{:S(2)}, u32[]{:S(2)}) collective-permute-start(f32[16,128]{1,0:T(8,128)S(1)} %add.82), channel_id=1, source_target_pairs={{0,8},{2,10},{4,12},{6,14},{8,0},{10,2},{12,4},{14,6},{1,9},{3,11}... | collective-permute-start | bytes 24584 | tf_op jit(solution)/shard_map/ppermute | solution.py:72
  138.7 2.2 %copy-start.1 = (bf16[2,64,64,256]{3,2,1,0:T(8,128)(2,1)S(1)}, bf16[2,64,64,256]{3,2,1,0:T(8,128)(2,1)}, u32[]{:S(2)}) copy-start(bf16[2,64,64,256]{3,2,1,0:T(8,128)(2,1)} %copy-done) | copy-start | bytes 12582916
  140.9 2.2 %copy-start.4 = (bf16[2,64,64,256]{3,2,1,0:T(8,128)(2,1)S(1)}, bf16[2,64,64,256]{3,2,1,0:T(8,128)(2,1)}, u32[]{:S(2)}) copy-start(bf16[2,64,64,256]{3,2,1,0:T(8,128)(2,1)} %copy-done.3) | copy-start | bytes 12582916

commit v5 on v4

--- a/solution.py
+++ b/solution.py
@@ -31,24 +31,11 @@
     return moved(block, "gz", [(i, i ^ 1) for i in range(lax.axis_size("gz"))])
 
 
-def swapped_far(block):
-    count = lax.axis_size("gz")
-    steps = [(i, i - 1 + 2 * (i % 2)) for i in range(count)]
-    return moved(block, "gz", [(i, j) for i, j in steps if 0 <= j < count])
-
-
 def relayed(block, back=False):
     count = lax.axis_size("gz")
     steps = [(i, i + 2 - 4 * (i % 2)) for i in range(count)]
     pairs = [(i, j) for i, j in steps if 0 <= j < count]
     return moved(block, "gz", [(j, i) for i, j in pairs] if back else pairs)
-
-
-def after(value, *earlier):
-    here = True
-    for block in earlier:
-        here = here & (block[(0,) * block.ndim] >= jnp.finfo(f32).min)
-    return jnp.where(here, value, 0.0)
 
 
 def rows_beside(before, after):
@@ -138,17 +125,17 @@
     return max(REACH - plane, plane - (REACH + depth - 1), 0)
 
 
-def scale_plane(rows, plane, piece, inverse, dst):
-    reach = REACH - spread(plane)
-    ref, index = piece
+def scale_rows(plane, source, first, dst, start, count, inverse, part=slice(None)):
     out, place = dst
-    shift = (ref.shape[1] - rows) // 2 - REACH
-
-    def body(y):
-        for j in range(8):
-            out[place, y + j] = ref[index, y + (j + shift)] * inverse[plane, pl.ds(y + j, 1), :]
-
-    row_blocks(REACH - reach, REACH + rows + reach, body)
+
+    def body(j, size=8):
+        for i in range(size):
+            out[place, start + j + i, part] = source[first + j + i] * inverse[plane, pl.ds(start + j + i, 1), :]
+
+    if count < 8:
+        body(0, count)
+    else:
+        row_blocks(0, count, body)
 
 
 def apply_plane(rows, power, plane, operator, fields):
@@ -164,6 +151,7 @@
 
 
 LATE = 1
+BESIDE = ((5, 0, 2), (6, 2, 1), (2, 3, 2))
 
 
 def halves(blocks):
@@ -183,17 +171,26 @@
 
 
 def early_kernel(
-    rows, far3, far1, own, near1, near2, near3, inverse, sx, sy, sz,
-    u0_out, u1_out, u2_out, split, moments, u0, u1,
+    rows, far3, far1, own, own_before, own_behind, near1a, near1b, near2, near3, before, behind,
+    inverse, sx, sy, sz, u0_out, u1_out, u2_out, split, moments, u0, u1,
 ):
     operator = (sx, sy, sz)
-    fields = {(0, plane): (u0_out, plane) for plane in range(5)}
-    fields.update({(0, plane): (u0, plane - 5) for plane in range(5, 8)})
+    fields = {(0, plane): (u0_out, index) for index, plane in enumerate((0, 2, 3))}
+    fields.update({(0, plane): (u0, plane - 4) for plane in range(4, 8)})
     fields.update({(1, 3): (u1_out, 0), (1, 4): (u1_out, 1), (1, 5): (u1, 0), (1, 6): (u1, 1)})
     fields.update({(2, 4): (u2_out, 0), (2, 5): (u2_out, 1)})
-    pieces = {0: (far3, 0), 2: (far1, 0), 3: (own, 0), 4: (own, 1), 5: (near1, 0), 6: (near2, 0), 7: (near3, 0)}
-    for plane, piece in pieces.items():
-        scale_plane(rows, plane, piece, inverse, fields[0, plane])
+    first, last = REACH, REACH + rows
+    half = near1a.shape[1]
+    for plane, source in ((0, far3), (2, far1), (3, own.at[0]), (4, own.at[1]), (6, near2), (7, near3)):
+        scale_rows(plane, source, 0, fields[0, plane], first, rows, inverse)
+    scale_rows(5, near1a, 0, fields[0, 5], first, rows, inverse, slice(0, half))
+    scale_rows(5, near1b, 0, fields[0, 5], first, rows, inverse, slice(half, None))
+    for plane in (3, 4):
+        scale_rows(plane, own_before.at[plane - 3], 0, fields[0, plane], 0, REACH, inverse)
+        scale_rows(plane, own_behind.at[plane - 3], 0, fields[0, plane], last, REACH, inverse)
+    for plane, place, count in BESIDE:
+        scale_rows(plane, before, place, fields[0, plane], first - count, count, inverse)
+        scale_rows(plane, behind, place, fields[0, plane], last, count, inverse)
     for power, plane in ((1, 3), (1, 4), (1, 5), (1, 6), (2, 4), (2, 5)):
         apply_plane(rows, power, plane, operator, fields)
 
@@ -219,25 +216,20 @@
 
 
 def late_kernel(
-    rows, far2a, far2b, u0_in, u1_in, u2_in, split_in, moments_in, inverse, sx, sy, sz, moments, split, u0, u1, u2
+    rows, far2a, far2b, u0_in, u1_in, u2_in, moments_in, inverse, sx, sy, sz, moments, split, u0, u1, u2
 ):
     operator = (sx, sy, sz)
-    fields = {(0, plane): (u0_in, plane) for plane in range(5)}
+    fields = {(0, plane): (u0_in, index) for index, plane in enumerate((0, 2, 3))}
     fields[0, LATE] = (u0, 0)
     fields.update({(1, 1): (u1, 0), (1, 2): (u1, 1), (1, 3): (u1_in, 0), (1, 4): (u1_in, 1)})
     fields.update({(2, 2): (u2, 0), (2, 3): (u2, 1), (2, 4): (u2_in, 0), (2, 5): (u2_in, 1)})
-
-    reach = REACH - spread(LATE)
-    shift = (far2a.shape[1] - rows) // 2 - REACH
-    part = far2a.shape[2]
-
-    def scale(y):
-        for j in range(8):
-            factor = inverse[LATE, pl.ds(y + j, 1), :]
-            u0[0, y + j, :part] = far2a[0, y + (j + shift)] * factor
-            u0[0, y + j, part:] = far2b[0, y + (j + shift)] * factor
-
-    row_blocks(REACH - reach, REACH + rows + reach, scale)
+    first, last = REACH, REACH + rows
+    half = far2a.shape[1]
+    for source, part in ((far2a, slice(0, half)), (far2b, slice(half, None))):
+        scale_rows(LATE, source, 0, fields[0, LATE], first, rows, inverse, part)
+    for place, y in ((rows, first - 1), (rows + 2, last)):
+        for index, part in enumerate((slice(0, half), slice(half, None))):
+            scale_rows(LATE, far2b, place + index, fields[0, LATE], y, 1, inverse, part)
     for power, plane in ((1, 1), (1, 2), (2, 2), (2, 3)):
         apply_plane(rows, power, plane, operator, fields)
 
@@ -255,8 +247,7 @@
                 ref, index = fields[2, level]
                 both = halves([ref[index, y + j], last[j]])
                 split[plane, start + j] = both
-                first = [split_in[plane, start + j, part * rhs : (part + 1) * rhs] for part in (1, 3)]
-                left.append(jnp.concatenate(first + [both], axis=0))
+                left.append(jnp.concatenate([halves([u1_in[plane, y + j]]), both], axis=0))
                 right.append(jnp.concatenate([both[:rhs], both[2 * rhs : 3 * rhs]], axis=0))
             return total + inner_products(jnp.concatenate(left, axis=1), jnp.concatenate(right, axis=1))
 
@@ -271,22 +262,28 @@
 
 
 def eliminate(stacked, size):
-    lane = lax.broadcasted_iota(jnp.int32, (1, stacked.shape[1]), 1)
-    done = 0
+    tiles, height, width = stacked.shape
+    lane = lax.broadcasted_iota(jnp.int32, (height, width), 1)
+
+    def everywhere(row):
+        return jnp.broadcast_to(row, (height, width))
+
     for k in range(0, size, 2):
-        if k - done == 8:
-            stacked, done = stacked[8:], k
-        at = k - done
-        row0, row1 = stacked[at : at + 1, :], stacked[at + 1 : at + 2, :]
-        col0, col1 = stacked[:, k : k + 1], stacked[:, k + 1 : k + 2]
-        a, b = row0[:, k : k + 1], row0[:, k + 1 : k + 2]
-        c, d = row1[:, k : k + 1], row1[:, k + 1 : k + 2]
+        if k and k % height == 0:
+            stacked = stacked[1:]
+        at = k % height
+        row0, row1 = everywhere(stacked[0, at : at + 1]), everywhere(stacked[0, at + 1 : at + 2])
+        col0 = jnp.broadcast_to(stacked[:, :, k : k + 1], stacked.shape)
+        col1 = jnp.broadcast_to(stacked[:, :, k + 1 : k + 2], stacked.shape)
+        a, c = everywhere(col0[0, at : at + 1]), everywhere(col0[0, at + 1 : at + 2])
+        b, d = everywhere(col1[0, at : at + 1]), everywhere(col1[0, at + 1 : at + 2])
         scale = 1.0 / (a * d - b * c)
-        new0 = col0 * (d * scale) - col1 * (c * scale)
-        new1 = col1 * (a * scale) - col0 * (b * scale)
-        rest = stacked - new0 * row0 - new1 * row1
-        stacked = jnp.where(lane == k, new0, jnp.where(lane == k + 1, new1, rest))
-    return stacked[size - done :]
+        first, second = lane == k, lane == k + 1
+        mix0 = scale * jnp.where(first, -d, jnp.where(second, b, d * row0 - b * row1))
+        mix1 = scale * jnp.where(first, c, jnp.where(second, -a, a * row1 - c * row0))
+        rest = jnp.where((first | second)[None], 0.0, stacked)
+        stacked = rest - col0 * mix0[None] - col1 * mix1[None]
+    return stacked[1:]
 
 
 def mixing(moments, rhs):
@@ -296,7 +293,8 @@
     size = REACH * rhs
     rolled = [moments] + [pltpu.roll(moments, width - i * rhs, 1) for i in range(1, REACH + 1)]
     energy = [rolled[i] - rolled[i + 1] for i in range(REACH)]
-    solved = eliminate(jnp.concatenate(energy + [moments], axis=0), size)
+    tiles = jnp.concatenate(energy + [moments], axis=0).reshape(-1, 8, width)
+    solved = eliminate(tiles, size).reshape(rhs, width)
     solved = jnp.where(lane < size, solved, 0.0)
     residual = (row == lane).astype(f32) - (solved - pltpu.roll(solved, rhs, 1))
     return solved, residual
@@ -341,30 +339,28 @@
     coef = jnp.exp(cells[0].astype(f32) * (contrast_log / (NCLASS - 1)))
     inner = (1 - cells[1]).astype(f32)
     fields = jnp.stack([coef, inner])
-    field_pair = swapped(fields)
-    field_beyond = swapped_far(fields)
-
     own = mirrored(jnp.transpose(residual, (1, 2, 0, 3)), 0)
-    before, behind = rows_beside(own[:, :REACH], own[:, -REACH:])
-    def with_fields(plane, *cells):
+
+    def with_cells(plane, *cells):
         return jnp.concatenate([plane] + [block.reshape(-1, rhs, nx) for block in cells], axis=0)
 
-    def without_fields(message):
-        return message[None, :rows], message[rows:].reshape(-1, rows, nx)
-
-    far3, field_far = without_fields(relayed(with_fields(own[1], coef, inner[1:])))
-    near3, field_near = without_fields(relayed(with_fields(own[0], coef, inner[:1]), back=True))
-    own = jnp.concatenate([before, own, behind], axis=1)
-    sent = after(own, field_pair, field_beyond)[:, 1:-1]
-    near2 = swapped(sent[:1])
-    last = after(sent[1:], near2)
-    near1a = swapped(last[:, :, :half])
-    near1b = swapped(last[:, :, half:])
+    def cells_of(message):
+        return message[rows:].reshape(-1, rows, nx)
+
+    near2 = swapped(with_cells(own[0], fields))
+    far3 = relayed(with_cells(own[1], coef, inner[1:]))
+    near3 = relayed(with_cells(own[0], coef, inner[:1]), back=True)
+    own_before, own_behind = rows_beside(own[:, :REACH], own[:, -REACH:])
+    near1a = swapped(own[1, :, :half])
+    edges = [own_before[1, -1:], own_behind[1, :1]]
+    near1b = swapped(jnp.concatenate([own[1, :, half:]] + [edge.reshape(2, half, nx) for edge in edges], axis=0))
     far1 = relayed(near2)
     far2a = relayed(near1a)
     far2b = relayed(near1b)
-    near1 = jnp.concatenate([near1a, near1b], axis=2)
-
+
+    field_pair = cells_of(near2).reshape(2, depth, rows, nx)
+    field_beyond = cells_of(far1).reshape(2, depth, rows, nx)
+    field_far, field_near = cells_of(far3), cells_of(near3)
     none = jnp.zeros_like(coef[:1])
     coef = jnp.concatenate(
         [
@@ -382,8 +378,21 @@
     )
     fields = jnp.stack([coef, inner])
     wide = REACH + 1
-    before, behind = rows_beside(fields[:, :, :wide], fields[:, :, -wide:])
-    fields = jnp.concatenate([before, fields, behind], axis=2)
+
+    def edges_of(last):
+        def cut(block, count, axis=0):
+            low, high = (rows - count, rows) if last else (0, count)
+            return lax.slice_in_dim(block, low, high, axis=axis)
+
+        pair = jnp.concatenate([cut(near1a, 2), cut(near1b, 2)], axis=1)
+        planes = jnp.concatenate([pair, cut(near2, 1), cut(far1, 2)], axis=0)
+        return jnp.concatenate([planes.reshape(-1, nx), cut(fields, wide, 2).reshape(-1, nx)], axis=0)
+
+    sides = rows_beside(edges_of(False), edges_of(True))
+    count = sum(number for _, _, number in BESIDE) * rhs
+    before, behind = [side[:count].reshape(-1, rhs, nx) for side in sides]
+    fields_beside = [side[count:].reshape(2, -1, wide, nx) for side in sides]
+    fields = jnp.concatenate([fields_beside[0], fields, fields_beside[1]], axis=2)
     root, inverse, sx, sy, sz = symmetric_operator(fields[0], fields[1])
 
     extended = rows + 2 * REACH
@@ -396,23 +405,25 @@
     sums = jax.ShapeDtypeStruct((rhs, 128), f32)
     u0, u1, u2, split01, moments = pl.pallas_call(
         partial(early_kernel, rows),
-        out_shape=tuple(jax.ShapeDtypeStruct(planes(count), f32) for count in (5, 2, 2)) + (spl, sums),
-        in_specs=[vmem] * 10,
+        out_shape=tuple(jax.ShapeDtypeStruct(planes(count), f32) for count in (3, 2, 2)) + (spl, sums),
+        in_specs=[vmem] * 15,
         out_specs=(vmem,) * 5,
-        scratch_shapes=[pltpu.VMEM(planes(count), f32) for count in (3, 2)],
+        scratch_shapes=[pltpu.VMEM(planes(count), f32) for count in (4, 2)],
         compiler_params=pltpu.CompilerParams(vmem_limit_bytes=32 * 2**20),
         cost_estimate=pl.CostEstimate(flops=0, bytes_accessed=50 * 2**20, transcendentals=0),
-    )(far3, far1, own, near1, near2, near3, inverse, sx, sy, sz)
+    )(
+        far3, far1, own, own_before, own_behind, near1a, near1b, near2, near3, before, behind, inverse, sx, sy, sz
+    )
 
     moments, split23 = pl.pallas_call(
         partial(late_kernel, rows),
         out_shape=(sums, spl),
-        in_specs=[vmem] * 11,
+        in_specs=[vmem] * 10,
         out_specs=(vmem, vmem),
         scratch_shapes=[pltpu.VMEM(planes(count), f32) for count in (1, 2, 2)],
         compiler_params=pltpu.CompilerParams(vmem_limit_bytes=32 * 2**20),
         cost_estimate=pl.CostEstimate(flops=0, bytes_accessed=50 * 2**20, transcendentals=0),
-    )(far2a, far2b, u0, u1, u2, split01, moments, inverse, sx, sy, sz)
+    )(far2a, far2b, u0, u1, u2, moments, inverse, sx, sy, sz)
 
     moments = all_sum(moments, ("gy", "gz"))
 

time: 162 us -> 157 us (0.969)
  starting transfers between devices: 35.8 us -> 22.6 us
  local copies, waits for them, and re-layouts: 17.6 us -> 28.3 us
  Pallas kernels: 43.3 us -> 38.7 us
  other arithmetic: 6.12 us -> 9.99 us
  between operations: 3.06 us -> 1.19 us
    ppermute x12 -> x10, starting transfers between devices: 30.3 us -> 20 us  [moved(): return lax.ppermute(block, axis, pairs)]
    pallas_call x1, Pallas kernels: 18.3 us -> 11.4 us  [on_device(): pl.pallas_call(outputs_kernel, out_shape=(jax.ShapeDtypeStruct(iterate.sh...]
    reshape x0 -> x4, local copies, waits for them, and re-layouts: none -> 5.53 us  [the longest x2 3.09 us: edges_of(): cut(fields, wide, 2).reshape(-1, nx)]
    slice x6 -> x9, local copies, waits for them, and re-layouts: 1.84 us -> 5.51 us  [the longest x2 2.31 us: on_device(): fields_beside = [side[count:].reshape(2, -1, wide, nx) for side in sides]]
    ppermute x4, starting transfers between devices: 5.56 us -> 2.55 us  [all_sum(): lax.ppermute(values, axis, [(i, i ^ step) for i in range(count)])]
    unnamed x21 -> x59, local copies, waits for them, and re-layouts: 11.9 us -> 14.5 us
    ppermute x12 -> x10, waiting for transfers between devices: 47.6 us -> 45.7 us  [moved(): return lax.ppermute(block, axis, pairs)]
    ppermute x4, waiting for transfers between devices: 7.89 us -> 9.53 us  [all_sum(): lax.ppermute(values, axis, [(i, i ^ step) for i in range(count)])]
  transfers between devices with their start and end apart: 16 -> 14, of which waited for: 12 -> 8; matrix products, arithmetic and copies ran while one was open for 5% -> 9% of each run, Pallas kernels for 9% -> 10%
where the time goes in v5:
time: 157 us; the launch traced here: 156 us
  waiting for transfers between devices  55.2 us (35%)
  Pallas kernels  38.7 us (25%)
  local copies, waits for them, and re-layouts  28.3 us (18%)
  starting transfers between devices  22.6 us (14%)
  other arithmetic  9.99 us (6%)
    ppermute x10, waiting for transfers between devices, moved(): return lax.ppermute(block, axis, pairs)  45.7 us
    ppermute x10, starting transfers between devices, moved(): return lax.ppermute(block, axis, pairs)  20 us
    pallas_call x1, Pallas kernels, on_device(): pl.pallas_call(partial(early_kernel, rows), out_shape=tuple((jax.ShapeDty...  15.4 us
    unnamed x59, local copies, waits for them, and re-layouts  14.5 us
    pallas_call x1, Pallas kernels, on_device(): pl.pallas_call(partial(late_kernel, rows), out_shape=(sums, spl), in_spec...  11.8 us
    pallas_call x1, Pallas kernels, on_device(): pl.pallas_call(outputs_kernel, out_shape=(jax.ShapeDtypeStruct(iterate.sh...  11.4 us
    ppermute x4, waiting for transfers between devices, all_sum(): lax.ppermute(values, axis, [(i, i ^ step) for i in range(count)])  9.53 us
  transfers between devices with their start and end apart: 14, of which 8 were waited for; matrix products, arithmetic and copies ran while one was open for 9% of the time, Pallas kernels for 10%

profile of v5, /device:TPU:0, one launch (start us, length us, event | category | flops | bytes accessed | tf_op | source)
XLA Modules:
  0.0 155.9 jit_solution(16645959209341943429)
XLA Ops:
  0.6 1.0 pad_add_fusion
  1.7 0.7 copy-done.23
  2.4 2.8 %copy.8 = f32[16,2,64,256]{3,0,2,1:T(8,128)S(1)} copy(f32[16,2,64,256]{3,2,1,0:T(8,128)} %param.5) | data formatting | bytes 4194304 | tf_op args[1]
  5.2 0.2 reverse_select_fusion.own
  5.4 1.1 slice_bitcast_fusion
  6.6 1.2 pad_maximum_fusion.3
  7.8 2.9 %collective-permute-start.6 = (f32[80,16,256]{2,1,0:T(8,128)}, f32[80,16,256]{2,1,0:T(8,128)}, u32[]{:S(2)}, u32[]{:S(2)}) collective-permute-start(f32[80,16,256]{2,1,0:T(8,128)} %pad_maximum_fusion.3), channel_id=1, source_target_pairs={{0,2},{2,0},{4,6},{6,4},{8,10},{10,8},{12,14},{14,12},{1,3},{3,1},... | collective-permute-start | bytes 3932168 | tf_op jit(solution)/shard_map/ppermute | solution.py:22
  10.8 0.1 slice_bitcast_fusion.4
  11.0 0.9 copy-done.18
  11.9 0.2 fusion.1
  12.2 3.6 %collective-permute-start.5 = (f32[76,16,256]{2,1,0:T(8,128)S(1)}, f32[76,16,256]{2,1,0:T(8,128)S(1)}, u32[]{:S(2)}, u32[]{:S(2)}) collective-permute-start(f32[76,16,256]{2,1,0:T(8,128)S(1)} %get-tuple-element.53), channel_id=1, source_target_pairs={{0,4},{4,8},{6,2},{8,12},{10,6},{14,10},{1,5},{5,9},{7,3},{9,13},{... | collective-permute-start | bytes 3735560 | tf_op jit(solution)/shard_map/ppermute | solution.py:22
  15.7 1.3 collective-permute-start.8
  17.1 0.6 copy-done.14
  17.7 22.9 %collective-permute-done.6.near2 = f32[80,16,256]{2,1,0:T(8,128)} collective-permute-done((f32[80,16,256]{2,1,0:T(8,128)}, f32[80,16,256]{2,1,0:T(8,128)}, u32[]{:S(2)}, u32[]{:S(2)}) %collective-permute-start.6) | collective-permute-done | bytes 1310752 | tf_op jit(solution)/shard_map/ppermute | solution.py:22
  40.6 4.1 %collective-permute-start.7 = (f32[80,16,256]{2,1,0:T(8,128)}, f32[80,16,256]{2,1,0:T(8,128)S(1)}, u32[]{:S(2)}, u32[]{:S(2)}) collective-permute-start(f32[80,16,256]{2,1,0:T(8,128)} %collective-permute-done.6.near2), channel_id=1, source_target_pairs={{0,4},{4,8},{6,2},{8,12},{10,6},{14,10},{1,5},{5,9},{7,3},{9,13},{... | collective-permute-start | bytes 3932168 | tf_op jit(solution)/shard_map/ppermute | solution.py:22
  44.8 0.1 collective-permute-start.3
  44.9 6.9 %collective-permute-done.near1a = f32[64,8,256]{2,1,0:T(8,128)S(1)} collective-permute-done((f32[64,8,256]{2,1,0:T(8,128)S(1)}, f32[64,8,256]{2,1,0:T(8,128)S(1)}, u32[]{:S(2)}, u32[]{:S(2)}) %collective-permute-start) | collective-permute-done | bytes 524320 | tf_op jit(solution)/shard_map/ppermute | solution.py:22
  51.8 11.1 %collective-permute-done.3.near1b = f32[68,8,256]{2,1,0:T(8,128)S(1)} collective-permute-done((f32[68,8,256]{2,1,0:T(8,128)S(1)}, f32[68,8,256]{2,1,0:T(8,128)S(1)}, u32[]{:S(2)}, u32[]{:S(2)}) %collective-permute-start.3) | collective-permute-done | bytes 557088 | tf_op jit(solution)/shard_map/ppermute | solution.py:22
  62.9 0.6 fusion.24
  63.6 1.2 slice.296
  64.8 1.4 fusion.21
  66.1 4.8 %collective-permute-done.7.far1 = f32[80,16,256]{2,1,0:T(8,128)S(1)} collective-permute-done((f32[80,16,256]{2,1,0:T(8,128)}, f32[80,16,256]{2,1,0:T(8,128)S(1)}, u32[]{:S(2)}, u32[]{:S(2)}) %collective-permute-start.7) | collective-permute-done | bytes 1310752 | tf_op jit(solution)/shard_map/ppermute | solution.py:22
  71.2 1.1 copy-done.19
  72.3 0.7 pad_maximum_fusion.6
  73.0 1.5 reshape.72
  74.6 1.5 reshape.74
  76.1 0.8 pad_maximum_fusion.9
  76.9 0.7 pad_maximum_fusion.8
  77.7 0.9 maximum_select_fusion
  78.6 0.1 collective-permute-start.9
  78.7 5.1 %collective-permute-start.1 = (f32[64,8,256]{2,1,0:T(8,128)}, f32[64,8,256]{2,1,0:T(8,128)}, u32[]{:S(2)}, u32[]{:S(2)}) collective-permute-start(f32[64,8,256]{2,1,0:T(8,128)} %copy-done.12), channel_id=1, source_target_pairs={{0,4},{4,8},{6,2},{8,12},{10,6},{14,10},{1,5},{5,9},{7,3},{9,13},{... | collective-permute-start | bytes 1572872 | tf_op jit(solution)/shard_map/ppermute | solution.py:22
  83.8 2.7 %collective-permute-start.4 = (f32[68,8,256]{2,1,0:T(8,128)}, f32[68,8,256]{2,1,0:T(8,128)S(1)}, u32[]{:S(2)}, u32[]{:S(2)}) collective-permute-start(f32[68,8,256]{2,1,0:T(8,128)} %copy-done.10), channel_id=1, source_target_pairs={{0,4},{4,8},{6,2},{8,12},{10,6},{14,10},{1,5},{5,9},{7,3},{9,13},{... | collective-permute-start | bytes 1671176 | tf_op jit(solution)/shard_map/ppermute | solution.py:22
  86.5 0.7 broadcast_select_fusion
  87.2 0.7 fusion.26
  87.9 0.9 reshape.77
  88.8 1.6 %fusion.27 = (f32[80,256]{1,0:T(8,128)}, f32[80,256]{1,0:T(8,128)}) fusion(f32[160,256]{1,0:T(8,128)} %get-tuple-element.50), kind=kLoop, calls=%fused_computation.85 | loop fusion | bytes 327680 | tf_op jit(solution)/shard_map/slice | solution.py:394
  90.4 1.5 reshape.78
  92.0 1.3 pad_maximum_fusion.2
  93.3 0.1 slice_bitcast_fusion.2
  93.4 0.2 fusion.23
  93.6 1.2 slice_multiply_fusion.2
  94.8 0.3 slice_multiply_fusion.sy
  95.1 0.2 slice_multiply_fusion.3.sz
  95.3 0.2 slice.324
  95.6 0.1 broadcast_divide_fusion.inverse
  95.8 0.3 pad_multiply_fusion.sx
  96.0 0.3 copy-done.11
  96.4 0.2 copy-done.13
  96.5 0.5 copy-done.9
  97.0 0.4 copy-done.5
  97.4 0.4 copy-done.7
  97.8 15.4 %shard_map.59 = (f32[3,70,16,256]{3,2,1,0:T(8,128)S(1)}, f32[2,70,16,256]{3,2,1,0:T(8,128)S(1)}, f32[2,70,16,256]{3,2,1,0:T(8,128)S(1)}, bf16[2,64,64,256]{3,2,1,0:T(8,128)(2,1)}, f32[16,128]{1,0:T(8,128)S(1)}) custom-call(f32[76,16,256]{2,1,0:T(8,128)S(1)} %copy-done.7, f32[80,16,256]{2,1,0:T(8,128)S(1)} %copy-done.5, ...), custom_call_target="tpu_custom_call" | custom-call | bytes 52428800 | tf_op jit(solution)/shard_map/pallas_call | solution.py:406
  113.2 11.8 %shard_map.60 = (f32[16,128]{1,0:T(8,128)S(1)}, bf16[2,64,64,256]{3,2,1,0:T(8,128)(2,1)S(1)}) custom-call(f32[64,8,256]{2,1,0:T(8,128)} %collective-permute-done.1.far2a, f32[68,8,256]{2,1,0:T(8,128)S(1)} %collective-permute-done.4.far2b, f32[3,70,16,256]{3,2,1,0:T(8,128)S(1)} %get-tuple-element.9.u0_in, f32[2,70,16,256]{3,2,1,0:T(8,128)S(1)} %get-tuple-element.10.u1_in, ...), custom_call_target="tpu_custom_call" | custom-call | bytes 52428800 | tf_op jit(solution)/shard_map/pallas_call | solution.py:418
  125.1 2.0 %copy-done.1 = bf16[2,64,64,256]{3,2,1,0:T(8,128)(2,1)} copy-done((bf16[2,64,64,256]{3,2,1,0:T(8,128)(2,1)}, bf16[2,64,64,256]{3,2,1,0:T(8,128)(2,1)S(1)}, u32[]{:S(2)}) %copy-start.1) | copy-done | bytes 4194328
  127.1 1.2 collective-permute-done.10
  128.3 3.6 %collective-permute-done.11 = f32[16,128]{1,0:T(8,128)S(1)} collective-permute-done((f32[16,128]{1,0:T(8,128)S(1)}, f32[16,128]{1,0:T(8,128)S(1)}, u32[]{:S(2)}, u32[]{:S(2)}) %collective-permute-start.11) | collective-permute-done | bytes 8224 | tf_op jit(solution)/shard_map/ppermute | solution.py:59
  131.9 1.5 collective-permute-start.12
  133.5 2.1 %collective-permute-done.12 = f32[16,128]{1,0:T(8,128)S(1)} collective-permute-done((f32[16,128]{1,0:T(8,128)S(1)}, f32[16,128]{1,0:T(8,128)S(1)}, u32[]{:S(2)}, u32[]{:S(2)}) %collective-permute-start.12) | collective-permute-done | bytes 8224 | tf_op jit(solution)/shard_map/ppermute | solution.py:59
  135.6 1.0 collective-permute-start.13
  136.6 0.9 slice.334.root
  137.5 2.6 %collective-permute-done.13 = f32[16,128]{1,0:T(8,128)S(1)} collective-permute-done((f32[16,128]{1,0:T(8,128)S(1)}, f32[16,128]{1,0:T(8,128)S(1)}, u32[]{:S(2)}, u32[]{:S(2)}) %collective-permute-start.13) | collective-permute-done | bytes 8224 | tf_op jit(solution)/shard_map/ppermute | solution.py:59
  140.1 2.2 %copy-done = bf16[2,64,64,256]{3,2,1,0:T(8,128)(2,1)S(1)} copy-done((bf16[2,64,64,256]{3,2,1,0:T(8,128)(2,1)S(1)}, bf16[2,64,64,256]{3,2,1,0:T(8,128)(2,1)}, u32[]{:S(2)}) %copy-start) | copy-done | bytes 4194328
  142.3 2.2 %copy-done.2 = bf16[2,64,64,256]{3,2,1,0:T(8,128)(2,1)S(1)} copy-done((bf16[2,64,64,256]{3,2,1,0:T(8,128)(2,1)S(1)}, bf16[2,64,64,256]{3,2,1,0:T(8,128)(2,1)}, u32[]{:S(2)}) %copy-start.2) | copy-done | bytes 4194328
  144.5 11.4 %shard_map.61 = (f32[16,2,64,256]{3,2,1,0:T(8,128)}, f32[16,2,64,256]{3,2,1,0:T(8,128)}) custom-call(s32[1]{0:T(128)} %bitcast.odd, f32[16,128]{1,0:T(8,128)S(1)} %add.83.moments, bf16[2,64,64,256]{3,2,1,0:T(8,128)(2,1)S(1)} %copy-done, bf16[2,64,64,256]{3,2,1,0:T(8,128)(2,1)S(1)} %copy-done.2, f32[2,64,256]{2,1,0:T(8,128)S(1)} %slice.333.inverse, ...), custom_call_target="tpu_custom_call" | custom-call | tf_op jit(solution)/shard_map/pallas_call | solution.py:435
  (80 shorter events, 0.7 us)
Async XLA Ops:
  1.7 0.7 copy-start.23
  7.8 32.9 %collective-permute-start.6 = (f32[80,16,256]{2,1,0:T(8,128)}, f32[80,16,256]{2,1,0:T(8,128)}, u32[]{:S(2)}, u32[]{:S(2)}) collective-permute-start(f32[80,16,256]{2,1,0:T(8,128)} %pad_maximum_fusion.3), channel_id=1, source_target_pairs={{0,2},{2,0},{4,6},{6,4},{8,10},{10,8},{12,14},{14,12},{1,3},{3,1},... | collective-permute-start | bytes 3932168 | tf_op jit(solution)/shard_map/ppermute | solution.py:22
  10.7 1.2 copy-start.18
  10.7 6.3 %collective-permute-start.2 = (f32[2,3,16,256]{3,2,1,0:T(8,128)S(1)}, f32[2,3,16,256]{3,2,1,0:T(8,128)S(1)}, u32[]{:S(2)}, u32[]{:S(2)}) collective-permute-start(f32[2,3,16,256]{3,2,1,0:T(8,128)S(1)} %slice_select_fusion), channel_id=1, source_target_pairs={{0,1},{1,0},{2,3},{3,2},{4,5},{5,4},{6,7},{7,6},{8,9},{9,8},{10,11... | collective-permute-start | bytes 294920 | tf_op jit(solution)/shard_map/ppermute | solution.py:22
  10.9 40.9 %collective-permute-start = (f32[64,8,256]{2,1,0:T(8,128)S(1)}, f32[64,8,256]{2,1,0:T(8,128)S(1)}, u32[]{:S(2)}, u32[]{:S(2)}) collective-permute-start(f32[64,8,256]{2,1,0:T(8,128)S(1)} %get-tuple-element.21), channel_id=1, source_target_pairs={{0,2},{2,0},{4,6},{6,4},{8,10},{10,8},{12,14},{14,12},{1,3},{3,1},... | collective-permute-start | bytes 1572872 | tf_op jit(solution)/shard_map/ppermute | solution.py:22
  12.2 51.3 %collective-permute-start.5 = (f32[76,16,256]{2,1,0:T(8,128)S(1)}, f32[76,16,256]{2,1,0:T(8,128)S(1)}, u32[]{:S(2)}, u32[]{:S(2)}) collective-permute-start(f32[76,16,256]{2,1,0:T(8,128)S(1)} %get-tuple-element.53), channel_id=1, source_target_pairs={{0,4},{4,8},{6,2},{8,12},{10,6},{14,10},{1,5},{5,9},{7,3},{9,13},{... | collective-permute-start | bytes 3735560 | tf_op jit(solution)/shard_map/ppermute | solution.py:22
  15.7 47.8 %collective-permute-start.8 = (f32[76,16,256]{2,1,0:T(8,128)S(1)}, f32[76,16,256]{2,1,0:T(8,128)S(1)}, u32[]{:S(2)}, u32[]{:S(2)}) collective-permute-start(f32[76,16,256]{2,1,0:T(8,128)S(1)} %get-tuple-element.52), channel_id=1, source_target_pairs={{4,0},{8,4},{2,6},{12,8},{6,10},{10,14},{5,1},{9,5},{3,7},{13,9},{... | collective-permute-start | bytes 3735560 | tf_op jit(solution)/shard_map/ppermute | solution.py:22
  17.1 0.6 copy-start.14
  40.6 30.4 %collective-permute-start.7 = (f32[80,16,256]{2,1,0:T(8,128)}, f32[80,16,256]{2,1,0:T(8,128)S(1)}, u32[]{:S(2)}, u32[]{:S(2)}) collective-permute-start(f32[80,16,256]{2,1,0:T(8,128)} %collective-permute-done.6.near2), channel_id=1, source_target_pairs={{0,4},{4,8},{6,2},{8,12},{10,6},{14,10},{1,5},{5,9},{7,3},{9,13},{... | collective-permute-start | bytes 3932168 | tf_op jit(solution)/shard_map/ppermute | solution.py:22
  44.8 18.1 %collective-permute-start.3 = (f32[68,8,256]{2,1,0:T(8,128)S(1)}, f32[68,8,256]{2,1,0:T(8,128)S(1)}, u32[]{:S(2)}, u32[]{:S(2)}) collective-permute-start(f32[68,8,256]{2,1,0:T(8,128)S(1)} %pad_maximum_fusion.4), channel_id=1, source_target_pairs={{0,2},{2,0},{4,6},{6,4},{8,10},{10,8},{12,14},{14,12},{1,3},{3,1},... | collective-permute-start | bytes 1671176 | tf_op jit(solution)/shard_map/ppermute | solution.py:22
  44.9 26.2 %copy-start.24 = (s32[2,2,64,256]{3,2,1,0:T(8,128)S(1)}, s32[2,2,64,256]{3,2,1,0:T(8,128)}, u32[]{:S(2)}) copy-start(s32[2,2,64,256]{3,2,1,0:T(8,128)} %copy-done.23) | copy-start | bytes 786436
  51.7 19.4 %copy-start.12 = (f32[64,8,256]{2,1,0:T(8,128)}, f32[64,8,256]{2,1,0:T(8,128)S(1)}, u32[]{:S(2)}) copy-start(f32[64,8,256]{2,1,0:T(8,128)S(1)} %collective-permute-done.near1a) | copy-start | bytes 1572868
  62.9 8.2 %copy-start.10 = (f32[68,8,256]{2,1,0:T(8,128)}, f32[68,8,256]{2,1,0:T(8,128)S(1)}, u32[]{:S(2)}) copy-start(f32[68,8,256]{2,1,0:T(8,128)S(1)} %collective-permute-done.3.near1b) | copy-start | bytes 1671172
  63.5 7.6 %copy-start.6 = (f32[76,16,256]{2,1,0:T(8,128)}, f32[76,16,256]{2,1,0:T(8,128)S(1)}, u32[]{:S(2)}) copy-start(f32[76,16,256]{2,1,0:T(8,128)S(1)} %collective-permute-done.5.far3) | copy-start | bytes 3735556
  63.5 7.6 %copy-start.8 = (f32[76,16,256]{2,1,0:T(8,128)}, f32[76,16,256]{2,1,0:T(8,128)S(1)}, u32[]{:S(2)}) copy-start(f32[76,16,256]{2,1,0:T(8,128)S(1)} %collective-permute-done.8.near3) | copy-start | bytes 3735556
  71.0 5.1 %copy-start.4 = (f32[80,16,256]{2,1,0:T(8,128)}, f32[80,16,256]{2,1,0:T(8,128)S(1)}, u32[]{:S(2)}) copy-start(f32[80,16,256]{2,1,0:T(8,128)S(1)} %collective-permute-done.7.far1) | copy-start | bytes 3932164
  71.2 1.8 %copy-start.22 = (f32[10,64,256]{2,1,0:T(8,128)}, f32[10,64,256]{2,1,0:T(8,128)S(1)}, u32[]{:S(2)}) copy-start(f32[10,64,256]{2,1,0:T(8,128)S(1)} %constant_dynamic-update-slice_fusion) | copy-start | bytes 1966084
  71.2 1.1 copy-start.19
  76.1 15.9 %copy-start.20 = (f32[10,64,256]{2,1,0:T(8,128)S(1)}, f32[10,64,256]{2,1,0:T(8,128)}, u32[]{:S(2)}) copy-start(f32[10,64,256]{2,1,0:T(8,128)} %copy-done.19) | copy-start | bytes 1966084
  78.6 7.9 %collective-permute-start.9 = (f32[160,256]{1,0:T(8,128)S(1)}, f32[160,256]{1,0:T(8,128)S(1)}, u32[]{:S(2)}, u32[]{:S(2)}) collective-permute-start(f32[160,256]{1,0:T(8,128)S(1)} %maximum_select_fusion), channel_id=1, source_target_pairs={{0,1},{1,0},{2,3},{3,2},{4,5},{5,4},{6,7},{7,6},{8,9},{9,8},{10,11... | collective-permute-start | bytes 491528 | tf_op jit(solution)/shard_map/ppermute | solution.py:22
  78.7 34.5 %collective-permute-start.1 = (f32[64,8,256]{2,1,0:T(8,128)}, f32[64,8,256]{2,1,0:T(8,128)}, u32[]{:S(2)}, u32[]{:S(2)}) collective-permute-start(f32[64,8,256]{2,1,0:T(8,128)} %copy-done.12), channel_id=1, source_target_pairs={{0,4},{4,8},{6,2},{8,12},{10,6},{14,10},{1,5},{5,9},{7,3},{9,13},{... | collective-permute-start | bytes 1572872 | tf_op jit(solution)/shard_map/ppermute | solution.py:22
  83.8 29.4 %collective-permute-start.4 = (f32[68,8,256]{2,1,0:T(8,128)}, f32[68,8,256]{2,1,0:T(8,128)S(1)}, u32[]{:S(2)}, u32[]{:S(2)}) collective-permute-start(f32[68,8,256]{2,1,0:T(8,128)} %copy-done.10), channel_id=1, source_target_pairs={{0,4},{4,8},{6,2},{8,12},{10,6},{14,10},{1,5},{5,9},{7,3},{9,13},{... | collective-permute-start | bytes 1671176 | tf_op jit(solution)/shard_map/ppermute | solution.py:22
  94.8 0.8 copy-start.21
  95.3 1.1 copy-start.11
  95.3 1.2 copy-start.13
  95.6 1.4 copy-start.9
  95.7 1.7 %copy-start.5 = (f32[80,16,256]{2,1,0:T(8,128)S(1)}, f32[80,16,256]{2,1,0:T(8,128)}, u32[]{:S(2)}) copy-start(f32[80,16,256]{2,1,0:T(8,128)} %copy-done.4) | copy-start | bytes 3932164
  95.7 2.1 %copy-start.7 = (f32[76,16,256]{2,1,0:T(8,128)S(1)}, f32[76,16,256]{2,1,0:T(8,128)}, u32[]{:S(2)}) copy-start(f32[76,16,256]{2,1,0:T(8,128)} %copy-done.6) | copy-start | bytes 3735556
  95.7 2.1 %copy-start.15 = (f32[2,3,16,256]{3,2,1,0:T(8,128)S(1)}, f32[2,3,16,256]{3,2,1,0:T(8,128)}, u32[]{:S(2)}) copy-start(f32[2,3,16,256]{3,2,1,0:T(8,128)} %copy-done.14) | copy-start | bytes 294916
  95.7 2.0 %copy-start.16 = (f32[80,256]{1,0:T(8,128)S(1)}, f32[80,256]{1,0:T(8,128)}, u32[]{:S(2)}) copy-start(f32[80,256]{1,0:T(8,128)} %get-tuple-element.47) | copy-start | bytes 245764
  95.8 2.1 %copy-start.17 = (f32[80,256]{1,0:T(8,128)S(1)}, f32[80,256]{1,0:T(8,128)}, u32[]{:S(2)}) copy-start(f32[80,256]{1,0:T(8,128)} %get-tuple-element.49) | copy-start | bytes 245764
  113.2 26.9 %copy-start.3 = (f32[16,2,64,256]{3,2,1,0:T(8,128)S(1)}, f32[16,2,64,256]{3,2,1,0:T(8,128)}, u32[]{:S(2)}) copy-start(f32[16,2,64,256]{3,2,1,0:T(8,128)} %iterate.1) | copy-start | bytes 6291460
  125.1 2.0 %copy-start.1 = (bf16[2,64,64,256]{3,2,1,0:T(8,128)(2,1)}, bf16[2,64,64,256]{3,2,1,0:T(8,128)(2,1)S(1)}, u32[]{:S(2)}) copy-start(bf16[2,64,64,256]{3,2,1,0:T(8,128)(2,1)S(1)} %get-tuple-element.15.split23) | copy-start | bytes 12582916
  127.1 1.2 collective-permute-start.10
  128.3 3.7 %collective-permute-start.11 = (f32[16,128]{1,0:T(8,128)S(1)}, f32[16,128]{1,0:T(8,128)S(1)}, u32[]{:S(2)}, u32[]{:S(2)}) collective-permute-start(f32[16,128]{1,0:T(8,128)S(1)} %add.80), channel_id=1, source_target_pairs={{0,2},{2,0},{4,6},{6,4},{8,10},{10,8},{12,14},{14,12},{1,3},{3,1},... | collective-permute-start | bytes 24584 | tf_op jit(solution)/shard_map/ppermute | solution.py:59
  131.9 3.7 %collective-permute-start.12 = (f32[16,128]{1,0:T(8,128)S(1)}, f32[16,128]{1,0:T(8,128)S(1)}, u32[]{:S(2)}, u32[]{:S(2)}) collective-permute-start(f32[16,128]{1,0:T(8,128)S(1)} %add.81), channel_id=1, source_target_pairs={{0,4},{2,6},{4,0},{6,2},{8,12},{10,14},{12,8},{14,10},{1,5},{3,7},... | collective-permute-start | bytes 24584 | tf_op jit(solution)/shard_map/ppermute | solution.py:59
  135.6 4.5 %collective-permute-start.13 = (f32[16,128]{1,0:T(8,128)S(1)}, f32[16,128]{1,0:T(8,128)S(1)}, u32[]{:S(2)}, u32[]{:S(2)}) collective-permute-start(f32[16,128]{1,0:T(8,128)S(1)} %add.82), channel_id=1, source_target_pairs={{0,8},{2,10},{4,12},{6,14},{8,0},{10,2},{12,4},{14,6},{1,9},{3,11}... | collective-permute-start | bytes 24584 | tf_op jit(solution)/shard_map/ppermute | solution.py:59
  140.1 2.2 %copy-start = (bf16[2,64,64,256]{3,2,1,0:T(8,128)(2,1)S(1)}, bf16[2,64,64,256]{3,2,1,0:T(8,128)(2,1)}, u32[]{:S(2)}) copy-start(bf16[2,64,64,256]{3,2,1,0:T(8,128)(2,1)} %get-tuple-element.14.split01) | copy-start | bytes 12582916
  142.3 2.2 %copy-start.2 = (bf16[2,64,64,256]{3,2,1,0:T(8,128)(2,1)S(1)}, bf16[2,64,64,256]{3,2,1,0:T(8,128)(2,1)}, u32[]{:S(2)}) copy-start(bf16[2,64,64,256]{3,2,1,0:T(8,128)(2,1)} %copy-done.1) | copy-start | bytes 12582916

commit v6 on v5

--- a/solution.py
+++ b/solution.py
@@ -65,29 +65,112 @@
     return jnp.where(beside > 0.0, 2.0 * center * beside / (center + beside), center)
 
 
-def symmetric_operator(coef, inner):
-    def pad_x(a, forward):
-        return jnp.pad(a[..., 1:], ((0, 0), (0, 0), (0, 1))) if forward else jnp.pad(a[..., :-1], ((0, 0), (0, 0), (1, 0)))
-
-    center = coef[1:-1, 1:-1]
-    here = inner[1:-1, 1:-1]
-    total = jnp.zeros_like(center)
-    for beside in (
-        coef[2:, 1:-1], coef[:-2, 1:-1], coef[1:-1, 2:], coef[1:-1, :-2], pad_x(center, True), pad_x(center, False)
-    ):
-        total = total + face_of(center, beside)
-    diagonal = here * total + (1.0 - here)
-    root = jnp.sqrt(diagonal)
-    inverse = 1.0 / root
-    masked = here * inverse
-
-    def coupling(a, b, ma, mb):
-        return ma * face_of(a, b) * mb
-
-    along_x = coupling(center, pad_x(center, True), masked, pad_x(masked, True))
-    along_y = coupling(center[:, :-1], center[:, 1:], masked[:, :-1], masked[:, 1:])
-    along_z = coupling(center[:-1], center[1:], masked[:-1], masked[1:])
-    return root, inverse, along_x, along_y, along_z
+LATE = 1
+BESIDE = ((5, 0, 2), (6, 2, 1), (2, 3, 2))
+EDGES = 5
+FIELDS = (
+    ("far3", 0, None), ("far3", 1, 2), ("far1", 1, 3), ("far1", 0, 2), ("mine", 0, 2),
+    ("mine", 1, 3), ("near2", 1, 3), ("near2", 0, 2), ("near3", 0, 2), ("near3", 1, None),
+)
+MARGIN = 8
+
+
+def prepare_kernel(odd, residual, labels, boundary, mine, ahead):
+    rhs, depth, rows, nx = residual.shape
+    for place, out in ((0, mine), (1, ahead)):
+        plane = jnp.bitwise_xor(place, odd[0])
+
+        def turn(block, carry, plane=plane, out=out):
+            rows_here = pl.ds(block * 8, 8)
+            out[rows_here] = pltpu.einshape("abc->bac", residual[:, plane, rows_here, :])
+            return carry
+
+        lax.fori_loop(0, rows // 8, turn, 0)
+        for part in range(rows // rhs):
+            cells = pl.ds(part * rhs, rhs)
+            coef = jnp.exp(labels[plane, cells, :].astype(f32) * (contrast_log / (NCLASS - 1)))
+            inner = (1 - boundary[plane, cells, :]).astype(f32)
+            count = rows // rhs
+            for message in (mine, ahead):
+                message[rows + place * count + part] = coef
+            mine[rows + (2 + place) * count + part] = inner
+            if place == 1:
+                ahead[rows + 2 * count + part] = inner
+
+
+def edges_kernel(rows, near1, near2, far1, far3, near3, mine, first, last):
+    messages = {"near2": near2, "far1": far1, "far3": far3, "near3": near3, "mine": mine}
+    rhs = mine.shape[1]
+    count = rows // rhs
+    for (_, place, number), source in zip(BESIDE, (near1, near2, far1)):
+        first[place : place + number] = source[:number]
+        last[place : place + number] = source[rows - number : rows]
+    place = EDGES
+    for name, *parts in FIELDS:
+        for part in parts:
+            if part is not None:
+                start = rows + part * count
+                first[place] = messages[name][start]
+                last[place] = messages[name][start + count - 1]
+                place += 1
+
+
+def fill_cells(rows, messages, before, behind, coef, inner):
+    place = EDGES
+    for plane, (name, *parts) in enumerate(FIELDS):
+        for part, out in zip(parts, (coef, inner)):
+            if part is None:
+                continue
+            rhs = messages[name].shape[1]
+            count = rows // rhs
+            for block in range(count):
+                out[plane, MARGIN + block * rhs : MARGIN + (block + 1) * rhs] = messages[name][
+                    rows + part * count + block
+                ]
+            out[plane, :MARGIN] = before[place, rhs - MARGIN :]
+            out[plane, MARGIN + rows :] = behind[place, :MARGIN]
+            place += 1
+
+
+def make_operator(coef, inner, inverse, sx, sy, sz, root, masked):
+    planes, height, nx = inverse.shape
+    lane = lax.broadcasted_iota(jnp.int32, (height, nx), 1)
+    inside = lane < nx - 1
+
+    def one_plane(plane, carry):
+        here = coef[plane + 1]
+        flag = inner[plane + 1]
+        right = jnp.where(inside, pltpu.roll(here, nx - 1, 1), 0.0)
+        left = jnp.where(lane > 0, pltpu.roll(here, 1, 1), 0.0)
+        behind, before = pltpu.roll(here, height - 1, 0), pltpu.roll(here, 1, 0)
+        along_x, along_y = face_of(here, right), face_of(here, behind)
+        along_z = face_of(here, coef[plane + 2])
+        total = along_x + jnp.where(left > 0.0, pltpu.roll(along_x, 1, 1), here)
+        total += along_y + jnp.where(before > 0.0, pltpu.roll(along_y, 1, 0), here)
+        total += along_z + face_of(here, coef[plane])
+        diagonal = flag * total + (1.0 - flag)
+        square = jnp.sqrt(diagonal)
+        reciprocal = 1.0 / square
+        root[plane] = square
+        inverse[plane] = reciprocal
+        scale = flag * reciprocal
+        masked[plane] = scale
+        sx[plane] = jnp.where(inside, scale * along_x * pltpu.roll(scale, nx - 1, 1), 0.0)
+        sy[plane] = scale * along_y * pltpu.roll(scale, height - 1, 0)
+        sz[plane] = scale * along_z
+        return carry
+
+    lax.fori_loop(0, planes, one_plane, 0)
+
+    def next_plane(plane, carry):
+        sz[plane] = sz[plane] * masked[plane + 1]
+        return carry
+
+    lax.fori_loop(0, planes - 1, next_plane, 0)
+
+
+def cell_row(ref, plane, y):
+    return ref[plane, pl.ds(y + (MARGIN - REACH), 1), :]
 
 
 def row_blocks(start, stop, body, size=8):
@@ -105,17 +188,17 @@
     ref, index = here
     out = []
     last, center = ref[index, start - 1], ref[index, start]
-    below = sy[plane, pl.ds(start - 1, 1), :]
+    below = cell_row(sy, plane, start - 1)
     width = center.shape[-1]
     for j in range(size):
         y = start + j
         following = ref[index, y + 1]
-        above = sy[plane, pl.ds(y, 1), :]
-        ahead = sx[plane, pl.ds(y, 1), :]
+        above = cell_row(sy, plane, y)
+        ahead = cell_row(sx, plane, y)
         total = ahead * pltpu.roll(center, width - 1, 1) + pltpu.roll(ahead * center, 1, 1)
         total += above * following + below * last
-        total += sz[plane, pl.ds(y, 1), :] * after[0][after[1], y]
-        total += sz[plane - 1, pl.ds(y, 1), :] * before[0][before[1], y]
+        total += cell_row(sz, plane, y) * after[0][after[1], y]
+        total += cell_row(sz, plane - 1, y) * before[0][before[1], y]
         out.append(total)
         last, center, below = center, following, above
     return out
@@ -125,12 +208,12 @@
     return max(REACH - plane, plane - (REACH + depth - 1), 0)
 
 
-def scale_rows(plane, source, first, dst, start, count, inverse, part=slice(None)):
+def scale_rows(plane, source, first, dst, start, count, inverse):
     out, place = dst
 
     def body(j, size=8):
         for i in range(size):
-            out[place, start + j + i, part] = source[first + j + i] * inverse[plane, pl.ds(start + j + i, 1), :]
+            out[place, start + j + i] = source[first + j + i] * cell_row(inverse, plane, start + j + i)
 
     if count < 8:
         body(0, count)
@@ -148,10 +231,6 @@
             out[place, y + j] = values
 
     row_blocks(REACH - reach, REACH + rows + reach, body)
-
-
-LATE = 1
-BESIDE = ((5, 0, 2), (6, 2, 1), (2, 3, 2))
 
 
 def halves(blocks):
@@ -171,20 +250,20 @@
 
 
 def early_kernel(
-    rows, far3, far1, own, own_before, own_behind, near1a, near1b, near2, near3, before, behind,
-    inverse, sx, sy, sz, u0_out, u1_out, u2_out, split, moments, u0, u1,
+    rows, far3, far1, mine, ahead, own_before, own_behind, near1, near2, near3, before, behind,
+    inverse, sx, sy, sz, root, u0_out, u1_out, u2_out, split, moments, u0, u1, coef, inner, masked,
 ):
+    messages = {"near2": near2, "far1": far1, "far3": far3, "near3": near3, "mine": mine}
+    fill_cells(rows, messages, before, behind, coef, inner)
+    make_operator(coef, inner, inverse, sx, sy, sz, root, masked)
     operator = (sx, sy, sz)
     fields = {(0, plane): (u0_out, index) for index, plane in enumerate((0, 2, 3))}
     fields.update({(0, plane): (u0, plane - 4) for plane in range(4, 8)})
     fields.update({(1, 3): (u1_out, 0), (1, 4): (u1_out, 1), (1, 5): (u1, 0), (1, 6): (u1, 1)})
     fields.update({(2, 4): (u2_out, 0), (2, 5): (u2_out, 1)})
     first, last = REACH, REACH + rows
-    half = near1a.shape[1]
-    for plane, source in ((0, far3), (2, far1), (3, own.at[0]), (4, own.at[1]), (6, near2), (7, near3)):
+    for plane, source in ((0, far3), (2, far1), (3, mine), (4, ahead), (5, near1), (6, near2), (7, near3)):
         scale_rows(plane, source, 0, fields[0, plane], first, rows, inverse)
-    scale_rows(5, near1a, 0, fields[0, 5], first, rows, inverse, slice(0, half))
-    scale_rows(5, near1b, 0, fields[0, 5], first, rows, inverse, slice(half, None))
     for plane in (3, 4):
         scale_rows(plane, own_before.at[plane - 3], 0, fields[0, plane], 0, REACH, inverse)
         scale_rows(plane, own_behind.at[plane - 3], 0, fields[0, plane], last, REACH, inverse)
@@ -216,7 +295,7 @@
 
 
 def late_kernel(
-    rows, far2a, far2b, u0_in, u1_in, u2_in, moments_in, inverse, sx, sy, sz, moments, split, u0, u1, u2
+    rows, far2, u0_in, u1_in, u2_in, moments_in, inverse, sx, sy, sz, moments, split, u0, u1, u2
 ):
     operator = (sx, sy, sz)
     fields = {(0, plane): (u0_in, index) for index, plane in enumerate((0, 2, 3))}
@@ -224,12 +303,8 @@
     fields.update({(1, 1): (u1, 0), (1, 2): (u1, 1), (1, 3): (u1_in, 0), (1, 4): (u1_in, 1)})
     fields.update({(2, 2): (u2, 0), (2, 3): (u2, 1), (2, 4): (u2_in, 0), (2, 5): (u2_in, 1)})
     first, last = REACH, REACH + rows
-    half = far2a.shape[1]
-    for source, part in ((far2a, slice(0, half)), (far2b, slice(half, None))):
-        scale_rows(LATE, source, 0, fields[0, LATE], first, rows, inverse, part)
-    for place, y in ((rows, first - 1), (rows + 2, last)):
-        for index, part in enumerate((slice(0, half), slice(half, None))):
-            scale_rows(LATE, far2b, place + index, fields[0, LATE], y, 1, inverse, part)
+    for place, start, count in ((0, first, rows), (rows, first - 1, 1), (rows + 1, last, 1)):
+        scale_rows(LATE, far2, place, fields[0, LATE], start, count, inverse)
     for power, plane in ((1, 1), (1, 2), (2, 2), (2, 3)):
         apply_plane(rows, power, plane, operator, fields)
 
@@ -327,120 +402,89 @@
 
 def on_device(iterate, residual, labels, boundary):
     rhs, depth, rows, nx = residual.shape
-    assert depth == 2 and REACH == 3 and lax.axis_size("gz") % 2 == 0
-    half = rhs // 2
-    odd = lax.axis_index("gz") % 2 == 1
-
-    def mirrored(block, dim):
-        return jnp.where(odd, jnp.flip(block, dim), block)
-
-    cells = jnp.stack([labels, boundary])
-    cells = mirrored(cells, 1)
-    coef = jnp.exp(cells[0].astype(f32) * (contrast_log / (NCLASS - 1)))
-    inner = (1 - cells[1]).astype(f32)
-    fields = jnp.stack([coef, inner])
-    own = mirrored(jnp.transpose(residual, (1, 2, 0, 3)), 0)
-
-    def with_cells(plane, *cells):
-        return jnp.concatenate([plane] + [block.reshape(-1, rhs, nx) for block in cells], axis=0)
-
-    def cells_of(message):
-        return message[rows:].reshape(-1, rows, nx)
-
-    near2 = swapped(with_cells(own[0], fields))
-    far3 = relayed(with_cells(own[1], coef, inner[1:]))
-    near3 = relayed(with_cells(own[0], coef, inner[:1]), back=True)
-    own_before, own_behind = rows_beside(own[:, :REACH], own[:, -REACH:])
-    near1a = swapped(own[1, :, :half])
-    edges = [own_before[1, -1:], own_behind[1, :1]]
-    near1b = swapped(jnp.concatenate([own[1, :, half:]] + [edge.reshape(2, half, nx) for edge in edges], axis=0))
+    assert depth == 2 and REACH == 3 and rows % rhs == 0 and rhs % 8 == 0 and lax.axis_size("gz") % 2 == 0
+    odd = (lax.axis_index("gz") % 2).astype(jnp.int32).reshape(1)
+    vmem = pl.BlockSpec(memory_space=pltpu.VMEM)
+    smem = pl.BlockSpec(memory_space=pltpu.SMEM)
+
+    def array(*shape, dtype=f32):
+        return jax.ShapeDtypeStruct(shape, dtype)
+
+    def params(mib):
+        return pltpu.CompilerParams(vmem_limit_bytes=mib * 2**20)
+
+    count = rows // rhs
+    mine, ahead = pl.pallas_call(
+        prepare_kernel,
+        out_shape=(array(rows + 4 * count, rhs, nx), array(rows + 3 * count, rhs, nx)),
+        in_specs=[smem, vmem, vmem, vmem],
+        out_specs=(vmem, vmem),
+        compiler_params=params(16),
+    )(odd, residual, labels, boundary)
+
+    near2 = swapped(mine)
+    far3 = relayed(ahead)
+    near3 = relayed(mine, back=True)
+    own_before, own_behind = rows_beside(
+        jnp.stack([mine[:REACH], ahead[:REACH]]), jnp.stack([mine[rows - REACH : rows], ahead[rows - REACH : rows]])
+    )
+    last = jnp.concatenate([ahead[:rows], own_before[1, -1:], own_behind[1, :1]], axis=0)
+    here = jnp.minimum(near2[0, 0, 0], far3[0, 0, 0]) >= jnp.finfo(f32).min
+    near1 = swapped(jnp.where(here, last, 0.0))
     far1 = relayed(near2)
-    far2a = relayed(near1a)
-    far2b = relayed(near1b)
-
-    field_pair = cells_of(near2).reshape(2, depth, rows, nx)
-    field_beyond = cells_of(far1).reshape(2, depth, rows, nx)
-    field_far, field_near = cells_of(far3), cells_of(near3)
-    none = jnp.zeros_like(coef[:1])
-    coef = jnp.concatenate(
-        [
-            field_far[:2], field_beyond[0, 1:], field_beyond[0, :1], coef,
-            field_pair[0, 1:], field_pair[0, :1], field_near[:2],
-        ],
-        axis=0,
+    far2 = relayed(near1)
+
+    edges = EDGES + sum(part is not None for _, *parts in FIELDS for part in parts)
+    before, behind = rows_beside(
+        *pl.pallas_call(
+            partial(edges_kernel, rows),
+            out_shape=(array(edges, rhs, nx),) * 2,
+            in_specs=[vmem] * 6,
+            out_specs=(vmem, vmem),
+            compiler_params=params(12),
+        )(near1, near2, far1, far3, near3, mine)
     )
-    inner = jnp.concatenate(
-        [
-            none, field_far[2:], field_beyond[1, 1:], field_beyond[1, :1], inner,
-            field_pair[1, 1:], field_pair[1, :1], field_near[2:], none,
-        ],
-        axis=0,
-    )
-    fields = jnp.stack([coef, inner])
-    wide = REACH + 1
-
-    def edges_of(last):
-        def cut(block, count, axis=0):
-            low, high = (rows - count, rows) if last else (0, count)
-            return lax.slice_in_dim(block, low, high, axis=axis)
-
-        pair = jnp.concatenate([cut(near1a, 2), cut(near1b, 2)], axis=1)
-        planes = jnp.concatenate([pair, cut(near2, 1), cut(far1, 2)], axis=0)
-        return jnp.concatenate([planes.reshape(-1, nx), cut(fields, wide, 2).reshape(-1, nx)], axis=0)
-
-    sides = rows_beside(edges_of(False), edges_of(True))
-    count = sum(number for _, _, number in BESIDE) * rhs
-    before, behind = [side[:count].reshape(-1, rhs, nx) for side in sides]
-    fields_beside = [side[count:].reshape(2, -1, wide, nx) for side in sides]
-    fields = jnp.concatenate([fields_beside[0], fields, fields_beside[1]], axis=2)
-    root, inverse, sx, sy, sz = symmetric_operator(fields[0], fields[1])
-
-    extended = rows + 2 * REACH
-    vmem = pl.BlockSpec(memory_space=pltpu.VMEM)
-
-    def planes(count):
-        return (count, extended, rhs, nx)
-
-    spl = jax.ShapeDtypeStruct((depth, rows, 4 * rhs, nx), bf16)
-    sums = jax.ShapeDtypeStruct((rhs, 128), f32)
-    u0, u1, u2, split01, moments = pl.pallas_call(
+
+    def planes(number):
+        return (number, rows + 2 * REACH, rhs, nx)
+
+    cells = (depth + 2 * REACH, rows + 2 * MARGIN, nx)
+    inverse, sx, sy, sz, root, u0, u1, u2, split01, moments = pl.pallas_call(
         partial(early_kernel, rows),
-        out_shape=tuple(jax.ShapeDtypeStruct(planes(count), f32) for count in (3, 2, 2)) + (spl, sums),
-        in_specs=[vmem] * 15,
-        out_specs=(vmem,) * 5,
-        scratch_shapes=[pltpu.VMEM(planes(count), f32) for count in (4, 2)],
-        compiler_params=pltpu.CompilerParams(vmem_limit_bytes=32 * 2**20),
-        cost_estimate=pl.CostEstimate(flops=0, bytes_accessed=50 * 2**20, transcendentals=0),
-    )(
-        far3, far1, own, own_before, own_behind, near1a, near1b, near2, near3, before, behind, inverse, sx, sy, sz
-    )
+        out_shape=(array(*cells),) * 5
+        + tuple(array(*planes(number)) for number in (3, 2, 2))
+        + (array(depth, rows, 4 * rhs, nx, dtype=bf16), array(rhs, 128)),
+        in_specs=[vmem] * 11,
+        out_specs=(vmem,) * 10,
+        scratch_shapes=[pltpu.VMEM(planes(number), f32) for number in (4, 2)]
+        + [pltpu.VMEM((cells[0] + 2,) + cells[1:], f32)] * 2
+        + [pltpu.VMEM(cells, f32)],
+        compiler_params=params(24),
+    )(far3, far1, mine, ahead, own_before, own_behind, near1, near2, near3, before, behind)
 
     moments, split23 = pl.pallas_call(
         partial(late_kernel, rows),
-        out_shape=(sums, spl),
-        in_specs=[vmem] * 10,
+        out_shape=(array(rhs, 128), array(depth, rows, 4 * rhs, nx, dtype=bf16)),
+        in_specs=[vmem] * 9,
         out_specs=(vmem, vmem),
-        scratch_shapes=[pltpu.VMEM(planes(count), f32) for count in (1, 2, 2)],
-        compiler_params=pltpu.CompilerParams(vmem_limit_bytes=32 * 2**20),
-        cost_estimate=pl.CostEstimate(flops=0, bytes_accessed=50 * 2**20, transcendentals=0),
-    )(far2a, far2b, u0, u1, u2, moments, inverse, sx, sy, sz)
+        scratch_shapes=[pltpu.VMEM(planes(number), f32) for number in (1, 2, 2)],
+        compiler_params=params(20),
+    )(far2, u0, u1, u2, moments, inverse, sx, sy, sz)
 
     moments = all_sum(moments, ("gy", "gz"))
 
-    inverse = inverse[REACH : REACH + depth, REACH : REACH + rows]
-    root = root[REACH : REACH + depth, REACH : REACH + rows]
     tile = 8
     plane_rows = pl.BlockSpec((rhs, 1, tile, nx), lambda z, y, odd: (0, jnp.bitwise_xor(z, odd[0]), y, 0))
-    cell_rows = pl.BlockSpec((None, tile, nx), lambda z, y, odd: (z, y, 0))
+    cell_rows = pl.BlockSpec((None, tile, nx), lambda z, y, odd: (z + REACH, y + MARGIN // tile, 0))
     return pl.pallas_call(
         outputs_kernel,
-        out_shape=(jax.ShapeDtypeStruct(iterate.shape, f32), jax.ShapeDtypeStruct(residual.shape, f32)),
+        out_shape=(array(*iterate.shape), array(*residual.shape)),
         grid_spec=pltpu.PrefetchScalarGridSpec(
             num_scalar_prefetch=1,
             grid=(depth, rows // tile),
             in_specs=[
                 pl.BlockSpec((rhs, 128), lambda z, y, odd: (0, 0)),
-                *[pl.BlockSpec((1, tile) + spl.shape[2:], lambda z, y, odd: (z, y, 0, 0))] * 2,
+                *[pl.BlockSpec((1, tile, 4 * rhs, nx), lambda z, y, odd: (z, y, 0, 0))] * 2,
                 cell_rows,
                 cell_rows,
                 plane_rows,
@@ -448,8 +492,8 @@
             out_specs=(plane_rows, plane_rows),
             scratch_shapes=[pltpu.VMEM((4 * rhs, 8 * rhs), bf16)],
         ),
-        compiler_params=pltpu.CompilerParams(vmem_limit_bytes=16 * 2**20),
-    )(odd.astype(jnp.int32).reshape(1), moments, split01, split23, inverse, root, iterate)
+        compiler_params=params(10),
+    )(odd, moments, split01, split23, inverse, root, iterate)
 
 
 def solution(mesh):

time: 157 us -> 132 us (0.84)
  local copies, waits for them, and re-layouts: 28.3 us -> 7.2 us
  other arithmetic: 9.99 us -> 0.28 us
  Pallas kernels: 38.7 us -> 41.6 us
    unnamed x59 -> x8, local copies, waits for them, and re-layouts: 14.5 us -> 3.4 us
    reshape x4 -> x0, local copies, waits for them, and re-layouts: 5.53 us -> none  [the longest x2 3.09 us: edges_of(): cut(fields, wide, 2).reshape(-1, nx)]
    ppermute x4, starting transfers between devices: 2.55 us -> 7.16 us  [all_sum(): lax.ppermute(values, axis, [(i, i ^ step) for i in range(count)])]
    concatenate x6 -> x0, other arithmetic: 4.26 us -> none  [the longest x2 1.53 us: edges_of(): planes = jnp.concatenate([pair, cut(near2, 1), cut(far1, 2)], axis=0)]
    ppermute x10 -> x8, waiting for transfers between devices: 45.7 us -> 49.9 us  [moved(): return lax.ppermute(block, axis, pairs)]
    slice x17 -> x3, local copies, waits for them, and re-layouts: 6.93 us -> 2.97 us  [the longest x2 1.67 us: on_device(): here = jnp.minimum(near2[0, 0, 0], far3[0, 0, 0]) >= jnp.finfo(f32).min]
    ppermute x10 -> x8, starting transfers between devices: 20 us -> 16.9 us  [moved(): return lax.ppermute(block, axis, pairs)]
    ppermute x4, waiting for transfers between devices: 9.53 us -> 6.45 us  [all_sum(): lax.ppermute(values, axis, [(i, i ^ step) for i in range(count)])]
  transfers between devices with their start and end apart: 14 -> 12, of which waited for: 8 -> 9; matrix products, arithmetic and copies ran while one was open for 9% -> 3% of each run, Pallas kernels for 10% -> 14%
where the time goes in v6:
time: 132 us; the launch traced here: 131 us
  waiting for transfers between devices  56.3 us (43%)
  Pallas kernels  41.6 us (32%)
  starting transfers between devices  24.1 us (18%)
  local copies, waits for them, and re-layouts  7.2 us (5%)
  between operations  2 us (2%)
    ppermute x8, waiting for transfers between devices, moved(): return lax.ppermute(block, axis, pairs)  49.9 us
    ppermute x8, starting transfers between devices, moved(): return lax.ppermute(block, axis, pairs)  16.9 us
    pallas_call x1, Pallas kernels, on_device(): pl.pallas_call(partial(early_kernel, rows), out_shape=(array(*cells),) *...  16.8 us
    pallas_call x1, Pallas kernels, on_device(): pl.pallas_call(outputs_kernel, out_shape=(array(*iterate.shape), array(*r...  11.4 us
    pallas_call x1, Pallas kernels, on_device(): pl.pallas_call(partial(late_kernel, rows), out_shape=(array(rhs, 128), ar...  10.5 us
    ppermute x4, starting transfers between devices, all_sum(): lax.ppermute(values, axis, [(i, i ^ step) for i in range(count)])  7.16 us
    ppermute x4, waiting for transfers between devices, all_sum(): lax.ppermute(values, axis, [(i, i ^ step) for i in range(count)])  6.45 us
    unnamed x8, local copies, waits for them, and re-layouts  3.4 us
  transfers between devices with their start and end apart: 12, of which 9 were waited for; matrix products, arithmetic and copies ran while one was open for 3% of the time, Pallas kernels for 14%

profile of v6, /device:TPU:0, one launch (start us, length us, event | category | flops | bytes accessed | tf_op | source)
XLA Modules:
  0.0 131.5 jit_solution(8850578668100088501)
XLA Ops:
  0.6 0.0 copy-start.1
  0.7 1.6 %copy-done.1 = f32[16,2,64,256]{3,2,1,0:T(8,128)S(1)} copy-done((f32[16,2,64,256]{3,2,1,0:T(8,128)S(1)}, f32[16,2,64,256]{3,2,1,0:T(8,128)}, u32[]{:S(2)}) %copy-start.1) | copy-done | bytes 2097176
  2.2 0.0 copy-start.2
  2.2 0.9 copy-done.2
  3.1 0.0 copy-start.3
  3.1 0.9 copy-done.3
  4.0 1.6 %shard_map.59 = (f32[80,16,256]{2,1,0:T(8,128)S(1)}, f32[76,16,256]{2,1,0:T(8,128)}) custom-call(s32[1]{0:T(128)} %bitcast.odd, f32[16,2,64,256]{3,2,1,0:T(8,128)S(1)} %copy-done.1, s32[2,64,256]{2,1,0:T(8,128)S(1)} %copy-done.2, s32[2,64,256]{2,1,0:T(8,128)S(1)} %copy-done.3), custom_call_target="tpu_custom_call" | custom-call | tf_op jit(solution)/shard_map/pallas_call | solution.py:417
  5.6 2.9 %collective-permute-start = (f32[80,16,256]{2,1,0:T(8,128)S(1)}, f32[80,16,256]{2,1,0:T(8,128)S(1)}, u32[]{:S(2)}, u32[]{:S(2)}) collective-permute-start(f32[80,16,256]{2,1,0:T(8,128)S(1)} %get-tuple-element.18.mine), channel_id=1, source_target_pairs={{0,2},{2,0},{4,6},{6,4},{8,10},{10,8},{12,14},{14,12},{1,3},{3,1},... | collective-permute-start | bytes 3932168 | tf_op jit(solution)/shard_map/ppermute | solution.py:22
  8.6 4.6 %collective-permute-start.1 = (f32[76,16,256]{2,1,0:T(8,128)}, f32[76,16,256]{2,1,0:T(8,128)}, u32[]{:S(2)}, u32[]{:S(2)}) collective-permute-start(f32[76,16,256]{2,1,0:T(8,128)} %get-tuple-element.19.ahead), channel_id=1, source_target_pairs={{0,4},{4,8},{6,2},{8,12},{10,6},{14,10},{1,5},{5,9},{7,3},{9,13},{... | collective-permute-start | bytes 3735560 | tf_op jit(solution)/shard_map/ppermute | solution.py:22
  13.1 0.8 slice_bitcast_fusion
  14.0 0.1 collective-permute-start.2
  14.1 1.3 collective-permute-start.6
  15.4 1.3 slice.29
  16.7 0.0 collective-permute-done.2
  16.7 22.0 %collective-permute-done.1.far3 = f32[76,16,256]{2,1,0:T(8,128)} collective-permute-done((f32[76,16,256]{2,1,0:T(8,128)}, f32[76,16,256]{2,1,0:T(8,128)}, u32[]{:S(2)}, u32[]{:S(2)}) %collective-permute-start.1) | collective-permute-done | bytes 1245216 | tf_op jit(solution)/shard_map/ppermute | solution.py:22
  38.7 1.2 slice.37
  39.8 0.0 collective-permute-done.near2
  39.8 0.5 slice.36
  41.6 4.5 %collective-permute-start.5 = (f32[80,16,256]{2,1,0:T(8,128)S(1)}, f32[80,16,256]{2,1,0:T(8,128)S(1)}, u32[]{:S(2)}, u32[]{:S(2)}) collective-permute-start(f32[80,16,256]{2,1,0:T(8,128)S(1)} %collective-permute-done.near2), channel_id=1, source_target_pairs={{0,4},{4,8},{6,2},{8,12},{10,6},{14,10},{1,5},{5,9},{7,3},{9,13},{... | collective-permute-start | bytes 3932168 | tf_op jit(solution)/shard_map/ppermute | solution.py:22
  46.0 0.1 maximum_select_fusion
  46.1 0.1 collective-permute-start.3
  46.2 24.1 %collective-permute-done.3.near1 = f32[66,16,256]{2,1,0:T(8,128)S(1)} collective-permute-done((f32[66,16,256]{2,1,0:T(8,128)S(1)}, f32[66,16,256]{2,1,0:T(8,128)S(1)}, u32[]{:S(2)}, u32[]{:S(2)}) %collective-permute-start.3) | collective-permute-done | bytes 1081376 | tf_op jit(solution)/shard_map/ppermute | solution.py:22
  70.3 3.5 %collective-permute-start.4 = (f32[66,16,256]{2,1,0:T(8,128)S(1)}, f32[66,16,256]{2,1,0:T(8,128)S(1)}, u32[]{:S(2)}, u32[]{:S(2)}) collective-permute-start(f32[66,16,256]{2,1,0:T(8,128)S(1)} %collective-permute-done.3.near1), channel_id=1, source_target_pairs={{0,4},{4,8},{6,2},{8,12},{10,6},{14,10},{1,5},{5,9},{7,3},{9,13},{... | collective-permute-start | bytes 3244040 | tf_op jit(solution)/shard_map/ppermute | solution.py:22
  73.8 0.0 collective-permute-done.6.near3
  73.8 0.4 collective-permute-done.5.far1
  74.2 1.3 %shard_map.60 = (f32[23,16,256]{2,1,0:T(8,128)S(1)}, f32[23,16,256]{2,1,0:T(8,128)S(1)}) custom-call(f32[66,16,256]{2,1,0:T(8,128)S(1)} %collective-permute-done.3.near1, f32[80,16,256]{2,1,0:T(8,128)S(1)} %collective-permute-done.near2, f32[80,16,256]{2,1,0:T(8,128)S(1)} %collective-permute-done.5.far1, f32[76,16,256]{2,1,0:T(8,128)} %collective-permute-done.1.far3, ...), custom_call_target="tpu_custom_call" | custom-call | tf_op jit(solution)/shard_map/pallas_call | solution.py:439
  75.6 0.1 broadcast_select_fusion.2
  75.6 0.1 collective-permute-start.7
  75.7 1.7 %collective-permute-done.7 = f32[23,16,256]{2,1,0:T(8,128)S(1)} collective-permute-done((f32[23,16,256]{2,1,0:T(8,128)S(1)}, f32[23,16,256]{2,1,0:T(8,128)S(1)}, u32[]{:S(2)}, u32[]{:S(2)}) %collective-permute-start.7) | collective-permute-done | bytes 376864 | tf_op jit(solution)/shard_map/ppermute | solution.py:22
  77.4 0.1 broadcast_select_fusion
  77.5 16.8 %shard_map.61 = (f32[8,80,256]{2,1,0:T(8,128)S(1)}, f32[8,80,256]{2,1,0:T(8,128)S(1)}, f32[8,80,256]{2,1,0:T(8,128)S(1)}, f32[8,80,256]{2,1,0:T(8,128)S(1)}, f32...) custom-call(f32[76,16,256]{2,1,0:T(8,128)} %collective-permute-done., ...), custom_call_target="tpu_custom_call" | custom-call | tf_op jit(solution)/shard_map/pallas_call | solution.py:452
  94.3 1.7 %collective-permute-done.4.far2 = f32[66,16,256]{2,1,0:T(8,128)S(1)} collective-permute-done((f32[66,16,256]{2,1,0:T(8,128)S(1)}, f32[66,16,256]{2,1,0:T(8,128)S(1)}, u32[]{:S(2)}, u32[]{:S(2)}) %collective-permute-start.4) | collective-permute-done | bytes 1081376 | tf_op jit(solution)/shard_map/ppermute | solution.py:22
  96.0 0.0 copy-start
  96.0 10.5 %shard_map.62 = (f32[16,128]{1,0:T(8,128)S(1)}, bf16[2,64,64,256]{3,2,1,0:T(8,128)(2,1)S(1)}) custom-call(f32[66,16,256]{2,1,0:T(8,128)S(1)} %collective-permute-done.4.far2, f32[3,70,16,256]{3,2,1,0:T(8,128)S(1)} %get-tuple-element.22.u0_in, f32[2,70,16,256]{3,2,1,0:T(8,128)S(1)} %get-tuple-element.23.u1_in, ...), custom_call_target="tpu_custom_call" | custom-call | tf_op jit(solution)/shard_map/pallas_call | solution.py:465
  106.4 0.0 collective-permute-start.8
  106.4 1.2 collective-permute-done.8
  107.6 1.6 %collective-permute-start.9 = (f32[16,128]{1,0:T(8,128)S(1)}, f32[16,128]{1,0:T(8,128)S(1)}, u32[]{:S(2)}, u32[]{:S(2)}) collective-permute-start(f32[16,128]{1,0:T(8,128)S(1)} %add.17), channel_id=1, source_target_pairs={{0,2},{2,0},{4,6},{6,4},{8,10},{10,8},{12,14},{14,12},{1,3},{3,1},... | collective-permute-start | bytes 24584 | tf_op jit(solution)/shard_map/ppermute | solution.py:59
  109.2 2.0 %collective-permute-done.9 = f32[16,128]{1,0:T(8,128)S(1)} collective-permute-done((f32[16,128]{1,0:T(8,128)S(1)}, f32[16,128]{1,0:T(8,128)S(1)}, u32[]{:S(2)}, u32[]{:S(2)}) %collective-permute-start.9) | collective-permute-done | bytes 8224 | tf_op jit(solution)/shard_map/ppermute | solution.py:59
  111.3 2.5 %collective-permute-start.10 = (f32[16,128]{1,0:T(8,128)S(1)}, f32[16,128]{1,0:T(8,128)S(1)}, u32[]{:S(2)}, u32[]{:S(2)}) collective-permute-start(f32[16,128]{1,0:T(8,128)S(1)} %add.18), channel_id=1, source_target_pairs={{0,4},{2,6},{4,0},{6,2},{8,12},{10,14},{12,8},{14,10},{1,5},{3,7},... | collective-permute-start | bytes 24584 | tf_op jit(solution)/shard_map/ppermute | solution.py:59
  113.7 1.6 %collective-permute-done.10 = f32[16,128]{1,0:T(8,128)S(1)} collective-permute-done((f32[16,128]{1,0:T(8,128)S(1)}, f32[16,128]{1,0:T(8,128)S(1)}, u32[]{:S(2)}, u32[]{:S(2)}) %collective-permute-start.10) | collective-permute-done | bytes 8224 | tf_op jit(solution)/shard_map/ppermute | solution.py:59
  115.4 3.0 %collective-permute-start.11 = (f32[16,128]{1,0:T(8,128)S(1)}, f32[16,128]{1,0:T(8,128)S(1)}, u32[]{:S(2)}, u32[]{:S(2)}) collective-permute-start(f32[16,128]{1,0:T(8,128)S(1)} %add.19), channel_id=1, source_target_pairs={{0,8},{2,10},{4,12},{6,14},{8,0},{10,2},{12,4},{14,6},{1,9},{3,11}... | collective-permute-start | bytes 24584 | tf_op jit(solution)/shard_map/ppermute | solution.py:59
  118.4 1.6 %collective-permute-done.11 = f32[16,128]{1,0:T(8,128)S(1)} collective-permute-done((f32[16,128]{1,0:T(8,128)S(1)}, f32[16,128]{1,0:T(8,128)S(1)}, u32[]{:S(2)}, u32[]{:S(2)}) %collective-permute-start.11) | collective-permute-done | bytes 8224 | tf_op jit(solution)/shard_map/ppermute | solution.py:59
  120.0 0.0 copy-done
  120.1 11.4 %shard_map.63 = (f32[16,2,64,256]{3,2,1,0:T(8,128)}, f32[16,2,64,256]{3,2,1,0:T(8,128)}) custom-call(s32[1]{0:T(128)} %bitcast.odd, f32[16,128]{1,0:T(8,128)S(1)} %add.20.moments, bf16[2,64,64,256]{3,2,1,0:T(8,128)(2,1)S(1)} %get-tuple-element.31.split01, bf16[2,64,64,256]{3,2,1,0:T(8,128)(2,1)S(1)} %get-tuple-element.32.split23, ...), custom_call_target="tpu_custom_call" | custom-call | tf_op jit(solution)/shard_map/pallas_call | solution.py:479
  (8 shorter events, 0.1 us)
Async XLA Ops:
  0.6 1.6 %copy-start.1 = (f32[16,2,64,256]{3,2,1,0:T(8,128)S(1)}, f32[16,2,64,256]{3,2,1,0:T(8,128)}, u32[]{:S(2)}) copy-start(f32[16,2,64,256]{3,2,1,0:T(8,128)} %residual.1) | copy-start | bytes 6291460
  2.2 0.9 copy-start.2
  3.1 0.9 copy-start.3
  5.6 34.2 %collective-permute-start = (f32[80,16,256]{2,1,0:T(8,128)S(1)}, f32[80,16,256]{2,1,0:T(8,128)S(1)}, u32[]{:S(2)}, u32[]{:S(2)}) collective-permute-start(f32[80,16,256]{2,1,0:T(8,128)S(1)} %get-tuple-element.18.mine), channel_id=1, source_target_pairs={{0,2},{2,0},{4,6},{6,4},{8,10},{10,8},{12,14},{14,12},{1,3},{3,1},... | collective-permute-start | bytes 3932168 | tf_op jit(solution)/shard_map/ppermute | solution.py:22
  8.6 30.1 %collective-permute-start.1 = (f32[76,16,256]{2,1,0:T(8,128)}, f32[76,16,256]{2,1,0:T(8,128)}, u32[]{:S(2)}, u32[]{:S(2)}) collective-permute-start(f32[76,16,256]{2,1,0:T(8,128)} %get-tuple-element.19.ahead), channel_id=1, source_target_pairs={{0,4},{4,8},{6,2},{8,12},{10,6},{14,10},{1,5},{5,9},{7,3},{9,13},{... | collective-permute-start | bytes 3735560 | tf_op jit(solution)/shard_map/ppermute | solution.py:22
  14.0 2.7 %collective-permute-start.2 = (f32[2,3,16,256]{3,2,1,0:T(8,128)S(1)}, f32[2,3,16,256]{3,2,1,0:T(8,128)S(1)}, u32[]{:S(2)}, u32[]{:S(2)}) collective-permute-start(f32[2,3,16,256]{3,2,1,0:T(8,128)S(1)} %maximum_select_fusion.1), channel_id=1, source_target_pairs={{0,1},{1,0},{2,3},{3,2},{4,5},{5,4},{6,7},{7,6},{8,9},{9,8},{10,11... | collective-permute-start | bytes 294920 | tf_op jit(solution)/shard_map/ppermute | solution.py:22
  14.1 59.8 %collective-permute-start.6 = (f32[80,16,256]{2,1,0:T(8,128)S(1)}, f32[80,16,256]{2,1,0:T(8,128)S(1)}, u32[]{:S(2)}, u32[]{:S(2)}) collective-permute-start(f32[80,16,256]{2,1,0:T(8,128)S(1)} %get-tuple-element.18.mine), channel_id=1, source_target_pairs={{4,0},{8,4},{2,6},{12,8},{6,10},{10,14},{5,1},{9,5},{3,7},{13,9},{... | collective-permute-start | bytes 3932168 | tf_op jit(solution)/shard_map/ppermute | solution.py:22
  41.6 32.7 %collective-permute-start.5 = (f32[80,16,256]{2,1,0:T(8,128)S(1)}, f32[80,16,256]{2,1,0:T(8,128)S(1)}, u32[]{:S(2)}, u32[]{:S(2)}) collective-permute-start(f32[80,16,256]{2,1,0:T(8,128)S(1)} %collective-permute-done.near2), channel_id=1, source_target_pairs={{0,4},{4,8},{6,2},{8,12},{10,6},{14,10},{1,5},{5,9},{7,3},{9,13},{... | collective-permute-start | bytes 3932168 | tf_op jit(solution)/shard_map/ppermute | solution.py:22
  46.1 24.2 %collective-permute-start.3 = (f32[66,16,256]{2,1,0:T(8,128)S(1)}, f32[66,16,256]{2,1,0:T(8,128)S(1)}, u32[]{:S(2)}, u32[]{:S(2)}) collective-permute-start(f32[66,16,256]{2,1,0:T(8,128)S(1)} %maximum_select_fusion), channel_id=1, source_target_pairs={{0,2},{2,0},{4,6},{6,4},{8,10},{10,8},{12,14},{14,12},{1,3},{3,1},... | collective-permute-start | bytes 3244040 | tf_op jit(solution)/shard_map/ppermute | solution.py:22
  70.3 25.6 %collective-permute-start.4 = (f32[66,16,256]{2,1,0:T(8,128)S(1)}, f32[66,16,256]{2,1,0:T(8,128)S(1)}, u32[]{:S(2)}, u32[]{:S(2)}) collective-permute-start(f32[66,16,256]{2,1,0:T(8,128)S(1)} %collective-permute-done.3.near1), channel_id=1, source_target_pairs={{0,4},{4,8},{6,2},{8,12},{10,6},{14,10},{1,5},{5,9},{7,3},{9,13},{... | collective-permute-start | bytes 3244040 | tf_op jit(solution)/shard_map/ppermute | solution.py:22
  75.6 1.8 %collective-permute-start.7 = (f32[23,16,256]{2,1,0:T(8,128)S(1)}, f32[23,16,256]{2,1,0:T(8,128)S(1)}, u32[]{:S(2)}, u32[]{:S(2)}) collective-permute-start(f32[23,16,256]{2,1,0:T(8,128)S(1)} %broadcast_select_fusion.2), channel_id=1, source_target_pairs={{0,1},{1,0},{2,3},{3,2},{4,5},{5,4},{6,7},{7,6},{8,9},{9,8},{10,11... | collective-permute-start | bytes 1130504 | tf_op jit(solution)/shard_map/ppermute | solution.py:22
  96.0 24.1 %copy-start = (f32[16,2,64,256]{3,2,1,0:T(8,128)S(1)}, f32[16,2,64,256]{3,2,1,0:T(8,128)}, u32[]{:S(2)}) copy-start(f32[16,2,64,256]{3,2,1,0:T(8,128)} %iterate.1) | copy-start | bytes 6291460
  106.4 1.2 collective-permute-start.8
  107.6 3.7 %collective-permute-start.9 = (f32[16,128]{1,0:T(8,128)S(1)}, f32[16,128]{1,0:T(8,128)S(1)}, u32[]{:S(2)}, u32[]{:S(2)}) collective-permute-start(f32[16,128]{1,0:T(8,128)S(1)} %add.17), channel_id=1, source_target_pairs={{0,2},{2,0},{4,6},{6,4},{8,10},{10,8},{12,14},{14,12},{1,3},{3,1},... | collective-permute-start | bytes 24584 | tf_op jit(solution)/shard_map/ppermute | solution.py:59
  111.3 4.1 %collective-permute-start.10 = (f32[16,128]{1,0:T(8,128)S(1)}, f32[16,128]{1,0:T(8,128)S(1)}, u32[]{:S(2)}, u32[]{:S(2)}) collective-permute-start(f32[16,128]{1,0:T(8,128)S(1)} %add.18), channel_id=1, source_target_pairs={{0,4},{2,6},{4,0},{6,2},{8,12},{10,14},{12,8},{14,10},{1,5},{3,7},... | collective-permute-start | bytes 24584 | tf_op jit(solution)/shard_map/ppermute | solution.py:59
  115.4 4.7 %collective-permute-start.11 = (f32[16,128]{1,0:T(8,128)S(1)}, f32[16,128]{1,0:T(8,128)S(1)}, u32[]{:S(2)}, u32[]{:S(2)}) collective-permute-start(f32[16,128]{1,0:T(8,128)S(1)} %add.19), channel_id=1, source_target_pairs={{0,8},{2,10},{4,12},{6,14},{8,0},{10,2},{12,4},{14,6},{1,9},{3,11}... | collective-permute-start | bytes 24584 | tf_op jit(solution)/shard_map/ppermute | solution.py:59

commit v7 on v6

--- a/solution.py
+++ b/solution.py
@@ -75,48 +75,102 @@
 MARGIN = 8
 
 
-def prepare_kernel(odd, residual, labels, boundary, mine, ahead):
+def prepare_kernel(
+    odd, residual, labels, boundary, mine_a, mine_b, ahead, back, block, label_cells, boundary_cells, arrived
+):
     rhs, depth, rows, nx = residual.shape
-    for place, out in ((0, mine), (1, ahead)):
+    half = rhs // 2
+    copies = [
+        pltpu.make_async_copy(labels, label_cells, arrived.at[0]),
+        pltpu.make_async_copy(boundary, boundary_cells, arrived.at[1]),
+    ] + [
+        pltpu.make_async_copy(
+            residual.at[:, jnp.bitwise_xor(place, odd[0])], block.at[place], arrived.at[2 + place]
+        )
+        for place in range(depth)
+    ]
+    for copy in copies:
+        copy.start()
+    for copy in copies[:2]:
+        copy.wait()
+    for place in range(depth):
         plane = jnp.bitwise_xor(place, odd[0])
-
-        def turn(block, carry, plane=plane, out=out):
-            rows_here = pl.ds(block * 8, 8)
-            out[rows_here] = pltpu.einshape("abc->bac", residual[:, plane, rows_here, :])
+        for message, order in ((mine_a, (0, 1, 2, 3)), (ahead, (0, 1, None, 2)), (back, (0, 1, 2, None))):
+            size = message.shape[1]
+            count = rows // size
+            for part in range(count):
+                cells = pl.ds(part * size, size)
+                values = (
+                    jnp.exp(label_cells[plane, cells, :].astype(f32) * (contrast_log / (NCLASS - 1))),
+                    (1 - boundary_cells[plane, cells, :]).astype(f32),
+                )
+                for kind, value in enumerate(values):
+                    at = order[2 * kind + place]
+                    if at is not None:
+                        message[rows + at * count + part] = value
+
+    for place in range(depth):
+        copies[2 + place].wait()
+
+        def turn(group, carry, place=place):
+            here = pl.ds(group * 8, 8)
+            turned = pltpu.einshape("abc->bac", block[place, :, here, :])
+            if place == 0:
+                mine_a[here] = turned[:, :half]
+                mine_b[here] = turned[:, half:]
+                back[here] = turned
+            else:
+                ahead[here] = turned
             return carry
 
         lax.fori_loop(0, rows // 8, turn, 0)
-        for part in range(rows // rhs):
-            cells = pl.ds(part * rhs, rhs)
-            coef = jnp.exp(labels[plane, cells, :].astype(f32) * (contrast_log / (NCLASS - 1)))
-            inner = (1 - boundary[plane, cells, :]).astype(f32)
-            count = rows // rhs
-            for message in (mine, ahead):
-                message[rows + place * count + part] = coef
-            mine[rows + (2 + place) * count + part] = inner
-            if place == 1:
-                ahead[rows + 2 * count + part] = inner
-
-
-def edges_kernel(rows, near1, near2, far1, far3, near3, mine, first, last):
+
+
+def second_kernel(rows, ahead, own_before, own_behind, near2, out):
+    del near2
+
+    def copy_rows(y, size):
+        for j in range(size):
+            out[y + j] = ahead[y + j]
+
+    row_blocks(0, rows, copy_rows, 16)
+    out[rows] = own_before[1, REACH - 1]
+    out[rows + 1] = own_behind[1, 0]
+
+
+def field_edges_kernel(rows, near2, far1, far3, near3, mine, first, last):
     messages = {"near2": near2, "far1": far1, "far3": far3, "near3": near3, "mine": mine}
-    rhs = mine.shape[1]
-    count = rows // rhs
-    for (_, place, number), source in zip(BESIDE, (near1, near2, far1)):
-        first[place : place + number] = source[:number]
-        last[place : place + number] = source[rows - number : rows]
-    place = EDGES
+    place = 0
     for name, *parts in FIELDS:
+        message = messages[name]
+        size = message.shape[1]
+        count = rows // size
         for part in parts:
             if part is not None:
                 start = rows + part * count
-                first[place] = messages[name][start]
-                last[place] = messages[name][start + count - 1]
+                first[place] = message[start, :MARGIN]
+                last[place] = message[start + count - 1, size - MARGIN :]
                 place += 1
 
 
+def edges_kernel(rows, near1, near2a, near2b, far1a, far1b, inverse, first, last):
+    del inverse
+    half = near2a.shape[1]
+    for (_, place, number), sources in zip(BESIDE, ((near1,), (near2a, near2b), (far1a, far1b))):
+        for index, source in enumerate(sources):
+            part = slice(None) if len(sources) == 1 else slice(index * half, (index + 1) * half)
+            first[place : place + number, part] = source[:number]
+            last[place : place + number, part] = source[rows - number : rows]
+
+
+def couplings_kernel(rows, far3, far1, mine, near2, near3, before, behind, inverse, sx, sy, sz, root, coef, inner, masked):
+    messages = {"near2": near2, "far1": far1, "far3": far3, "near3": near3, "mine": mine}
+    fill_cells(rows, messages, before, behind, coef, inner)
+    make_operator(coef, inner, inverse, sx, sy, sz, root, masked)
+
+
 def fill_cells(rows, messages, before, behind, coef, inner):
-    place = EDGES
+    place = 0
     for plane, (name, *parts) in enumerate(FIELDS):
         for part, out in zip(parts, (coef, inner)):
             if part is None:
@@ -127,8 +181,8 @@
                 out[plane, MARGIN + block * rhs : MARGIN + (block + 1) * rhs] = messages[name][
                     rows + part * count + block
                 ]
-            out[plane, :MARGIN] = before[place, rhs - MARGIN :]
-            out[plane, MARGIN + rows :] = behind[place, :MARGIN]
+            out[plane, :MARGIN] = before[place]
+            out[plane, MARGIN + rows :] = behind[place]
             place += 1
 
 
@@ -173,17 +227,18 @@
     return ref[plane, pl.ds(y + (MARGIN - REACH), 1), :]
 
 
-def row_blocks(start, stop, body, size=8):
+def row_blocks(start, stop, body, size):
     blocks = -(-(stop - start) // size)
+    size = -(-(stop - start) // blocks)
 
     def step(block, carry):
-        body(jnp.minimum(start + block * size, stop - size))
+        body(jnp.minimum(start + block * size, stop - size), size)
         return carry
 
     lax.fori_loop(0, blocks, step, 0)
 
 
-def apply_rows(operator, plane, start, before, here, after, size=8):
+def apply_rows(operator, plane, start, before, here, after, size):
     sx, sy, sz = operator
     ref, index = here
     out = []
@@ -208,17 +263,17 @@
     return max(REACH - plane, plane - (REACH + depth - 1), 0)
 
 
-def scale_rows(plane, source, first, dst, start, count, inverse):
+def scale_rows(plane, source, first, dst, start, count, inverse, part=slice(None)):
     out, place = dst
 
-    def body(j, size=8):
+    def body(j, size):
         for i in range(size):
-            out[place, start + j + i] = source[first + j + i] * cell_row(inverse, plane, start + j + i)
+            out[place, start + j + i, part] = source[first + j + i] * cell_row(inverse, plane, start + j + i)
 
     if count < 8:
         body(0, count)
     else:
-        row_blocks(0, count, body)
+        row_blocks(0, count, body, 16)
 
 
 def apply_plane(rows, power, plane, operator, fields):
@@ -226,11 +281,11 @@
     src = [fields[power - 1, plane + offset] for offset in (-1, 0, 1)]
     out, place = fields[power, plane]
 
-    def body(y):
-        for j, values in enumerate(apply_rows(operator, plane, y, *src)):
+    def body(y, size):
+        for j, values in enumerate(apply_rows(operator, plane, y, *src, size)):
             out[place, y + j] = values
 
-    row_blocks(REACH - reach, REACH + rows + reach, body)
+    row_blocks(REACH - reach, REACH + rows + reach, body, 34)
 
 
 def halves(blocks):
@@ -250,20 +305,21 @@
 
 
 def early_kernel(
-    rows, far3, far1, mine, ahead, own_before, own_behind, near1, near2, near3, before, behind,
-    inverse, sx, sy, sz, root, u0_out, u1_out, u2_out, split, moments, u0, u1, coef, inner, masked,
+    rows, far3, far1a, far1b, mine_a, mine_b, ahead, own_before, own_behind, near1, near2a, near2b, near3,
+    before, behind, inverse, sx, sy, sz, u0_out, u1_out, u2_out, split, moments, u0, u1,
 ):
-    messages = {"near2": near2, "far1": far1, "far3": far3, "near3": near3, "mine": mine}
-    fill_cells(rows, messages, before, behind, coef, inner)
-    make_operator(coef, inner, inverse, sx, sy, sz, root, masked)
     operator = (sx, sy, sz)
     fields = {(0, plane): (u0_out, index) for index, plane in enumerate((0, 2, 3))}
     fields.update({(0, plane): (u0, plane - 4) for plane in range(4, 8)})
     fields.update({(1, 3): (u1_out, 0), (1, 4): (u1_out, 1), (1, 5): (u1, 0), (1, 6): (u1, 1)})
     fields.update({(2, 4): (u2_out, 0), (2, 5): (u2_out, 1)})
     first, last = REACH, REACH + rows
-    for plane, source in ((0, far3), (2, far1), (3, mine), (4, ahead), (5, near1), (6, near2), (7, near3)):
+    half = mine_a.shape[1]
+    for plane, source in ((0, far3), (4, ahead), (5, near1), (7, near3)):
         scale_rows(plane, source, 0, fields[0, plane], first, rows, inverse)
+    for plane, sources in ((2, (far1a, far1b)), (3, (mine_a, mine_b)), (6, (near2a, near2b))):
+        for source, part in zip(sources, (slice(0, half), slice(half, None))):
+            scale_rows(plane, source, 0, fields[0, plane], first, rows, inverse, part)
     for plane in (3, 4):
         scale_rows(plane, own_before.at[plane - 3], 0, fields[0, plane], 0, REACH, inverse)
         scale_rows(plane, own_behind.at[plane - 3], 0, fields[0, plane], last, REACH, inverse)
@@ -278,17 +334,19 @@
     for plane in range(2):
 
         def gram_rows(block, total, plane=plane):
-            parts = []
-            for j in range(8):
-                y = block * 8 + j
-                sources = [fields[power, plane + REACH] for power in range(2)]
-                both = halves([ref[index, y + REACH] for ref, index in sources])
-                split[plane, y] = both
-                parts.append(both)
-            wide = jnp.concatenate(parts, axis=1)
-            return total + inner_products(wide, wide)
-
-        gram = lax.fori_loop(0, rows // 8, gram_rows, gram)
+            for group in range(4):
+                parts = []
+                for j in range(4):
+                    y = block * 16 + group * 4 + j
+                    sources = [fields[power, plane + REACH] for power in range(2)]
+                    both = halves([ref[index, y + REACH] for ref, index in sources])
+                    split[plane, y] = both
+                    parts.append(both)
+                wide = jnp.concatenate(parts, axis=1)
+                total = total + inner_products(wide, wide)
+            return total
+
+        gram = lax.fori_loop(0, rows // 16, gram_rows, gram)
     gram = whole(gram, 2 * rhs, 2 * rhs)
     moments[:, : 2 * rhs] = gram[:rhs]
     moments[:, 2 * rhs : 3 * rhs] = gram[rhs:, rhs:]
@@ -314,19 +372,21 @@
         level = plane + REACH
 
         def gram_rows(block, total, plane=plane, level=level):
-            start = block * 8
+            start = block * 16
             y = start + REACH
-            last = apply_rows(operator, level, y, *[fields[2, level + offset] for offset in (-1, 0, 1)])
-            left, right = [], []
-            for j in range(8):
-                ref, index = fields[2, level]
-                both = halves([ref[index, y + j], last[j]])
-                split[plane, start + j] = both
-                left.append(jnp.concatenate([halves([u1_in[plane, y + j]]), both], axis=0))
-                right.append(jnp.concatenate([both[:rhs], both[2 * rhs : 3 * rhs]], axis=0))
-            return total + inner_products(jnp.concatenate(left, axis=1), jnp.concatenate(right, axis=1))
-
-        gram = lax.fori_loop(0, rows // 8, gram_rows, gram)
+            last = apply_rows(operator, level, y, *[fields[2, level + offset] for offset in (-1, 0, 1)], 16)
+            for group in range(4):
+                left, right = [], []
+                for j in range(group * 4, group * 4 + 4):
+                    ref, index = fields[2, level]
+                    both = halves([ref[index, y + j], last[j]])
+                    split[plane, start + j] = both
+                    left.append(jnp.concatenate([halves([u1_in[plane, y + j]]), both], axis=0))
+                    right.append(jnp.concatenate([both[:rhs], both[2 * rhs : 3 * rhs]], axis=0))
+                total = total + inner_products(jnp.concatenate(left, axis=1), jnp.concatenate(right, axis=1))
+            return total
+
+        gram = lax.fori_loop(0, rows // 16, gram_rows, gram)
     gram = gram[:, :rhs] + gram[:, rhs:]
     blocks = [gram[part * rhs : (part + 1) * rhs] for part in range(6)]
     moments[:, : 3 * rhs] = moments_in[:, : 3 * rhs]
@@ -336,6 +396,34 @@
     moments[:, 6 * rhs :] = jnp.zeros((rhs, moments.shape[1] - 6 * rhs), f32)
 
 
+def inverse_of_pair(a, b, c, d):
+    scale = 1.0 / (a * d - b * c)
+    return d * scale, -b * scale, -c * scale, a * scale
+
+
+def times(p, q):
+    a, b, c, d = p
+    e, f, g, h = q
+    return a * e + b * g, a * f + b * h, c * e + d * g, c * f + d * h
+
+
+def inverse_of_four(m):
+    p, q = (m[0][0], m[0][1], m[1][0], m[1][1]), (m[0][2], m[0][3], m[1][2], m[1][3])
+    r, s = (m[2][0], m[2][1], m[3][0], m[3][1]), (m[2][2], m[2][3], m[3][2], m[3][3])
+    inner = inverse_of_pair(*p)
+    right, left = times(inner, q), times(r, inner)
+    outer = inverse_of_pair(*[x - y for x, y in zip(s, times(r, right))])
+    lower = [-x for x in times(outer, left)]
+    upper = [-x for x in times(right, outer)]
+    corner = [x - y for x, y in zip(inner, times(right, lower))]
+    return (
+        (corner[0], corner[1], upper[0], upper[1]),
+        (corner[2], corner[3], upper[2], upper[3]),
+        (lower[0], lower[1], outer[0], outer[1]),
+        (lower[2], lower[3], outer[2], outer[3]),
+    )
+
+
 def eliminate(stacked, size):
     tiles, height, width = stacked.shape
     lane = lax.broadcasted_iota(jnp.int32, (height, width), 1)
@@ -343,21 +431,24 @@
     def everywhere(row):
         return jnp.broadcast_to(row, (height, width))
 
-    for k in range(0, size, 2):
+    for k in range(0, size, 4):
         if k and k % height == 0:
             stacked = stacked[1:]
         at = k % height
-        row0, row1 = everywhere(stacked[0, at : at + 1]), everywhere(stacked[0, at + 1 : at + 2])
-        col0 = jnp.broadcast_to(stacked[:, :, k : k + 1], stacked.shape)
-        col1 = jnp.broadcast_to(stacked[:, :, k + 1 : k + 2], stacked.shape)
-        a, c = everywhere(col0[0, at : at + 1]), everywhere(col0[0, at + 1 : at + 2])
-        b, d = everywhere(col1[0, at : at + 1]), everywhere(col1[0, at + 1 : at + 2])
-        scale = 1.0 / (a * d - b * c)
-        first, second = lane == k, lane == k + 1
-        mix0 = scale * jnp.where(first, -d, jnp.where(second, b, d * row0 - b * row1))
-        mix1 = scale * jnp.where(first, c, jnp.where(second, -a, a * row1 - c * row0))
-        rest = jnp.where((first | second)[None], 0.0, stacked)
-        stacked = rest - col0 * mix0[None] - col1 * mix1[None]
+        rows = [everywhere(stacked[0, at + i : at + i + 1]) for i in range(4)]
+        columns = [jnp.broadcast_to(stacked[:, :, k + i : k + i + 1], stacked.shape) for i in range(4)]
+        block = [[everywhere(columns[j][0, at + i : at + i + 1]) for j in range(4)] for i in range(4)]
+        inverse = inverse_of_four(block)
+        pivots = (lane >= k) & (lane < k + 4)
+        result = jnp.where(pivots[None], 0.0, stacked)
+        for i in range(4):
+            mix = (inverse[i][0] * rows[0] + inverse[i][1] * rows[1]) + (
+                inverse[i][2] * rows[2] + inverse[i][3] * rows[3]
+            )
+            for j in range(4):
+                mix = jnp.where(lane == k + j, -inverse[i][j], mix)
+            result = result - columns[i] * mix[None]
+        stacked = result
     return stacked[1:]
 
 
@@ -413,54 +504,95 @@
     def params(mib):
         return pltpu.CompilerParams(vmem_limit_bytes=mib * 2**20)
 
-    count = rows // rhs
-    mine, ahead = pl.pallas_call(
+    anywhere = pl.BlockSpec(memory_space=pl.ANY)
+
+    half = rhs // 2
+    wide = rows + 3 * rows // rhs
+    mine_a, mine_b, ahead, back = pl.pallas_call(
         prepare_kernel,
-        out_shape=(array(rows + 4 * count, rhs, nx), array(rows + 3 * count, rhs, nx)),
-        in_specs=[smem, vmem, vmem, vmem],
-        out_specs=(vmem, vmem),
-        compiler_params=params(16),
+        out_shape=(
+            array(rows + 4 * rows // half, half, nx), array(rows, half, nx), array(wide, rhs, nx), array(wide, rhs, nx)
+        ),
+        in_specs=[smem] + [pl.BlockSpec(memory_space=pltpu.HBM)] * 3,
+        out_specs=(vmem,) * 4,
+        scratch_shapes=[
+            pltpu.VMEM((depth, rhs, rows, nx), f32),
+            pltpu.VMEM(labels.shape, jnp.int32),
+            pltpu.VMEM(boundary.shape, jnp.int32),
+            pltpu.SemaphoreType.DMA((2 + depth,)),
+        ],
+        compiler_params=params(55),
     )(odd, residual, labels, boundary)
 
-    near2 = swapped(mine)
+    near2a = swapped(mine_a)
     far3 = relayed(ahead)
-    near3 = relayed(mine, back=True)
+    near3 = relayed(back, back=True)
+    near2b = swapped(mine_b)
+
+    def both(first, last, second):
+        return jnp.stack([jnp.concatenate([first[second], last[second]], axis=1), ahead[second]])
+
     own_before, own_behind = rows_beside(
-        jnp.stack([mine[:REACH], ahead[:REACH]]), jnp.stack([mine[rows - REACH : rows], ahead[rows - REACH : rows]])
-    )
-    last = jnp.concatenate([ahead[:rows], own_before[1, -1:], own_behind[1, :1]], axis=0)
-    here = jnp.minimum(near2[0, 0, 0], far3[0, 0, 0]) >= jnp.finfo(f32).min
-    near1 = swapped(jnp.where(here, last, 0.0))
-    far1 = relayed(near2)
+        both(mine_a, mine_b, slice(0, REACH)), both(mine_a, mine_b, slice(rows - REACH, rows))
+    )
+    near1 = swapped(
+        pl.pallas_call(
+            partial(second_kernel, rows),
+            out_shape=array(rows + 2, rhs, nx),
+            in_specs=[vmem, vmem, vmem, anywhere],
+            out_specs=vmem,
+            compiler_params=params(8),
+        )(ahead, own_before, own_behind, near2b)
+    )
+    far1a = relayed(near2a)
+    far1b = relayed(near2b)
     far2 = relayed(near1)
 
-    edges = EDGES + sum(part is not None for _, *parts in FIELDS for part in parts)
+    number = sum(part is not None for _, *parts in FIELDS for part in parts)
+    fields_before, fields_behind = rows_beside(
+        *pl.pallas_call(
+            partial(field_edges_kernel, rows),
+            out_shape=(array(number, MARGIN, nx),) * 2,
+            in_specs=[vmem] * 5,
+            out_specs=(vmem, vmem),
+            compiler_params=params(8),
+        )(near2a, far1a, far3, near3, mine_a)
+    )
+    cells = (depth + 2 * REACH, rows + 2 * MARGIN, nx)
+    inverse, sx, sy, sz, root = pl.pallas_call(
+        partial(couplings_kernel, rows),
+        out_shape=(array(*cells),) * 5,
+        in_specs=[vmem] * 7,
+        out_specs=(vmem,) * 5,
+        scratch_shapes=[pltpu.VMEM((cells[0] + 2,) + cells[1:], f32)] * 2 + [pltpu.VMEM(cells, f32)],
+        compiler_params=params(14),
+    )(far3, far1a, mine_a, near2a, near3, fields_before, fields_behind)
+
     before, behind = rows_beside(
         *pl.pallas_call(
             partial(edges_kernel, rows),
-            out_shape=(array(edges, rhs, nx),) * 2,
-            in_specs=[vmem] * 6,
+            out_shape=(array(EDGES, rhs, nx),) * 2,
+            in_specs=[vmem] * 5 + [anywhere],
             out_specs=(vmem, vmem),
-            compiler_params=params(12),
-        )(near1, near2, far1, far3, near3, mine)
+            compiler_params=params(8),
+        )(near1, near2a, near2b, far1a, far1b, inverse)
     )
 
     def planes(number):
         return (number, rows + 2 * REACH, rhs, nx)
 
-    cells = (depth + 2 * REACH, rows + 2 * MARGIN, nx)
-    inverse, sx, sy, sz, root, u0, u1, u2, split01, moments = pl.pallas_call(
+    u0, u1, u2, split01, moments = pl.pallas_call(
         partial(early_kernel, rows),
-        out_shape=(array(*cells),) * 5
-        + tuple(array(*planes(number)) for number in (3, 2, 2))
+        out_shape=tuple(array(*planes(number)) for number in (3, 2, 2))
         + (array(depth, rows, 4 * rhs, nx, dtype=bf16), array(rhs, 128)),
-        in_specs=[vmem] * 11,
-        out_specs=(vmem,) * 10,
-        scratch_shapes=[pltpu.VMEM(planes(number), f32) for number in (4, 2)]
-        + [pltpu.VMEM((cells[0] + 2,) + cells[1:], f32)] * 2
-        + [pltpu.VMEM(cells, f32)],
+        in_specs=[vmem] * 18,
+        out_specs=(vmem,) * 5,
+        scratch_shapes=[pltpu.VMEM(planes(number), f32) for number in (4, 2)],
         compiler_params=params(24),
-    )(far3, far1, mine, ahead, own_before, own_behind, near1, near2, near3, before, behind)
+    )(
+        far3, far1a, far1b, mine_a, mine_b, ahead, own_before, own_behind, near1, near2a, near2b, near3,
+        before, behind, inverse, sx, sy, sz,
+    )
 
     moments, split23 = pl.pallas_call(
         partial(late_kernel, rows),

time: 132 us -> 125 us (0.947)
  Pallas kernels: 41.6 us -> 32.4 us
  local copies, waits for them, and re-layouts: 7.2 us -> 2.99 us
  starting transfers between devices: 24.1 us -> 27.9 us
  waiting for transfers between devices: 56.3 us -> 59.9 us
    pallas_call x3 -> x6, Pallas kernels: 19.7 us -> 15.1 us  [the longest x1 8.24 us: on_device(): pl.pallas_call(partial(early_kernel, rows), out_shape=tuple((array(*plane...]
    ppermute x8 -> x11, starting transfers between devices: 16.9 us -> 20.8 us  [moved(): return lax.ppermute(block, axis, pairs)]
    pallas_call x1, Pallas kernels: 10.5 us -> 6.85 us  [on_device(): pl.pallas_call(partial(late_kernel, rows), out_shape=(array(rhs, 128), ar...]
    ppermute x8 -> x11, waiting for transfers between devices: 49.9 us -> 53.3 us  [moved(): return lax.ppermute(block, axis, pairs)]
    slice x3 -> x1, local copies, waits for them, and re-layouts: 2.97 us -> 0.85 us  [both(): first[second]]
    unnamed x8 -> x10, local copies, waits for them, and re-layouts: 3.4 us -> 1.31 us
  transfers between devices with their start and end apart: 12 -> 15, of which waited for: 9 -> 11; matrix products, arithmetic and copies ran while one was open for 3% -> 1% of each run, Pallas kernels for 14% -> 9%
where the time goes in v7:
time: 125 us; the launch traced here: 124 us
  waiting for transfers between devices  59.9 us (48%)
  Pallas kernels  32.4 us (26%)
  starting transfers between devices  27.9 us (22%)
  local copies, waits for them, and re-layouts  2.99 us (2%)
    ppermute x11, waiting for transfers between devices, moved(): return lax.ppermute(block, axis, pairs)  53.3 us
    ppermute x11, starting transfers between devices, moved(): return lax.ppermute(block, axis, pairs)  20.8 us
    pallas_call x1, Pallas kernels, on_device(): pl.pallas_call(outputs_kernel, out_shape=(array(*iterate.shape), array(*r...  10.5 us
    pallas_call x1, Pallas kernels, on_device(): pl.pallas_call(partial(early_kernel, rows), out_shape=tuple((array(*plane...  8.24 us
    ppermute x4, starting transfers between devices, all_sum(): lax.ppermute(values, axis, [(i, i ^ step) for i in range(count)])  7.05 us
    pallas_call x1, Pallas kernels, on_device(): pl.pallas_call(partial(late_kernel, rows), out_shape=(array(rhs, 128), ar...  6.85 us
    ppermute x4, waiting for transfers between devices, all_sum(): lax.ppermute(values, axis, [(i, i ^ step) for i in range(count)])  6.55 us
    pallas_call x1, Pallas kernels, on_device(): pl.pallas_call(prepare_kernel, out_shape=(array(rows + 4 * rows // half,...  3.81 us
  transfers between devices with their start and end apart: 15, of which 11 were waited for; matrix products, arithmetic and copies ran while one was open for 1% of the time, Pallas kernels for 9%

profile of v7, /device:TPU:0, one launch (start us, length us, event | category | flops | bytes accessed | tf_op | source)
XLA Modules:
  0.0 124.2 jit_solution(7417926512837040607)
XLA Ops:
  0.6 3.8 %shard_map.59 = (f32[96,8,256]{2,1,0:T(8,128)}, f32[64,8,256]{2,1,0:T(8,128)}, f32[76,16,256]{2,1,0:T(8,128)}, f32[76,16,256]{2,1,0:T(8,128)}) custom-call(s32[1]{0:T(128)} %bitcast.odd, f32[16,2,64,256]{3,2,1,0:T(8,128)} %residual.1, s32[2,64,256]{2,1,0:T(8,128)} %labels.1, s32[2,64,256]{2,1,0:T(8,128)} %boundary.1), custom_call_target="tpu_custom_call" | custom-call | tf_op jit(solution)/shard_map/pallas_call | solution.py:511
  4.5 3.0 %collective-permute-start.5 = (f32[96,8,256]{2,1,0:T(8,128)}, f32[96,8,256]{2,1,0:T(8,128)S(1)}, u32[]{:S(2)}, u32[]{:S(2)}) collective-permute-start(f32[96,8,256]{2,1,0:T(8,128)} %get-tuple-element.23.mine.mine_a), channel_id=1, source_target_pairs={{0,2},{2,0},{4,6},{6,4},{8,10},{10,8},{12,14},{14,12},{1,3},{3,1},... | collective-permute-start | bytes 2359304 | tf_op jit(solution)/shard_map/ppermute | solution.py:22
  7.5 0.0 copy-start
  7.5 0.1 collective-permute-start.1
  7.5 0.8 fusion
  8.4 0.8 slice_bitcast_fusion
  9.3 0.1 collective-permute-start
  9.4 4.0 %collective-permute-start.4 = (f32[76,16,256]{2,1,0:T(8,128)}, f32[76,16,256]{2,1,0:T(8,128)S(1)}, u32[]{:S(2)}, u32[]{:S(2)}) collective-permute-start(f32[76,16,256]{2,1,0:T(8,128)} %get-tuple-element.22.ahead), channel_id=1, source_target_pairs={{0,4},{4,8},{6,2},{8,12},{10,6},{14,10},{1,5},{5,9},{7,3},{9,13},{... | collective-permute-start | bytes 3735560 | tf_op jit(solution)/shard_map/ppermute | solution.py:22
  13.3 1.3 %collective-permute-start.8 = (f32[76,16,256]{2,1,0:T(8,128)}, f32[76,16,256]{2,1,0:T(8,128)S(1)}, u32[]{:S(2)}, u32[]{:S(2)}) collective-permute-start(f32[76,16,256]{2,1,0:T(8,128)} %get-tuple-element.25), channel_id=1, source_target_pairs={{4,0},{8,4},{2,6},{12,8},{6,10},{10,14},{5,1},{9,5},{3,7},{13,9},{... | collective-permute-start | bytes 3735560 | tf_op jit(solution)/shard_map/ppermute | solution.py:22
  14.6 0.0 collective-permute-done
  14.7 21.8 %collective-permute-done.1.near2.near2b = f32[64,8,256]{2,1,0:T(8,128)S(1)} collective-permute-done((f32[64,8,256]{2,1,0:T(8,128)}, f32[64,8,256]{2,1,0:T(8,128)S(1)}, u32[]{:S(2)}, u32[]{:S(2)}) %collective-permute-start.1) | collective-permute-done | bytes 524320 | tf_op jit(solution)/shard_map/ppermute | solution.py:22
  36.4 0.0 copy-start.1
  36.5 1.3 %copy-done.1 = f32[76,16,256]{2,1,0:T(8,128)S(1)} copy-done((f32[76,16,256]{2,1,0:T(8,128)S(1)}, f32[76,16,256]{2,1,0:T(8,128)}, u32[]{:S(2)}) %copy-start.1) | copy-done | bytes 1245208
  37.7 0.1 shard_map.60
  37.8 1.8 %collective-permute-start.2 = (f32[66,16,256]{2,1,0:T(8,128)S(1)}, f32[66,16,256]{2,1,0:T(8,128)S(1)}, u32[]{:S(2)}, u32[]{:S(2)}) collective-permute-start(f32[66,16,256]{2,1,0:T(8,128)S(1)} %shard_map.60), channel_id=1, source_target_pairs={{0,2},{2,0},{4,6},{6,4},{8,10},{10,8},{12,14},{14,12},{1,3},{3,1},... | collective-permute-start | bytes 3244040 | tf_op jit(solution)/shard_map/ppermute | solution.py:22
  39.6 0.0 collective-permute-done.5.near2.near2a
  39.6 3.5 %collective-permute-start.6 = (f32[96,8,256]{2,1,0:T(8,128)S(1)}, f32[96,8,256]{2,1,0:T(8,128)S(1)}, u32[]{:S(2)}, u32[]{:S(2)}) collective-permute-start(f32[96,8,256]{2,1,0:T(8,128)S(1)} %collective-permute-done.5.near2.near2a), channel_id=1, source_target_pairs={{0,4},{4,8},{6,2},{8,12},{10,6},{14,10},{1,5},{5,9},{7,3},{9,13},{... | collective-permute-start | bytes 2359304 | tf_op jit(solution)/shard_map/ppermute | solution.py:22
  43.2 3.5 %collective-permute-start.7 = (f32[64,8,256]{2,1,0:T(8,128)S(1)}, f32[64,8,256]{2,1,0:T(8,128)S(1)}, u32[]{:S(2)}, u32[]{:S(2)}) collective-permute-start(f32[64,8,256]{2,1,0:T(8,128)S(1)} %collective-permute-done.1.near2.near2b), channel_id=1, source_target_pairs={{0,4},{4,8},{6,2},{8,12},{10,6},{14,10},{1,5},{5,9},{7,3},{9,13},{... | collective-permute-start | bytes 1572872 | tf_op jit(solution)/shard_map/ppermute | solution.py:22
  46.6 0.0 collective-permute-done.4.far3
  46.6 0.0 collective-permute-done.8.near3
  46.7 14.4 %collective-permute-done.6.far1.far1a = f32[96,8,256]{2,1,0:T(8,128)S(1)} collective-permute-done((f32[96,8,256]{2,1,0:T(8,128)S(1)}, f32[96,8,256]{2,1,0:T(8,128)S(1)}, u32[]{:S(2)}, u32[]{:S(2)}) %collective-permute-start.6) | collective-permute-done | bytes 786464 | tf_op jit(solution)/shard_map/ppermute | solution.py:22
  61.1 0.0 copy-done
  61.1 1.8 %collective-permute-done.2.near1 = f32[66,16,256]{2,1,0:T(8,128)S(1)} collective-permute-done((f32[66,16,256]{2,1,0:T(8,128)S(1)}, f32[66,16,256]{2,1,0:T(8,128)S(1)}, u32[]{:S(2)}, u32[]{:S(2)}) %collective-permute-start.2) | collective-permute-done | bytes 1081376 | tf_op jit(solution)/shard_map/ppermute | solution.py:22
  62.9 3.5 %collective-permute-start.3 = (f32[66,16,256]{2,1,0:T(8,128)S(1)}, f32[66,16,256]{2,1,0:T(8,128)S(1)}, u32[]{:S(2)}, u32[]{:S(2)}) collective-permute-start(f32[66,16,256]{2,1,0:T(8,128)S(1)} %collective-permute-done.2.near1), channel_id=1, source_target_pairs={{0,4},{4,8},{6,2},{8,12},{10,6},{14,10},{1,5},{5,9},{7,3},{9,13},{... | collective-permute-start | bytes 3244040 | tf_op jit(solution)/shard_map/ppermute | solution.py:22
  66.4 0.1 collective-permute-start.9
  66.5 1.4 %collective-permute-done.9 = f32[18,8,256]{2,1,0:T(8,128)S(1)} collective-permute-done((f32[18,8,256]{2,1,0:T(8,128)S(1)}, f32[18,8,256]{2,1,0:T(8,128)S(1)}, u32[]{:S(2)}, u32[]{:S(2)}) %collective-permute-start.9) | collective-permute-done | bytes 147488 | tf_op jit(solution)/shard_map/ppermute | solution.py:22
  67.9 2.9 %shard_map.62 = (f32[8,80,256]{2,1,0:T(8,128)S(1)}, f32[8,80,256]{2,1,0:T(8,128)S(1)}, f32[8,80,256]{2,1,0:T(8,128)S(1)}, f32[8,80,256]{2,1,0:T(8,128)S(1)}, f32[8,80,256]{2,1,0:T(8,128)S(1)}) custom-call(f32[76,16,256]{2,1,0:T(8,128)S(1)} %collective-permute-done.4.far3, f32[96,8,256]{2,1,0:T(8,128)S(1)} %collective-permute-done.6.far1.far1a, ...), custom_call_target="tpu_custom_call" | custom-call | tf_op jit(solution)/shard_map/pallas_call | solution.py:562
  70.8 1.5 %collective-permute-done.7.far1b = f32[64,8,256]{2,1,0:T(8,128)S(1)} collective-permute-done((f32[64,8,256]{2,1,0:T(8,128)S(1)}, f32[64,8,256]{2,1,0:T(8,128)S(1)}, u32[]{:S(2)}, u32[]{:S(2)}) %collective-permute-start.7) | collective-permute-done | bytes 524320 | tf_op jit(solution)/shard_map/ppermute | solution.py:22
  72.3 0.0 copy-start.2
  72.3 0.0 copy-start.4
  72.4 0.1 collective-permute-start.10
  72.4 1.3 %collective-permute-done.10 = f32[5,16,256]{2,1,0:T(8,128)S(1)} collective-permute-done((f32[5,16,256]{2,1,0:T(8,128)S(1)}, f32[5,16,256]{2,1,0:T(8,128)S(1)}, u32[]{:S(2)}, u32[]{:S(2)}) %collective-permute-start.10) | collective-permute-done | bytes 81952 | tf_op jit(solution)/shard_map/ppermute | solution.py:22
  73.7 0.0 copy-done.2
  73.7 0.0 copy-done.4
  73.8 8.2 %shard_map.64 = (f32[3,70,16,256]{3,2,1,0:T(8,128)S(1)}, f32[2,70,16,256]{3,2,1,0:T(8,128)S(1)}, f32[2,70,16,256]{3,2,1,0:T(8,128)S(1)}, bf16[2,64,64,256]{3,2,1,0:T(8,128)(2,1)S(1)}, f32[16,128]{1,0:T(8,128)S(1)}) custom-call(f32[76,16,256]{2,1,0:T(8,128)S(1)} %collective-permute-done.4.far3, f32[96,8,256]{2,1,0:T(8,128)S(1)} %collective-permute-done.6.far1.far1a, ...), custom_call_target="tpu_custom_call" | custom-call | tf_op jit(solution)/shard_map/pallas_call | solution.py:584
  82.0 11.2 %collective-permute-done.3.far2 = f32[66,16,256]{2,1,0:T(8,128)S(1)} collective-permute-done((f32[66,16,256]{2,1,0:T(8,128)S(1)}, f32[66,16,256]{2,1,0:T(8,128)S(1)}, u32[]{:S(2)}, u32[]{:S(2)}) %collective-permute-start.3) | collective-permute-done | bytes 1081376 | tf_op jit(solution)/shard_map/ppermute | solution.py:22
  93.2 0.0 copy-start.3
  93.2 6.8 %shard_map.65 = (f32[16,128]{1,0:T(8,128)S(1)}, bf16[2,64,64,256]{3,2,1,0:T(8,128)(2,1)S(1)}) custom-call(f32[66,16,256]{2,1,0:T(8,128)S(1)} %collective-permute-done.3.far2, f32[3,70,16,256]{3,2,1,0:T(8,128)S(1)} %get-tuple-element.34.u0_in, f32[2,70,16,256]{3,2,1,0:T(8,128)S(1)} %get-tuple-element.35.u1_in, ...), custom_call_target="tpu_custom_call" | custom-call | tf_op jit(solution)/shard_map/pallas_call | solution.py:597
  100.0 0.0 collective-permute-start.11
  100.0 1.2 collective-permute-done.11
  101.2 1.5 %collective-permute-start.12 = (f32[16,128]{1,0:T(8,128)S(1)}, f32[16,128]{1,0:T(8,128)S(1)}, u32[]{:S(2)}, u32[]{:S(2)}) collective-permute-start(f32[16,128]{1,0:T(8,128)S(1)} %add.17), channel_id=1, source_target_pairs={{0,2},{2,0},{4,6},{6,4},{8,10},{10,8},{12,14},{14,12},{1,3},{3,1},... | collective-permute-start | bytes 24584 | tf_op jit(solution)/shard_map/ppermute | solution.py:59
  102.7 2.1 %collective-permute-done.12 = f32[16,128]{1,0:T(8,128)S(1)} collective-permute-done((f32[16,128]{1,0:T(8,128)S(1)}, f32[16,128]{1,0:T(8,128)S(1)}, u32[]{:S(2)}, u32[]{:S(2)}) %collective-permute-start.12) | collective-permute-done | bytes 8224 | tf_op jit(solution)/shard_map/ppermute | solution.py:59
  104.8 2.5 %collective-permute-start.13 = (f32[16,128]{1,0:T(8,128)S(1)}, f32[16,128]{1,0:T(8,128)S(1)}, u32[]{:S(2)}, u32[]{:S(2)}) collective-permute-start(f32[16,128]{1,0:T(8,128)S(1)} %add.18), channel_id=1, source_target_pairs={{0,4},{2,6},{4,0},{6,2},{8,12},{10,14},{12,8},{14,10},{1,5},{3,7},... | collective-permute-start | bytes 24584 | tf_op jit(solution)/shard_map/ppermute | solution.py:59
  107.3 1.6 %collective-permute-done.13 = f32[16,128]{1,0:T(8,128)S(1)} collective-permute-done((f32[16,128]{1,0:T(8,128)S(1)}, f32[16,128]{1,0:T(8,128)S(1)}, u32[]{:S(2)}, u32[]{:S(2)}) %collective-permute-start.13) | collective-permute-done | bytes 8224 | tf_op jit(solution)/shard_map/ppermute | solution.py:59
  109.0 3.0 %collective-permute-start.14 = (f32[16,128]{1,0:T(8,128)S(1)}, f32[16,128]{1,0:T(8,128)S(1)}, u32[]{:S(2)}, u32[]{:S(2)}) collective-permute-start(f32[16,128]{1,0:T(8,128)S(1)} %add.19), channel_id=1, source_target_pairs={{0,8},{2,10},{4,12},{6,14},{8,0},{10,2},{12,4},{14,6},{1,9},{3,11}... | collective-permute-start | bytes 24584 | tf_op jit(solution)/shard_map/ppermute | solution.py:59
  112.0 1.6 %collective-permute-done.14 = f32[16,128]{1,0:T(8,128)S(1)} collective-permute-done((f32[16,128]{1,0:T(8,128)S(1)}, f32[16,128]{1,0:T(8,128)S(1)}, u32[]{:S(2)}, u32[]{:S(2)}) %collective-permute-start.14) | collective-permute-done | bytes 8224 | tf_op jit(solution)/shard_map/ppermute | solution.py:59
  113.6 0.0 copy-done.3
  113.6 10.5 %shard_map.66 = (f32[16,2,64,256]{3,2,1,0:T(8,128)}, f32[16,2,64,256]{3,2,1,0:T(8,128)}) custom-call(s32[1]{0:T(128)} %bitcast.odd, f32[16,128]{1,0:T(8,128)S(1)} %add.20.moments, bf16[2,64,64,256]{3,2,1,0:T(8,128)(2,1)S(1)} %get-tuple-element.39.split01, bf16[2,64,64,256]{3,2,1,0:T(8,128)(2,1)S(1)} %get-tuple-element.40.split23, ...), custom_call_target="tpu_custom_call" | custom-call | tf_op jit(solution)/shard_map/pallas_call | solution.py:611
  (14 shorter events, 0.2 us)
Async XLA Ops:
  4.5 35.2 %collective-permute-start.5 = (f32[96,8,256]{2,1,0:T(8,128)}, f32[96,8,256]{2,1,0:T(8,128)S(1)}, u32[]{:S(2)}, u32[]{:S(2)}) collective-permute-start(f32[96,8,256]{2,1,0:T(8,128)} %get-tuple-element.23.mine.mine_a), channel_id=1, source_target_pairs={{0,2},{2,0},{4,6},{6,4},{8,10},{10,8},{12,14},{14,12},{1,3},{3,1},... | collective-permute-start | bytes 2359304 | tf_op jit(solution)/shard_map/ppermute | solution.py:22
  7.5 53.6 %copy-start = (f32[96,8,256]{2,1,0:T(8,128)S(1)}, f32[96,8,256]{2,1,0:T(8,128)}, u32[]{:S(2)}) copy-start(f32[96,8,256]{2,1,0:T(8,128)} %get-tuple-element.23.mine.mine_a) | copy-start | bytes 2359300
  7.5 29.0 %collective-permute-start.1 = (f32[64,8,256]{2,1,0:T(8,128)}, f32[64,8,256]{2,1,0:T(8,128)S(1)}, u32[]{:S(2)}, u32[]{:S(2)}) collective-permute-start(f32[64,8,256]{2,1,0:T(8,128)} %get-tuple-element.24.mine_b), channel_id=1, source_target_pairs={{0,2},{2,0},{4,6},{6,4},{8,10},{10,8},{12,14},{14,12},{1,3},{3,1},... | collective-permute-start | bytes 1572872 | tf_op jit(solution)/shard_map/ppermute | solution.py:22
  9.3 5.4 %collective-permute-start = (f32[2,3,16,256]{3,2,1,0:T(8,128)S(1)}, f32[2,3,16,256]{3,2,1,0:T(8,128)S(1)}, u32[]{:S(2)}, u32[]{:S(2)}) collective-permute-start(f32[2,3,16,256]{3,2,1,0:T(8,128)S(1)} %maximum_select_fusion), channel_id=1, source_target_pairs={{0,1},{1,0},{2,3},{3,2},{4,5},{5,4},{6,7},{7,6},{8,9},{9,8},{10,11... | collective-permute-start | bytes 294920 | tf_op jit(solution)/shard_map/ppermute | solution.py:22
  9.4 37.3 %collective-permute-start.4 = (f32[76,16,256]{2,1,0:T(8,128)}, f32[76,16,256]{2,1,0:T(8,128)S(1)}, u32[]{:S(2)}, u32[]{:S(2)}) collective-permute-start(f32[76,16,256]{2,1,0:T(8,128)} %get-tuple-element.22.ahead), channel_id=1, source_target_pairs={{0,4},{4,8},{6,2},{8,12},{10,6},{14,10},{1,5},{5,9},{7,3},{9,13},{... | collective-permute-start | bytes 3735560 | tf_op jit(solution)/shard_map/ppermute | solution.py:22
  13.3 33.3 %collective-permute-start.8 = (f32[76,16,256]{2,1,0:T(8,128)}, f32[76,16,256]{2,1,0:T(8,128)S(1)}, u32[]{:S(2)}, u32[]{:S(2)}) collective-permute-start(f32[76,16,256]{2,1,0:T(8,128)} %get-tuple-element.25), channel_id=1, source_target_pairs={{4,0},{8,4},{2,6},{12,8},{6,10},{10,14},{5,1},{9,5},{3,7},{13,9},{... | collective-permute-start | bytes 3735560 | tf_op jit(solution)/shard_map/ppermute | solution.py:22
  36.4 1.3 %copy-start.1 = (f32[76,16,256]{2,1,0:T(8,128)S(1)}, f32[76,16,256]{2,1,0:T(8,128)}, u32[]{:S(2)}) copy-start(f32[76,16,256]{2,1,0:T(8,128)} %get-tuple-element.22.ahead) | copy-start | bytes 3735556
  37.8 25.1 %collective-permute-start.2 = (f32[66,16,256]{2,1,0:T(8,128)S(1)}, f32[66,16,256]{2,1,0:T(8,128)S(1)}, u32[]{:S(2)}, u32[]{:S(2)}) collective-permute-start(f32[66,16,256]{2,1,0:T(8,128)S(1)} %shard_map.60), channel_id=1, source_target_pairs={{0,2},{2,0},{4,6},{6,4},{8,10},{10,8},{12,14},{14,12},{1,3},{3,1},... | collective-permute-start | bytes 3244040 | tf_op jit(solution)/shard_map/ppermute | solution.py:22
  39.6 21.5 %collective-permute-start.6 = (f32[96,8,256]{2,1,0:T(8,128)S(1)}, f32[96,8,256]{2,1,0:T(8,128)S(1)}, u32[]{:S(2)}, u32[]{:S(2)}) collective-permute-start(f32[96,8,256]{2,1,0:T(8,128)S(1)} %collective-permute-done.5.near2.near2a), channel_id=1, source_target_pairs={{0,4},{4,8},{6,2},{8,12},{10,6},{14,10},{1,5},{5,9},{7,3},{9,13},{... | collective-permute-start | bytes 2359304 | tf_op jit(solution)/shard_map/ppermute | solution.py:22
  43.2 29.2 %collective-permute-start.7 = (f32[64,8,256]{2,1,0:T(8,128)S(1)}, f32[64,8,256]{2,1,0:T(8,128)S(1)}, u32[]{:S(2)}, u32[]{:S(2)}) collective-permute-start(f32[64,8,256]{2,1,0:T(8,128)S(1)} %collective-permute-done.1.near2.near2b), channel_id=1, source_target_pairs={{0,4},{4,8},{6,2},{8,12},{10,6},{14,10},{1,5},{5,9},{7,3},{9,13},{... | collective-permute-start | bytes 1572872 | tf_op jit(solution)/shard_map/ppermute | solution.py:22
  62.9 30.2 %collective-permute-start.3 = (f32[66,16,256]{2,1,0:T(8,128)S(1)}, f32[66,16,256]{2,1,0:T(8,128)S(1)}, u32[]{:S(2)}, u32[]{:S(2)}) collective-permute-start(f32[66,16,256]{2,1,0:T(8,128)S(1)} %collective-permute-done.2.near1), channel_id=1, source_target_pairs={{0,4},{4,8},{6,2},{8,12},{10,6},{14,10},{1,5},{5,9},{7,3},{9,13},{... | collective-permute-start | bytes 3244040 | tf_op jit(solution)/shard_map/ppermute | solution.py:22
  66.4 1.4 %collective-permute-start.9 = (f32[18,8,256]{2,1,0:T(8,128)S(1)}, f32[18,8,256]{2,1,0:T(8,128)S(1)}, u32[]{:S(2)}, u32[]{:S(2)}) collective-permute-start(f32[18,8,256]{2,1,0:T(8,128)S(1)} %broadcast_select_fusion.2), channel_id=1, source_target_pairs={{0,1},{1,0},{2,3},{3,2},{4,5},{5,4},{6,7},{7,6},{8,9},{9,8},{10,11... | collective-permute-start | bytes 442376 | tf_op jit(solution)/shard_map/ppermute | solution.py:22
  72.3 1.4 %copy-start.2 = (f32[76,16,256]{2,1,0:T(8,128)S(1)}, f32[76,16,256]{2,1,0:T(8,128)}, u32[]{:S(2)}) copy-start(f32[76,16,256]{2,1,0:T(8,128)} %get-tuple-element.22.ahead) | copy-start | bytes 3735556
  72.3 1.4 %copy-start.4 = (f32[64,8,256]{2,1,0:T(8,128)S(1)}, f32[64,8,256]{2,1,0:T(8,128)}, u32[]{:S(2)}) copy-start(f32[64,8,256]{2,1,0:T(8,128)} %get-tuple-element.24.mine_b) | copy-start | bytes 1572868
  72.4 1.3 %collective-permute-start.10 = (f32[5,16,256]{2,1,0:T(8,128)S(1)}, f32[5,16,256]{2,1,0:T(8,128)S(1)}, u32[]{:S(2)}, u32[]{:S(2)}) collective-permute-start(f32[5,16,256]{2,1,0:T(8,128)S(1)} %broadcast_select_fusion.7), channel_id=1, source_target_pairs={{0,1},{1,0},{2,3},{3,2},{4,5},{5,4},{6,7},{7,6},{8,9},{9,8},{10,11... | collective-permute-start | bytes 245768 | tf_op jit(solution)/shard_map/ppermute | solution.py:22
  93.2 20.5 %copy-start.3 = (f32[16,2,64,256]{3,2,1,0:T(8,128)S(1)}, f32[16,2,64,256]{3,2,1,0:T(8,128)}, u32[]{:S(2)}) copy-start(f32[16,2,64,256]{3,2,1,0:T(8,128)} %iterate.1) | copy-start | bytes 6291460
  100.0 1.2 collective-permute-start.11
  101.2 3.7 %collective-permute-start.12 = (f32[16,128]{1,0:T(8,128)S(1)}, f32[16,128]{1,0:T(8,128)S(1)}, u32[]{:S(2)}, u32[]{:S(2)}) collective-permute-start(f32[16,128]{1,0:T(8,128)S(1)} %add.17), channel_id=1, source_target_pairs={{0,2},{2,0},{4,6},{6,4},{8,10},{10,8},{12,14},{14,12},{1,3},{3,1},... | collective-permute-start | bytes 24584 | tf_op jit(solution)/shard_map/ppermute | solution.py:59
  104.8 4.1 %collective-permute-start.13 = (f32[16,128]{1,0:T(8,128)S(1)}, f32[16,128]{1,0:T(8,128)S(1)}, u32[]{:S(2)}, u32[]{:S(2)}) collective-permute-start(f32[16,128]{1,0:T(8,128)S(1)} %add.18), channel_id=1, source_target_pairs={{0,4},{2,6},{4,0},{6,2},{8,12},{10,14},{12,8},{14,10},{1,5},{3,7},... | collective-permute-start | bytes 24584 | tf_op jit(solution)/shard_map/ppermute | solution.py:59
  109.0 4.7 %collective-permute-start.14 = (f32[16,128]{1,0:T(8,128)S(1)}, f32[16,128]{1,0:T(8,128)S(1)}, u32[]{:S(2)}, u32[]{:S(2)}) collective-permute-start(f32[16,128]{1,0:T(8,128)S(1)} %add.19), channel_id=1, source_target_pairs={{0,8},{2,10},{4,12},{6,14},{8,0},{10,2},{12,4},{14,6},{1,9},{3,11}... | collective-permute-start | bytes 24584 | tf_op jit(solution)/shard_map/ppermute | solution.py:59

commit v8 on v7

--- a/solution.py
+++ b/solution.py
@@ -76,10 +76,9 @@
 
 
 def prepare_kernel(
-    odd, residual, labels, boundary, mine_a, mine_b, ahead, back, block, label_cells, boundary_cells, arrived
+    odd, residual, labels, boundary, mine, ahead, first, last, block, label_cells, boundary_cells, arrived
 ):
     rhs, depth, rows, nx = residual.shape
-    half = rhs // 2
     copies = [
         pltpu.make_async_copy(labels, label_cells, arrived.at[0]),
         pltpu.make_async_copy(boundary, boundary_cells, arrived.at[1]),
@@ -93,41 +92,34 @@
         copy.start()
     for copy in copies[:2]:
         copy.wait()
+    count = rows // rhs
     for place in range(depth):
         plane = jnp.bitwise_xor(place, odd[0])
-        for message, order in ((mine_a, (0, 1, 2, 3)), (ahead, (0, 1, None, 2)), (back, (0, 1, 2, None))):
-            size = message.shape[1]
-            count = rows // size
-            for part in range(count):
-                cells = pl.ds(part * size, size)
-                values = (
-                    jnp.exp(label_cells[plane, cells, :].astype(f32) * (contrast_log / (NCLASS - 1))),
-                    (1 - boundary_cells[plane, cells, :]).astype(f32),
-                )
-                for kind, value in enumerate(values):
-                    at = order[2 * kind + place]
-                    if at is not None:
-                        message[rows + at * count + part] = value
-
-    for place in range(depth):
+        for part in range(count):
+            cells = pl.ds(part * rhs, rhs)
+            coef = jnp.exp(label_cells[plane, cells, :].astype(f32) * (contrast_log / (NCLASS - 1)))
+            inner = (1 - boundary_cells[plane, cells, :]).astype(f32)
+            for message in (mine, ahead):
+                message[rows + place * count + part] = coef
+            mine[rows + (2 + place) * count + part] = inner
+            if place == 1:
+                ahead[rows + 2 * count + part] = inner
+
+    for place, out in ((0, mine), (1, ahead)):
         copies[2 + place].wait()
 
-        def turn(group, carry, place=place):
+        def turn(group, carry, place=place, out=out):
             here = pl.ds(group * 8, 8)
-            turned = pltpu.einshape("abc->bac", block[place, :, here, :])
-            if place == 0:
-                mine_a[here] = turned[:, :half]
-                mine_b[here] = turned[:, half:]
-                back[here] = turned
-            else:
-                ahead[here] = turned
+            out[here] = pltpu.einshape("abc->bac", block[place, :, here, :])
             return carry
 
         lax.fori_loop(0, rows // 8, turn, 0)
-
-
-def second_kernel(rows, ahead, own_before, own_behind, near2, out):
-    del near2
+        first[place] = out[:REACH]
+        last[place] = out[rows - REACH : rows]
+
+
+def second_kernel(rows, ahead, own_before, own_behind, near2, far3, out):
+    del near2, far3
 
     def copy_rows(y, size):
         for j in range(size):
@@ -138,39 +130,27 @@
     out[rows + 1] = own_behind[1, 0]
 
 
-def field_edges_kernel(rows, near2, far1, far3, near3, mine, first, last):
+def edges_kernel(rows, near1, near2, far1, far3, near3, mine, first, last):
     messages = {"near2": near2, "far1": far1, "far3": far3, "near3": near3, "mine": mine}
-    place = 0
+    rhs = mine.shape[1]
+    count = rows // rhs
+    for (_, place, number), source in zip(BESIDE, (near1, near2, far1)):
+        first[place : place + number] = source[:number]
+        last[place : place + number] = source[rows - number : rows]
+    place = EDGES
     for name, *parts in FIELDS:
-        message = messages[name]
-        size = message.shape[1]
-        count = rows // size
         for part in parts:
             if part is not None:
                 start = rows + part * count
-                first[place] = message[start, :MARGIN]
-                last[place] = message[start + count - 1, size - MARGIN :]
+                first[place, :MARGIN] = messages[name][start, :MARGIN]
+                last[place, :MARGIN] = messages[name][start + count - 1, rhs - MARGIN :]
                 place += 1
-
-
-def edges_kernel(rows, near1, near2a, near2b, far1a, far1b, inverse, first, last):
-    del inverse
-    half = near2a.shape[1]
-    for (_, place, number), sources in zip(BESIDE, ((near1,), (near2a, near2b), (far1a, far1b))):
-        for index, source in enumerate(sources):
-            part = slice(None) if len(sources) == 1 else slice(index * half, (index + 1) * half)
-            first[place : place + number, part] = source[:number]
-            last[place : place + number, part] = source[rows - number : rows]
-
-
-def couplings_kernel(rows, far3, far1, mine, near2, near3, before, behind, inverse, sx, sy, sz, root, coef, inner, masked):
-    messages = {"near2": near2, "far1": far1, "far3": far3, "near3": near3, "mine": mine}
-    fill_cells(rows, messages, before, behind, coef, inner)
-    make_operator(coef, inner, inverse, sx, sy, sz, root, masked)
+                first[place - 1, MARGIN:] = jnp.zeros_like(first[place - 1, MARGIN:])
+                last[place - 1, MARGIN:] = jnp.zeros_like(last[place - 1, MARGIN:])
 
 
 def fill_cells(rows, messages, before, behind, coef, inner):
-    place = 0
+    place = EDGES
     for plane, (name, *parts) in enumerate(FIELDS):
         for part, out in zip(parts, (coef, inner)):
             if part is None:
@@ -181,8 +161,8 @@
                 out[plane, MARGIN + block * rhs : MARGIN + (block + 1) * rhs] = messages[name][
                     rows + part * count + block
                 ]
-            out[plane, :MARGIN] = before[place]
-            out[plane, MARGIN + rows :] = behind[place]
+            out[plane, :MARGIN] = before[place, :MARGIN]
+            out[plane, MARGIN + rows :] = behind[place, :MARGIN]
             place += 1
 
 
@@ -263,12 +243,12 @@
     return max(REACH - plane, plane - (REACH + depth - 1), 0)
 
 
-def scale_rows(plane, source, first, dst, start, count, inverse, part=slice(None)):
+def scale_rows(plane, source, first, dst, start, count, inverse):
     out, place = dst
 
     def body(j, size):
         for i in range(size):
-            out[place, start + j + i, part] = source[first + j + i] * cell_row(inverse, plane, start + j + i)
+            out[place, start + j + i] = source[first + j + i] * cell_row(inverse, plane, start + j + i)
 
     if count < 8:
         body(0, count)
@@ -305,21 +285,20 @@
 
 
 def early_kernel(
-    rows, far3, far1a, far1b, mine_a, mine_b, ahead, own_before, own_behind, near1, near2a, near2b, near3,
-    before, behind, inverse, sx, sy, sz, u0_out, u1_out, u2_out, split, moments, u0, u1,
+    rows, far3, far1, mine, ahead, own_before, own_behind, near1, near2, near3, before, behind,
+    inverse, sx, sy, sz, root, u0_out, u1_out, u2_out, split, moments, u0, u1, coef, inner, masked,
 ):
+    messages = {"near2": near2, "far1": far1, "far3": far3, "near3": near3, "mine": mine}
+    fill_cells(rows, messages, before, behind, coef, inner)
+    make_operator(coef, inner, inverse, sx, sy, sz, root, masked)
     operator = (sx, sy, sz)
     fields = {(0, plane): (u0_out, index) for index, plane in enumerate((0, 2, 3))}
     fields.update({(0, plane): (u0, plane - 4) for plane in range(4, 8)})
     fields.update({(1, 3): (u1_out, 0), (1, 4): (u1_out, 1), (1, 5): (u1, 0), (1, 6): (u1, 1)})
     fields.update({(2, 4): (u2_out, 0), (2, 5): (u2_out, 1)})
     first, last = REACH, REACH + rows
-    half = mine_a.shape[1]
-    for plane, source in ((0, far3), (4, ahead), (5, near1), (7, near3)):
+    for plane, source in ((0, far3), (2, far1), (3, mine), (4, ahead), (5, near1), (6, near2), (7, near3)):
         scale_rows(plane, source, 0, fields[0, plane], first, rows, inverse)
-    for plane, sources in ((2, (far1a, far1b)), (3, (mine_a, mine_b)), (6, (near2a, near2b))):
-        for source, part in zip(sources, (slice(0, half), slice(half, None))):
-            scale_rows(plane, source, 0, fields[0, plane], first, rows, inverse, part)
     for plane in (3, 4):
         scale_rows(plane, own_before.at[plane - 3], 0, fields[0, plane], 0, REACH, inverse)
         scale_rows(plane, own_behind.at[plane - 3], 0, fields[0, plane], last, REACH, inverse)
@@ -467,10 +446,10 @@
 
 
 def outputs_kernel(odd, moments, split01, split23, inverse, root, iterate, iterate_out, residual_out, coefs):
-    rhs = iterate.shape[0]
-    rows = split01.shape[1]
-
-    @pl.when((pl.program_id(0) == 0) & (pl.program_id(1) == 0))
+    rhs, _, rows, nx = iterate.shape
+    plane, block = pl.program_id(0), pl.program_id(1)
+
+    @pl.when((plane == 0) & (block == 0))
     def _():
         solved, residual = mixing(moments[...], rhs)
         both = jnp.concatenate([solved[:, : 4 * rhs], residual[:, : 4 * rhs]], axis=0)
@@ -479,16 +458,22 @@
         pair01, pair23 = stacked[:, : 2 * rhs], stacked[:, 2 * rhs :]
         coefs[...] = jnp.concatenate([pair01, pair01, pair23, pair23], axis=1).astype(bf16)
 
-    wide = jnp.concatenate(
-        [jnp.concatenate([split01[0, j], split23[0, j]], axis=0) for j in range(rows)], axis=1
-    )
-    mixed = jnp.dot(coefs[...], wide, preferred_element_type=f32)
-    mixed = mixed[: 2 * rhs] + mixed[2 * rhs :]
-    nx = split01.shape[-1]
-    by_row = jnp.stack([mixed[:, j * nx : (j + 1) * nx] for j in range(rows)], axis=0)
-    by_rhs = pltpu.einshape("abc->bac", by_row)
-    iterate_out[:, 0] = iterate[:, 0] + by_rhs[:rhs] * inverse[...]
-    residual_out[:, 0] = by_rhs[rhs:] * root[...]
+    def group_of_rows(group, carry):
+        y = block * rows + group * 8
+        wide = jnp.concatenate(
+            [jnp.concatenate([split01[plane, y + j], split23[plane, y + j]], axis=0) for j in range(8)], axis=1
+        )
+        mixed = jnp.dot(coefs[...], wide, preferred_element_type=f32)
+        mixed = mixed[: 2 * rhs] + mixed[2 * rhs :]
+        by_row = jnp.stack([mixed[:, j * nx : (j + 1) * nx] for j in range(8)], axis=0)
+        by_rhs = pltpu.einshape("abc->bac", by_row)
+        cells = pl.ds(pl.multiple_of(y + MARGIN, 8), 8)
+        here = pl.ds(group * 8, 8)
+        iterate_out[:, 0, here] = iterate[:, 0, here] + by_rhs[:rhs] * inverse[plane + REACH, cells]
+        residual_out[:, 0, here] = by_rhs[rhs:] * root[plane + REACH, cells]
+        return carry
+
+    lax.fori_loop(0, rows // 8, group_of_rows, 0)
 
 
 def on_device(iterate, residual, labels, boundary):
@@ -506,13 +491,11 @@
 
     anywhere = pl.BlockSpec(memory_space=pl.ANY)
 
-    half = rhs // 2
-    wide = rows + 3 * rows // rhs
-    mine_a, mine_b, ahead, back = pl.pallas_call(
+    count = rows // rhs
+    mine, ahead, *edges = pl.pallas_call(
         prepare_kernel,
-        out_shape=(
-            array(rows + 4 * rows // half, half, nx), array(rows, half, nx), array(wide, rhs, nx), array(wide, rhs, nx)
-        ),
+        out_shape=(array(rows + 4 * count, rhs, nx), array(rows + 3 * count, rhs, nx))
+        + (array(depth, REACH, rhs, nx),) * 2,
         in_specs=[smem] + [pl.BlockSpec(memory_space=pltpu.HBM)] * 3,
         out_specs=(vmem,) * 4,
         scratch_shapes=[
@@ -524,75 +507,49 @@
         compiler_params=params(55),
     )(odd, residual, labels, boundary)
 
-    near2a = swapped(mine_a)
+    near2 = swapped(mine)
     far3 = relayed(ahead)
-    near3 = relayed(back, back=True)
-    near2b = swapped(mine_b)
-
-    def both(first, last, second):
-        return jnp.stack([jnp.concatenate([first[second], last[second]], axis=1), ahead[second]])
-
-    own_before, own_behind = rows_beside(
-        both(mine_a, mine_b, slice(0, REACH)), both(mine_a, mine_b, slice(rows - REACH, rows))
-    )
+    near3 = relayed(mine, back=True)
+    own_before, own_behind = rows_beside(*edges)
     near1 = swapped(
         pl.pallas_call(
             partial(second_kernel, rows),
             out_shape=array(rows + 2, rhs, nx),
-            in_specs=[vmem, vmem, vmem, anywhere],
+            in_specs=[vmem, vmem, vmem, anywhere, anywhere],
             out_specs=vmem,
             compiler_params=params(8),
-        )(ahead, own_before, own_behind, near2b)
+        )(ahead, own_before, own_behind, near2, far3)
     )
-    far1a = relayed(near2a)
-    far1b = relayed(near2b)
+    far1 = relayed(near2)
     far2 = relayed(near1)
 
-    number = sum(part is not None for _, *parts in FIELDS for part in parts)
-    fields_before, fields_behind = rows_beside(
-        *pl.pallas_call(
-            partial(field_edges_kernel, rows),
-            out_shape=(array(number, MARGIN, nx),) * 2,
-            in_specs=[vmem] * 5,
-            out_specs=(vmem, vmem),
-            compiler_params=params(8),
-        )(near2a, far1a, far3, near3, mine_a)
-    )
-    cells = (depth + 2 * REACH, rows + 2 * MARGIN, nx)
-    inverse, sx, sy, sz, root = pl.pallas_call(
-        partial(couplings_kernel, rows),
-        out_shape=(array(*cells),) * 5,
-        in_specs=[vmem] * 7,
-        out_specs=(vmem,) * 5,
-        scratch_shapes=[pltpu.VMEM((cells[0] + 2,) + cells[1:], f32)] * 2 + [pltpu.VMEM(cells, f32)],
-        compiler_params=params(14),
-    )(far3, far1a, mine_a, near2a, near3, fields_before, fields_behind)
-
+    edges = EDGES + sum(part is not None for _, *parts in FIELDS for part in parts)
     before, behind = rows_beside(
         *pl.pallas_call(
             partial(edges_kernel, rows),
-            out_shape=(array(EDGES, rhs, nx),) * 2,
-            in_specs=[vmem] * 5 + [anywhere],
+            out_shape=(array(edges, rhs, nx),) * 2,
+            in_specs=[vmem] * 6,
             out_specs=(vmem, vmem),
-            compiler_params=params(8),
-        )(near1, near2a, near2b, far1a, far1b, inverse)
+            compiler_params=params(12),
+        )(near1, near2, far1, far3, near3, mine)
     )
 
     def planes(number):
         return (number, rows + 2 * REACH, rhs, nx)
 
-    u0, u1, u2, split01, moments = pl.pallas_call(
+    cells = (depth + 2 * REACH, rows + 2 * MARGIN, nx)
+    inverse, sx, sy, sz, root, u0, u1, u2, split01, moments = pl.pallas_call(
         partial(early_kernel, rows),
-        out_shape=tuple(array(*planes(number)) for number in (3, 2, 2))
+        out_shape=(array(*cells),) * 5
+        + tuple(array(*planes(number)) for number in (3, 2, 2))
         + (array(depth, rows, 4 * rhs, nx, dtype=bf16), array(rhs, 128)),
-        in_specs=[vmem] * 18,
-        out_specs=(vmem,) * 5,
-        scratch_shapes=[pltpu.VMEM(planes(number), f32) for number in (4, 2)],
+        in_specs=[vmem] * 11,
+        out_specs=(vmem,) * 10,
+        scratch_shapes=[pltpu.VMEM(planes(number), f32) for number in (4, 2)]
+        + [pltpu.VMEM((cells[0] + 2,) + cells[1:], f32)] * 2
+        + [pltpu.VMEM(cells, f32)],
         compiler_params=params(24),
-    )(
-        far3, far1a, far1b, mine_a, mine_b, ahead, own_before, own_behind, near1, near2a, near2b, near3,
-        before, behind, inverse, sx, sy, sz,
-    )
+    )(far3, far1, mine, ahead, own_before, own_behind, near1, near2, near3, before, behind)
 
     moments, split23 = pl.pallas_call(
         partial(late_kernel, rows),
@@ -605,26 +562,19 @@
 
     moments = all_sum(moments, ("gy", "gz"))
 
-    tile = 8
+    tile = math.gcd(rows, 32)
     plane_rows = pl.BlockSpec((rhs, 1, tile, nx), lambda z, y, odd: (0, jnp.bitwise_xor(z, odd[0]), y, 0))
-    cell_rows = pl.BlockSpec((None, tile, nx), lambda z, y, odd: (z + REACH, y + MARGIN // tile, 0))
     return pl.pallas_call(
         outputs_kernel,
         out_shape=(array(*iterate.shape), array(*residual.shape)),
         grid_spec=pltpu.PrefetchScalarGridSpec(
             num_scalar_prefetch=1,
             grid=(depth, rows // tile),
-            in_specs=[
-                pl.BlockSpec((rhs, 128), lambda z, y, odd: (0, 0)),
-                *[pl.BlockSpec((1, tile, 4 * rhs, nx), lambda z, y, odd: (z, y, 0, 0))] * 2,
-                cell_rows,
-                cell_rows,
-                plane_rows,
-            ],
+            in_specs=[vmem] * 5 + [plane_rows],
             out_specs=(plane_rows, plane_rows),
             scratch_shapes=[pltpu.VMEM((4 * rhs, 8 * rhs), bf16)],
         ),
-        compiler_params=params(10),
+        compiler_params=params(16),
     )(odd, moments, split01, split23, inverse, root, iterate)
 
 

time: 125 us -> 119 us (0.952)
  starting transfers between devices: 27.9 us -> 22.9 us
  waiting for transfers between devices: 59.9 us -> 63.5 us
  Pallas kernels: 32.4 us -> 29.2 us
  local copies, waits for them, and re-layouts: 2.99 us -> 1.3 us
    ppermute x11 -> x8, starting transfers between devices: 20.8 us -> 15.3 us  [moved(): return lax.ppermute(block, axis, pairs)]
    ppermute x11 -> x8, waiting for transfers between devices: 53.3 us -> 57.5 us  [moved(): return lax.ppermute(block, axis, pairs)]
    pallas_call x1, Pallas kernels: 10.5 us -> 8.15 us  [on_device(): pl.pallas_call(outputs_kernel, out_shape=(array(*iterate.shape), array(*r...]
    pallas_call x5 -> x3, Pallas kernels: 15 us -> 14.2 us  [the longest x1 10.7 us: on_device(): pl.pallas_call(partial(early_kernel, rows), out_shape=(array(*cells),) *...]
  transfers between devices with their start and end apart: 15 -> 12, of which waited for: 11 -> 8; matrix products, arithmetic and copies ran while one was open for 1% -> 1% of each run, Pallas kernels for 9% -> 9%
where the time goes in v8:
time: 119 us
  waiting for transfers between devices  63.5 us (53%)
  Pallas kernels  29.2 us (25%)
  starting transfers between devices  22.9 us (19%)
  local copies, waits for them, and re-layouts  1.3 us (1%)
    ppermute x8, waiting for transfers between devices, moved(): return lax.ppermute(block, axis, pairs)  57.5 us
    ppermute x8, starting transfers between devices, moved(): return lax.ppermute(block, axis, pairs)  15.3 us
    pallas_call x1, Pallas kernels, on_device(): pl.pallas_call(partial(early_kernel, rows), out_shape=(array(*cells),) *...  10.7 us
    pallas_call x1, Pallas kernels, on_device(): pl.pallas_call(outputs_kernel, out_shape=(array(*iterate.shape), array(*r...  8.15 us
    ppermute x4, starting transfers between devices, all_sum(): lax.ppermute(values, axis, [(i, i ^ step) for i in range(count)])  7.55 us
    pallas_call x1, Pallas kernels, on_device(): pl.pallas_call(partial(late_kernel, rows), out_shape=(array(rhs, 128), ar...  6.8 us
    ppermute x4, waiting for transfers between devices, all_sum(): lax.ppermute(values, axis, [(i, i ^ step) for i in range(count)])  6.04 us
    pallas_call x1, Pallas kernels, on_device(): pl.pallas_call(prepare_kernel, out_shape=(array(rows + 4 * count, rhs, nx...  3.43 us
  transfers between devices with their start and end apart: 12, of which 8 were waited for; matrix products, arithmetic and copies ran while one was open for 1% of the time, Pallas kernels for 9%

profile of v8, /device:TPU:0, one launch (start us, length us, event | category | flops | bytes accessed | tf_op | source)
XLA Modules:
  0.0 118.8 jit_solution(16100686583796309425)
XLA Ops:
  0.6 3.4 %shard_map.59 = (f32[80,16,256]{2,1,0:T(8,128)}, f32[76,16,256]{2,1,0:T(8,128)}, f32[2,3,16,256]{3,2,1,0:T(8,128)}, f32[2,3,16,256]{3,2,1,0:T(8,128)}) custom-call(s32[1]{0:T(128)} %bitcast.odd, f32[16,2,64,256]{3,2,1,0:T(8,128)} %residual.1, s32[2,64,256]{2,1,0:T(8,128)} %labels.1, s32[2,64,256]{2,1,0:T(8,128)} %boundary.1), custom_call_target="tpu_custom_call" | custom-call | tf_op jit(solution)/shard_map/pallas_call | solution.py:495
  4.1 3.0 %collective-permute-start.1 = (f32[80,16,256]{2,1,0:T(8,128)}, f32[80,16,256]{2,1,0:T(8,128)S(1)}, u32[]{:S(2)}, u32[]{:S(2)}) collective-permute-start(f32[80,16,256]{2,1,0:T(8,128)} %get-tuple-element.23.mine), channel_id=1, source_target_pairs={{0,2},{2,0},{4,6},{6,4},{8,10},{10,8},{12,14},{14,12},{1,3},{3,1},... | collective-permute-start | bytes 3932168 | tf_op jit(solution)/shard_map/ppermute | solution.py:22
  7.1 3.5 %collective-permute-start.2 = (f32[76,16,256]{2,1,0:T(8,128)}, f32[76,16,256]{2,1,0:T(8,128)S(1)}, u32[]{:S(2)}, u32[]{:S(2)}) collective-permute-start(f32[76,16,256]{2,1,0:T(8,128)} %get-tuple-element.20.ahead), channel_id=1, source_target_pairs={{0,4},{4,8},{6,2},{8,12},{10,6},{14,10},{1,5},{5,9},{7,3},{9,13},{... | collective-permute-start | bytes 3735560 | tf_op jit(solution)/shard_map/ppermute | solution.py:22
  10.6 0.9 broadcast_select_fusion.5
  11.6 0.1 collective-permute-start
  11.7 1.3 %collective-permute-start.6 = (f32[80,16,256]{2,1,0:T(8,128)}, f32[80,16,256]{2,1,0:T(8,128)S(1)}, u32[]{:S(2)}, u32[]{:S(2)}) collective-permute-start(f32[80,16,256]{2,1,0:T(8,128)} %get-tuple-element.23.mine), channel_id=1, source_target_pairs={{4,0},{8,4},{2,6},{12,8},{6,10},{10,14},{5,1},{9,5},{3,7},{13,9},{... | collective-permute-start | bytes 3932168 | tf_op jit(solution)/shard_map/ppermute | solution.py:22
  12.9 23.1 %collective-permute-done.1.near2 = f32[80,16,256]{2,1,0:T(8,128)S(1)} collective-permute-done((f32[80,16,256]{2,1,0:T(8,128)}, f32[80,16,256]{2,1,0:T(8,128)S(1)}, u32[]{:S(2)}, u32[]{:S(2)}) %collective-permute-start.1) | collective-permute-done | bytes 1310752 | tf_op jit(solution)/shard_map/ppermute | solution.py:22
  36.1 3.8 %collective-permute-start.5 = (f32[80,16,256]{2,1,0:T(8,128)S(1)}, f32[80,16,256]{2,1,0:T(8,128)S(1)}, u32[]{:S(2)}, u32[]{:S(2)}) collective-permute-start(f32[80,16,256]{2,1,0:T(8,128)S(1)} %collective-permute-done.1.near2), channel_id=1, source_target_pairs={{0,4},{4,8},{6,2},{8,12},{10,6},{14,10},{1,5},{5,9},{7,3},{9,13},{... | collective-permute-start | bytes 3932168 | tf_op jit(solution)/shard_map/ppermute | solution.py:22
  39.9 0.0 collective-permute-done
  39.9 0.0 collective-permute-done.2.far3
  39.9 0.0 copy-start.1
  39.9 1.3 %copy-done.1 = f32[76,16,256]{2,1,0:T(8,128)S(1)} copy-done((f32[76,16,256]{2,1,0:T(8,128)S(1)}, f32[76,16,256]{2,1,0:T(8,128)}, u32[]{:S(2)}) %copy-start.1) | copy-done | bytes 1245208
  41.2 0.0 copy-start
  41.2 0.1 shard_map.60
  41.3 0.1 collective-permute-start.3
  41.4 24.4 %collective-permute-done.3.near1 = f32[66,16,256]{2,1,0:T(8,128)S(1)} collective-permute-done((f32[66,16,256]{2,1,0:T(8,128)S(1)}, f32[66,16,256]{2,1,0:T(8,128)S(1)}, u32[]{:S(2)}, u32[]{:S(2)}) %collective-permute-start.3) | collective-permute-done | bytes 1081376 | tf_op jit(solution)/shard_map/ppermute | solution.py:22
  65.8 3.5 %collective-permute-start.4 = (f32[66,16,256]{2,1,0:T(8,128)S(1)}, f32[66,16,256]{2,1,0:T(8,128)S(1)}, u32[]{:S(2)}, u32[]{:S(2)}) collective-permute-start(f32[66,16,256]{2,1,0:T(8,128)S(1)} %collective-permute-done.3.near1), channel_id=1, source_target_pairs={{0,4},{4,8},{6,2},{8,12},{10,6},{14,10},{1,5},{5,9},{7,3},{9,13},{... | collective-permute-start | bytes 3244040 | tf_op jit(solution)/shard_map/ppermute | solution.py:22
  69.3 0.0 collective-permute-done.6.near3
  69.3 0.0 collective-permute-done.5.far1
  69.3 0.0 copy-done
  69.3 0.1 shard_map.61
  69.4 0.0 copy-start.2
  69.4 0.1 broadcast_select_fusion.2
  69.5 0.1 collective-permute-start.7
  69.5 1.7 %collective-permute-done.7 = f32[23,16,256]{2,1,0:T(8,128)S(1)} collective-permute-done((f32[23,16,256]{2,1,0:T(8,128)S(1)}, f32[23,16,256]{2,1,0:T(8,128)S(1)}, u32[]{:S(2)}, u32[]{:S(2)}) %collective-permute-start.7) | collective-permute-done | bytes 376864 | tf_op jit(solution)/shard_map/ppermute | solution.py:22
  71.2 0.1 broadcast_select_fusion
  71.3 0.0 copy-done.2
  71.3 10.7 %shard_map.62 = (f32[8,80,256]{2,1,0:T(8,128)S(1)}, f32[8,80,256]{2,1,0:T(8,128)S(1)}, f32[8,80,256]{2,1,0:T(8,128)S(1)}, f32[8,80,256]{2,1,0:T(8,128)S(1)}, f32...) custom-call(f32[76,16,256]{2,1,0:T(8,128)S(1)} %collective-permute-d, ...), custom_call_target="tpu_custom_call" | custom-call | tf_op jit(solution)/shard_map/pallas_call | solution.py:541
  82.1 8.2 %collective-permute-done.4.far2 = f32[66,16,256]{2,1,0:T(8,128)S(1)} collective-permute-done((f32[66,16,256]{2,1,0:T(8,128)S(1)}, f32[66,16,256]{2,1,0:T(8,128)S(1)}, u32[]{:S(2)}, u32[]{:S(2)}) %collective-permute-start.4) | collective-permute-done | bytes 1081376 | tf_op jit(solution)/shard_map/ppermute | solution.py:22
  90.3 0.0 copy-start.3
  90.3 6.8 %shard_map.63 = (f32[16,128]{1,0:T(8,128)S(1)}, bf16[2,64,64,256]{3,2,1,0:T(8,128)(2,1)S(1)}) custom-call(f32[66,16,256]{2,1,0:T(8,128)S(1)} %collective-permute-done.4.far2, f32[3,70,16,256]{3,2,1,0:T(8,128)S(1)} %get-tuple-element.26.u0_in, f32[2,70,16,256]{3,2,1,0:T(8,128)S(1)} %get-tuple-element.27.u1_in, ...), custom_call_target="tpu_custom_call" | custom-call | tf_op jit(solution)/shard_map/pallas_call | solution.py:554
  97.1 0.0 collective-permute-start.8
  97.1 1.2 collective-permute-done.8
  98.2 2.3 %collective-permute-start.9 = (f32[16,128]{1,0:T(8,128)S(1)}, f32[16,128]{1,0:T(8,128)S(1)}, u32[]{:S(2)}, u32[]{:S(2)}) collective-permute-start(f32[16,128]{1,0:T(8,128)S(1)} %add.17), channel_id=1, source_target_pairs={{0,2},{2,0},{4,6},{6,4},{8,10},{10,8},{12,14},{14,12},{1,3},{3,1},... | collective-permute-start | bytes 24584 | tf_op jit(solution)/shard_map/ppermute | solution.py:59
  100.5 1.6 %collective-permute-done.9 = f32[16,128]{1,0:T(8,128)S(1)} collective-permute-done((f32[16,128]{1,0:T(8,128)S(1)}, f32[16,128]{1,0:T(8,128)S(1)}, u32[]{:S(2)}, u32[]{:S(2)}) %collective-permute-start.9) | collective-permute-done | bytes 8224 | tf_op jit(solution)/shard_map/ppermute | solution.py:59
  102.1 2.2 %collective-permute-start.10 = (f32[16,128]{1,0:T(8,128)S(1)}, f32[16,128]{1,0:T(8,128)S(1)}, u32[]{:S(2)}, u32[]{:S(2)}) collective-permute-start(f32[16,128]{1,0:T(8,128)S(1)} %add.18), channel_id=1, source_target_pairs={{0,4},{2,6},{4,0},{6,2},{8,12},{10,14},{12,8},{14,10},{1,5},{3,7},... | collective-permute-start | bytes 24584 | tf_op jit(solution)/shard_map/ppermute | solution.py:59
  104.4 1.6 %collective-permute-done.10 = f32[16,128]{1,0:T(8,128)S(1)} collective-permute-done((f32[16,128]{1,0:T(8,128)S(1)}, f32[16,128]{1,0:T(8,128)S(1)}, u32[]{:S(2)}, u32[]{:S(2)}) %collective-permute-start.10) | collective-permute-done | bytes 8224 | tf_op jit(solution)/shard_map/ppermute | solution.py:59
  106.0 3.0 %collective-permute-start.11 = (f32[16,128]{1,0:T(8,128)S(1)}, f32[16,128]{1,0:T(8,128)S(1)}, u32[]{:S(2)}, u32[]{:S(2)}) collective-permute-start(f32[16,128]{1,0:T(8,128)S(1)} %add.19), channel_id=1, source_target_pairs={{0,8},{2,10},{4,12},{6,14},{8,0},{10,2},{12,4},{14,6},{1,9},{3,11}... | collective-permute-start | bytes 24584 | tf_op jit(solution)/shard_map/ppermute | solution.py:59
  109.0 1.6 %collective-permute-done.11 = f32[16,128]{1,0:T(8,128)S(1)} collective-permute-done((f32[16,128]{1,0:T(8,128)S(1)}, f32[16,128]{1,0:T(8,128)S(1)}, u32[]{:S(2)}, u32[]{:S(2)}) %collective-permute-start.11) | collective-permute-done | bytes 8224 | tf_op jit(solution)/shard_map/ppermute | solution.py:59
  110.7 0.0 copy-done.3
  110.7 8.1 %shard_map.64 = (f32[16,2,64,256]{3,2,1,0:T(8,128)}, f32[16,2,64,256]{3,2,1,0:T(8,128)}) custom-call(s32[1]{0:T(128)} %bitcast.odd, f32[16,128]{1,0:T(8,128)S(1)} %add.20.moments, bf16[2,64,64,256]{3,2,1,0:T(8,128)(2,1)S(1)} %get-tuple-element.35.split01, bf16[2,64,64,256]{3,2,1,0:T(8,128)(2,1)S(1)} %get-tuple-element.36.split23, ...), custom_call_target="tpu_custom_call" | custom-call | tf_op jit(solution)/shard_map/pallas_call | solution.py:567
  (5 shorter events, 0.0 us)
Async XLA Ops:
  4.1 32.0 %collective-permute-start.1 = (f32[80,16,256]{2,1,0:T(8,128)}, f32[80,16,256]{2,1,0:T(8,128)S(1)}, u32[]{:S(2)}, u32[]{:S(2)}) collective-permute-start(f32[80,16,256]{2,1,0:T(8,128)} %get-tuple-element.23.mine), channel_id=1, source_target_pairs={{0,2},{2,0},{4,6},{6,4},{8,10},{10,8},{12,14},{14,12},{1,3},{3,1},... | collective-permute-start | bytes 3932168 | tf_op jit(solution)/shard_map/ppermute | solution.py:22
  7.1 32.8 %collective-permute-start.2 = (f32[76,16,256]{2,1,0:T(8,128)}, f32[76,16,256]{2,1,0:T(8,128)S(1)}, u32[]{:S(2)}, u32[]{:S(2)}) collective-permute-start(f32[76,16,256]{2,1,0:T(8,128)} %get-tuple-element.20.ahead), channel_id=1, source_target_pairs={{0,4},{4,8},{6,2},{8,12},{10,6},{14,10},{1,5},{5,9},{7,3},{9,13},{... | collective-permute-start | bytes 3735560 | tf_op jit(solution)/shard_map/ppermute | solution.py:22
  11.6 28.3 %collective-permute-start = (f32[2,3,16,256]{3,2,1,0:T(8,128)S(1)}, f32[2,3,16,256]{3,2,1,0:T(8,128)S(1)}, u32[]{:S(2)}, u32[]{:S(2)}) collective-permute-start(f32[2,3,16,256]{3,2,1,0:T(8,128)S(1)} %broadcast_select_fusion.5), channel_id=1, source_target_pairs={{0,1},{1,0},{2,3},{3,2},{4,5},{5,4},{6,7},{7,6},{8,9},{9,8},{10,11... | collective-permute-start | bytes 294920 | tf_op jit(solution)/shard_map/ppermute | solution.py:22
  11.7 57.6 %collective-permute-start.6 = (f32[80,16,256]{2,1,0:T(8,128)}, f32[80,16,256]{2,1,0:T(8,128)S(1)}, u32[]{:S(2)}, u32[]{:S(2)}) collective-permute-start(f32[80,16,256]{2,1,0:T(8,128)} %get-tuple-element.23.mine), channel_id=1, source_target_pairs={{4,0},{8,4},{2,6},{12,8},{6,10},{10,14},{5,1},{9,5},{3,7},{13,9},{... | collective-permute-start | bytes 3932168 | tf_op jit(solution)/shard_map/ppermute | solution.py:22
  36.1 33.2 %collective-permute-start.5 = (f32[80,16,256]{2,1,0:T(8,128)S(1)}, f32[80,16,256]{2,1,0:T(8,128)S(1)}, u32[]{:S(2)}, u32[]{:S(2)}) collective-permute-start(f32[80,16,256]{2,1,0:T(8,128)S(1)} %collective-permute-done.1.near2), channel_id=1, source_target_pairs={{0,4},{4,8},{6,2},{8,12},{10,6},{14,10},{1,5},{5,9},{7,3},{9,13},{... | collective-permute-start | bytes 3932168 | tf_op jit(solution)/shard_map/ppermute | solution.py:22
  39.9 1.3 %copy-start.1 = (f32[76,16,256]{2,1,0:T(8,128)S(1)}, f32[76,16,256]{2,1,0:T(8,128)}, u32[]{:S(2)}) copy-start(f32[76,16,256]{2,1,0:T(8,128)} %get-tuple-element.20.ahead) | copy-start | bytes 3735556
  41.2 28.1 %copy-start = (f32[80,16,256]{2,1,0:T(8,128)S(1)}, f32[80,16,256]{2,1,0:T(8,128)}, u32[]{:S(2)}) copy-start(f32[80,16,256]{2,1,0:T(8,128)} %get-tuple-element.23.mine) | copy-start | bytes 3932164
  41.3 24.5 %collective-permute-start.3 = (f32[66,16,256]{2,1,0:T(8,128)S(1)}, f32[66,16,256]{2,1,0:T(8,128)S(1)}, u32[]{:S(2)}, u32[]{:S(2)}) collective-permute-start(f32[66,16,256]{2,1,0:T(8,128)S(1)} %shard_map.60), channel_id=1, source_target_pairs={{0,2},{2,0},{4,6},{6,4},{8,10},{10,8},{12,14},{14,12},{1,3},{3,1},... | collective-permute-start | bytes 3244040 | tf_op jit(solution)/shard_map/ppermute | solution.py:22
  65.8 24.4 %collective-permute-start.4 = (f32[66,16,256]{2,1,0:T(8,128)S(1)}, f32[66,16,256]{2,1,0:T(8,128)S(1)}, u32[]{:S(2)}, u32[]{:S(2)}) collective-permute-start(f32[66,16,256]{2,1,0:T(8,128)S(1)} %collective-permute-done.3.near1), channel_id=1, source_target_pairs={{0,4},{4,8},{6,2},{8,12},{10,6},{14,10},{1,5},{5,9},{7,3},{9,13},{... | collective-permute-start | bytes 3244040 | tf_op jit(solution)/shard_map/ppermute | solution.py:22
  69.4 1.9 %copy-start.2 = (f32[76,16,256]{2,1,0:T(8,128)S(1)}, f32[76,16,256]{2,1,0:T(8,128)}, u32[]{:S(2)}) copy-start(f32[76,16,256]{2,1,0:T(8,128)} %get-tuple-element.20.ahead) | copy-start | bytes 3735556
  69.5 1.8 %collective-permute-start.7 = (f32[23,16,256]{2,1,0:T(8,128)S(1)}, f32[23,16,256]{2,1,0:T(8,128)S(1)}, u32[]{:S(2)}, u32[]{:S(2)}) collective-permute-start(f32[23,16,256]{2,1,0:T(8,128)S(1)} %broadcast_select_fusion.2), channel_id=1, source_target_pairs={{0,1},{1,0},{2,3},{3,2},{4,5},{5,4},{6,7},{7,6},{8,9},{9,8},{10,11... | collective-permute-start | bytes 1130504 | tf_op jit(solution)/shard_map/ppermute | solution.py:22
  90.3 20.4 %copy-start.3 = (f32[16,2,64,256]{3,2,1,0:T(8,128)S(1)}, f32[16,2,64,256]{3,2,1,0:T(8,128)}, u32[]{:S(2)}) copy-start(f32[16,2,64,256]{3,2,1,0:T(8,128)} %iterate.1) | copy-start | bytes 6291460
  97.1 1.2 collective-permute-start.8
  98.2 3.9 %collective-permute-start.9 = (f32[16,128]{1,0:T(8,128)S(1)}, f32[16,128]{1,0:T(8,128)S(1)}, u32[]{:S(2)}, u32[]{:S(2)}) collective-permute-start(f32[16,128]{1,0:T(8,128)S(1)} %add.17), channel_id=1, source_target_pairs={{0,2},{2,0},{4,6},{6,4},{8,10},{10,8},{12,14},{14,12},{1,3},{3,1},... | collective-permute-start | bytes 24584 | tf_op jit(solution)/shard_map/ppermute | solution.py:59
  102.1 3.9 %collective-permute-start.10 = (f32[16,128]{1,0:T(8,128)S(1)}, f32[16,128]{1,0:T(8,128)S(1)}, u32[]{:S(2)}, u32[]{:S(2)}) collective-permute-start(f32[16,128]{1,0:T(8,128)S(1)} %add.18), channel_id=1, source_target_pairs={{0,4},{2,6},{4,0},{6,2},{8,12},{10,14},{12,8},{14,10},{1,5},{3,7},... | collective-permute-start | bytes 24584 | tf_op jit(solution)/shard_map/ppermute | solution.py:59
  106.0 4.7 %collective-permute-start.11 = (f32[16,128]{1,0:T(8,128)S(1)}, f32[16,128]{1,0:T(8,128)S(1)}, u32[]{:S(2)}, u32[]{:S(2)}) collective-permute-start(f32[16,128]{1,0:T(8,128)S(1)} %add.19), channel_id=1, source_target_pairs={{0,8},{2,10},{4,12},{6,14},{8,0},{10,2},{12,4},{14,6},{1,9},{3,11}... | collective-permute-start | bytes 24584 | tf_op jit(solution)/shard_map/ppermute | solution.py:59

commit v9 on v8

--- a/solution.py
+++ b/solution.py
@@ -54,10 +54,16 @@
         if count & (count - 1):
             values = lax.psum(values, axis)
             continue
-        step = 1
-        while step < count:
-            values = values + lax.ppermute(values, axis, [(i, i ^ step) for i in range(count)])
-            step *= 2
+        bits = count.bit_length() - 1
+        done = 0
+        while done < bits:
+            taken = 1 if (bits - done) % 2 else 2
+            others = [
+                lax.ppermute(values, axis, [(i, i ^ (step << done)) for i in range(count)])
+                for step in range(1, 1 << taken)
+            ]
+            values = sum(others, values)
+            done += taken
     return values
 
 
@@ -69,14 +75,15 @@
 BESIDE = ((5, 0, 2), (6, 2, 1), (2, 3, 2))
 EDGES = 5
 FIELDS = (
-    ("far3", 0, None), ("far3", 1, 2), ("far1", 1, 3), ("far1", 0, 2), ("mine", 0, 2),
-    ("mine", 1, 3), ("near2", 1, 3), ("near2", 0, 2), ("near3", 0, 2), ("near3", 1, None),
+    ("far3", 0, None), ("far3", 1, 2), ("beyond", 1, 3), ("beyond", 0, 2), ("own", 0, 2),
+    ("own", 1, 3), ("pair", 1, 3), ("pair", 0, 2), ("near3", 0, 2), ("near3", 1, None),
 )
+BEHIND_ROWS = ("far3", "near3")
 MARGIN = 8
 
 
 def prepare_kernel(
-    odd, residual, labels, boundary, mine, ahead, first, last, block, label_cells, boundary_cells, arrived
+    odd, residual, labels, boundary, mine, ahead, back, cells, first, last, block, label_cells, boundary_cells, arrived
 ):
     rhs, depth, rows, nx = residual.shape
     copies = [
@@ -96,74 +103,83 @@
     for place in range(depth):
         plane = jnp.bitwise_xor(place, odd[0])
         for part in range(count):
-            cells = pl.ds(part * rhs, rhs)
-            coef = jnp.exp(label_cells[plane, cells, :].astype(f32) * (contrast_log / (NCLASS - 1)))
-            inner = (1 - boundary_cells[plane, cells, :]).astype(f32)
-            for message in (mine, ahead):
+            here = pl.ds(part * rhs, rhs)
+            coef = jnp.exp(label_cells[plane, here, :].astype(f32) * (contrast_log / (NCLASS - 1)))
+            inner = (1 - boundary_cells[plane, here, :]).astype(f32)
+            cells[place * count + part] = coef
+            cells[(2 + place) * count + part] = inner
+            for message in (ahead, back):
                 message[rows + place * count + part] = coef
-            mine[rows + (2 + place) * count + part] = inner
-            if place == 1:
-                ahead[rows + 2 * count + part] = inner
-
-    for place, out in ((0, mine), (1, ahead)):
+            (back, ahead)[place][rows + 2 * count + part] = inner
+
+    for place, outs in ((0, (mine, back)), (1, (ahead,))):
         copies[2 + place].wait()
 
-        def turn(group, carry, place=place, out=out):
+        def turn(group, carry, place=place, outs=outs):
             here = pl.ds(group * 8, 8)
-            out[here] = pltpu.einshape("abc->bac", block[place, :, here, :])
+            turned = pltpu.einshape("abc->bac", block[place, :, here, :])
+            for out in outs:
+                out[here] = turned
             return carry
 
         lax.fori_loop(0, rows // 8, turn, 0)
-        first[place] = out[:REACH]
-        last[place] = out[rows - REACH : rows]
-
-
-def second_kernel(rows, ahead, own_before, own_behind, near2, far3, out):
-    del near2, far3
-
-    def copy_rows(y, size):
+        first[place] = outs[0][:REACH]
+        last[place] = outs[0][rows - REACH : rows]
+
+
+def copy_rows(source, first, out, start, count):
+    def body(y, size):
         for j in range(size):
-            out[y + j] = ahead[y + j]
-
-    row_blocks(0, rows, copy_rows, 16)
-    out[rows] = own_before[1, REACH - 1]
-    out[rows + 1] = own_behind[1, 0]
-
-
-def edges_kernel(rows, near1, near2, far1, far3, near3, mine, first, last):
-    messages = {"near2": near2, "far1": far1, "far3": far3, "near3": near3, "mine": mine}
-    rhs = mine.shape[1]
-    count = rows // rhs
-    for (_, place, number), source in zip(BESIDE, (near1, near2, far1)):
-        first[place : place + number] = source[:number]
-        last[place : place + number] = source[rows - number : rows]
-    place = EDGES
-    for name, *parts in FIELDS:
-        for part in parts:
+            out[start + y + j] = source[first + y + j]
+
+    row_blocks(0, count, body, 16)
+
+
+def second_kernel(rows, ahead, own_before, own_behind, near2, out_a, out_b):
+    del near2
+    middle = rows // 2
+    out_a[0] = own_before[1, REACH - 1]
+    copy_rows(ahead, 0, out_a, 1, middle)
+    copy_rows(ahead, middle, out_b, 0, rows - middle)
+    out_b[rows - middle] = own_behind[1, 0]
+
+
+def field_blocks(rows, messages):
+    for plane, (name, *parts) in enumerate(FIELDS):
+        count = rows // messages[name].shape[1]
+        for kind, part in enumerate(parts):
             if part is not None:
-                start = rows + part * count
-                first[place, :MARGIN] = messages[name][start, :MARGIN]
-                last[place, :MARGIN] = messages[name][start + count - 1, rhs - MARGIN :]
-                place += 1
-                first[place - 1, MARGIN:] = jnp.zeros_like(first[place - 1, MARGIN:])
-                last[place - 1, MARGIN:] = jnp.zeros_like(last[place - 1, MARGIN:])
-
-
-def fill_cells(rows, messages, before, behind, coef, inner):
-    place = EDGES
-    for plane, (name, *parts) in enumerate(FIELDS):
-        for part, out in zip(parts, (coef, inner)):
-            if part is None:
-                continue
-            rhs = messages[name].shape[1]
-            count = rows // rhs
-            for block in range(count):
-                out[plane, MARGIN + block * rhs : MARGIN + (block + 1) * rhs] = messages[name][
-                    rows + part * count + block
-                ]
-            out[plane, :MARGIN] = before[place, :MARGIN]
-            out[plane, MARGIN + rows :] = behind[place, :MARGIN]
-            place += 1
+                yield plane, kind, messages[name], part * count + (rows if name in BEHIND_ROWS else 0), count
+
+
+def field_edges_kernel(rows, far3, beyond, own, pair, near3, first, last):
+    messages = {"far3": far3, "beyond": beyond, "own": own, "pair": pair, "near3": near3}
+    for place, (_, _, message, start, count) in enumerate(field_blocks(rows, messages)):
+        first[place] = message[start, :MARGIN]
+        last[place] = message[start + count - 1, message.shape[1] - MARGIN :]
+
+
+def edges_kernel(rows, near1a, near1b, near2, far1, inverse, first, last):
+    del inverse
+    for (_, place, number), (head, start), (tail, stop) in zip(
+        BESIDE, ((near1a, 1), (near2, 0), (far1, 0)), ((near1b, rows // 2), (near2, rows), (far1, rows))
+    ):
+        first[place : place + number] = head[start : start + number]
+        last[place : place + number] = tail[stop - number : stop]
+
+
+def couplings_kernel(
+    rows, far3, beyond, own, pair, near3, before, behind, inverse, sx, sy, sz, root, coef, inner, masked
+):
+    messages = {"far3": far3, "beyond": beyond, "own": own, "pair": pair, "near3": near3}
+    for place, (plane, kind, message, start, count) in enumerate(field_blocks(rows, messages)):
+        out = (coef, inner)[kind]
+        size = message.shape[1]
+        for block in range(count):
+            out[plane, MARGIN + block * size : MARGIN + (block + 1) * size] = message[start + block]
+        out[plane, :MARGIN] = before[place]
+        out[plane, MARGIN + rows :] = behind[place]
+    make_operator(coef, inner, inverse, sx, sy, sz, root, masked)
 
 
 def make_operator(coef, inner, inverse, sx, sy, sz, root, masked):
@@ -285,20 +301,21 @@
 
 
 def early_kernel(
-    rows, far3, far1, mine, ahead, own_before, own_behind, near1, near2, near3, before, behind,
-    inverse, sx, sy, sz, root, u0_out, u1_out, u2_out, split, moments, u0, u1, coef, inner, masked,
+    rows, far3, far1, mine, ahead, own_before, own_behind, near1a, near1b, near2, near3, before, behind,
+    inverse, sx, sy, sz,
+    u0_out, u1_out, u2_out, split, moments, u0, u1,
 ):
-    messages = {"near2": near2, "far1": far1, "far3": far3, "near3": near3, "mine": mine}
-    fill_cells(rows, messages, before, behind, coef, inner)
-    make_operator(coef, inner, inverse, sx, sy, sz, root, masked)
     operator = (sx, sy, sz)
     fields = {(0, plane): (u0_out, index) for index, plane in enumerate((0, 2, 3))}
     fields.update({(0, plane): (u0, plane - 4) for plane in range(4, 8)})
     fields.update({(1, 3): (u1_out, 0), (1, 4): (u1_out, 1), (1, 5): (u1, 0), (1, 6): (u1, 1)})
     fields.update({(2, 4): (u2_out, 0), (2, 5): (u2_out, 1)})
     first, last = REACH, REACH + rows
-    for plane, source in ((0, far3), (2, far1), (3, mine), (4, ahead), (5, near1), (6, near2), (7, near3)):
+    for plane, source in ((0, far3), (2, far1), (3, mine), (4, ahead), (6, near2), (7, near3)):
         scale_rows(plane, source, 0, fields[0, plane], first, rows, inverse)
+    middle = rows // 2
+    scale_rows(5, near1a, 1, fields[0, 5], first, middle, inverse)
+    scale_rows(5, near1b, 0, fields[0, 5], first + middle, rows - middle, inverse)
     for plane in (3, 4):
         scale_rows(plane, own_before.at[plane - 3], 0, fields[0, plane], 0, REACH, inverse)
         scale_rows(plane, own_behind.at[plane - 3], 0, fields[0, plane], last, REACH, inverse)
@@ -332,7 +349,7 @@
 
 
 def late_kernel(
-    rows, far2, u0_in, u1_in, u2_in, moments_in, inverse, sx, sy, sz, moments, split, u0, u1, u2
+    rows, far2a, far2b, u0_in, u1_in, u2_in, moments_in, inverse, sx, sy, sz, moments, split, u0, u1, u2
 ):
     operator = (sx, sy, sz)
     fields = {(0, plane): (u0_in, index) for index, plane in enumerate((0, 2, 3))}
@@ -340,8 +357,8 @@
     fields.update({(1, 1): (u1, 0), (1, 2): (u1, 1), (1, 3): (u1_in, 0), (1, 4): (u1_in, 1)})
     fields.update({(2, 2): (u2, 0), (2, 3): (u2, 1), (2, 4): (u2_in, 0), (2, 5): (u2_in, 1)})
     first, last = REACH, REACH + rows
-    for place, start, count in ((0, first, rows), (rows, first - 1, 1), (rows + 1, last, 1)):
-        scale_rows(LATE, far2, place, fields[0, LATE], start, count, inverse)
+    scale_rows(LATE, far2a, 0, fields[0, LATE], first - 1, far2a.shape[0], inverse)
+    scale_rows(LATE, far2b, 0, fields[0, LATE], last + 1 - far2b.shape[0], far2b.shape[0], inverse)
     for power, plane in ((1, 1), (1, 2), (2, 2), (2, 3)):
         apply_plane(rows, power, plane, operator, fields)
 
@@ -492,12 +509,15 @@
     anywhere = pl.BlockSpec(memory_space=pl.ANY)
 
     count = rows // rhs
-    mine, ahead, *edges = pl.pallas_call(
+    hbm = pl.BlockSpec(memory_space=pltpu.HBM)
+    mine, ahead, back, cells, *edges = pl.pallas_call(
         prepare_kernel,
-        out_shape=(array(rows + 4 * count, rhs, nx), array(rows + 3 * count, rhs, nx))
+        out_shape=(array(rows, rhs, nx),)
+        + (array(rows + 3 * count, rhs, nx),) * 2
+        + (array(4 * count, rhs, nx),)
         + (array(depth, REACH, rhs, nx),) * 2,
-        in_specs=[smem] + [pl.BlockSpec(memory_space=pltpu.HBM)] * 3,
-        out_specs=(vmem,) * 4,
+        in_specs=[smem, hbm, hbm, hbm],
+        out_specs=(vmem,) * 6,
         scratch_shapes=[
             pltpu.VMEM((depth, rhs, rows, nx), f32),
             pltpu.VMEM(labels.shape, jnp.int32),
@@ -509,56 +529,76 @@
 
     near2 = swapped(mine)
     far3 = relayed(ahead)
-    near3 = relayed(mine, back=True)
+    near3 = relayed(back, back=True)
     own_before, own_behind = rows_beside(*edges)
-    near1 = swapped(
-        pl.pallas_call(
-            partial(second_kernel, rows),
-            out_shape=array(rows + 2, rhs, nx),
-            in_specs=[vmem, vmem, vmem, anywhere, anywhere],
-            out_specs=vmem,
+    second = pl.pallas_call(
+        partial(second_kernel, rows),
+        out_shape=(array(rows // 2 + 1, rhs, nx), array(rows - rows // 2 + 1, rhs, nx)),
+        in_specs=[vmem] * 3 + [anywhere],
+        out_specs=(vmem,) * 2,
+        compiler_params=params(8),
+    )(ahead, own_before, own_behind, near2)
+    near1a, near1b = [swapped(message) for message in second]
+    pair = swapped(cells)
+    far1 = relayed(near2)
+    beyond = relayed(pair)
+    far2a, far2b = relayed(near1a), relayed(near1b)
+
+    number = sum(part is not None for _, *parts in FIELDS for part in parts)
+    fields = (far3, beyond, cells, pair, near3)
+    fields_beside = rows_beside(
+        *pl.pallas_call(
+            partial(field_edges_kernel, rows),
+            out_shape=(array(number, MARGIN, nx),) * 2,
+            in_specs=[vmem] * 5,
+            out_specs=(vmem, vmem),
             compiler_params=params(8),
-        )(ahead, own_before, own_behind, near2, far3)
+        )(*fields)
     )
-    far1 = relayed(near2)
-    far2 = relayed(near1)
-
-    edges = EDGES + sum(part is not None for _, *parts in FIELDS for part in parts)
+    grid = (depth + 2 * REACH, rows + 2 * MARGIN, nx)
+    inverse, sx, sy, sz, root = pl.pallas_call(
+        partial(couplings_kernel, rows),
+        out_shape=(array(*grid),) * 5,
+        in_specs=[vmem] * 7,
+        out_specs=(vmem,) * 5,
+        scratch_shapes=[pltpu.VMEM((grid[0] + 2,) + grid[1:], f32)] * 2 + [pltpu.VMEM(grid, f32)],
+        compiler_params=params(14),
+    )(*fields, *fields_beside)
+
     before, behind = rows_beside(
         *pl.pallas_call(
             partial(edges_kernel, rows),
-            out_shape=(array(edges, rhs, nx),) * 2,
-            in_specs=[vmem] * 6,
+            out_shape=(array(EDGES, rhs, nx),) * 2,
+            in_specs=[vmem] * 4 + [anywhere],
             out_specs=(vmem, vmem),
-            compiler_params=params(12),
-        )(near1, near2, far1, far3, near3, mine)
+            compiler_params=params(8),
+        )(near1a, near1b, near2, far1, inverse)
     )
 
     def planes(number):
         return (number, rows + 2 * REACH, rhs, nx)
 
-    cells = (depth + 2 * REACH, rows + 2 * MARGIN, nx)
-    inverse, sx, sy, sz, root, u0, u1, u2, split01, moments = pl.pallas_call(
+    u0, u1, u2, split01, moments = pl.pallas_call(
         partial(early_kernel, rows),
-        out_shape=(array(*cells),) * 5
-        + tuple(array(*planes(number)) for number in (3, 2, 2))
+        out_shape=tuple(array(*planes(number)) for number in (3, 2, 2))
         + (array(depth, rows, 4 * rhs, nx, dtype=bf16), array(rhs, 128)),
-        in_specs=[vmem] * 11,
-        out_specs=(vmem,) * 10,
-        scratch_shapes=[pltpu.VMEM(planes(number), f32) for number in (4, 2)]
-        + [pltpu.VMEM((cells[0] + 2,) + cells[1:], f32)] * 2
-        + [pltpu.VMEM(cells, f32)],
+        in_specs=[vmem] * 16,
+        out_specs=(vmem,) * 5,
+        scratch_shapes=[pltpu.VMEM(planes(number), f32) for number in (4, 2)],
         compiler_params=params(24),
-    )(far3, far1, mine, ahead, own_before, own_behind, near1, near2, near3, before, behind)
+    )(
+        far3, far1, mine, ahead, own_before, own_behind, near1a, near1b, near2, near3, before, behind,
+        inverse, sx, sy, sz,
+    )
 
     moments, split23 = pl.pallas_call(
         partial(late_kernel, rows),
         out_shape=(array(rhs, 128), array(depth, rows, 4 * rhs, nx, dtype=bf16)),
-        in_specs=[vmem] * 9,
+        in_specs=[vmem] * 10,
         out_specs=(vmem, vmem),
         scratch_shapes=[pltpu.VMEM(planes(number), f32) for number in (1, 2, 2)],
         compiler_params=params(20),
-    )(far2, u0, u1, u2, moments, inverse, sx, sy, sz)
+    )(far2a, far2b, u0, u1, u2, moments, inverse, sx, sy, sz)
 
     moments = all_sum(moments, ("gy", "gz"))
 

time: 119 us -> 130 us (1.092)
  starting transfers between devices: 22.9 us -> 33.1 us
  Pallas kernels: 29.2 us -> 31.5 us
  waiting for transfers between devices: 63.5 us -> 62.1 us
    ppermute x8 -> x13, starting transfers between devices: 15.3 us -> 26.1 us  [moved(): return lax.ppermute(block, axis, pairs)]
    ppermute x8 -> x13, waiting for transfers between devices: 57.5 us -> 54.3 us  [moved(): return lax.ppermute(block, axis, pairs)]
    pallas_call x4 -> x6, Pallas kernels: 14.3 us -> 16.6 us  [the longest x1 7.8 us: on_device(): pl.pallas_call(partial(early_kernel, rows), out_shape=tuple((array(*plane...]
    ppermute x4 -> x5, waiting for transfers between devices: 6.04 us -> 7.83 us  [all_sum(): lax.ppermute(values, axis, [(i, i ^ step << done) for i in range(count)])]
    ppermute x4 -> x5, starting transfers between devices: 7.55 us -> 6.99 us  [all_sum(): lax.ppermute(values, axis, [(i, i ^ step << done) for i in range(count)])]
  transfers between devices with their start and end apart: 12 -> 18, of which waited for: 8 -> 10; matrix products, arithmetic and copies ran while one was open for 1% -> 1% of each run, Pallas kernels for 9% -> 10%
where the time goes in v9:
time: 130 us
  waiting for transfers between devices  62.1 us (48%)
  starting transfers between devices  33.1 us (25%)
  Pallas kernels  31.5 us (24%)
  local copies, waits for them, and re-layouts  1.47 us (1%)
    ppermute x13, waiting for transfers between devices, moved(): return lax.ppermute(block, axis, pairs)  54.3 us
    ppermute x13, starting transfers between devices, moved(): return lax.ppermute(block, axis, pairs)  26.1 us
    pallas_call x1, Pallas kernels, on_device(): pl.pallas_call(outputs_kernel, out_shape=(array(*iterate.shape), array(*r...  8.09 us
    ppermute x5, waiting for transfers between devices, all_sum(): lax.ppermute(values, axis, [(i, i ^ step << done) for i in range(count)])  7.83 us
    pallas_call x1, Pallas kernels, on_device(): pl.pallas_call(partial(early_kernel, rows), out_shape=tuple((array(*plane...  7.8 us
    ppermute x5, starting transfers between devices, all_sum(): lax.ppermute(values, axis, [(i, i ^ step << done) for i in range(count)])  6.99 us
    pallas_call x1, Pallas kernels, on_device(): pl.pallas_call(partial(late_kernel, rows), out_shape=(array(rhs, 128), ar...  6.82 us
    pallas_call x1, Pallas kernels, on_device(): pl.pallas_call(partial(couplings_kernel, rows), out_shape=(array(*grid),)...  3.87 us
  transfers between devices with their start and end apart: 18, of which 10 were waited for; matrix products, arithmetic and copies ran while one was open for 1% of the time, Pallas kernels for 10%

profile of v9, /device:TPU:0, one launch (start us, length us, event | category | flops | bytes accessed | tf_op | source)
XLA Modules:
  0.0 130.1 jit_solution(1616761520060661701)
XLA Ops:
  0.6 3.8 %shard_map.59 = (f32[64,16,256]{2,1,0:T(8,128)}, f32[76,16,256]{2,1,0:T(8,128)}, f32[76,16,256]{2,1,0:T(8,128)}, f32[16,16,256]{2,1,0:T(8,128)}, f32[2,3,16,256]{3,2,1,0:T(8,128)}, /*index=5*/f32[2,3,16,256]{3,2,1,0:T(8,128)}) custom-call(s32[1]{0:T(128)} %bitcast.odd, f32[16,2,64,256]{3,2,1,0:T(8,128)} %residual.1, s32[2,64,256]{2,1,0:T(8,128)} %labels.1, ...), custom_call_target="tpu_custom_call" | custom-call | tf_op jit(solution)/shard_map/pallas_call | solution.py:513
  4.5 3.0 %collective-permute-start.1 = (f32[64,16,256]{2,1,0:T(8,128)}, f32[64,16,256]{2,1,0:T(8,128)S(1)}, u32[]{:S(2)}, u32[]{:S(2)}) collective-permute-start(f32[64,16,256]{2,1,0:T(8,128)} %get-tuple-element.29.mine), channel_id=1, source_target_pairs={{0,2},{2,0},{4,6},{6,4},{8,10},{10,8},{12,14},{14,12},{1,3},{3,1},... | collective-permute-start | bytes 3145736 | tf_op jit(solution)/shard_map/ppermute | solution.py:22
  7.5 3.5 %collective-permute-start.6 = (f32[76,16,256]{2,1,0:T(8,128)}, f32[76,16,256]{2,1,0:T(8,128)S(1)}, u32[]{:S(2)}, u32[]{:S(2)}) collective-permute-start(f32[76,16,256]{2,1,0:T(8,128)} %get-tuple-element.26.ahead), channel_id=1, source_target_pairs={{0,4},{4,8},{6,2},{8,12},{10,6},{14,10},{1,5},{5,9},{7,3},{9,13},{... | collective-permute-start | bytes 3735560 | tf_op jit(solution)/shard_map/ppermute | solution.py:22
  11.1 1.3 collective-permute-start.8
  12.4 1.2 collective-permute-start.9
  13.6 0.0 copy-start.3
  13.6 18.1 %collective-permute-done.1.near2 = f32[64,16,256]{2,1,0:T(8,128)S(1)} collective-permute-done((f32[64,16,256]{2,1,0:T(8,128)}, f32[64,16,256]{2,1,0:T(8,128)S(1)}, u32[]{:S(2)}, u32[]{:S(2)}) %collective-permute-start.1) | collective-permute-done | bytes 1048608 | tf_op jit(solution)/shard_map/ppermute | solution.py:22
  31.7 4.1 %collective-permute-start.7 = (f32[64,16,256]{2,1,0:T(8,128)S(1)}, f32[64,16,256]{2,1,0:T(8,128)S(1)}, u32[]{:S(2)}, u32[]{:S(2)}) collective-permute-start(f32[64,16,256]{2,1,0:T(8,128)S(1)} %collective-permute-done.1.near2), channel_id=1, source_target_pairs={{0,4},{4,8},{6,2},{8,12},{10,6},{14,10},{1,5},{5,9},{7,3},{9,13},{... | collective-permute-start | bytes 3145736 | tf_op jit(solution)/shard_map/ppermute | solution.py:22
  35.8 0.9 broadcast_select_fusion.5
  36.7 0.1 collective-permute-start
  36.8 0.0 collective-permute-done.9.pair
  36.8 3.5 %collective-permute-start.10 = (f32[16,16,256]{2,1,0:T(8,128)}, f32[16,16,256]{2,1,0:T(8,128)S(1)}, u32[]{:S(2)}, u32[]{:S(2)}) collective-permute-start(f32[16,16,256]{2,1,0:T(8,128)} %collective-permute-done.9.pair), channel_id=1, source_target_pairs={{0,4},{4,8},{6,2},{8,12},{10,6},{14,10},{1,5},{5,9},{7,3},{9,13},{... | collective-permute-start | bytes 786440 | tf_op jit(solution)/shard_map/ppermute | solution.py:22
  40.3 0.0 collective-permute-done
  40.4 0.0 copy-start
  40.4 1.3 copy-done
  41.7 0.1 shard_map.60
  41.8 0.1 collective-permute-start.2
  41.8 23.9 %collective-permute-done.10.beyond = f32[16,16,256]{2,1,0:T(8,128)S(1)} collective-permute-done((f32[16,16,256]{2,1,0:T(8,128)}, f32[16,16,256]{2,1,0:T(8,128)S(1)}, u32[]{:S(2)}, u32[]{:S(2)}) %collective-permute-start.10) | collective-permute-done | bytes 262176 | tf_op jit(solution)/shard_map/ppermute | solution.py:22
  65.7 1.2 collective-permute-start.4
  66.9 0.0 collective-permute-done.6.far3
  66.9 0.0 collective-permute-done.8.near3
  66.9 0.0 copy-done.3
  66.9 1.0 shard_map.61
  67.9 0.1 collective-permute-start.11
  68.0 1.4 %collective-permute-done.11 = f32[18,8,256]{2,1,0:T(8,128)S(1)} collective-permute-done((f32[18,8,256]{2,1,0:T(8,128)S(1)}, f32[18,8,256]{2,1,0:T(8,128)S(1)}, u32[]{:S(2)}, u32[]{:S(2)}) %collective-permute-start.11) | collective-permute-done | bytes 147488 | tf_op jit(solution)/shard_map/ppermute | solution.py:22
  69.4 3.9 %shard_map.62 = (f32[8,80,256]{2,1,0:T(8,128)S(1)}, f32[8,80,256]{2,1,0:T(8,128)S(1)}, f32[8,80,256]{2,1,0:T(8,128)S(1)}, f32[8,80,256]{2,1,0:T(8,128)S(1)}, f32[8,80,256]{2,1,0:T(8,128)S(1)}) custom-call(f32[76,16,256]{2,1,0:T(8,128)S(1)} %collective-permute-done.6.far3, f32[16,16,256]{2,1,0:T(8,128)S(1)} %collective-permute-done.10.beyond, ...), custom_call_target="tpu_custom_call" | custom-call | tf_op jit(solution)/shard_map/pallas_call | solution.py:559
  73.2 0.0 collective-permute-done.2.near1a
  73.3 3.7 %collective-permute-start.3 = (f32[33,16,256]{2,1,0:T(8,128)S(1)}, f32[33,16,256]{2,1,0:T(8,128)S(1)}, u32[]{:S(2)}, u32[]{:S(2)}) collective-permute-start(f32[33,16,256]{2,1,0:T(8,128)S(1)} %collective-permute-done.2.near1a), channel_id=1, source_target_pairs={{0,4},{4,8},{6,2},{8,12},{10,6},{14,10},{1,5},{5,9},{7,3},{9,13},{... | collective-permute-start | bytes 1622024 | tf_op jit(solution)/shard_map/ppermute | solution.py:22
  76.9 1.6 %collective-permute-done.4.near1b = f32[33,16,256]{2,1,0:T(8,128)S(1)} collective-permute-done((f32[33,16,256]{2,1,0:T(8,128)S(1)}, f32[33,16,256]{2,1,0:T(8,128)S(1)}, u32[]{:S(2)}, u32[]{:S(2)}) %collective-permute-start.4) | collective-permute-done | bytes 540704 | tf_op jit(solution)/shard_map/ppermute | solution.py:22
  78.5 4.3 %collective-permute-start.5 = (f32[33,16,256]{2,1,0:T(8,128)S(1)}, f32[33,16,256]{2,1,0:T(8,128)S(1)}, u32[]{:S(2)}, u32[]{:S(2)}) collective-permute-start(f32[33,16,256]{2,1,0:T(8,128)S(1)} %collective-permute-done.4.near1b), channel_id=1, source_target_pairs={{0,4},{4,8},{6,2},{8,12},{10,6},{14,10},{1,5},{5,9},{7,3},{9,13},{... | collective-permute-start | bytes 1622024 | tf_op jit(solution)/shard_map/ppermute | solution.py:22
  82.8 0.0 collective-permute-done.7.far1
  82.9 0.0 copy-start.1
  82.9 0.0 copy-start.4
  82.9 0.1 collective-permute-start.12
  83.0 1.3 collective-permute-done.12
  84.3 0.0 copy-done.1
  84.3 0.2 copy-done.4
  84.5 7.8 %shard_map.64 = (f32[3,70,16,256]{3,2,1,0:T(8,128)S(1)}, f32[2,70,16,256]{3,2,1,0:T(8,128)S(1)}, f32[2,70,16,256]{3,2,1,0:T(8,128)S(1)}, bf16[2,64,64,256]{3,2,1,0:T(8,128)(2,1)S(1)}, f32[16,128]{1,0:T(8,128)S(1)}) custom-call(f32[76,16,256]{2,1,0:T(8,128)S(1)} %collective-permute-done.6.far3, f32[64,16,256]{2,1,0:T(8,128)S(1)} %collective-permute-done.7.far1, ...), custom_call_target="tpu_custom_call" | custom-call | tf_op jit(solution)/shard_map/pallas_call | solution.py:581
  92.3 0.0 collective-permute-done.3.far2a
  92.3 8.0 %collective-permute-done.5.far2b = f32[33,16,256]{2,1,0:T(8,128)S(1)} collective-permute-done((f32[33,16,256]{2,1,0:T(8,128)S(1)}, f32[33,16,256]{2,1,0:T(8,128)S(1)}, u32[]{:S(2)}, u32[]{:S(2)}) %collective-permute-start.5) | collective-permute-done | bytes 540704 | tf_op jit(solution)/shard_map/ppermute | solution.py:22
  100.3 0.0 copy-start.2
  100.3 6.8 %shard_map.65 = (f32[16,128]{1,0:T(8,128)S(1)}, bf16[2,64,64,256]{3,2,1,0:T(8,128)(2,1)S(1)}) custom-call(f32[33,16,256]{2,1,0:T(8,128)S(1)} %collective-permute-done.3.far2a, f32[33,16,256]{2,1,0:T(8,128)S(1)} %collective-permute-done.5.far2b, f32[3,70,16,256]{3,2,1,0:T(8,128)S(1)} %get-tuple-element.42.u0_in, ...), custom_call_target="tpu_custom_call" | custom-call | tf_op jit(solution)/shard_map/pallas_call | solution.py:594
  107.1 0.0 collective-permute-start.13
  107.2 1.2 collective-permute-done.13
  108.3 2.2 %collective-permute-start.14 = (f32[16,128]{1,0:T(8,128)S(1)}, f32[16,128]{1,0:T(8,128)S(1)}, u32[]{:S(2)}, u32[]{:S(2)}) collective-permute-start(f32[16,128]{1,0:T(8,128)S(1)} %add.20), channel_id=1, source_target_pairs={{0,2},{2,0},{4,6},{6,4},{8,10},{10,8},{12,14},{14,12},{1,3},{3,1},... | collective-permute-start | bytes 24584 | tf_op jit(solution)/shard_map/ppermute | solution.py:62
  110.6 1.6 %collective-permute-done.14 = f32[16,128]{1,0:T(8,128)S(1)} collective-permute-done((f32[16,128]{1,0:T(8,128)S(1)}, f32[16,128]{1,0:T(8,128)S(1)}, u32[]{:S(2)}, u32[]{:S(2)}) %collective-permute-start.14) | collective-permute-done | bytes 8224 | tf_op jit(solution)/shard_map/ppermute | solution.py:62
  112.2 2.3 %collective-permute-start.15 = (f32[16,128]{1,0:T(8,128)S(1)}, f32[16,128]{1,0:T(8,128)S(1)}, u32[]{:S(2)}, u32[]{:S(2)}) collective-permute-start(f32[16,128]{1,0:T(8,128)S(1)} %add.21), channel_id=1, source_target_pairs={{0,4},{2,6},{4,0},{6,2},{8,12},{10,14},{12,8},{14,10},{1,5},{3,7},... | collective-permute-start | bytes 24584 | tf_op jit(solution)/shard_map/ppermute | solution.py:62
  114.5 2.1 %collective-permute-start.16 = (f32[16,128]{1,0:T(8,128)S(1)}, f32[16,128]{1,0:T(8,128)S(1)}, u32[]{:S(2)}, u32[]{:S(2)}) collective-permute-start(f32[16,128]{1,0:T(8,128)S(1)} %add.21), channel_id=1, source_target_pairs={{0,8},{2,10},{4,12},{6,14},{8,0},{10,2},{12,4},{14,6},{1,9},{3,11}... | collective-permute-start | bytes 24584 | tf_op jit(solution)/shard_map/ppermute | solution.py:62
  116.5 0.4 collective-permute-start.17
  116.9 0.0 collective-permute-done.15
  116.9 2.1 %collective-permute-done.16 = f32[16,128]{1,0:T(8,128)S(1)} collective-permute-done((f32[16,128]{1,0:T(8,128)S(1)}, f32[16,128]{1,0:T(8,128)S(1)}, u32[]{:S(2)}, u32[]{:S(2)}) %collective-permute-start.16) | collective-permute-done | bytes 8224 | tf_op jit(solution)/shard_map/ppermute | solution.py:62
  119.0 3.0 %collective-permute-done.17 = f32[16,128]{1,0:T(8,128)S(1)} collective-permute-done((f32[16,128]{1,0:T(8,128)S(1)}, f32[16,128]{1,0:T(8,128)S(1)}, u32[]{:S(2)}, u32[]{:S(2)}) %collective-permute-start.17) | collective-permute-done | bytes 8224 | tf_op jit(solution)/shard_map/ppermute | solution.py:62
  122.0 0.0 copy-done.2
  122.0 8.1 %shard_map.66 = (f32[16,2,64,256]{3,2,1,0:T(8,128)}, f32[16,2,64,256]{3,2,1,0:T(8,128)}) custom-call(s32[1]{0:T(128)} %bitcast.odd, f32[16,128]{1,0:T(8,128)S(1)} %add_add_fusion.moments, bf16[2,64,64,256]{3,2,1,0:T(8,128)(2,1)S(1)} %get-tuple-element.47.split01, bf16[2,64,64,256]{3,2,1,0:T(8,128)(2,1)S(1)} %get-tuple-element.48.split23, ...), custom_call_target="tpu_custom_call" | custom-call | tf_op jit(solution)/shard_map/pallas_call | solution.py:607
  (9 shorter events, 0.1 us)
Async XLA Ops:
  4.5 27.2 %collective-permute-start.1 = (f32[64,16,256]{2,1,0:T(8,128)}, f32[64,16,256]{2,1,0:T(8,128)S(1)}, u32[]{:S(2)}, u32[]{:S(2)}) collective-permute-start(f32[64,16,256]{2,1,0:T(8,128)} %get-tuple-element.29.mine), channel_id=1, source_target_pairs={{0,2},{2,0},{4,6},{6,4},{8,10},{10,8},{12,14},{14,12},{1,3},{3,1},... | collective-permute-start | bytes 3145736 | tf_op jit(solution)/shard_map/ppermute | solution.py:22
  7.5 59.4 %collective-permute-start.6 = (f32[76,16,256]{2,1,0:T(8,128)}, f32[76,16,256]{2,1,0:T(8,128)S(1)}, u32[]{:S(2)}, u32[]{:S(2)}) collective-permute-start(f32[76,16,256]{2,1,0:T(8,128)} %get-tuple-element.26.ahead), channel_id=1, source_target_pairs={{0,4},{4,8},{6,2},{8,12},{10,6},{14,10},{1,5},{5,9},{7,3},{9,13},{... | collective-permute-start | bytes 3735560 | tf_op jit(solution)/shard_map/ppermute | solution.py:22
  11.1 55.8 %collective-permute-start.8 = (f32[76,16,256]{2,1,0:T(8,128)}, f32[76,16,256]{2,1,0:T(8,128)S(1)}, u32[]{:S(2)}, u32[]{:S(2)}) collective-permute-start(f32[76,16,256]{2,1,0:T(8,128)} %get-tuple-element.32), channel_id=1, source_target_pairs={{4,0},{8,4},{2,6},{12,8},{6,10},{10,14},{5,1},{9,5},{3,7},{13,9},{... | collective-permute-start | bytes 3735560 | tf_op jit(solution)/shard_map/ppermute | solution.py:22
  12.4 24.5 %collective-permute-start.9 = (f32[16,16,256]{2,1,0:T(8,128)}, f32[16,16,256]{2,1,0:T(8,128)}, u32[]{:S(2)}, u32[]{:S(2)}) collective-permute-start(f32[16,16,256]{2,1,0:T(8,128)} %get-tuple-element.33.own), channel_id=1, source_target_pairs={{0,2},{2,0},{4,6},{6,4},{8,10},{10,8},{12,14},{14,12},{1,3},{3,1},... | collective-permute-start | bytes 786440 | tf_op jit(solution)/shard_map/ppermute | solution.py:22
  13.6 53.3 %copy-start.3 = (f32[16,16,256]{2,1,0:T(8,128)S(1)}, f32[16,16,256]{2,1,0:T(8,128)}, u32[]{:S(2)}) copy-start(f32[16,16,256]{2,1,0:T(8,128)} %get-tuple-element.33.own) | copy-start | bytes 786436
  31.7 51.2 %collective-permute-start.7 = (f32[64,16,256]{2,1,0:T(8,128)S(1)}, f32[64,16,256]{2,1,0:T(8,128)S(1)}, u32[]{:S(2)}, u32[]{:S(2)}) collective-permute-start(f32[64,16,256]{2,1,0:T(8,128)S(1)} %collective-permute-done.1.near2), channel_id=1, source_target_pairs={{0,4},{4,8},{6,2},{8,12},{10,6},{14,10},{1,5},{5,9},{7,3},{9,13},{... | collective-permute-start | bytes 3145736 | tf_op jit(solution)/shard_map/ppermute | solution.py:22
  36.7 3.6 %collective-permute-start = (f32[2,3,16,256]{3,2,1,0:T(8,128)S(1)}, f32[2,3,16,256]{3,2,1,0:T(8,128)S(1)}, u32[]{:S(2)}, u32[]{:S(2)}) collective-permute-start(f32[2,3,16,256]{3,2,1,0:T(8,128)S(1)} %broadcast_select_fusion.5), channel_id=1, source_target_pairs={{0,1},{1,0},{2,3},{3,2},{4,5},{5,4},{6,7},{7,6},{8,9},{9,8},{10,11... | collective-permute-start | bytes 294920 | tf_op jit(solution)/shard_map/ppermute | solution.py:22
  36.8 28.9 %collective-permute-start.10 = (f32[16,16,256]{2,1,0:T(8,128)}, f32[16,16,256]{2,1,0:T(8,128)S(1)}, u32[]{:S(2)}, u32[]{:S(2)}) collective-permute-start(f32[16,16,256]{2,1,0:T(8,128)} %collective-permute-done.9.pair), channel_id=1, source_target_pairs={{0,4},{4,8},{6,2},{8,12},{10,6},{14,10},{1,5},{5,9},{7,3},{9,13},{... | collective-permute-start | bytes 786440 | tf_op jit(solution)/shard_map/ppermute | solution.py:22
  40.4 1.3 copy-start
  41.8 31.5 %collective-permute-start.2 = (f32[33,16,256]{2,1,0:T(8,128)S(1)}, f32[33,16,256]{2,1,0:T(8,128)S(1)}, u32[]{:S(2)}, u32[]{:S(2)}) collective-permute-start(f32[33,16,256]{2,1,0:T(8,128)S(1)} %get-tuple-element.30), channel_id=1, source_target_pairs={{0,2},{2,0},{4,6},{6,4},{8,10},{10,8},{12,14},{14,12},{1,3},{3,1},... | collective-permute-start | bytes 1622024 | tf_op jit(solution)/shard_map/ppermute | solution.py:22
  65.7 12.8 %collective-permute-start.4 = (f32[33,16,256]{2,1,0:T(8,128)S(1)}, f32[33,16,256]{2,1,0:T(8,128)S(1)}, u32[]{:S(2)}, u32[]{:S(2)}) collective-permute-start(f32[33,16,256]{2,1,0:T(8,128)S(1)} %get-tuple-element.31), channel_id=1, source_target_pairs={{0,2},{2,0},{4,6},{6,4},{8,10},{10,8},{12,14},{14,12},{1,3},{3,1},... | collective-permute-start | bytes 1622024 | tf_op jit(solution)/shard_map/ppermute | solution.py:22
  67.9 1.4 %collective-permute-start.11 = (f32[18,8,256]{2,1,0:T(8,128)S(1)}, f32[18,8,256]{2,1,0:T(8,128)S(1)}, u32[]{:S(2)}, u32[]{:S(2)}) collective-permute-start(f32[18,8,256]{2,1,0:T(8,128)S(1)} %broadcast_select_fusion.2), channel_id=1, source_target_pairs={{0,1},{1,0},{2,3},{3,2},{4,5},{5,4},{6,7},{7,6},{8,9},{9,8},{10,11... | collective-permute-start | bytes 442376 | tf_op jit(solution)/shard_map/ppermute | solution.py:22
  73.3 19.0 %collective-permute-start.3 = (f32[33,16,256]{2,1,0:T(8,128)S(1)}, f32[33,16,256]{2,1,0:T(8,128)S(1)}, u32[]{:S(2)}, u32[]{:S(2)}) collective-permute-start(f32[33,16,256]{2,1,0:T(8,128)S(1)} %collective-permute-done.2.near1a), channel_id=1, source_target_pairs={{0,4},{4,8},{6,2},{8,12},{10,6},{14,10},{1,5},{5,9},{7,3},{9,13},{... | collective-permute-start | bytes 1622024 | tf_op jit(solution)/shard_map/ppermute | solution.py:22
  78.5 21.8 %collective-permute-start.5 = (f32[33,16,256]{2,1,0:T(8,128)S(1)}, f32[33,16,256]{2,1,0:T(8,128)S(1)}, u32[]{:S(2)}, u32[]{:S(2)}) collective-permute-start(f32[33,16,256]{2,1,0:T(8,128)S(1)} %collective-permute-done.4.near1b), channel_id=1, source_target_pairs={{0,4},{4,8},{6,2},{8,12},{10,6},{14,10},{1,5},{5,9},{7,3},{9,13},{... | collective-permute-start | bytes 1622024 | tf_op jit(solution)/shard_map/ppermute | solution.py:22
  82.9 1.4 %copy-start.1 = (f32[76,16,256]{2,1,0:T(8,128)S(1)}, f32[76,16,256]{2,1,0:T(8,128)}, u32[]{:S(2)}) copy-start(f32[76,16,256]{2,1,0:T(8,128)} %get-tuple-element.26.ahead) | copy-start | bytes 3735556
  82.9 1.6 %copy-start.4 = (f32[64,16,256]{2,1,0:T(8,128)S(1)}, f32[64,16,256]{2,1,0:T(8,128)}, u32[]{:S(2)}) copy-start(f32[64,16,256]{2,1,0:T(8,128)} %get-tuple-element.29.mine) | copy-start | bytes 3145732
  82.9 1.3 %collective-permute-start.12 = (f32[5,16,256]{2,1,0:T(8,128)S(1)}, f32[5,16,256]{2,1,0:T(8,128)S(1)}, u32[]{:S(2)}, u32[]{:S(2)}) collective-permute-start(f32[5,16,256]{2,1,0:T(8,128)S(1)} %broadcast_select_fusion.8), channel_id=1, source_target_pairs={{0,1},{1,0},{2,3},{3,2},{4,5},{5,4},{6,7},{7,6},{8,9},{9,8},{10,11... | collective-permute-start | bytes 245768 | tf_op jit(solution)/shard_map/ppermute | solution.py:22
  100.3 21.7 %copy-start.2 = (f32[16,2,64,256]{3,2,1,0:T(8,128)S(1)}, f32[16,2,64,256]{3,2,1,0:T(8,128)}, u32[]{:S(2)}) copy-start(f32[16,2,64,256]{3,2,1,0:T(8,128)} %iterate.1) | copy-start | bytes 6291460
  107.1 1.2 collective-permute-start.13
  108.3 3.9 %collective-permute-start.14 = (f32[16,128]{1,0:T(8,128)S(1)}, f32[16,128]{1,0:T(8,128)S(1)}, u32[]{:S(2)}, u32[]{:S(2)}) collective-permute-start(f32[16,128]{1,0:T(8,128)S(1)} %add.20), channel_id=1, source_target_pairs={{0,2},{2,0},{4,6},{6,4},{8,10},{10,8},{12,14},{14,12},{1,3},{3,1},... | collective-permute-start | bytes 24584 | tf_op jit(solution)/shard_map/ppermute | solution.py:62
  112.2 4.7 %collective-permute-start.15 = (f32[16,128]{1,0:T(8,128)S(1)}, f32[16,128]{1,0:T(8,128)S(1)}, u32[]{:S(2)}, u32[]{:S(2)}) collective-permute-start(f32[16,128]{1,0:T(8,128)S(1)} %add.21), channel_id=1, source_target_pairs={{0,4},{2,6},{4,0},{6,2},{8,12},{10,14},{12,8},{14,10},{1,5},{3,7},... | collective-permute-start | bytes 24584 | tf_op jit(solution)/shard_map/ppermute | solution.py:62
  114.5 4.5 %collective-permute-start.16 = (f32[16,128]{1,0:T(8,128)S(1)}, f32[16,128]{1,0:T(8,128)S(1)}, u32[]{:S(2)}, u32[]{:S(2)}) collective-permute-start(f32[16,128]{1,0:T(8,128)S(1)} %add.21), channel_id=1, source_target_pairs={{0,8},{2,10},{4,12},{6,14},{8,0},{10,2},{12,4},{14,6},{1,9},{3,11}... | collective-permute-start | bytes 24584 | tf_op jit(solution)/shard_map/ppermute | solution.py:62
  116.5 5.4 %collective-permute-start.17 = (f32[16,128]{1,0:T(8,128)S(1)}, f32[16,128]{1,0:T(8,128)S(1)}, u32[]{:S(2)}, u32[]{:S(2)}) collective-permute-start(f32[16,128]{1,0:T(8,128)S(1)} %add.21), channel_id=1, source_target_pairs={{0,12},{2,14},{4,8},{6,10},{8,4},{10,6},{12,0},{14,2},{1,13},{3,15... | collective-permute-start | bytes 24584 | tf_op jit(solution)/shard_map/ppermute | solution.py:62

commit v10 on v8

--- a/solution.py
+++ b/solution.py
@@ -48,19 +48,6 @@
     return jnp.where(second, other, zero), jnp.where(second, zero, other)
 
 
-def all_sum(values, axes):
-    for axis in axes:
-        count = lax.axis_size(axis)
-        if count & (count - 1):
-            values = lax.psum(values, axis)
-            continue
-        step = 1
-        while step < count:
-            values = values + lax.ppermute(values, axis, [(i, i ^ step) for i in range(count)])
-            step *= 2
-    return values
-
-
 def face_of(center, beside):
     return jnp.where(beside > 0.0, 2.0 * center * beside / (center + beside), center)
 
@@ -75,18 +62,21 @@
 MARGIN = 8
 
 
-def prepare_kernel(
-    odd, residual, labels, boundary, mine, ahead, first, last, block, label_cells, boundary_cells, arrived
-):
+def turn_plane(block, out):
+    def turn(group, carry):
+        here = pl.ds(group * 8, 8)
+        out[here] = pltpu.einshape("abc->bac", block[:, here, :])
+        return carry
+
+    lax.fori_loop(0, block.shape[1] // 8, turn, 0)
+
+
+def far_kernel(odd, residual, labels, boundary, mine, first, last, block, label_cells, boundary_cells, arrived):
     rhs, depth, rows, nx = residual.shape
     copies = [
         pltpu.make_async_copy(labels, label_cells, arrived.at[0]),
         pltpu.make_async_copy(boundary, boundary_cells, arrived.at[1]),
-    ] + [
-        pltpu.make_async_copy(
-            residual.at[:, jnp.bitwise_xor(place, odd[0])], block.at[place], arrived.at[2 + place]
-        )
-        for place in range(depth)
+        pltpu.make_async_copy(residual.at[:, odd[0]], block, arrived.at[2]),
     ]
     for copy in copies:
         copy.start()
@@ -97,25 +87,29 @@
         plane = jnp.bitwise_xor(place, odd[0])
         for part in range(count):
             cells = pl.ds(part * rhs, rhs)
-            coef = jnp.exp(label_cells[plane, cells, :].astype(f32) * (contrast_log / (NCLASS - 1)))
-            inner = (1 - boundary_cells[plane, cells, :]).astype(f32)
-            for message in (mine, ahead):
-                message[rows + place * count + part] = coef
-            mine[rows + (2 + place) * count + part] = inner
-            if place == 1:
-                ahead[rows + 2 * count + part] = inner
-
-    for place, out in ((0, mine), (1, ahead)):
-        copies[2 + place].wait()
-
-        def turn(group, carry, place=place, out=out):
-            here = pl.ds(group * 8, 8)
-            out[here] = pltpu.einshape("abc->bac", block[place, :, here, :])
-            return carry
-
-        lax.fori_loop(0, rows // 8, turn, 0)
-        first[place] = out[:REACH]
-        last[place] = out[rows - REACH : rows]
+            mine[rows + place * count + part] = jnp.exp(
+                label_cells[plane, cells, :].astype(f32) * (contrast_log / (NCLASS - 1))
+            )
+            mine[rows + (2 + place) * count + part] = (1 - boundary_cells[plane, cells, :]).astype(f32)
+    copies[2].wait()
+    turn_plane(block, mine)
+    first[...] = mine[:REACH]
+    last[...] = mine[rows - REACH : rows]
+
+
+def near_kernel(odd, residual, mine, ahead, first, last, block, arrived):
+    rhs, _, rows, _ = residual.shape
+    copy = pltpu.make_async_copy(residual.at[:, 1 - odd[0]], block, arrived)
+    copy.start()
+    count = rows // rhs
+    for part in range(2 * count):
+        ahead[rows + part] = mine[rows + part]
+    for part in range(count):
+        ahead[rows + 2 * count + part] = mine[rows + 3 * count + part]
+    copy.wait()
+    turn_plane(block, ahead)
+    first[...] = ahead[:REACH]
+    last[...] = ahead[rows - REACH : rows]
 
 
 def second_kernel(rows, ahead, own_before, own_behind, near2, far3, out):
@@ -492,20 +486,31 @@
     anywhere = pl.BlockSpec(memory_space=pl.ANY)
 
     count = rows // rhs
-    mine, ahead, *edges = pl.pallas_call(
-        prepare_kernel,
-        out_shape=(array(rows + 4 * count, rhs, nx), array(rows + 3 * count, rhs, nx))
-        + (array(depth, REACH, rhs, nx),) * 2,
-        in_specs=[smem] + [pl.BlockSpec(memory_space=pltpu.HBM)] * 3,
-        out_specs=(vmem,) * 4,
+    hbm = pl.BlockSpec(memory_space=pltpu.HBM)
+    edge = (array(REACH, rhs, nx),) * 2
+    plane_block = pltpu.VMEM((rhs, rows, nx), f32)
+    mine, far_first, far_last = pl.pallas_call(
+        far_kernel,
+        out_shape=(array(rows + 4 * count, rhs, nx),) + edge,
+        in_specs=[smem, hbm, hbm, hbm],
+        out_specs=(vmem,) * 3,
         scratch_shapes=[
-            pltpu.VMEM((depth, rhs, rows, nx), f32),
+            plane_block,
             pltpu.VMEM(labels.shape, jnp.int32),
             pltpu.VMEM(boundary.shape, jnp.int32),
-            pltpu.SemaphoreType.DMA((2 + depth,)),
+            pltpu.SemaphoreType.DMA((3,)),
         ],
-        compiler_params=params(55),
+        compiler_params=params(58),
     )(odd, residual, labels, boundary)
+    ahead, near_first, near_last = pl.pallas_call(
+        near_kernel,
+        out_shape=(array(rows + 3 * count, rhs, nx),) + edge,
+        in_specs=[smem, hbm, vmem],
+        out_specs=(vmem,) * 3,
+        scratch_shapes=[plane_block, pltpu.SemaphoreType.DMA],
+        compiler_params=params(58),
+    )(odd, residual, mine)
+    edges = jnp.stack([far_first, near_first]), jnp.stack([far_last, near_last])
 
     near2 = swapped(mine)
     far3 = relayed(ahead)
@@ -560,7 +565,7 @@
         compiler_params=params(20),
     )(far2, u0, u1, u2, moments, inverse, sx, sy, sz)
 
-    moments = all_sum(moments, ("gy", "gz"))
+    moments = jnp.sum(lax.all_gather(moments, ("gz", "gy")), axis=0)
 
     tile = math.gcd(rows, 32)
     plane_rows = pl.BlockSpec((rhs, 1, tile, nx), lambda z, y, odd: (0, jnp.bitwise_xor(z, odd[0]), y, 0))

time: 119 us -> 134 us (1.13)
  blocking collectives: 0 us -> 19.9 us
  waiting for transfers between devices: 63.5 us -> 50.3 us
  local copies, waits for them, and re-layouts: 1.3 us -> 8.77 us
  Pallas kernels: 29.2 us -> 35 us
  starting transfers between devices: 22.9 us -> 18.1 us
    all_gather x0 -> x1, blocking collectives: none -> 19.9 us  [on_device(): moments = jnp.sum(lax.all_gather(moments, ('gz', 'gy')), axis=0)]
    ppermute x4 -> x0, starting transfers between devices: 7.55 us -> none  [all_sum(): lax.ppermute(values, axis, [(i, i ^ step) for i in range(count)])]
    unnamed x8 -> x24, local copies, waits for them, and re-layouts: 1.3 us -> 8.77 us
    ppermute x8, waiting for transfers between devices: 57.5 us -> 50.3 us  [moved(): return lax.ppermute(block, axis, pairs)]
    ppermute x4 -> x0, waiting for transfers between devices: 6.04 us -> none  [all_sum(): lax.ppermute(values, axis, [(i, i ^ step) for i in range(count)])]
    pallas_call x1 -> x2, Pallas kernels: 3.43 us -> 6.54 us  [the longest x1 3.85 us: on_device(): pl.pallas_call(near_kernel, out_shape=(array(rows + 3 * count, rhs, nx),)...]
    ppermute x8, starting transfers between devices: 15.3 us -> 18.1 us  [moved(): return lax.ppermute(block, axis, pairs)]
  transfers between devices with their start and end apart: 12 -> 8, of which waited for: 8 -> 5; matrix products, arithmetic and copies ran while one was open for 1% -> 1% of each run, Pallas kernels for 9% -> 13%
where the time goes in v10:
time: 134 us
  waiting for transfers between devices  50.3 us (38%)
  Pallas kernels  35 us (26%)
  blocking collectives  19.9 us (15%)
  starting transfers between devices  18.1 us (14%)
  local copies, waits for them, and re-layouts  8.77 us (7%)
    ppermute x8, waiting for transfers between devices, moved(): return lax.ppermute(block, axis, pairs)  50.3 us
    all_gather x1, blocking collectives, on_device(): moments = jnp.sum(lax.all_gather(moments, ('gz', 'gy')), axis=0)  19.9 us
    ppermute x8, starting transfers between devices, moved(): return lax.ppermute(block, axis, pairs)  18.1 us
    pallas_call x1, Pallas kernels, on_device(): pl.pallas_call(partial(early_kernel, rows), out_shape=(array(*cells),) *...  12.1 us
    unnamed x24, local copies, waits for them, and re-layouts  8.77 us
    pallas_call x1, Pallas kernels, on_device(): pl.pallas_call(outputs_kernel, out_shape=(array(*iterate.shape), array(*r...  8.06 us
    pallas_call x1, Pallas kernels, on_device(): pl.pallas_call(partial(late_kernel, rows), out_shape=(array(rhs, 128), ar...  6.89 us
    pallas_call x1, Pallas kernels, on_device(): pl.pallas_call(near_kernel, out_shape=(array(rows + 3 * count, rhs, nx),)...  3.85 us
  transfers between devices with their start and end apart: 8, of which 5 were waited for; matrix products, arithmetic and copies ran while one was open for 1% of the time, Pallas kernels for 13%

profile of v10, /device:TPU:0, one launch (start us, length us, event | category | flops | bytes accessed | tf_op | source)
XLA Modules:
  0.0 133.9 jit_solution(14268306731227355868)
XLA Ops:
  0.6 2.7 %shard_map.59 = (f32[80,16,256]{2,1,0:T(8,128)}, f32[3,16,256]{2,1,0:T(8,128)}, f32[3,16,256]{2,1,0:T(8,128)}) custom-call(s32[1]{0:T(128)} %bitcast.odd, f32[16,2,64,256]{3,2,1,0:T(8,128)} %residual.3, s32[2,64,256]{2,1,0:T(8,128)} %labels.1, s32[2,64,256]{2,1,0:T(8,128)} %boundary.1), custom_call_target="tpu_custom_call" | custom-call | tf_op jit(solution)/shard_map/pallas_call | solution.py:492
  3.3 0.0 copy-start.10
  3.3 0.0 copy-start.11
  3.4 0.0 copy-start
  3.4 3.0 %collective-permute-start.1 = (f32[80,16,256]{2,1,0:T(8,128)}, f32[80,16,256]{2,1,0:T(8,128)S(1)}, u32[]{:S(2)}, u32[]{:S(2)}) collective-permute-start(f32[80,16,256]{2,1,0:T(8,128)} %get-tuple-element.22.mine), channel_id=1, source_target_pairs={{0,2},{2,0},{4,6},{6,4},{8,10},{10,8},{12,14},{14,12},{1,3},{3,1},... | collective-permute-start | bytes 3932168 | tf_op jit(solution)/shard_map/ppermute | solution.py:22
  6.4 3.9 %shard_map.60 = (f32[76,16,256]{2,1,0:T(8,128)}, f32[3,16,256]{2,1,0:T(8,128)}, f32[3,16,256]{2,1,0:T(8,128)}) custom-call(s32[1]{0:T(128)} %bitcast.odd, f32[16,2,64,256]{3,2,1,0:T(8,128)} %residual.3, f32[80,16,256]{2,1,0:T(8,128)} %get-tuple-element.22.mine), custom_call_target="tpu_custom_call" | custom-call | tf_op jit(solution)/shard_map/pallas_call | solution.py:505
  10.2 4.6 %collective-permute-start.2 = (f32[76,16,256]{2,1,0:T(8,128)}, f32[76,16,256]{2,1,0:T(8,128)}, u32[]{:S(2)}, u32[]{:S(2)}) collective-permute-start(f32[76,16,256]{2,1,0:T(8,128)} %get-tuple-element.23.ahead), channel_id=1, source_target_pairs={{0,4},{4,8},{6,2},{8,12},{10,6},{14,10},{1,5},{5,9},{7,3},{9,13},{... | collective-permute-start | bytes 3735560 | tf_op jit(solution)/shard_map/ppermute | solution.py:22
  14.8 0.0 copy-done.10
  14.8 0.0 copy-done.11
  14.8 0.8 maximum_select_fusion
  15.6 0.1 collective-permute-start
  15.7 0.0 copy-done
  15.7 1.3 collective-permute-start.6
  17.0 18.3 %collective-permute-done.1.near2 = f32[80,16,256]{2,1,0:T(8,128)S(1)} collective-permute-done((f32[80,16,256]{2,1,0:T(8,128)}, f32[80,16,256]{2,1,0:T(8,128)S(1)}, u32[]{:S(2)}, u32[]{:S(2)}) %collective-permute-start.1) | collective-permute-done | bytes 1310752 | tf_op jit(solution)/shard_map/ppermute | solution.py:22
  35.4 3.8 %collective-permute-start.5 = (f32[80,16,256]{2,1,0:T(8,128)S(1)}, f32[80,16,256]{2,1,0:T(8,128)S(1)}, u32[]{:S(2)}, u32[]{:S(2)}) collective-permute-start(f32[80,16,256]{2,1,0:T(8,128)S(1)} %collective-permute-done.1.near2), channel_id=1, source_target_pairs={{0,4},{4,8},{6,2},{8,12},{10,6},{14,10},{1,5},{5,9},{7,3},{9,13},{... | collective-permute-start | bytes 3932168 | tf_op jit(solution)/shard_map/ppermute | solution.py:22
  39.2 0.0 collective-permute-done
  39.2 2.6 %collective-permute-done.2.far3 = f32[76,16,256]{2,1,0:T(8,128)} collective-permute-done((f32[76,16,256]{2,1,0:T(8,128)}, f32[76,16,256]{2,1,0:T(8,128)}, u32[]{:S(2)}, u32[]{:S(2)}) %collective-permute-start.2) | collective-permute-done | bytes 1245216 | tf_op jit(solution)/shard_map/ppermute | solution.py:22
  41.8 0.0 copy-start.1
  41.8 1.3 copy-done.1
  43.1 0.1 shard_map.61
  43.2 0.8 collective-permute-start.3
  44.0 22.2 %collective-permute-done.3.near1 = f32[66,16,256]{2,1,0:T(8,128)S(1)} collective-permute-done((f32[66,16,256]{2,1,0:T(8,128)S(1)}, f32[66,16,256]{2,1,0:T(8,128)S(1)}, u32[]{:S(2)}, u32[]{:S(2)}) %collective-permute-start.3) | collective-permute-done | bytes 1081376 | tf_op jit(solution)/shard_map/ppermute | solution.py:22
  66.2 4.4 %collective-permute-start.4 = (f32[66,16,256]{2,1,0:T(8,128)S(1)}, f32[66,16,256]{2,1,0:T(8,128)S(1)}, u32[]{:S(2)}, u32[]{:S(2)}) collective-permute-start(f32[66,16,256]{2,1,0:T(8,128)S(1)} %collective-permute-done.3.near1), channel_id=1, source_target_pairs={{0,4},{4,8},{6,2},{8,12},{10,6},{14,10},{1,5},{5,9},{7,3},{9,13},{... | collective-permute-start | bytes 3244040 | tf_op jit(solution)/shard_map/ppermute | solution.py:22
  70.7 0.0 collective-permute-done.6.near3
  70.7 0.0 collective-permute-done.5.far1
  70.7 1.3 %shard_map.62 = (f32[23,16,256]{2,1,0:T(8,128)S(1)}, f32[23,16,256]{2,1,0:T(8,128)S(1)}) custom-call(f32[66,16,256]{2,1,0:T(8,128)S(1)} %collective-permute-done.3.near1, f32[80,16,256]{2,1,0:T(8,128)S(1)} %collective-permute-done.1.near2, f32[80,16,256]{2,1,0:T(8,128)S(1)} %collective-permute-done.5.far1, f32[76,16,256]{2,1,0:T(8,128)} %collective-permute-done.2.far3, ...), custom_call_target="tpu_custom_call" | custom-call | tf_op jit(solution)/shard_map/pallas_call | solution.py:533
  72.0 0.0 copy-start.2
  72.1 0.1 broadcast_select_fusion.2
  72.1 0.1 collective-permute-start.7
  72.2 1.7 %collective-permute-done.7 = f32[23,16,256]{2,1,0:T(8,128)S(1)} collective-permute-done((f32[23,16,256]{2,1,0:T(8,128)S(1)}, f32[23,16,256]{2,1,0:T(8,128)S(1)}, u32[]{:S(2)}, u32[]{:S(2)}) %collective-permute-start.7) | collective-permute-done | bytes 376864 | tf_op jit(solution)/shard_map/ppermute | solution.py:22
  73.9 0.1 broadcast_select_fusion
  74.0 0.0 copy-done.2
  74.0 12.1 %shard_map.63 = (f32[8,80,256]{2,1,0:T(8,128)S(1)}, f32[8,80,256]{2,1,0:T(8,128)S(1)}, f32[8,80,256]{2,1,0:T(8,128)S(1)}, f32[8,80,256]{2,1,0:T(8,128)S(1)}, f32...) custom-call(f32[76,16,256]{2,1,0:T(8,128)} %collective-permute-done., ...), custom_call_target="tpu_custom_call" | custom-call | tf_op jit(solution)/shard_map/pallas_call | solution.py:546
  86.0 0.0 copy-start.3
  86.0 0.0 copy-start.8
  86.0 5.5 %collective-permute-done.4.far2 = f32[66,16,256]{2,1,0:T(8,128)S(1)} collective-permute-done((f32[66,16,256]{2,1,0:T(8,128)S(1)}, f32[66,16,256]{2,1,0:T(8,128)S(1)}, u32[]{:S(2)}, u32[]{:S(2)}) %collective-permute-start.4) | collective-permute-done | bytes 1081376 | tf_op jit(solution)/shard_map/ppermute | solution.py:22
  91.5 0.0 copy-start.7
  91.5 6.9 %shard_map.64 = (f32[16,128]{1,0:T(8,128)S(1)}, bf16[2,64,64,256]{3,2,1,0:T(8,128)(2,1)S(1)}) custom-call(f32[66,16,256]{2,1,0:T(8,128)S(1)} %collective-permute-done.4.far2, f32[3,70,16,256]{3,2,1,0:T(8,128)S(1)} %get-tuple-element.30.u0_in, f32[2,70,16,256]{3,2,1,0:T(8,128)S(1)} %get-tuple-element.31.u1_in, ...), custom_call_target="tpu_custom_call" | custom-call | tf_op jit(solution)/shard_map/pallas_call | solution.py:559
  98.4 0.0 copy-done.3
  98.4 0.0 copy-done.8
  98.4 0.0 copy-start.5
  98.4 2.0 %copy-done.5 = bf16[2,64,64,256]{3,2,1,0:T(8,128)(2,1)} copy-done((bf16[2,64,64,256]{3,2,1,0:T(8,128)(2,1)}, bf16[2,64,64,256]{3,2,1,0:T(8,128)(2,1)S(1)}, u32[]{:S(2)}) %copy-start.5) | copy-done | bytes 4194328
  100.4 19.9 %all-gather = f32[256,128]{1,0:T(8,128)S(1)} all-gather(f32[16,128]{1,0:T(8,128)S(1)} %get-tuple-element.38), channel_id=2, replica_groups=mesh['regions'=2,'gz'=8,'gy'=2] {'gz','gy'}, dimensions={0}, use_global_device_ids=true | all-gather | bytes 139264 | tf_op jit(solution)/shard_map/all_gather | solution.py:568
  120.4 0.0 copy-done.7
  120.4 0.0 copy-start.4
  120.4 2.2 %copy-done.4 = bf16[2,64,64,256]{3,2,1,0:T(8,128)(2,1)S(1)} copy-done((bf16[2,64,64,256]{3,2,1,0:T(8,128)(2,1)S(1)}, bf16[2,64,64,256]{3,2,1,0:T(8,128)(2,1)}, u32[]{:S(2)}) %copy-start.4) | copy-done | bytes 4194328
  122.6 0.0 copy-start.6
  122.6 2.2 %copy-done.6 = bf16[2,64,64,256]{3,2,1,0:T(8,128)(2,1)S(1)} copy-done((bf16[2,64,64,256]{3,2,1,0:T(8,128)(2,1)S(1)}, bf16[2,64,64,256]{3,2,1,0:T(8,128)(2,1)}, u32[]{:S(2)}) %copy-start.6) | copy-done | bytes 4194328
  124.8 0.0 copy-start.9
  124.8 1.1 copy-done.9
  125.9 8.1 %shard_map.65 = (f32[16,2,64,256]{3,2,1,0:T(8,128)}, f32[16,2,64,256]{3,2,1,0:T(8,128)}) custom-call(s32[1]{0:T(128)} %bitcast.odd, f32[16,128]{1,0:T(8,128)S(1)} %reduce_sum.9.moments, bf16[2,64,64,256]{3,2,1,0:T(8,128)(2,1)S(1)} %copy-done.4, bf16[2,64,64,256]{3,2,1,0:T(8,128)(2,1)S(1)} %copy-done.6, f32[8,80,256]{2,1,0:T(8,128)S(1)} %get-tuple-element.34.inverse, ...), custom_call_target="tpu_custom_call" | custom-call | tf_op jit(solution)/shard_map/pallas_call | solution.py:572
  (2 shorter events, 0.0 us)
Async XLA Ops:
  3.3 11.5 %copy-start.10 = (f32[3,16,256]{2,1,0:T(8,128)S(1)}, f32[3,16,256]{2,1,0:T(8,128)}, u32[]{:S(2)}) copy-start(f32[3,16,256]{2,1,0:T(8,128)} %get-tuple-element.24) | copy-start | bytes 147460
  3.3 11.4 %copy-start.11 = (f32[3,16,256]{2,1,0:T(8,128)S(1)}, f32[3,16,256]{2,1,0:T(8,128)}, u32[]{:S(2)}) copy-start(f32[3,16,256]{2,1,0:T(8,128)} %get-tuple-element.26) | copy-start | bytes 147460
  3.4 12.4 %copy-start = (f32[80,16,256]{2,1,0:T(8,128)S(1)}, f32[80,16,256]{2,1,0:T(8,128)}, u32[]{:S(2)}) copy-start(f32[80,16,256]{2,1,0:T(8,128)} %get-tuple-element.22.mine) | copy-start | bytes 3932164
  3.4 32.0 %collective-permute-start.1 = (f32[80,16,256]{2,1,0:T(8,128)}, f32[80,16,256]{2,1,0:T(8,128)S(1)}, u32[]{:S(2)}, u32[]{:S(2)}) collective-permute-start(f32[80,16,256]{2,1,0:T(8,128)} %get-tuple-element.22.mine), channel_id=1, source_target_pairs={{0,2},{2,0},{4,6},{6,4},{8,10},{10,8},{12,14},{14,12},{1,3},{3,1},... | collective-permute-start | bytes 3932168 | tf_op jit(solution)/shard_map/ppermute | solution.py:22
  10.2 31.6 %collective-permute-start.2 = (f32[76,16,256]{2,1,0:T(8,128)}, f32[76,16,256]{2,1,0:T(8,128)}, u32[]{:S(2)}, u32[]{:S(2)}) collective-permute-start(f32[76,16,256]{2,1,0:T(8,128)} %get-tuple-element.23.ahead), channel_id=1, source_target_pairs={{0,4},{4,8},{6,2},{8,12},{10,6},{14,10},{1,5},{5,9},{7,3},{9,13},{... | collective-permute-start | bytes 3735560 | tf_op jit(solution)/shard_map/ppermute | solution.py:22
  15.6 23.5 %collective-permute-start = (f32[2,3,16,256]{3,2,1,0:T(8,128)S(1)}, f32[2,3,16,256]{3,2,1,0:T(8,128)S(1)}, u32[]{:S(2)}, u32[]{:S(2)}) collective-permute-start(f32[2,3,16,256]{3,2,1,0:T(8,128)S(1)} %maximum_select_fusion), channel_id=1, source_target_pairs={{0,1},{1,0},{2,3},{3,2},{4,5},{5,4},{6,7},{7,6},{8,9},{9,8},{10,11... | collective-permute-start | bytes 294920 | tf_op jit(solution)/shard_map/ppermute | solution.py:22
  15.7 55.0 %collective-permute-start.6 = (f32[80,16,256]{2,1,0:T(8,128)S(1)}, f32[80,16,256]{2,1,0:T(8,128)S(1)}, u32[]{:S(2)}, u32[]{:S(2)}) collective-permute-start(f32[80,16,256]{2,1,0:T(8,128)S(1)} %copy-done), channel_id=1, source_target_pairs={{4,0},{8,4},{2,6},{12,8},{6,10},{10,14},{5,1},{9,5},{3,7},{13,9},{... | collective-permute-start | bytes 3932168 | tf_op jit(solution)/shard_map/ppermute | solution.py:22
  35.4 35.3 %collective-permute-start.5 = (f32[80,16,256]{2,1,0:T(8,128)S(1)}, f32[80,16,256]{2,1,0:T(8,128)S(1)}, u32[]{:S(2)}, u32[]{:S(2)}) collective-permute-start(f32[80,16,256]{2,1,0:T(8,128)S(1)} %collective-permute-done.1.near2), channel_id=1, source_target_pairs={{0,4},{4,8},{6,2},{8,12},{10,6},{14,10},{1,5},{5,9},{7,3},{9,13},{... | collective-permute-start | bytes 3932168 | tf_op jit(solution)/shard_map/ppermute | solution.py:22
  41.8 1.3 copy-start.1
  43.2 23.0 %collective-permute-start.3 = (f32[66,16,256]{2,1,0:T(8,128)S(1)}, f32[66,16,256]{2,1,0:T(8,128)S(1)}, u32[]{:S(2)}, u32[]{:S(2)}) collective-permute-start(f32[66,16,256]{2,1,0:T(8,128)S(1)} %shard_map.61), channel_id=1, source_target_pairs={{0,2},{2,0},{4,6},{6,4},{8,10},{10,8},{12,14},{14,12},{1,3},{3,1},... | collective-permute-start | bytes 3244040 | tf_op jit(solution)/shard_map/ppermute | solution.py:22
  66.2 25.3 %collective-permute-start.4 = (f32[66,16,256]{2,1,0:T(8,128)S(1)}, f32[66,16,256]{2,1,0:T(8,128)S(1)}, u32[]{:S(2)}, u32[]{:S(2)}) collective-permute-start(f32[66,16,256]{2,1,0:T(8,128)S(1)} %collective-permute-done.3.near1), channel_id=1, source_target_pairs={{0,4},{4,8},{6,2},{8,12},{10,6},{14,10},{1,5},{5,9},{7,3},{9,13},{... | collective-permute-start | bytes 3244040 | tf_op jit(solution)/shard_map/ppermute | solution.py:22
  72.0 1.9 %copy-start.2 = (f32[76,16,256]{2,1,0:T(8,128)S(1)}, f32[76,16,256]{2,1,0:T(8,128)}, u32[]{:S(2)}) copy-start(f32[76,16,256]{2,1,0:T(8,128)} %get-tuple-element.23.ahead) | copy-start | bytes 3735556
  72.1 1.8 %collective-permute-start.7 = (f32[23,16,256]{2,1,0:T(8,128)S(1)}, f32[23,16,256]{2,1,0:T(8,128)S(1)}, u32[]{:S(2)}, u32[]{:S(2)}) collective-permute-start(f32[23,16,256]{2,1,0:T(8,128)S(1)} %broadcast_select_fusion.2), channel_id=1, source_target_pairs={{0,1},{1,0},{2,3},{3,2},{4,5},{5,4},{6,7},{7,6},{8,9},{9,8},{10,11... | collective-permute-start | bytes 1130504 | tf_op jit(solution)/shard_map/ppermute | solution.py:22
  86.0 12.4 %copy-start.3 = (bf16[2,64,64,256]{3,2,1,0:T(8,128)(2,1)}, bf16[2,64,64,256]{3,2,1,0:T(8,128)(2,1)S(1)}, u32[]{:S(2)}) copy-start(bf16[2,64,64,256]{3,2,1,0:T(8,128)(2,1)S(1)} %get-tuple-element.39.split01) | copy-start | bytes 12582916
  86.0 12.4 %copy-start.8 = (f32[8,80,256]{2,1,0:T(8,128)}, f32[8,80,256]{2,1,0:T(8,128)S(1)}, u32[]{:S(2)}) copy-start(f32[8,80,256]{2,1,0:T(8,128)S(1)} %get-tuple-element.41.root) | copy-start | bytes 1966084
  91.5 28.8 %copy-start.7 = (f32[16,2,64,256]{3,2,1,0:T(8,128)S(1)}, f32[16,2,64,256]{3,2,1,0:T(8,128)}, u32[]{:S(2)}) copy-start(f32[16,2,64,256]{3,2,1,0:T(8,128)} %iterate.1) | copy-start | bytes 6291460
  98.4 2.0 %copy-start.5 = (bf16[2,64,64,256]{3,2,1,0:T(8,128)(2,1)}, bf16[2,64,64,256]{3,2,1,0:T(8,128)(2,1)S(1)}, u32[]{:S(2)}) copy-start(bf16[2,64,64,256]{3,2,1,0:T(8,128)(2,1)S(1)} %get-tuple-element.40.split23) | copy-start | bytes 12582916
  120.4 2.2 %copy-start.4 = (bf16[2,64,64,256]{3,2,1,0:T(8,128)(2,1)S(1)}, bf16[2,64,64,256]{3,2,1,0:T(8,128)(2,1)}, u32[]{:S(2)}) copy-start(bf16[2,64,64,256]{3,2,1,0:T(8,128)(2,1)} %copy-done.3) | copy-start | bytes 12582916
  122.6 2.2 %copy-start.6 = (bf16[2,64,64,256]{3,2,1,0:T(8,128)(2,1)S(1)}, bf16[2,64,64,256]{3,2,1,0:T(8,128)(2,1)}, u32[]{:S(2)}) copy-start(bf16[2,64,64,256]{3,2,1,0:T(8,128)(2,1)} %copy-done.5) | copy-start | bytes 12582916
  124.8 1.1 copy-start.9

commit v11 on v10

--- a/solution.py
+++ b/solution.py
@@ -46,6 +46,19 @@
     other = moved(jnp.where(second, before, after), "gy", [(0, 1), (1, 0)])
     zero = jnp.zeros_like(other)
     return jnp.where(second, other, zero), jnp.where(second, zero, other)
+
+
+def all_sum(values, axes):
+    for axis in axes:
+        count = lax.axis_size(axis)
+        if count & (count - 1):
+            values = lax.psum(values, axis)
+            continue
+        step = 1
+        while step < count:
+            values = values + lax.ppermute(values, axis, [(i, i ^ step) for i in range(count)])
+            step *= 2
+    return values
 
 
 def face_of(center, beside):
@@ -97,16 +110,21 @@
     last[...] = mine[rows - REACH : rows]
 
 
-def near_kernel(odd, residual, mine, ahead, first, last, block, arrived):
+def near_kernel(odd, residual, mine, ahead, first, last, block, cells, arrived):
     rhs, _, rows, _ = residual.shape
-    copy = pltpu.make_async_copy(residual.at[:, 1 - odd[0]], block, arrived)
-    copy.start()
+    copies = [
+        pltpu.make_async_copy(mine.at[pl.ds(rows, cells.shape[0])], cells, arrived.at[0]),
+        pltpu.make_async_copy(residual.at[:, 1 - odd[0]], block, arrived.at[1]),
+    ]
+    for copy in copies:
+        copy.start()
+    copies[0].wait()
     count = rows // rhs
     for part in range(2 * count):
-        ahead[rows + part] = mine[rows + part]
+        ahead[rows + part] = cells[part]
     for part in range(count):
-        ahead[rows + 2 * count + part] = mine[rows + 3 * count + part]
-    copy.wait()
+        ahead[rows + 2 * count + part] = cells[3 * count + part]
+    copies[1].wait()
     turn_plane(block, ahead)
     first[...] = ahead[:REACH]
     last[...] = ahead[rows - REACH : rows]
@@ -467,7 +485,7 @@
         residual_out[:, 0, here] = by_rhs[rhs:] * root[plane + REACH, cells]
         return carry
 
-    lax.fori_loop(0, rows // 8, group_of_rows, 0)
+    lax.fori_loop(0, rows // 8, group_of_rows, 0, unroll=True)
 
 
 def on_device(iterate, residual, labels, boundary):
@@ -505,10 +523,10 @@
     ahead, near_first, near_last = pl.pallas_call(
         near_kernel,
         out_shape=(array(rows + 3 * count, rhs, nx),) + edge,
-        in_specs=[smem, hbm, vmem],
+        in_specs=[smem, hbm, hbm],
         out_specs=(vmem,) * 3,
-        scratch_shapes=[plane_block, pltpu.SemaphoreType.DMA],
-        compiler_params=params(58),
+        scratch_shapes=[plane_block, pltpu.VMEM((4 * count, rhs, nx), f32), pltpu.SemaphoreType.DMA((2,))],
+        compiler_params=params(52),
     )(odd, residual, mine)
     edges = jnp.stack([far_first, near_first]), jnp.stack([far_last, near_last])
 
@@ -565,7 +583,7 @@
         compiler_params=params(20),
     )(far2, u0, u1, u2, moments, inverse, sx, sy, sz)
 
-    moments = jnp.sum(lax.all_gather(moments, ("gz", "gy")), axis=0)
+    moments = all_sum(moments, ("gy", "gz"))
 
     tile = math.gcd(rows, 32)
     plane_rows = pl.BlockSpec((rhs, 1, tile, nx), lambda z, y, odd: (0, jnp.bitwise_xor(z, odd[0]), y, 0))

time: 134 us -> 117 us (0.87)
  blocking collectives: 19.9 us -> 0 us
  local copies, waits for them, and re-layouts: 8.77 us -> 0.02 us
  starting transfers between devices: 18.1 us -> 25.3 us
  waiting for transfers between devices: 50.3 us -> 57.1 us
  Pallas kernels: 35 us -> 33.6 us
    all_gather x1 -> x0, blocking collectives: 19.9 us -> none  [on_device(): moments = jnp.sum(lax.all_gather(moments, ('gz', 'gy')), axis=0)]
    unnamed x24 -> x8, local copies, waits for them, and re-layouts: 8.77 us -> 0.02 us
    ppermute x0 -> x4, starting transfers between devices: none -> 7.56 us  [all_sum(): lax.ppermute(values, axis, [(i, i ^ step) for i in range(count)])]
    ppermute x0 -> x4, waiting for transfers between devices: none -> 6.04 us  [all_sum(): lax.ppermute(values, axis, [(i, i ^ step) for i in range(count)])]
    pallas_call x1, Pallas kernels: 8.06 us -> 6.26 us  [on_device(): pl.pallas_call(outputs_kernel, out_shape=(array(*iterate.shape), array(*r...]
  transfers between devices with their start and end apart: 8 -> 12, of which waited for: 5 -> 9; matrix products, arithmetic and copies ran while one was open for 1% -> 0% of each run, Pallas kernels for 13% -> 15%
where the time goes in v11:
time: 117 us
  waiting for transfers between devices  57.1 us (49%)
  Pallas kernels  33.6 us (29%)
  starting transfers between devices  25.3 us (22%)
    ppermute x8, waiting for transfers between devices, moved(): return lax.ppermute(block, axis, pairs)  51.1 us
    ppermute x8, starting transfers between devices, moved(): return lax.ppermute(block, axis, pairs)  17.7 us
    pallas_call x1, Pallas kernels, on_device(): pl.pallas_call(partial(early_kernel, rows), out_shape=(array(*cells),) *...  12.5 us
    ppermute x4, starting transfers between devices, all_sum(): lax.ppermute(values, axis, [(i, i ^ step) for i in range(count)])  7.56 us
    pallas_call x1, Pallas kernels, on_device(): pl.pallas_call(partial(late_kernel, rows), out_shape=(array(rhs, 128), ar...  6.89 us
    pallas_call x1, Pallas kernels, on_device(): pl.pallas_call(outputs_kernel, out_shape=(array(*iterate.shape), array(*r...  6.26 us
    ppermute x4, waiting for transfers between devices, all_sum(): lax.ppermute(values, axis, [(i, i ^ step) for i in range(count)])  6.04 us
    pallas_call x1, Pallas kernels, on_device(): pl.pallas_call(far_kernel, out_shape=(array(rows + 4 * count, rhs, nx),)...  2.69 us
  transfers between devices with their start and end apart: 12, of which 9 were waited for; matrix products, arithmetic and copies ran while one was open for 0% of the time, Pallas kernels for 15%

profile of v11, /device:TPU:0, one launch (start us, length us, event | category | flops | bytes accessed | tf_op | source)
XLA Modules:
  0.0 117.0 jit_solution(780966912698323314)
XLA Ops:
  0.6 2.7 %shard_map.59 = (f32[80,16,256]{2,1,0:T(8,128)}, f32[3,16,256]{2,1,0:T(8,128)}, f32[3,16,256]{2,1,0:T(8,128)}) custom-call(s32[1]{0:T(128)} %bitcast.odd, f32[16,2,64,256]{3,2,1,0:T(8,128)} %residual.3, s32[2,64,256]{2,1,0:T(8,128)} %labels.1, s32[2,64,256]{2,1,0:T(8,128)} %boundary.1), custom_call_target="tpu_custom_call" | custom-call | tf_op jit(solution)/shard_map/pallas_call | solution.py:510
  3.3 0.0 copy-start.2
  3.3 0.0 copy-start.3
  3.4 0.0 copy-start
  3.4 3.0 %collective-permute-start.1 = (f32[80,16,256]{2,1,0:T(8,128)}, f32[80,16,256]{2,1,0:T(8,128)S(1)}, u32[]{:S(2)}, u32[]{:S(2)}) collective-permute-start(f32[80,16,256]{2,1,0:T(8,128)} %get-tuple-element.22.mine), channel_id=1, source_target_pairs={{0,2},{2,0},{4,6},{6,4},{8,10},{10,8},{12,14},{14,12},{1,3},{3,1},... | collective-permute-start | bytes 3932168 | tf_op jit(solution)/shard_map/ppermute | solution.py:22
  6.4 2.6 %shard_map.60 = (f32[76,16,256]{2,1,0:T(8,128)}, f32[3,16,256]{2,1,0:T(8,128)S(1)}, f32[3,16,256]{2,1,0:T(8,128)S(1)}) custom-call(s32[1]{0:T(128)} %bitcast.odd, f32[16,2,64,256]{3,2,1,0:T(8,128)} %residual.3, f32[80,16,256]{2,1,0:T(8,128)} %get-tuple-element.22.mine), custom_call_target="tpu_custom_call" | custom-call | tf_op jit(solution)/shard_map/pallas_call | solution.py:523
  9.0 4.6 %collective-permute-start.2 = (f32[76,16,256]{2,1,0:T(8,128)}, f32[76,16,256]{2,1,0:T(8,128)}, u32[]{:S(2)}, u32[]{:S(2)}) collective-permute-start(f32[76,16,256]{2,1,0:T(8,128)} %get-tuple-element.23.ahead), channel_id=1, source_target_pairs={{0,4},{4,8},{6,2},{8,12},{10,6},{14,10},{1,5},{5,9},{7,3},{9,13},{... | collective-permute-start | bytes 3735560 | tf_op jit(solution)/shard_map/ppermute | solution.py:22
  13.5 0.0 copy-done.2
  13.5 0.0 copy-done.3
  13.6 0.1 collective-permute-start
  13.6 0.0 copy-done
  13.6 1.3 %collective-permute-start.6 = (f32[80,16,256]{2,1,0:T(8,128)S(1)}, f32[80,16,256]{2,1,0:T(8,128)S(1)}, u32[]{:S(2)}, u32[]{:S(2)}) collective-permute-start(f32[80,16,256]{2,1,0:T(8,128)S(1)} %copy-done), channel_id=1, source_target_pairs={{4,0},{8,4},{2,6},{12,8},{6,10},{10,14},{5,1},{9,5},{3,7},{13,9},{... | collective-permute-start | bytes 3932168 | tf_op jit(solution)/shard_map/ppermute | solution.py:22
  14.9 20.4 %collective-permute-done.1.near2 = f32[80,16,256]{2,1,0:T(8,128)S(1)} collective-permute-done((f32[80,16,256]{2,1,0:T(8,128)}, f32[80,16,256]{2,1,0:T(8,128)S(1)}, u32[]{:S(2)}, u32[]{:S(2)}) %collective-permute-start.1) | collective-permute-done | bytes 1310752 | tf_op jit(solution)/shard_map/ppermute | solution.py:22
  35.4 3.8 %collective-permute-start.5 = (f32[80,16,256]{2,1,0:T(8,128)S(1)}, f32[80,16,256]{2,1,0:T(8,128)S(1)}, u32[]{:S(2)}, u32[]{:S(2)}) collective-permute-start(f32[80,16,256]{2,1,0:T(8,128)S(1)} %collective-permute-done.1.near2), channel_id=1, source_target_pairs={{0,4},{4,8},{6,2},{8,12},{10,6},{14,10},{1,5},{5,9},{7,3},{9,13},{... | collective-permute-start | bytes 3932168 | tf_op jit(solution)/shard_map/ppermute | solution.py:22
  39.2 0.0 collective-permute-done
  39.2 0.6 collective-permute-done.2.far3
  39.8 1.4 %shard_map.61 = f32[66,16,256]{2,1,0:T(8,128)S(1)} custom-call(f32[76,16,256]{2,1,0:T(8,128)} %get-tuple-element.23.ahead, f32[2,3,16,256]{3,2,1,0:T(8,128)S(1)} %get-tuple-element.45.own_before, f32[2,3,16,256]{3,2,1,0:T(8,128)S(1)} %get-tuple-element.44.own_behind, f32[80,16,256]{2,1,0:T(8,128)S(1)} %collective-permute-done.1.near2, ...), custom_call_target="tpu_custom_call" | custom-call | tf_op jit(solution)/shard_map/pallas_call | solution.py:538
  41.2 0.8 collective-permute-start.3
  41.9 23.3 %collective-permute-done.3.near1 = f32[66,16,256]{2,1,0:T(8,128)S(1)} collective-permute-done((f32[66,16,256]{2,1,0:T(8,128)S(1)}, f32[66,16,256]{2,1,0:T(8,128)S(1)}, u32[]{:S(2)}, u32[]{:S(2)}) %collective-permute-start.3) | collective-permute-done | bytes 1081376 | tf_op jit(solution)/shard_map/ppermute | solution.py:22
  65.2 4.2 %collective-permute-start.4 = (f32[66,16,256]{2,1,0:T(8,128)S(1)}, f32[66,16,256]{2,1,0:T(8,128)S(1)}, u32[]{:S(2)}, u32[]{:S(2)}) collective-permute-start(f32[66,16,256]{2,1,0:T(8,128)S(1)} %collective-permute-done.3.near1), channel_id=1, source_target_pairs={{0,4},{4,8},{6,2},{8,12},{10,6},{14,10},{1,5},{5,9},{7,3},{9,13},{... | collective-permute-start | bytes 3244040 | tf_op jit(solution)/shard_map/ppermute | solution.py:22
  69.4 0.0 collective-permute-done.6.near3
  69.4 0.0 collective-permute-done.5.far1
  69.4 1.3 %shard_map.62 = (f32[23,16,256]{2,1,0:T(8,128)S(1)}, f32[23,16,256]{2,1,0:T(8,128)S(1)}) custom-call(f32[66,16,256]{2,1,0:T(8,128)S(1)} %collective-permute-done.3.near1, f32[80,16,256]{2,1,0:T(8,128)S(1)} %collective-permute-done.1.near2, f32[80,16,256]{2,1,0:T(8,128)S(1)} %collective-permute-done.5.far1, f32[76,16,256]{2,1,0:T(8,128)} %collective-permute-done.2.far3, ...), custom_call_target="tpu_custom_call" | custom-call | tf_op jit(solution)/shard_map/pallas_call | solution.py:551
  70.8 0.1 broadcast_select_fusion.2
  70.8 0.1 collective-permute-start.7
  70.9 1.7 %collective-permute-done.7 = f32[23,16,256]{2,1,0:T(8,128)S(1)} collective-permute-done((f32[23,16,256]{2,1,0:T(8,128)S(1)}, f32[23,16,256]{2,1,0:T(8,128)S(1)}, u32[]{:S(2)}, u32[]{:S(2)}) %collective-permute-start.7) | collective-permute-done | bytes 376864 | tf_op jit(solution)/shard_map/ppermute | solution.py:22
  72.6 0.1 broadcast_select_fusion
  72.7 12.5 %shard_map.63 = (f32[8,80,256]{2,1,0:T(8,128)S(1)}, f32[8,80,256]{2,1,0:T(8,128)S(1)}, f32[8,80,256]{2,1,0:T(8,128)S(1)}, f32[8,80,256]{2,1,0:T(8,128)S(1)}, f32...) custom-call(f32[76,16,256]{2,1,0:T(8,128)} %collective-permute-done., ...), custom_call_target="tpu_custom_call" | custom-call | tf_op jit(solution)/shard_map/pallas_call | solution.py:564
  85.1 5.1 %collective-permute-done.4.far2 = f32[66,16,256]{2,1,0:T(8,128)S(1)} collective-permute-done((f32[66,16,256]{2,1,0:T(8,128)S(1)}, f32[66,16,256]{2,1,0:T(8,128)S(1)}, u32[]{:S(2)}, u32[]{:S(2)}) %collective-permute-start.4) | collective-permute-done | bytes 1081376 | tf_op jit(solution)/shard_map/ppermute | solution.py:22
  90.3 0.0 copy-start.1
  90.3 6.9 %shard_map.64 = (f32[16,128]{1,0:T(8,128)S(1)}, bf16[2,64,64,256]{3,2,1,0:T(8,128)(2,1)S(1)}) custom-call(f32[66,16,256]{2,1,0:T(8,128)S(1)} %collective-permute-done.4.far2, f32[3,70,16,256]{3,2,1,0:T(8,128)S(1)} %get-tuple-element.30.u0_in, f32[2,70,16,256]{3,2,1,0:T(8,128)S(1)} %get-tuple-element.31.u1_in, ...), custom_call_target="tpu_custom_call" | custom-call | tf_op jit(solution)/shard_map/pallas_call | solution.py:577
  97.2 0.0 collective-permute-start.8
  97.2 1.2 collective-permute-done.8
  98.3 2.3 %collective-permute-start.9 = (f32[16,128]{1,0:T(8,128)S(1)}, f32[16,128]{1,0:T(8,128)S(1)}, u32[]{:S(2)}, u32[]{:S(2)}) collective-permute-start(f32[16,128]{1,0:T(8,128)S(1)} %add.17), channel_id=1, source_target_pairs={{0,2},{2,0},{4,6},{6,4},{8,10},{10,8},{12,14},{14,12},{1,3},{3,1},... | collective-permute-start | bytes 24584 | tf_op jit(solution)/shard_map/ppermute | solution.py:59
  100.6 1.6 %collective-permute-done.9 = f32[16,128]{1,0:T(8,128)S(1)} collective-permute-done((f32[16,128]{1,0:T(8,128)S(1)}, f32[16,128]{1,0:T(8,128)S(1)}, u32[]{:S(2)}, u32[]{:S(2)}) %collective-permute-start.9) | collective-permute-done | bytes 8224 | tf_op jit(solution)/shard_map/ppermute | solution.py:59
  102.2 2.3 %collective-permute-start.10 = (f32[16,128]{1,0:T(8,128)S(1)}, f32[16,128]{1,0:T(8,128)S(1)}, u32[]{:S(2)}, u32[]{:S(2)}) collective-permute-start(f32[16,128]{1,0:T(8,128)S(1)} %add.18), channel_id=1, source_target_pairs={{0,4},{2,6},{4,0},{6,2},{8,12},{10,14},{12,8},{14,10},{1,5},{3,7},... | collective-permute-start | bytes 24584 | tf_op jit(solution)/shard_map/ppermute | solution.py:59
  104.5 1.6 %collective-permute-done.10 = f32[16,128]{1,0:T(8,128)S(1)} collective-permute-done((f32[16,128]{1,0:T(8,128)S(1)}, f32[16,128]{1,0:T(8,128)S(1)}, u32[]{:S(2)}, u32[]{:S(2)}) %collective-permute-start.10) | collective-permute-done | bytes 8224 | tf_op jit(solution)/shard_map/ppermute | solution.py:59
  106.1 3.0 %collective-permute-start.11 = (f32[16,128]{1,0:T(8,128)S(1)}, f32[16,128]{1,0:T(8,128)S(1)}, u32[]{:S(2)}, u32[]{:S(2)}) collective-permute-start(f32[16,128]{1,0:T(8,128)S(1)} %add.19), channel_id=1, source_target_pairs={{0,8},{2,10},{4,12},{6,14},{8,0},{10,2},{12,4},{14,6},{1,9},{3,11}... | collective-permute-start | bytes 24584 | tf_op jit(solution)/shard_map/ppermute | solution.py:59
  109.2 1.6 %collective-permute-done.11 = f32[16,128]{1,0:T(8,128)S(1)} collective-permute-done((f32[16,128]{1,0:T(8,128)S(1)}, f32[16,128]{1,0:T(8,128)S(1)}, u32[]{:S(2)}, u32[]{:S(2)}) %collective-permute-start.11) | collective-permute-done | bytes 8224 | tf_op jit(solution)/shard_map/ppermute | solution.py:59
  110.8 0.0 copy-done.1
  110.8 6.3 %shard_map.65 = (f32[16,2,64,256]{3,2,1,0:T(8,128)}, f32[16,2,64,256]{3,2,1,0:T(8,128)}) custom-call(s32[1]{0:T(128)} %bitcast.odd, f32[16,128]{1,0:T(8,128)S(1)} %add.20.moments, bf16[2,64,64,256]{3,2,1,0:T(8,128)(2,1)S(1)} %get-tuple-element.39.split01, bf16[2,64,64,256]{3,2,1,0:T(8,128)(2,1)S(1)} %get-tuple-element.40.split23, ...), custom_call_target="tpu_custom_call" | custom-call | tf_op jit(solution)/shard_map/pallas_call | solution.py:590
  (6 shorter events, 0.0 us)
Async XLA Ops:
  3.3 10.2 %copy-start.2 = (f32[3,16,256]{2,1,0:T(8,128)S(1)}, f32[3,16,256]{2,1,0:T(8,128)}, u32[]{:S(2)}) copy-start(f32[3,16,256]{2,1,0:T(8,128)} %get-tuple-element.24) | copy-start | bytes 147460
  3.3 10.2 %copy-start.3 = (f32[3,16,256]{2,1,0:T(8,128)S(1)}, f32[3,16,256]{2,1,0:T(8,128)}, u32[]{:S(2)}) copy-start(f32[3,16,256]{2,1,0:T(8,128)} %get-tuple-element.26) | copy-start | bytes 147460
  3.4 10.3 %copy-start = (f32[80,16,256]{2,1,0:T(8,128)S(1)}, f32[80,16,256]{2,1,0:T(8,128)}, u32[]{:S(2)}) copy-start(f32[80,16,256]{2,1,0:T(8,128)} %get-tuple-element.22.mine) | copy-start | bytes 3932164
  3.4 32.0 %collective-permute-start.1 = (f32[80,16,256]{2,1,0:T(8,128)}, f32[80,16,256]{2,1,0:T(8,128)S(1)}, u32[]{:S(2)}, u32[]{:S(2)}) collective-permute-start(f32[80,16,256]{2,1,0:T(8,128)} %get-tuple-element.22.mine), channel_id=1, source_target_pairs={{0,2},{2,0},{4,6},{6,4},{8,10},{10,8},{12,14},{14,12},{1,3},{3,1},... | collective-permute-start | bytes 3932168 | tf_op jit(solution)/shard_map/ppermute | solution.py:22
  9.0 30.8 %collective-permute-start.2 = (f32[76,16,256]{2,1,0:T(8,128)}, f32[76,16,256]{2,1,0:T(8,128)}, u32[]{:S(2)}, u32[]{:S(2)}) collective-permute-start(f32[76,16,256]{2,1,0:T(8,128)} %get-tuple-element.23.ahead), channel_id=1, source_target_pairs={{0,4},{4,8},{6,2},{8,12},{10,6},{14,10},{1,5},{5,9},{7,3},{9,13},{... | collective-permute-start | bytes 3735560 | tf_op jit(solution)/shard_map/ppermute | solution.py:22
  13.6 25.6 %collective-permute-start = (f32[2,3,16,256]{3,2,1,0:T(8,128)S(1)}, f32[2,3,16,256]{3,2,1,0:T(8,128)S(1)}, u32[]{:S(2)}, u32[]{:S(2)}) collective-permute-start(f32[2,3,16,256]{3,2,1,0:T(8,128)S(1)} %maximum_select_fusion), channel_id=1, source_target_pairs={{0,1},{1,0},{2,3},{3,2},{4,5},{5,4},{6,7},{7,6},{8,9},{9,8},{10,11... | collective-permute-start | bytes 294920 | tf_op jit(solution)/shard_map/ppermute | solution.py:22
  13.6 55.8 %collective-permute-start.6 = (f32[80,16,256]{2,1,0:T(8,128)S(1)}, f32[80,16,256]{2,1,0:T(8,128)S(1)}, u32[]{:S(2)}, u32[]{:S(2)}) collective-permute-start(f32[80,16,256]{2,1,0:T(8,128)S(1)} %copy-done), channel_id=1, source_target_pairs={{4,0},{8,4},{2,6},{12,8},{6,10},{10,14},{5,1},{9,5},{3,7},{13,9},{... | collective-permute-start | bytes 3932168 | tf_op jit(solution)/shard_map/ppermute | solution.py:22
  35.4 34.1 %collective-permute-start.5 = (f32[80,16,256]{2,1,0:T(8,128)S(1)}, f32[80,16,256]{2,1,0:T(8,128)S(1)}, u32[]{:S(2)}, u32[]{:S(2)}) collective-permute-start(f32[80,16,256]{2,1,0:T(8,128)S(1)} %collective-permute-done.1.near2), channel_id=1, source_target_pairs={{0,4},{4,8},{6,2},{8,12},{10,6},{14,10},{1,5},{5,9},{7,3},{9,13},{... | collective-permute-start | bytes 3932168 | tf_op jit(solution)/shard_map/ppermute | solution.py:22
  41.2 24.1 %collective-permute-start.3 = (f32[66,16,256]{2,1,0:T(8,128)S(1)}, f32[66,16,256]{2,1,0:T(8,128)S(1)}, u32[]{:S(2)}, u32[]{:S(2)}) collective-permute-start(f32[66,16,256]{2,1,0:T(8,128)S(1)} %shard_map.61), channel_id=1, source_target_pairs={{0,2},{2,0},{4,6},{6,4},{8,10},{10,8},{12,14},{14,12},{1,3},{3,1},... | collective-permute-start | bytes 3244040 | tf_op jit(solution)/shard_map/ppermute | solution.py:22
  65.2 25.0 %collective-permute-start.4 = (f32[66,16,256]{2,1,0:T(8,128)S(1)}, f32[66,16,256]{2,1,0:T(8,128)S(1)}, u32[]{:S(2)}, u32[]{:S(2)}) collective-permute-start(f32[66,16,256]{2,1,0:T(8,128)S(1)} %collective-permute-done.3.near1), channel_id=1, source_target_pairs={{0,4},{4,8},{6,2},{8,12},{10,6},{14,10},{1,5},{5,9},{7,3},{9,13},{... | collective-permute-start | bytes 3244040 | tf_op jit(solution)/shard_map/ppermute | solution.py:22
  70.8 1.8 %collective-permute-start.7 = (f32[23,16,256]{2,1,0:T(8,128)S(1)}, f32[23,16,256]{2,1,0:T(8,128)S(1)}, u32[]{:S(2)}, u32[]{:S(2)}) collective-permute-start(f32[23,16,256]{2,1,0:T(8,128)S(1)} %broadcast_select_fusion.2), channel_id=1, source_target_pairs={{0,1},{1,0},{2,3},{3,2},{4,5},{5,4},{6,7},{7,6},{8,9},{9,8},{10,11... | collective-permute-start | bytes 1130504 | tf_op jit(solution)/shard_map/ppermute | solution.py:22
  90.3 20.5 %copy-start.1 = (f32[16,2,64,256]{3,2,1,0:T(8,128)S(1)}, f32[16,2,64,256]{3,2,1,0:T(8,128)}, u32[]{:S(2)}) copy-start(f32[16,2,64,256]{3,2,1,0:T(8,128)} %iterate.1) | copy-start | bytes 6291460
  97.2 1.2 %collective-permute-start.8 = (f32[16,128]{1,0:T(8,128)S(1)}, f32[16,128]{1,0:T(8,128)S(1)}, u32[]{:S(2)}, u32[]{:S(2)}) collective-permute-start(f32[16,128]{1,0:T(8,128)S(1)} %get-tuple-element.38), channel_id=1, source_target_pairs={{0,1},{1,0},{2,3},{3,2},{4,5},{5,4},{6,7},{7,6},{8,9},{9,8},{10,11... | collective-permute-start | bytes 24584 | tf_op jit(solution)/shard_map/ppermute | solution.py:59
  98.3 3.9 %collective-permute-start.9 = (f32[16,128]{1,0:T(8,128)S(1)}, f32[16,128]{1,0:T(8,128)S(1)}, u32[]{:S(2)}, u32[]{:S(2)}) collective-permute-start(f32[16,128]{1,0:T(8,128)S(1)} %add.17), channel_id=1, source_target_pairs={{0,2},{2,0},{4,6},{6,4},{8,10},{10,8},{12,14},{14,12},{1,3},{3,1},... | collective-permute-start | bytes 24584 | tf_op jit(solution)/shard_map/ppermute | solution.py:59
  102.2 3.9 %collective-permute-start.10 = (f32[16,128]{1,0:T(8,128)S(1)}, f32[16,128]{1,0:T(8,128)S(1)}, u32[]{:S(2)}, u32[]{:S(2)}) collective-permute-start(f32[16,128]{1,0:T(8,128)S(1)} %add.18), channel_id=1, source_target_pairs={{0,4},{2,6},{4,0},{6,2},{8,12},{10,14},{12,8},{14,10},{1,5},{3,7},... | collective-permute-start | bytes 24584 | tf_op jit(solution)/shard_map/ppermute | solution.py:59
  106.1 4.7 %collective-permute-start.11 = (f32[16,128]{1,0:T(8,128)S(1)}, f32[16,128]{1,0:T(8,128)S(1)}, u32[]{:S(2)}, u32[]{:S(2)}) collective-permute-start(f32[16,128]{1,0:T(8,128)S(1)} %add.19), channel_id=1, source_target_pairs={{0,8},{2,10},{4,12},{6,14},{8,0},{10,2},{12,4},{14,6},{1,9},{3,11}... | collective-permute-start | bytes 24584 | tf_op jit(solution)/shard_map/ppermute | solution.py:59

commit v12 on v11

--- a/solution.py
+++ b/solution.py
@@ -130,9 +130,11 @@
     last[...] = ahead[rows - REACH : rows]
 
 
-def second_kernel(rows, ahead, own_before, own_behind, near2, far3, out):
-    del near2, far3
-
+def hand_on(message, earlier, out):
+    del message, earlier, out
+
+
+def second_kernel(rows, ahead, own_before, own_behind, out):
     def copy_rows(y, size):
         for j in range(size):
             out[y + j] = ahead[y + j]
@@ -219,7 +221,7 @@
     return ref[plane, pl.ds(y + (MARGIN - REACH), 1), :]
 
 
-def row_blocks(start, stop, body, size):
+def row_blocks(start, stop, body, size, unroll=1):
     blocks = -(-(stop - start) // size)
     size = -(-(stop - start) // blocks)
 
@@ -227,7 +229,7 @@
         body(jnp.minimum(start + block * size, stop - size), size)
         return carry
 
-    lax.fori_loop(0, blocks, step, 0)
+    lax.fori_loop(0, blocks, step, 0, unroll=min(unroll, blocks))
 
 
 def apply_rows(operator, plane, start, before, here, after, size):
@@ -268,7 +270,7 @@
         row_blocks(0, count, body, 16)
 
 
-def apply_plane(rows, power, plane, operator, fields):
+def apply_plane(rows, power, plane, operator, fields, unroll=1):
     reach = REACH - power - spread(plane)
     src = [fields[power - 1, plane + offset] for offset in (-1, 0, 1)]
     out, place = fields[power, plane]
@@ -277,7 +279,7 @@
         for j, values in enumerate(apply_rows(operator, plane, y, *src, size)):
             out[place, y + j] = values
 
-    row_blocks(REACH - reach, REACH + rows + reach, body, 34)
+    row_blocks(REACH - reach, REACH + rows + reach, body, 34, unroll)
 
 
 def halves(blocks):
@@ -355,7 +357,7 @@
     for place, start, count in ((0, first, rows), (rows, first - 1, 1), (rows + 1, last, 1)):
         scale_rows(LATE, far2, place, fields[0, LATE], start, count, inverse)
     for power, plane in ((1, 1), (1, 2), (2, 2), (2, 3)):
-        apply_plane(rows, power, plane, operator, fields)
+        apply_plane(rows, power, plane, operator, fields, 2)
 
     rhs = u0.shape[2]
     gram = jnp.zeros((6 * rhs, 2 * rhs), f32)
@@ -377,7 +379,7 @@
                 total = total + inner_products(jnp.concatenate(left, axis=1), jnp.concatenate(right, axis=1))
             return total
 
-        gram = lax.fori_loop(0, rows // 16, gram_rows, gram)
+        gram = lax.fori_loop(0, rows // 16, gram_rows, gram, unroll=2)
     gram = gram[:, :rhs] + gram[:, rhs:]
     blocks = [gram[part * rhs : (part + 1) * rhs] for part in range(6)]
     moments[:, : 3 * rhs] = moments_in[:, : 3 * rhs]
@@ -530,19 +532,29 @@
     )(odd, residual, mine)
     edges = jnp.stack([far_first, near_first]), jnp.stack([far_last, near_last])
 
-    near2 = swapped(mine)
+    first_swap = swapped(mine)
     far3 = relayed(ahead)
     near3 = relayed(mine, back=True)
     own_before, own_behind = rows_beside(*edges)
-    near1 = swapped(
-        pl.pallas_call(
-            partial(second_kernel, rows),
-            out_shape=array(rows + 2, rhs, nx),
-            in_specs=[vmem, vmem, vmem, anywhere, anywhere],
-            out_specs=vmem,
+    second = pl.pallas_call(
+        partial(second_kernel, rows),
+        out_shape=array(rows + 2, rhs, nx),
+        in_specs=[vmem] * 3,
+        out_specs=vmem,
+        compiler_params=params(8),
+    )(ahead, own_before, own_behind)
+    def handed_on(block, earlier):
+        return pl.pallas_call(
+            hand_on,
+            out_shape=array(*block.shape),
+            in_specs=[anywhere] * 2,
+            out_specs=anywhere,
+            input_output_aliases={0: 0},
             compiler_params=params(8),
-        )(ahead, own_before, own_behind, near2, far3)
-    )
+        )(block, earlier)
+
+    near2 = handed_on(first_swap, second)
+    near1 = swapped(handed_on(second, far3))
     far1 = relayed(near2)
     far2 = relayed(near1)
 

time: 117 us -> 117 us (level)
  transfers between devices with their start and end apart: 12 -> 12, of which waited for: 9 -> 10; matrix products, arithmetic and copies ran while one was open for 0% -> 0% of each run, Pallas kernels for 15% -> 15%
where the time goes in v12:
time: 117 us
  waiting for transfers between devices  57.6 us (49%)
  Pallas kernels  33.1 us (28%)
  starting transfers between devices  24.8 us (21%)
    ppermute x8, waiting for transfers between devices, moved(): return lax.ppermute(block, axis, pairs)  51.2 us
    ppermute x8, starting transfers between devices, moved(): return lax.ppermute(block, axis, pairs)  17.6 us
    pallas_call x1, Pallas kernels, on_device(): pl.pallas_call(partial(early_kernel, rows), out_shape=(array(*cells),) *...  12.5 us
    ppermute x4, starting transfers between devices, all_sum(): lax.ppermute(values, axis, [(i, i ^ step) for i in range(count)])  7.18 us
    ppermute x4, waiting for transfers between devices, all_sum(): lax.ppermute(values, axis, [(i, i ^ step) for i in range(count)])  6.42 us
    pallas_call x1, Pallas kernels, on_device(): pl.pallas_call(partial(late_kernel, rows), out_shape=(array(rhs, 128), ar...  6.39 us
    pallas_call x1, Pallas kernels, on_device(): pl.pallas_call(outputs_kernel, out_shape=(array(*iterate.shape), array(*r...  6.26 us
    pallas_call x1, Pallas kernels, on_device(): pl.pallas_call(far_kernel, out_shape=(array(rows + 4 * count, rhs, nx),)...  2.69 us
  transfers between devices with their start and end apart: 12, of which 10 were waited for; matrix products, arithmetic and copies ran while one was open for 0% of the time, Pallas kernels for 15%

profile of v12, /device:TPU:0, one launch (start us, length us, event | category | flops | bytes accessed | tf_op | source)
XLA Modules:
  0.0 116.5 jit_solution(14561272284078429299)
XLA Ops:
  0.6 2.7 %shard_map.59 = (f32[80,16,256]{2,1,0:T(8,128)}, f32[3,16,256]{2,1,0:T(8,128)}, f32[3,16,256]{2,1,0:T(8,128)}) custom-call(s32[1]{0:T(128)} %bitcast.odd, f32[16,2,64,256]{3,2,1,0:T(8,128)} %residual.3, s32[2,64,256]{2,1,0:T(8,128)} %labels.1, s32[2,64,256]{2,1,0:T(8,128)} %boundary.1), custom_call_target="tpu_custom_call" | custom-call | tf_op jit(solution)/shard_map/pallas_call | solution.py:512
  3.3 0.0 copy-start.2
  3.3 0.0 copy-start.3
  3.4 0.0 copy-start
  3.4 3.0 %collective-permute-start.4 = (f32[80,16,256]{2,1,0:T(8,128)}, f32[80,16,256]{2,1,0:T(8,128)S(1)}, u32[]{:S(2)}, u32[]{:S(2)}) collective-permute-start(f32[80,16,256]{2,1,0:T(8,128)} %get-tuple-element.22.mine), channel_id=1, source_target_pairs={{0,2},{2,0},{4,6},{6,4},{8,10},{10,8},{12,14},{14,12},{1,3},{3,1},... | collective-permute-start | bytes 3932168 | tf_op jit(solution)/shard_map/ppermute | solution.py:22
  6.4 2.6 %shard_map.60 = (f32[76,16,256]{2,1,0:T(8,128)}, f32[3,16,256]{2,1,0:T(8,128)S(1)}, f32[3,16,256]{2,1,0:T(8,128)S(1)}) custom-call(s32[1]{0:T(128)} %bitcast.odd, f32[16,2,64,256]{3,2,1,0:T(8,128)} %residual.3, f32[80,16,256]{2,1,0:T(8,128)} %get-tuple-element.22.mine), custom_call_target="tpu_custom_call" | custom-call | tf_op jit(solution)/shard_map/pallas_call | solution.py:525
  9.0 4.6 %collective-permute-start.1 = (f32[76,16,256]{2,1,0:T(8,128)}, f32[76,16,256]{2,1,0:T(8,128)}, u32[]{:S(2)}, u32[]{:S(2)}) collective-permute-start(f32[76,16,256]{2,1,0:T(8,128)} %get-tuple-element.23.ahead), channel_id=1, source_target_pairs={{0,4},{4,8},{6,2},{8,12},{10,6},{14,10},{1,5},{5,9},{7,3},{9,13},{... | collective-permute-start | bytes 3735560 | tf_op jit(solution)/shard_map/ppermute | solution.py:22
  13.5 0.0 copy-done.2
  13.5 0.0 copy-done.3
  13.6 0.1 collective-permute-start
  13.6 0.0 copy-done
  13.6 1.3 %collective-permute-start.6 = (f32[80,16,256]{2,1,0:T(8,128)S(1)}, f32[80,16,256]{2,1,0:T(8,128)S(1)}, u32[]{:S(2)}, u32[]{:S(2)}) collective-permute-start(f32[80,16,256]{2,1,0:T(8,128)S(1)} %copy-done), channel_id=1, source_target_pairs={{4,0},{8,4},{2,6},{12,8},{6,10},{10,14},{5,1},{9,5},{3,7},{13,9},{... | collective-permute-start | bytes 3932168 | tf_op jit(solution)/shard_map/ppermute | solution.py:22
  14.9 0.0 collective-permute-done
  15.0 1.4 %shard_map.61.message.earlier = f32[66,16,256]{2,1,0:T(8,128)S(1)} custom-call(f32[76,16,256]{2,1,0:T(8,128)} %get-tuple-element.23.ahead, f32[2,3,16,256]{3,2,1,0:T(8,128)S(1)} %get-tuple-element.45.own_before, f32[2,3,16,256]{3,2,1,0:T(8,128)S(1)} %get-tuple-element.44.own_behind), custom_call_target="tpu_custom_call" | custom-call | tf_op jit(solution)/shard_map/pallas_call | solution.py:539
  16.4 19.0 %collective-permute-done.4.message = f32[80,16,256]{2,1,0:T(8,128)S(1)} collective-permute-done((f32[80,16,256]{2,1,0:T(8,128)}, f32[80,16,256]{2,1,0:T(8,128)S(1)}, u32[]{:S(2)}, u32[]{:S(2)}) %collective-permute-start.4) | collective-permute-done | bytes 1310752 | tf_op jit(solution)/shard_map/ppermute | solution.py:22
  35.4 3.8 %collective-permute-start.5 = (f32[80,16,256]{2,1,0:T(8,128)S(1)}, f32[80,16,256]{2,1,0:T(8,128)S(1)}, u32[]{:S(2)}, u32[]{:S(2)}) collective-permute-start(f32[80,16,256]{2,1,0:T(8,128)S(1)} %shard_map.63.near2), channel_id=1, source_target_pairs={{0,4},{4,8},{6,2},{8,12},{10,6},{14,10},{1,5},{5,9},{7,3},{9,13},{... | collective-permute-start | bytes 3932168 | tf_op jit(solution)/shard_map/ppermute | solution.py:22
  39.2 0.6 collective-permute-done.1.earlier.far3
  39.8 0.7 collective-permute-start.2
  40.5 23.3 %collective-permute-done.2.near1 = f32[66,16,256]{2,1,0:T(8,128)S(1)} collective-permute-done((f32[66,16,256]{2,1,0:T(8,128)S(1)}, f32[66,16,256]{2,1,0:T(8,128)S(1)}, u32[]{:S(2)}, u32[]{:S(2)}) %collective-permute-start.2) | collective-permute-done | bytes 1081376 | tf_op jit(solution)/shard_map/ppermute | solution.py:22
  63.8 4.1 %collective-permute-start.3 = (f32[66,16,256]{2,1,0:T(8,128)S(1)}, f32[66,16,256]{2,1,0:T(8,128)S(1)}, u32[]{:S(2)}, u32[]{:S(2)}) collective-permute-start(f32[66,16,256]{2,1,0:T(8,128)S(1)} %collective-permute-done.2.near1), channel_id=1, source_target_pairs={{0,4},{4,8},{6,2},{8,12},{10,6},{14,10},{1,5},{5,9},{7,3},{9,13},{... | collective-permute-start | bytes 3244040 | tf_op jit(solution)/shard_map/ppermute | solution.py:22
  68.0 0.0 collective-permute-done.6.near3
  68.0 0.3 collective-permute-done.5.far1
  68.3 1.3 %shard_map.64 = (f32[23,16,256]{2,1,0:T(8,128)S(1)}, f32[23,16,256]{2,1,0:T(8,128)S(1)}) custom-call(f32[66,16,256]{2,1,0:T(8,128)S(1)} %collective-permute-done.2.near1, f32[80,16,256]{2,1,0:T(8,128)S(1)} %shard_map.63.near2, f32[80,16,256]{2,1,0:T(8,128)S(1)} %collective-permute-done.5.far1, f32[76,16,256]{2,1,0:T(8,128)} %collective-permute-done.1.earlier.far3, ...), custom_call_target="tpu_custom_call" | custom-call | tf_op jit(solution)/shard_map/pallas_call | solution.py:563
  69.6 0.1 broadcast_select_fusion.2
  69.7 0.1 collective-permute-start.7
  69.8 1.7 %collective-permute-done.7 = f32[23,16,256]{2,1,0:T(8,128)S(1)} collective-permute-done((f32[23,16,256]{2,1,0:T(8,128)S(1)}, f32[23,16,256]{2,1,0:T(8,128)S(1)}, u32[]{:S(2)}, u32[]{:S(2)}) %collective-permute-start.7) | collective-permute-done | bytes 376864 | tf_op jit(solution)/shard_map/ppermute | solution.py:22
  71.5 0.1 broadcast_select_fusion
  71.6 12.5 %shard_map.65 = (f32[8,80,256]{2,1,0:T(8,128)S(1)}, f32[8,80,256]{2,1,0:T(8,128)S(1)}, f32[8,80,256]{2,1,0:T(8,128)S(1)}, f32[8,80,256]{2,1,0:T(8,128)S(1)}, f32...) custom-call(f32[76,16,256]{2,1,0:T(8,128)} %collective-permute-done., ...), custom_call_target="tpu_custom_call" | custom-call | tf_op jit(solution)/shard_map/pallas_call | solution.py:576
  84.0 6.2 %collective-permute-done.3.far2 = f32[66,16,256]{2,1,0:T(8,128)S(1)} collective-permute-done((f32[66,16,256]{2,1,0:T(8,128)S(1)}, f32[66,16,256]{2,1,0:T(8,128)S(1)}, u32[]{:S(2)}, u32[]{:S(2)}) %collective-permute-start.3) | collective-permute-done | bytes 1081376 | tf_op jit(solution)/shard_map/ppermute | solution.py:22
  90.3 0.0 copy-start.1
  90.3 6.4 %shard_map.66 = (f32[16,128]{1,0:T(8,128)S(1)}, bf16[2,64,64,256]{3,2,1,0:T(8,128)(2,1)S(1)}) custom-call(f32[66,16,256]{2,1,0:T(8,128)S(1)} %collective-permute-done.3.far2, f32[3,70,16,256]{3,2,1,0:T(8,128)S(1)} %get-tuple-element.30.u0_in, f32[2,70,16,256]{3,2,1,0:T(8,128)S(1)} %get-tuple-element.31.u1_in, ...), custom_call_target="tpu_custom_call" | custom-call | tf_op jit(solution)/shard_map/pallas_call | solution.py:589
  96.7 0.0 collective-permute-start.8
  96.7 1.2 collective-permute-done.8
  97.8 1.6 %collective-permute-start.9 = (f32[16,128]{1,0:T(8,128)S(1)}, f32[16,128]{1,0:T(8,128)S(1)}, u32[]{:S(2)}, u32[]{:S(2)}) collective-permute-start(f32[16,128]{1,0:T(8,128)S(1)} %add.17), channel_id=1, source_target_pairs={{0,2},{2,0},{4,6},{6,4},{8,10},{10,8},{12,14},{14,12},{1,3},{3,1},... | collective-permute-start | bytes 24584 | tf_op jit(solution)/shard_map/ppermute | solution.py:59
  99.5 2.0 %collective-permute-done.9 = f32[16,128]{1,0:T(8,128)S(1)} collective-permute-done((f32[16,128]{1,0:T(8,128)S(1)}, f32[16,128]{1,0:T(8,128)S(1)}, u32[]{:S(2)}, u32[]{:S(2)}) %collective-permute-start.9) | collective-permute-done | bytes 8224 | tf_op jit(solution)/shard_map/ppermute | solution.py:59
  101.5 2.5 %collective-permute-start.10 = (f32[16,128]{1,0:T(8,128)S(1)}, f32[16,128]{1,0:T(8,128)S(1)}, u32[]{:S(2)}, u32[]{:S(2)}) collective-permute-start(f32[16,128]{1,0:T(8,128)S(1)} %add.18), channel_id=1, source_target_pairs={{0,4},{2,6},{4,0},{6,2},{8,12},{10,14},{12,8},{14,10},{1,5},{3,7},... | collective-permute-start | bytes 24584 | tf_op jit(solution)/shard_map/ppermute | solution.py:59
  104.0 1.6 %collective-permute-done.10 = f32[16,128]{1,0:T(8,128)S(1)} collective-permute-done((f32[16,128]{1,0:T(8,128)S(1)}, f32[16,128]{1,0:T(8,128)S(1)}, u32[]{:S(2)}, u32[]{:S(2)}) %collective-permute-start.10) | collective-permute-done | bytes 8224 | tf_op jit(solution)/shard_map/ppermute | solution.py:59
  105.6 3.0 %collective-permute-start.11 = (f32[16,128]{1,0:T(8,128)S(1)}, f32[16,128]{1,0:T(8,128)S(1)}, u32[]{:S(2)}, u32[]{:S(2)}) collective-permute-start(f32[16,128]{1,0:T(8,128)S(1)} %add.19), channel_id=1, source_target_pairs={{0,8},{2,10},{4,12},{6,14},{8,0},{10,2},{12,4},{14,6},{1,9},{3,11}... | collective-permute-start | bytes 24584 | tf_op jit(solution)/shard_map/ppermute | solution.py:59
  108.6 1.6 %collective-permute-done.11 = f32[16,128]{1,0:T(8,128)S(1)} collective-permute-done((f32[16,128]{1,0:T(8,128)S(1)}, f32[16,128]{1,0:T(8,128)S(1)}, u32[]{:S(2)}, u32[]{:S(2)}) %collective-permute-start.11) | collective-permute-done | bytes 8224 | tf_op jit(solution)/shard_map/ppermute | solution.py:59
  110.3 0.0 copy-done.1
  110.3 6.3 %shard_map.67 = (f32[16,2,64,256]{3,2,1,0:T(8,128)}, f32[16,2,64,256]{3,2,1,0:T(8,128)}) custom-call(s32[1]{0:T(128)} %bitcast.odd, f32[16,128]{1,0:T(8,128)S(1)} %add.20.moments, bf16[2,64,64,256]{3,2,1,0:T(8,128)(2,1)S(1)} %get-tuple-element.39.split01, bf16[2,64,64,256]{3,2,1,0:T(8,128)(2,1)S(1)} %get-tuple-element.40.split23, ...), custom_call_target="tpu_custom_call" | custom-call | tf_op jit(solution)/shard_map/pallas_call | solution.py:602
  (8 shorter events, 0.0 us)
Async XLA Ops:
  3.3 10.2 %copy-start.2 = (f32[3,16,256]{2,1,0:T(8,128)S(1)}, f32[3,16,256]{2,1,0:T(8,128)}, u32[]{:S(2)}) copy-start(f32[3,16,256]{2,1,0:T(8,128)} %get-tuple-element.24) | copy-start | bytes 147460
  3.3 10.2 %copy-start.3 = (f32[3,16,256]{2,1,0:T(8,128)S(1)}, f32[3,16,256]{2,1,0:T(8,128)}, u32[]{:S(2)}) copy-start(f32[3,16,256]{2,1,0:T(8,128)} %get-tuple-element.26) | copy-start | bytes 147460
  3.4 10.3 %copy-start = (f32[80,16,256]{2,1,0:T(8,128)S(1)}, f32[80,16,256]{2,1,0:T(8,128)}, u32[]{:S(2)}) copy-start(f32[80,16,256]{2,1,0:T(8,128)} %get-tuple-element.22.mine) | copy-start | bytes 3932164
  3.4 32.0 %collective-permute-start.4 = (f32[80,16,256]{2,1,0:T(8,128)}, f32[80,16,256]{2,1,0:T(8,128)S(1)}, u32[]{:S(2)}, u32[]{:S(2)}) collective-permute-start(f32[80,16,256]{2,1,0:T(8,128)} %get-tuple-element.22.mine), channel_id=1, source_target_pairs={{0,2},{2,0},{4,6},{6,4},{8,10},{10,8},{12,14},{14,12},{1,3},{3,1},... | collective-permute-start | bytes 3932168 | tf_op jit(solution)/shard_map/ppermute | solution.py:22
  9.0 30.8 %collective-permute-start.1 = (f32[76,16,256]{2,1,0:T(8,128)}, f32[76,16,256]{2,1,0:T(8,128)}, u32[]{:S(2)}, u32[]{:S(2)}) collective-permute-start(f32[76,16,256]{2,1,0:T(8,128)} %get-tuple-element.23.ahead), channel_id=1, source_target_pairs={{0,4},{4,8},{6,2},{8,12},{10,6},{14,10},{1,5},{5,9},{7,3},{9,13},{... | collective-permute-start | bytes 3735560 | tf_op jit(solution)/shard_map/ppermute | solution.py:22
  13.6 1.4 %collective-permute-start = (f32[2,3,16,256]{3,2,1,0:T(8,128)S(1)}, f32[2,3,16,256]{3,2,1,0:T(8,128)S(1)}, u32[]{:S(2)}, u32[]{:S(2)}) collective-permute-start(f32[2,3,16,256]{3,2,1,0:T(8,128)S(1)} %maximum_select_fusion), channel_id=1, source_target_pairs={{0,1},{1,0},{2,3},{3,2},{4,5},{5,4},{6,7},{7,6},{8,9},{9,8},{10,11... | collective-permute-start | bytes 294920 | tf_op jit(solution)/shard_map/ppermute | solution.py:22
  13.6 54.3 %collective-permute-start.6 = (f32[80,16,256]{2,1,0:T(8,128)S(1)}, f32[80,16,256]{2,1,0:T(8,128)S(1)}, u32[]{:S(2)}, u32[]{:S(2)}) collective-permute-start(f32[80,16,256]{2,1,0:T(8,128)S(1)} %copy-done), channel_id=1, source_target_pairs={{4,0},{8,4},{2,6},{12,8},{6,10},{10,14},{5,1},{9,5},{3,7},{13,9},{... | collective-permute-start | bytes 3932168 | tf_op jit(solution)/shard_map/ppermute | solution.py:22
  35.4 32.9 %collective-permute-start.5 = (f32[80,16,256]{2,1,0:T(8,128)S(1)}, f32[80,16,256]{2,1,0:T(8,128)S(1)}, u32[]{:S(2)}, u32[]{:S(2)}) collective-permute-start(f32[80,16,256]{2,1,0:T(8,128)S(1)} %shard_map.63.near2), channel_id=1, source_target_pairs={{0,4},{4,8},{6,2},{8,12},{10,6},{14,10},{1,5},{5,9},{7,3},{9,13},{... | collective-permute-start | bytes 3932168 | tf_op jit(solution)/shard_map/ppermute | solution.py:22
  39.8 24.0 %collective-permute-start.2 = (f32[66,16,256]{2,1,0:T(8,128)S(1)}, f32[66,16,256]{2,1,0:T(8,128)S(1)}, u32[]{:S(2)}, u32[]{:S(2)}) collective-permute-start(f32[66,16,256]{2,1,0:T(8,128)S(1)} %shard_map.62), channel_id=1, source_target_pairs={{0,2},{2,0},{4,6},{6,4},{8,10},{10,8},{12,14},{14,12},{1,3},{3,1},... | collective-permute-start | bytes 3244040 | tf_op jit(solution)/shard_map/ppermute | solution.py:22
  63.8 26.4 %collective-permute-start.3 = (f32[66,16,256]{2,1,0:T(8,128)S(1)}, f32[66,16,256]{2,1,0:T(8,128)S(1)}, u32[]{:S(2)}, u32[]{:S(2)}) collective-permute-start(f32[66,16,256]{2,1,0:T(8,128)S(1)} %collective-permute-done.2.near1), channel_id=1, source_target_pairs={{0,4},{4,8},{6,2},{8,12},{10,6},{14,10},{1,5},{5,9},{7,3},{9,13},{... | collective-permute-start | bytes 3244040 | tf_op jit(solution)/shard_map/ppermute | solution.py:22
  69.7 1.8 %collective-permute-start.7 = (f32[23,16,256]{2,1,0:T(8,128)S(1)}, f32[23,16,256]{2,1,0:T(8,128)S(1)}, u32[]{:S(2)}, u32[]{:S(2)}) collective-permute-start(f32[23,16,256]{2,1,0:T(8,128)S(1)} %broadcast_select_fusion.2), channel_id=1, source_target_pairs={{0,1},{1,0},{2,3},{3,2},{4,5},{5,4},{6,7},{7,6},{8,9},{9,8},{10,11... | collective-permute-start | bytes 1130504 | tf_op jit(solution)/shard_map/ppermute | solution.py:22
  90.3 20.0 %copy-start.1 = (f32[16,2,64,256]{3,2,1,0:T(8,128)S(1)}, f32[16,2,64,256]{3,2,1,0:T(8,128)}, u32[]{:S(2)}) copy-start(f32[16,2,64,256]{3,2,1,0:T(8,128)} %iterate.1) | copy-start | bytes 6291460
  96.7 1.2 %collective-permute-start.8 = (f32[16,128]{1,0:T(8,128)S(1)}, f32[16,128]{1,0:T(8,128)S(1)}, u32[]{:S(2)}, u32[]{:S(2)}) collective-permute-start(f32[16,128]{1,0:T(8,128)S(1)} %get-tuple-element.38), channel_id=1, source_target_pairs={{0,1},{1,0},{2,3},{3,2},{4,5},{5,4},{6,7},{7,6},{8,9},{9,8},{10,11... | collective-permute-start | bytes 24584 | tf_op jit(solution)/shard_map/ppermute | solution.py:59
  97.8 3.7 %collective-permute-start.9 = (f32[16,128]{1,0:T(8,128)S(1)}, f32[16,128]{1,0:T(8,128)S(1)}, u32[]{:S(2)}, u32[]{:S(2)}) collective-permute-start(f32[16,128]{1,0:T(8,128)S(1)} %add.17), channel_id=1, source_target_pairs={{0,2},{2,0},{4,6},{6,4},{8,10},{10,8},{12,14},{14,12},{1,3},{3,1},... | collective-permute-start | bytes 24584 | tf_op jit(solution)/shard_map/ppermute | solution.py:59
  101.5 4.1 %collective-permute-start.10 = (f32[16,128]{1,0:T(8,128)S(1)}, f32[16,128]{1,0:T(8,128)S(1)}, u32[]{:S(2)}, u32[]{:S(2)}) collective-permute-start(f32[16,128]{1,0:T(8,128)S(1)} %add.18), channel_id=1, source_target_pairs={{0,4},{2,6},{4,0},{6,2},{8,12},{10,14},{12,8},{14,10},{1,5},{3,7},... | collective-permute-start | bytes 24584 | tf_op jit(solution)/shard_map/ppermute | solution.py:59
  105.6 4.7 %collective-permute-start.11 = (f32[16,128]{1,0:T(8,128)S(1)}, f32[16,128]{1,0:T(8,128)S(1)}, u32[]{:S(2)}, u32[]{:S(2)}) collective-permute-start(f32[16,128]{1,0:T(8,128)S(1)} %add.19), channel_id=1, source_target_pairs={{0,8},{2,10},{4,12},{6,14},{8,0},{10,2},{12,4},{14,6},{1,9},{3,11}... | collective-permute-start | bytes 24584 | tf_op jit(solution)/shard_map/ppermute | solution.py:59

commit v13 on v12

--- a/solution.py
+++ b/solution.py
@@ -69,7 +69,7 @@
 BESIDE = ((5, 0, 2), (6, 2, 1), (2, 3, 2))
 EDGES = 5
 FIELDS = (
-    ("far3", 0, None), ("far3", 1, 2), ("far1", 1, 3), ("far1", 0, 2), ("mine", 0, 2),
+    ("far3", 0, None), ("far3", 1, 2), ("beyond", 1, 3), ("beyond", 0, 2), ("mine", 0, 2),
     ("mine", 1, 3), ("near2", 1, 3), ("near2", 0, 2), ("near3", 0, 2), ("near3", 1, None),
 )
 MARGIN = 8
@@ -144,8 +144,18 @@
     out[rows + 1] = own_behind[1, 0]
 
 
-def edges_kernel(rows, near1, near2, far1, far3, near3, mine, first, last):
-    messages = {"near2": near2, "far1": far1, "far3": far3, "near3": near3, "mine": mine}
+def copy_kernel(first, source, *rest):
+    out = rest[-1]
+
+    def copy_rows(y, size):
+        for j in range(size):
+            out[y + j] = source[first + y + j]
+
+    row_blocks(0, out.shape[0], copy_rows, 16)
+
+
+def edges_kernel(rows, near1, near2, far1, beyond, far3, near3, mine, first, last):
+    messages = {"near2": near2, "beyond": beyond, "far3": far3, "near3": near3, "mine": mine}
     rhs = mine.shape[1]
     count = rows // rhs
     for (_, place, number), source in zip(BESIDE, (near1, near2, far1)):
@@ -155,7 +165,7 @@
     for name, *parts in FIELDS:
         for part in parts:
             if part is not None:
-                start = rows + part * count
+                start = part * count + (rows if name != "beyond" else 0)
                 first[place, :MARGIN] = messages[name][start, :MARGIN]
                 last[place, :MARGIN] = messages[name][start + count - 1, rhs - MARGIN :]
                 place += 1
@@ -171,9 +181,10 @@
                 continue
             rhs = messages[name].shape[1]
             count = rows // rhs
+            first = rows if name != "beyond" else 0
             for block in range(count):
                 out[plane, MARGIN + block * rhs : MARGIN + (block + 1) * rhs] = messages[name][
-                    rows + part * count + block
+                    first + part * count + block
                 ]
             out[plane, :MARGIN] = before[place, :MARGIN]
             out[plane, MARGIN + rows :] = behind[place, :MARGIN]
@@ -299,10 +310,10 @@
 
 
 def early_kernel(
-    rows, far3, far1, mine, ahead, own_before, own_behind, near1, near2, near3, before, behind,
+    rows, far3, far1, beyond, mine, ahead, own_before, own_behind, near1, near2, near3, before, behind,
     inverse, sx, sy, sz, root, u0_out, u1_out, u2_out, split, moments, u0, u1, coef, inner, masked,
 ):
-    messages = {"near2": near2, "far1": far1, "far3": far3, "near3": near3, "mine": mine}
+    messages = {"near2": near2, "beyond": beyond, "far3": far3, "near3": near3, "mine": mine}
     fill_cells(rows, messages, before, behind, coef, inner)
     make_operator(coef, inner, inverse, sx, sy, sz, root, masked)
     operator = (sx, sy, sz)
@@ -554,8 +565,18 @@
         )(block, earlier)
 
     near2 = handed_on(first_swap, second)
-    near1 = swapped(handed_on(second, far3))
-    far1 = relayed(near2)
+    near1 = swapped(handed_on(second, near2))
+    def copied(number, first, source, *earlier):
+        return pl.pallas_call(
+            partial(copy_kernel, first),
+            out_shape=array(number, rhs, nx),
+            in_specs=[vmem] + [anywhere] * len(earlier),
+            out_specs=vmem,
+            compiler_params=params(8),
+        )(source, *earlier)
+
+    far1 = relayed(copied(rows, 0, near2, far3))
+    beyond = swapped(copied(4 * count, rows, near3))
     far2 = relayed(near1)
 
     edges = EDGES + sum(part is not None for _, *parts in FIELDS for part in parts)
@@ -563,10 +584,10 @@
         *pl.pallas_call(
             partial(edges_kernel, rows),
             out_shape=(array(edges, rhs, nx),) * 2,
-            in_specs=[vmem] * 6,
+            in_specs=[vmem] * 7,
             out_specs=(vmem, vmem),
             compiler_params=params(12),
-        )(near1, near2, far1, far3, near3, mine)
+        )(near1, near2, far1, beyond, far3, near3, mine)
     )
 
     def planes(number):
@@ -578,13 +599,13 @@
         out_shape=(array(*cells),) * 5
         + tuple(array(*planes(number)) for number in (3, 2, 2))
         + (array(depth, rows, 4 * rhs, nx, dtype=bf16), array(rhs, 128)),
-        in_specs=[vmem] * 11,
+        in_specs=[vmem] * 12,
         out_specs=(vmem,) * 10,
         scratch_shapes=[pltpu.VMEM(planes(number), f32) for number in (4, 2)]
         + [pltpu.VMEM((cells[0] + 2,) + cells[1:], f32)] * 2
         + [pltpu.VMEM(cells, f32)],
         compiler_params=params(24),
-    )(far3, far1, mine, ahead, own_before, own_behind, near1, near2, near3, before, behind)
+    )(far3, far1, beyond, mine, ahead, own_before, own_behind, near1, near2, near3, before, behind)
 
     moments, split23 = pl.pallas_call(
         partial(late_kernel, rows),

time: 117 us -> 115 us (0.983)
  waiting for transfers between devices: 57.6 us -> 53.7 us
  starting transfers between devices: 24.8 us -> 26.4 us
    ppermute x8 -> x9, waiting for transfers between devices: 51.2 us -> 47.4 us  [moved(): return lax.ppermute(block, axis, pairs)]
    ppermute x8 -> x9, starting transfers between devices: 17.6 us -> 19 us  [moved(): return lax.ppermute(block, axis, pairs)]
  transfers between devices with their start and end apart: 12 -> 13, of which waited for: 10 -> 12; matrix products, arithmetic and copies ran while one was open for 0% -> 0% of each run, Pallas kernels for 15% -> 16%
where the time goes in v13:
time: 115 us; the launch traced here: 114 us
  waiting for transfers between devices  53.7 us (47%)
  Pallas kernels  33.2 us (29%)
  starting transfers between devices  26.4 us (23%)
    ppermute x9, waiting for transfers between devices, moved(): return lax.ppermute(block, axis, pairs)  47.4 us
    ppermute x9, starting transfers between devices, moved(): return lax.ppermute(block, axis, pairs)  19 us
    pallas_call x1, Pallas kernels, on_device(): pl.pallas_call(partial(early_kernel, rows), out_shape=(array(*cells),) *...  12.5 us
    ppermute x4, starting transfers between devices, all_sum(): lax.ppermute(values, axis, [(i, i ^ step) for i in range(count)])  7.31 us
    pallas_call x1, Pallas kernels, on_device(): pl.pallas_call(partial(late_kernel, rows), out_shape=(array(rhs, 128), ar...  6.4 us
    ppermute x4, waiting for transfers between devices, all_sum(): lax.ppermute(values, axis, [(i, i ^ step) for i in range(count)])  6.29 us
    pallas_call x1, Pallas kernels, on_device(): pl.pallas_call(outputs_kernel, out_shape=(array(*iterate.shape), array(*r...  6.26 us
    pallas_call x1, Pallas kernels, on_device(): pl.pallas_call(far_kernel, out_shape=(array(rows + 4 * count, rhs, nx),)...  2.69 us
  transfers between devices with their start and end apart: 13, of which 12 were waited for; matrix products, arithmetic and copies ran while one was open for 0% of the time, Pallas kernels for 16%

profile of v13, /device:TPU:0, one launch (start us, length us, event | category | flops | bytes accessed | tf_op | source)
XLA Modules:
  0.0 114.3 jit_solution(5050743966975360142)
XLA Ops:
  0.6 2.7 %shard_map.59 = (f32[80,16,256]{2,1,0:T(8,128)}, f32[3,16,256]{2,1,0:T(8,128)}, f32[3,16,256]{2,1,0:T(8,128)}) custom-call(s32[1]{0:T(128)} %bitcast.odd, f32[16,2,64,256]{3,2,1,0:T(8,128)} %residual.3, s32[2,64,256]{2,1,0:T(8,128)} %labels.1, s32[2,64,256]{2,1,0:T(8,128)} %boundary.1), custom_call_target="tpu_custom_call" | custom-call | tf_op jit(solution)/shard_map/pallas_call | solution.py:523
  3.3 0.0 copy-start.2
  3.4 0.0 copy-start.3
  3.4 0.0 copy-start
  3.4 3.0 %collective-permute-start.1 = (f32[80,16,256]{2,1,0:T(8,128)}, f32[80,16,256]{2,1,0:T(8,128)S(1)}, u32[]{:S(2)}, u32[]{:S(2)}) collective-permute-start(f32[80,16,256]{2,1,0:T(8,128)} %get-tuple-element.22.mine), channel_id=1, source_target_pairs={{0,2},{2,0},{4,6},{6,4},{8,10},{10,8},{12,14},{14,12},{1,3},{3,1},... | collective-permute-start | bytes 3932168 | tf_op jit(solution)/shard_map/ppermute | solution.py:22
  6.4 2.6 %shard_map.60 = (f32[76,16,256]{2,1,0:T(8,128)}, f32[3,16,256]{2,1,0:T(8,128)S(1)}, f32[3,16,256]{2,1,0:T(8,128)S(1)}) custom-call(s32[1]{0:T(128)} %bitcast.odd, f32[16,2,64,256]{3,2,1,0:T(8,128)} %residual.3, f32[80,16,256]{2,1,0:T(8,128)} %get-tuple-element.22.mine), custom_call_target="tpu_custom_call" | custom-call | tf_op jit(solution)/shard_map/pallas_call | solution.py:536
  9.0 4.6 %collective-permute-start.4 = (f32[76,16,256]{2,1,0:T(8,128)}, f32[76,16,256]{2,1,0:T(8,128)}, u32[]{:S(2)}, u32[]{:S(2)}) collective-permute-start(f32[76,16,256]{2,1,0:T(8,128)} %get-tuple-element.23.ahead), channel_id=1, source_target_pairs={{0,4},{4,8},{6,2},{8,12},{10,6},{14,10},{1,5},{5,9},{7,3},{9,13},{... | collective-permute-start | bytes 3735560 | tf_op jit(solution)/shard_map/ppermute | solution.py:22
  13.5 0.0 copy-done.2
  13.5 0.0 copy-done.3
  13.6 0.1 collective-permute-start
  13.6 0.0 copy-done
  13.6 1.3 %collective-permute-start.6 = (f32[80,16,256]{2,1,0:T(8,128)S(1)}, f32[80,16,256]{2,1,0:T(8,128)S(1)}, u32[]{:S(2)}, u32[]{:S(2)}) collective-permute-start(f32[80,16,256]{2,1,0:T(8,128)S(1)} %copy-done), channel_id=1, source_target_pairs={{4,0},{8,4},{2,6},{12,8},{6,10},{10,14},{5,1},{9,5},{3,7},{13,9},{... | collective-permute-start | bytes 3932168 | tf_op jit(solution)/shard_map/ppermute | solution.py:22
  14.9 0.0 collective-permute-done
  15.0 1.4 %shard_map.61.earlier.message = f32[66,16,256]{2,1,0:T(8,128)S(1)} custom-call(f32[76,16,256]{2,1,0:T(8,128)} %get-tuple-element.23.ahead, f32[2,3,16,256]{3,2,1,0:T(8,128)S(1)} %get-tuple-element.45.own_before, f32[2,3,16,256]{3,2,1,0:T(8,128)S(1)} %get-tuple-element.44.own_behind), custom_call_target="tpu_custom_call" | custom-call | tf_op jit(solution)/shard_map/pallas_call | solution.py:550
  16.4 19.0 %collective-permute-done.1.message = f32[80,16,256]{2,1,0:T(8,128)S(1)} collective-permute-done((f32[80,16,256]{2,1,0:T(8,128)}, f32[80,16,256]{2,1,0:T(8,128)S(1)}, u32[]{:S(2)}, u32[]{:S(2)}) %collective-permute-start.1) | collective-permute-done | bytes 1310752 | tf_op jit(solution)/shard_map/ppermute | solution.py:22
  35.4 1.7 %collective-permute-start.2 = (f32[66,16,256]{2,1,0:T(8,128)S(1)}, f32[66,16,256]{2,1,0:T(8,128)S(1)}, u32[]{:S(2)}, u32[]{:S(2)}) collective-permute-start(f32[66,16,256]{2,1,0:T(8,128)S(1)} %shard_map.63), channel_id=1, source_target_pairs={{0,2},{2,0},{4,6},{6,4},{8,10},{10,8},{12,14},{14,12},{1,3},{3,1},... | collective-permute-start | bytes 3244040 | tf_op jit(solution)/shard_map/ppermute | solution.py:22
  37.1 2.0 %collective-permute-done.4.rest_0_.far3 = f32[76,16,256]{2,1,0:T(8,128)} collective-permute-done((f32[76,16,256]{2,1,0:T(8,128)}, f32[76,16,256]{2,1,0:T(8,128)}, u32[]{:S(2)}, u32[]{:S(2)}) %collective-permute-start.4) | collective-permute-done | bytes 1245216 | tf_op jit(solution)/shard_map/ppermute | solution.py:22
  39.1 0.1 shard_map.64
  39.2 4.5 %collective-permute-start.5 = (f32[64,16,256]{2,1,0:T(8,128)S(1)}, f32[64,16,256]{2,1,0:T(8,128)S(1)}, u32[]{:S(2)}, u32[]{:S(2)}) collective-permute-start(f32[64,16,256]{2,1,0:T(8,128)S(1)} %shard_map.64), channel_id=1, source_target_pairs={{0,4},{4,8},{6,2},{8,12},{10,6},{14,10},{1,5},{5,9},{7,3},{9,13},{... | collective-permute-start | bytes 3145736 | tf_op jit(solution)/shard_map/ppermute | solution.py:22
  43.7 3.0 %collective-permute-done.6.source.near3 = f32[80,16,256]{2,1,0:T(8,128)S(1)} collective-permute-done((f32[80,16,256]{2,1,0:T(8,128)S(1)}, f32[80,16,256]{2,1,0:T(8,128)S(1)}, u32[]{:S(2)}, u32[]{:S(2)}) %collective-permute-start.6) | collective-permute-done | bytes 1310752 | tf_op jit(solution)/shard_map/ppermute | solution.py:22
  46.7 0.1 collective-permute-start.7
  46.8 15.4 %collective-permute-done.2.near1 = f32[66,16,256]{2,1,0:T(8,128)S(1)} collective-permute-done((f32[66,16,256]{2,1,0:T(8,128)S(1)}, f32[66,16,256]{2,1,0:T(8,128)S(1)}, u32[]{:S(2)}, u32[]{:S(2)}) %collective-permute-start.2) | collective-permute-done | bytes 1081376 | tf_op jit(solution)/shard_map/ppermute | solution.py:22
  62.2 3.8 %collective-permute-start.3 = (f32[66,16,256]{2,1,0:T(8,128)S(1)}, f32[66,16,256]{2,1,0:T(8,128)S(1)}, u32[]{:S(2)}, u32[]{:S(2)}) collective-permute-start(f32[66,16,256]{2,1,0:T(8,128)S(1)} %collective-permute-done.2.near1), channel_id=1, source_target_pairs={{0,4},{4,8},{6,2},{8,12},{10,6},{14,10},{1,5},{5,9},{7,3},{9,13},{... | collective-permute-start | bytes 3244040 | tf_op jit(solution)/shard_map/ppermute | solution.py:22
  66.0 0.1 collective-permute-done.7.beyond
  66.0 1.2 %collective-permute-done.5.far1 = f32[64,16,256]{2,1,0:T(8,128)S(1)} collective-permute-done((f32[64,16,256]{2,1,0:T(8,128)S(1)}, f32[64,16,256]{2,1,0:T(8,128)S(1)}, u32[]{:S(2)}, u32[]{:S(2)}) %collective-permute-start.5) | collective-permute-done | bytes 1048608 | tf_op jit(solution)/shard_map/ppermute | solution.py:22
  67.2 1.3 %shard_map.66 = (f32[23,16,256]{2,1,0:T(8,128)S(1)}, f32[23,16,256]{2,1,0:T(8,128)S(1)}) custom-call(f32[66,16,256]{2,1,0:T(8,128)S(1)} %collective-permute-done.2.near1, f32[80,16,256]{2,1,0:T(8,128)S(1)} %shard_map.62.earlier.source.near2, f32[64,16,256]{2,1,0:T(8,128)S(1)} %collective-permute-done.5.far1, ...), custom_call_target="tpu_custom_call" | custom-call | tf_op jit(solution)/shard_map/pallas_call | solution.py:584
  68.5 0.1 broadcast_select_fusion.2
  68.6 0.1 collective-permute-start.8
  68.7 1.7 %collective-permute-done.8 = f32[23,16,256]{2,1,0:T(8,128)S(1)} collective-permute-done((f32[23,16,256]{2,1,0:T(8,128)S(1)}, f32[23,16,256]{2,1,0:T(8,128)S(1)}, u32[]{:S(2)}, u32[]{:S(2)}) %collective-permute-start.8) | collective-permute-done | bytes 376864 | tf_op jit(solution)/shard_map/ppermute | solution.py:22
  70.4 0.1 broadcast_select_fusion
  70.4 12.5 %shard_map.67 = (f32[8,80,256]{2,1,0:T(8,128)S(1)}, f32[8,80,256]{2,1,0:T(8,128)S(1)}, f32[8,80,256]{2,1,0:T(8,128)S(1)}, f32[8,80,256]{2,1,0:T(8,128)S(1)}, f32...) custom-call(f32[76,16,256]{2,1,0:T(8,128)} %collective-permute-done., ...), custom_call_target="tpu_custom_call" | custom-call | tf_op jit(solution)/shard_map/pallas_call | solution.py:597
  82.9 5.1 %collective-permute-done.3.far2 = f32[66,16,256]{2,1,0:T(8,128)S(1)} collective-permute-done((f32[66,16,256]{2,1,0:T(8,128)S(1)}, f32[66,16,256]{2,1,0:T(8,128)S(1)}, u32[]{:S(2)}, u32[]{:S(2)}) %collective-permute-start.3) | collective-permute-done | bytes 1081376 | tf_op jit(solution)/shard_map/ppermute | solution.py:22
  88.0 0.0 copy-start.1
  88.0 6.4 %shard_map.68 = (f32[16,128]{1,0:T(8,128)S(1)}, bf16[2,64,64,256]{3,2,1,0:T(8,128)(2,1)S(1)}) custom-call(f32[66,16,256]{2,1,0:T(8,128)S(1)} %collective-permute-done.3.far2, f32[3,70,16,256]{3,2,1,0:T(8,128)S(1)} %get-tuple-element.30.u0_in, f32[2,70,16,256]{3,2,1,0:T(8,128)S(1)} %get-tuple-element.31.u1_in, ...), custom_call_target="tpu_custom_call" | custom-call | tf_op jit(solution)/shard_map/pallas_call | solution.py:610
  94.4 0.0 collective-permute-start.9
  94.4 1.2 %collective-permute-done.9 = f32[16,128]{1,0:T(8,128)S(1)} collective-permute-done((f32[16,128]{1,0:T(8,128)S(1)}, f32[16,128]{1,0:T(8,128)S(1)}, u32[]{:S(2)}, u32[]{:S(2)}) %collective-permute-start.9) | collective-permute-done | bytes 8224 | tf_op jit(solution)/shard_map/ppermute | solution.py:59
  95.6 1.8 %collective-permute-start.10 = (f32[16,128]{1,0:T(8,128)S(1)}, f32[16,128]{1,0:T(8,128)S(1)}, u32[]{:S(2)}, u32[]{:S(2)}) collective-permute-start(f32[16,128]{1,0:T(8,128)S(1)} %add.17), channel_id=1, source_target_pairs={{0,2},{2,0},{4,6},{6,4},{8,10},{10,8},{12,14},{14,12},{1,3},{3,1},... | collective-permute-start | bytes 24584 | tf_op jit(solution)/shard_map/ppermute | solution.py:59
  97.3 1.9 %collective-permute-done.10 = f32[16,128]{1,0:T(8,128)S(1)} collective-permute-done((f32[16,128]{1,0:T(8,128)S(1)}, f32[16,128]{1,0:T(8,128)S(1)}, u32[]{:S(2)}, u32[]{:S(2)}) %collective-permute-start.10) | collective-permute-done | bytes 8224 | tf_op jit(solution)/shard_map/ppermute | solution.py:59
  99.2 2.5 %collective-permute-start.11 = (f32[16,128]{1,0:T(8,128)S(1)}, f32[16,128]{1,0:T(8,128)S(1)}, u32[]{:S(2)}, u32[]{:S(2)}) collective-permute-start(f32[16,128]{1,0:T(8,128)S(1)} %add.18), channel_id=1, source_target_pairs={{0,4},{2,6},{4,0},{6,2},{8,12},{10,14},{12,8},{14,10},{1,5},{3,7},... | collective-permute-start | bytes 24584 | tf_op jit(solution)/shard_map/ppermute | solution.py:59
  101.7 1.6 %collective-permute-done.11 = f32[16,128]{1,0:T(8,128)S(1)} collective-permute-done((f32[16,128]{1,0:T(8,128)S(1)}, f32[16,128]{1,0:T(8,128)S(1)}, u32[]{:S(2)}, u32[]{:S(2)}) %collective-permute-start.11) | collective-permute-done | bytes 8224 | tf_op jit(solution)/shard_map/ppermute | solution.py:59
  103.3 3.0 %collective-permute-start.12 = (f32[16,128]{1,0:T(8,128)S(1)}, f32[16,128]{1,0:T(8,128)S(1)}, u32[]{:S(2)}, u32[]{:S(2)}) collective-permute-start(f32[16,128]{1,0:T(8,128)S(1)} %add.19), channel_id=1, source_target_pairs={{0,8},{2,10},{4,12},{6,14},{8,0},{10,2},{12,4},{14,6},{1,9},{3,11}... | collective-permute-start | bytes 24584 | tf_op jit(solution)/shard_map/ppermute | solution.py:59
  106.4 1.6 %collective-permute-done.12 = f32[16,128]{1,0:T(8,128)S(1)} collective-permute-done((f32[16,128]{1,0:T(8,128)S(1)}, f32[16,128]{1,0:T(8,128)S(1)}, u32[]{:S(2)}, u32[]{:S(2)}) %collective-permute-start.12) | collective-permute-done | bytes 8224 | tf_op jit(solution)/shard_map/ppermute | solution.py:59
  108.0 0.0 copy-done.1
  108.0 6.3 %shard_map.69 = (f32[16,2,64,256]{3,2,1,0:T(8,128)}, f32[16,2,64,256]{3,2,1,0:T(8,128)}) custom-call(s32[1]{0:T(128)} %bitcast.odd, f32[16,128]{1,0:T(8,128)S(1)} %add.20.moments, bf16[2,64,64,256]{3,2,1,0:T(8,128)(2,1)S(1)} %get-tuple-element.39.split01, bf16[2,64,64,256]{3,2,1,0:T(8,128)(2,1)S(1)} %get-tuple-element.40.split23, ...), custom_call_target="tpu_custom_call" | custom-call | tf_op jit(solution)/shard_map/pallas_call | solution.py:623
  (9 shorter events, 0.1 us)
Async XLA Ops:
  3.3 10.2 %copy-start.2 = (f32[3,16,256]{2,1,0:T(8,128)S(1)}, f32[3,16,256]{2,1,0:T(8,128)}, u32[]{:S(2)}) copy-start(f32[3,16,256]{2,1,0:T(8,128)} %get-tuple-element.24) | copy-start | bytes 147460
  3.4 10.2 %copy-start.3 = (f32[3,16,256]{2,1,0:T(8,128)S(1)}, f32[3,16,256]{2,1,0:T(8,128)}, u32[]{:S(2)}) copy-start(f32[3,16,256]{2,1,0:T(8,128)} %get-tuple-element.26) | copy-start | bytes 147460
  3.4 10.3 %copy-start = (f32[80,16,256]{2,1,0:T(8,128)S(1)}, f32[80,16,256]{2,1,0:T(8,128)}, u32[]{:S(2)}) copy-start(f32[80,16,256]{2,1,0:T(8,128)} %get-tuple-element.22.mine) | copy-start | bytes 3932164
  3.4 32.0 %collective-permute-start.1 = (f32[80,16,256]{2,1,0:T(8,128)}, f32[80,16,256]{2,1,0:T(8,128)S(1)}, u32[]{:S(2)}, u32[]{:S(2)}) collective-permute-start(f32[80,16,256]{2,1,0:T(8,128)} %get-tuple-element.22.mine), channel_id=1, source_target_pairs={{0,2},{2,0},{4,6},{6,4},{8,10},{10,8},{12,14},{14,12},{1,3},{3,1},... | collective-permute-start | bytes 3932168 | tf_op jit(solution)/shard_map/ppermute | solution.py:22
  9.0 30.1 %collective-permute-start.4 = (f32[76,16,256]{2,1,0:T(8,128)}, f32[76,16,256]{2,1,0:T(8,128)}, u32[]{:S(2)}, u32[]{:S(2)}) collective-permute-start(f32[76,16,256]{2,1,0:T(8,128)} %get-tuple-element.23.ahead), channel_id=1, source_target_pairs={{0,4},{4,8},{6,2},{8,12},{10,6},{14,10},{1,5},{5,9},{7,3},{9,13},{... | collective-permute-start | bytes 3735560 | tf_op jit(solution)/shard_map/ppermute | solution.py:22
  13.6 1.4 %collective-permute-start = (f32[2,3,16,256]{3,2,1,0:T(8,128)S(1)}, f32[2,3,16,256]{3,2,1,0:T(8,128)S(1)}, u32[]{:S(2)}, u32[]{:S(2)}) collective-permute-start(f32[2,3,16,256]{3,2,1,0:T(8,128)S(1)} %maximum_select_fusion), channel_id=1, source_target_pairs={{0,1},{1,0},{2,3},{3,2},{4,5},{5,4},{6,7},{7,6},{8,9},{9,8},{10,11... | collective-permute-start | bytes 294920 | tf_op jit(solution)/shard_map/ppermute | solution.py:22
  13.6 33.1 %collective-permute-start.6 = (f32[80,16,256]{2,1,0:T(8,128)S(1)}, f32[80,16,256]{2,1,0:T(8,128)S(1)}, u32[]{:S(2)}, u32[]{:S(2)}) collective-permute-start(f32[80,16,256]{2,1,0:T(8,128)S(1)} %copy-done), channel_id=1, source_target_pairs={{4,0},{8,4},{2,6},{12,8},{6,10},{10,14},{5,1},{9,5},{3,7},{13,9},{... | collective-permute-start | bytes 3932168 | tf_op jit(solution)/shard_map/ppermute | solution.py:22
  35.4 26.8 %collective-permute-start.2 = (f32[66,16,256]{2,1,0:T(8,128)S(1)}, f32[66,16,256]{2,1,0:T(8,128)S(1)}, u32[]{:S(2)}, u32[]{:S(2)}) collective-permute-start(f32[66,16,256]{2,1,0:T(8,128)S(1)} %shard_map.63), channel_id=1, source_target_pairs={{0,2},{2,0},{4,6},{6,4},{8,10},{10,8},{12,14},{14,12},{1,3},{3,1},... | collective-permute-start | bytes 3244040 | tf_op jit(solution)/shard_map/ppermute | solution.py:22
  39.2 28.0 %collective-permute-start.5 = (f32[64,16,256]{2,1,0:T(8,128)S(1)}, f32[64,16,256]{2,1,0:T(8,128)S(1)}, u32[]{:S(2)}, u32[]{:S(2)}) collective-permute-start(f32[64,16,256]{2,1,0:T(8,128)S(1)} %shard_map.64), channel_id=1, source_target_pairs={{0,4},{4,8},{6,2},{8,12},{10,6},{14,10},{1,5},{5,9},{7,3},{9,13},{... | collective-permute-start | bytes 3145736 | tf_op jit(solution)/shard_map/ppermute | solution.py:22
  46.7 19.3 %collective-permute-start.7 = (f32[16,16,256]{2,1,0:T(8,128)S(1)}, f32[16,16,256]{2,1,0:T(8,128)S(1)}, u32[]{:S(2)}, u32[]{:S(2)}) collective-permute-start(f32[16,16,256]{2,1,0:T(8,128)S(1)} %shard_map.65), channel_id=1, source_target_pairs={{0,2},{2,0},{4,6},{6,4},{8,10},{10,8},{12,14},{14,12},{1,3},{3,1},... | collective-permute-start | bytes 786440 | tf_op jit(solution)/shard_map/ppermute | solution.py:22
  62.2 25.8 %collective-permute-start.3 = (f32[66,16,256]{2,1,0:T(8,128)S(1)}, f32[66,16,256]{2,1,0:T(8,128)S(1)}, u32[]{:S(2)}, u32[]{:S(2)}) collective-permute-start(f32[66,16,256]{2,1,0:T(8,128)S(1)} %collective-permute-done.2.near1), channel_id=1, source_target_pairs={{0,4},{4,8},{6,2},{8,12},{10,6},{14,10},{1,5},{5,9},{7,3},{9,13},{... | collective-permute-start | bytes 3244040 | tf_op jit(solution)/shard_map/ppermute | solution.py:22
  68.6 1.8 %collective-permute-start.8 = (f32[23,16,256]{2,1,0:T(8,128)S(1)}, f32[23,16,256]{2,1,0:T(8,128)S(1)}, u32[]{:S(2)}, u32[]{:S(2)}) collective-permute-start(f32[23,16,256]{2,1,0:T(8,128)S(1)} %broadcast_select_fusion.2), channel_id=1, source_target_pairs={{0,1},{1,0},{2,3},{3,2},{4,5},{5,4},{6,7},{7,6},{8,9},{9,8},{10,11... | collective-permute-start | bytes 1130504 | tf_op jit(solution)/shard_map/ppermute | solution.py:22
  88.0 20.0 %copy-start.1 = (f32[16,2,64,256]{3,2,1,0:T(8,128)S(1)}, f32[16,2,64,256]{3,2,1,0:T(8,128)}, u32[]{:S(2)}) copy-start(f32[16,2,64,256]{3,2,1,0:T(8,128)} %iterate.1) | copy-start | bytes 6291460
  94.4 1.2 %collective-permute-start.9 = (f32[16,128]{1,0:T(8,128)S(1)}, f32[16,128]{1,0:T(8,128)S(1)}, u32[]{:S(2)}, u32[]{:S(2)}) collective-permute-start(f32[16,128]{1,0:T(8,128)S(1)} %get-tuple-element.38), channel_id=1, source_target_pairs={{0,1},{1,0},{2,3},{3,2},{4,5},{5,4},{6,7},{7,6},{8,9},{9,8},{10,11... | collective-permute-start | bytes 24584 | tf_op jit(solution)/shard_map/ppermute | solution.py:59
  95.6 3.7 %collective-permute-start.10 = (f32[16,128]{1,0:T(8,128)S(1)}, f32[16,128]{1,0:T(8,128)S(1)}, u32[]{:S(2)}, u32[]{:S(2)}) collective-permute-start(f32[16,128]{1,0:T(8,128)S(1)} %add.17), channel_id=1, source_target_pairs={{0,2},{2,0},{4,6},{6,4},{8,10},{10,8},{12,14},{14,12},{1,3},{3,1},... | collective-permute-start | bytes 24584 | tf_op jit(solution)/shard_map/ppermute | solution.py:59
  99.2 4.1 %collective-permute-start.11 = (f32[16,128]{1,0:T(8,128)S(1)}, f32[16,128]{1,0:T(8,128)S(1)}, u32[]{:S(2)}, u32[]{:S(2)}) collective-permute-start(f32[16,128]{1,0:T(8,128)S(1)} %add.18), channel_id=1, source_target_pairs={{0,4},{2,6},{4,0},{6,2},{8,12},{10,14},{12,8},{14,10},{1,5},{3,7},... | collective-permute-start | bytes 24584 | tf_op jit(solution)/shard_map/ppermute | solution.py:59
  103.3 4.7 %collective-permute-start.12 = (f32[16,128]{1,0:T(8,128)S(1)}, f32[16,128]{1,0:T(8,128)S(1)}, u32[]{:S(2)}, u32[]{:S(2)}) collective-permute-start(f32[16,128]{1,0:T(8,128)S(1)} %add.19), channel_id=1, source_target_pairs={{0,8},{2,10},{4,12},{6,14},{8,0},{10,2},{12,4},{14,6},{1,9},{3,11}... | collective-permute-start | bytes 24584 | tf_op jit(solution)/shard_map/ppermute | solution.py:59

commit v14 on v13

--- a/solution.py
+++ b/solution.py
@@ -575,8 +575,8 @@
             compiler_params=params(8),
         )(source, *earlier)
 
-    far1 = relayed(copied(rows, 0, near2, far3))
-    beyond = swapped(copied(4 * count, rows, near3))
+    far1 = relayed(copied(rows, 0, near2))
+    beyond = swapped(copied(4 * count, rows, near3, far3))
     far2 = relayed(near1)
 
     edges = EDGES + sum(part is not None for _, *parts in FIELDS for part in parts)

time: 115 us -> 114 us (level)
  Pallas kernels: 33.2 us -> 27.6 us
  local copies, waits for them, and re-layouts: 0.02 us -> 2.34 us
  starting transfers between devices: 26.4 us -> 28.1 us
    unnamed x8 -> x14, local copies, waits for them, and re-layouts: 0.02 us -> 2.34 us
    pallas_call x1, Pallas kernels: 12.5 us -> 10.8 us  [on_device(): pl.pallas_call(partial(early_kernel, rows), out_shape=(array(*cells),) *...]
    ppermute x9, starting transfers between devices: 19 us -> 20.7 us  [moved(): return lax.ppermute(block, axis, pairs)]
    pallas_call x1, Pallas kernels: 1.37 us -> 0.08 us  [on_device(): pl.pallas_call(partial(second_kernel, rows), out_shape=array(rows + 2, rh...]
    pallas_call x1, Pallas kernels: 1.34 us -> 0.05 us  [on_device(): pl.pallas_call(partial(edges_kernel, rows), out_shape=(array(edges, rhs,...]
  transfers between devices with their start and end apart: 13 -> 13, of which waited for: 12 -> 10; matrix products, arithmetic and copies ran while one was open for 0% -> 0% of each run, Pallas kernels for 16% -> 11%
where the time goes in v14:
time: 114 us
  waiting for transfers between devices  54.7 us (48%)
  starting transfers between devices  28.1 us (25%)
  Pallas kernels  27.6 us (24%)
  local copies, waits for them, and re-layouts  2.34 us (2%)
    ppermute x9, waiting for transfers between devices, moved(): return lax.ppermute(block, axis, pairs)  48.5 us
    ppermute x9, starting transfers between devices, moved(): return lax.ppermute(block, axis, pairs)  20.7 us
    pallas_call x1, Pallas kernels, on_device(): pl.pallas_call(partial(early_kernel, rows), out_shape=(array(*cells),) *...  10.8 us
    ppermute x4, starting transfers between devices, all_sum(): lax.ppermute(values, axis, [(i, i ^ step) for i in range(count)])  7.39 us
    pallas_call x1, Pallas kernels, on_device(): pl.pallas_call(outputs_kernel, out_shape=(array(*iterate.shape), array(*r...  6.31 us
    ppermute x4, waiting for transfers between devices, all_sum(): lax.ppermute(values, axis, [(i, i ^ step) for i in range(count)])  6.25 us
    pallas_call x1, Pallas kernels, on_device(): pl.pallas_call(partial(late_kernel, rows), out_shape=(array(rhs, 128), ar...  6.1 us
    pallas_call x1, Pallas kernels, on_device(): pl.pallas_call(far_kernel, out_shape=(array(rows + 4 * count, rhs, nx),)...  2.68 us
  transfers between devices with their start and end apart: 13, of which 10 were waited for; matrix products, arithmetic and copies ran while one was open for 0% of the time, Pallas kernels for 11%

profile of v14, /device:TPU:0, one launch (start us, length us, event | category | flops | bytes accessed | tf_op | source)
XLA Modules:
  0.0 113.9 jit_solution(1361101613541776382)
XLA Ops:
  0.6 2.7 %shard_map.59 = (f32[80,16,256]{2,1,0:T(8,128)}, f32[3,16,256]{2,1,0:T(8,128)}, f32[3,16,256]{2,1,0:T(8,128)}) custom-call(s32[1]{0:T(128)} %bitcast.odd, f32[16,2,64,256]{3,2,1,0:T(8,128)} %residual.3, s32[2,64,256]{2,1,0:T(8,128)} %labels.1, s32[2,64,256]{2,1,0:T(8,128)} %boundary.1), custom_call_target="tpu_custom_call" | custom-call | tf_op jit(solution)/shard_map/pallas_call | solution.py:523
  3.3 0.0 copy-start.5
  3.3 0.0 copy-start.6
  3.4 0.0 copy-start
  3.4 3.0 %collective-permute-start.1 = (f32[80,16,256]{2,1,0:T(8,128)}, f32[80,16,256]{2,1,0:T(8,128)S(1)}, u32[]{:S(2)}, u32[]{:S(2)}) collective-permute-start(f32[80,16,256]{2,1,0:T(8,128)} %get-tuple-element.22.mine), channel_id=1, source_target_pairs={{0,2},{2,0},{4,6},{6,4},{8,10},{10,8},{12,14},{14,12},{1,3},{3,1},... | collective-permute-start | bytes 3932168 | tf_op jit(solution)/shard_map/ppermute | solution.py:22
  6.4 1.6 %shard_map.60 = (f32[76,16,256]{2,1,0:T(8,128)S(1)}, f32[3,16,256]{2,1,0:T(8,128)S(1)}, f32[3,16,256]{2,1,0:T(8,128)S(1)}) custom-call(s32[1]{0:T(128)} %bitcast.odd, f32[16,2,64,256]{3,2,1,0:T(8,128)} %residual.3, f32[80,16,256]{2,1,0:T(8,128)} %get-tuple-element.22.mine), custom_call_target="tpu_custom_call" | custom-call | tf_op jit(solution)/shard_map/pallas_call | solution.py:536
  7.9 0.0 copy-start.1
  8.0 1.0 copy-done.1
  9.0 0.0 copy-done.5
  9.0 0.0 copy-done.6
  9.0 0.1 collective-permute-start
  9.1 0.0 copy-done
  9.1 1.3 %collective-permute-start.6 = (f32[80,16,256]{2,1,0:T(8,128)S(1)}, f32[80,16,256]{2,1,0:T(8,128)S(1)}, u32[]{:S(2)}, u32[]{:S(2)}) collective-permute-start(f32[80,16,256]{2,1,0:T(8,128)S(1)} %copy-done), channel_id=1, source_target_pairs={{4,0},{8,4},{2,6},{12,8},{6,10},{10,14},{5,1},{9,5},{3,7},{13,9},{... | collective-permute-start | bytes 3932168 | tf_op jit(solution)/shard_map/ppermute | solution.py:22
  10.4 4.6 %collective-permute-start.4 = (f32[76,16,256]{2,1,0:T(8,128)}, f32[76,16,256]{2,1,0:T(8,128)S(1)}, u32[]{:S(2)}, u32[]{:S(2)}) collective-permute-start(f32[76,16,256]{2,1,0:T(8,128)} %copy-done.1), channel_id=1, source_target_pairs={{0,4},{4,8},{6,2},{8,12},{10,6},{14,10},{1,5},{5,9},{7,3},{9,13},{... | collective-permute-start | bytes 3735560 | tf_op jit(solution)/shard_map/ppermute | solution.py:22
  15.0 0.0 collective-permute-done
  15.1 0.0 copy-start.2
  15.1 1.3 %copy-done.2 = f32[76,16,256]{2,1,0:T(8,128)S(1)} copy-done((f32[76,16,256]{2,1,0:T(8,128)S(1)}, f32[76,16,256]{2,1,0:T(8,128)}, u32[]{:S(2)}) %copy-start.2) | copy-done | bytes 1245208
  16.4 0.1 shard_map.61.earlier.message
  16.4 18.9 %collective-permute-done.1.message = f32[80,16,256]{2,1,0:T(8,128)S(1)} collective-permute-done((f32[80,16,256]{2,1,0:T(8,128)}, f32[80,16,256]{2,1,0:T(8,128)S(1)}, u32[]{:S(2)}, u32[]{:S(2)}) %collective-permute-start.1) | collective-permute-done | bytes 1310752 | tf_op jit(solution)/shard_map/ppermute | solution.py:22
  35.4 1.7 %collective-permute-start.2 = (f32[66,16,256]{2,1,0:T(8,128)S(1)}, f32[66,16,256]{2,1,0:T(8,128)S(1)}, u32[]{:S(2)}, u32[]{:S(2)}) collective-permute-start(f32[66,16,256]{2,1,0:T(8,128)S(1)} %shard_map.63), channel_id=1, source_target_pairs={{0,2},{2,0},{4,6},{6,4},{8,10},{10,8},{12,14},{14,12},{1,3},{3,1},... | collective-permute-start | bytes 3244040 | tf_op jit(solution)/shard_map/ppermute | solution.py:22
  37.1 0.1 shard_map.64
  37.2 3.5 %collective-permute-start.5 = (f32[64,16,256]{2,1,0:T(8,128)S(1)}, f32[64,16,256]{2,1,0:T(8,128)S(1)}, u32[]{:S(2)}, u32[]{:S(2)}) collective-permute-start(f32[64,16,256]{2,1,0:T(8,128)S(1)} %shard_map.64), channel_id=1, source_target_pairs={{0,4},{4,8},{6,2},{8,12},{10,6},{14,10},{1,5},{5,9},{7,3},{9,13},{... | collective-permute-start | bytes 3145736 | tf_op jit(solution)/shard_map/ppermute | solution.py:22
  40.7 2.2 %collective-permute-done.4.rest_0_.far3 = f32[76,16,256]{2,1,0:T(8,128)S(1)} collective-permute-done((f32[76,16,256]{2,1,0:T(8,128)}, f32[76,16,256]{2,1,0:T(8,128)S(1)}, u32[]{:S(2)}, u32[]{:S(2)}) %collective-permute-start.4) | collective-permute-done | bytes 1245216 | tf_op jit(solution)/shard_map/ppermute | solution.py:22
  43.0 0.0 collective-permute-done.6.source.near3
  43.0 2.6 %collective-permute-start.7 = (f32[16,16,256]{2,1,0:T(8,128)S(1)}, f32[16,16,256]{2,1,0:T(8,128)S(1)}, u32[]{:S(2)}, u32[]{:S(2)}) collective-permute-start(f32[16,16,256]{2,1,0:T(8,128)S(1)} %shard_map.65), channel_id=1, source_target_pairs={{0,2},{2,0},{4,6},{6,4},{8,10},{10,8},{12,14},{14,12},{1,3},{3,1},... | collective-permute-start | bytes 786440 | tf_op jit(solution)/shard_map/ppermute | solution.py:22
  45.6 16.6 %collective-permute-done.2.near1 = f32[66,16,256]{2,1,0:T(8,128)S(1)} collective-permute-done((f32[66,16,256]{2,1,0:T(8,128)S(1)}, f32[66,16,256]{2,1,0:T(8,128)S(1)}, u32[]{:S(2)}, u32[]{:S(2)}) %collective-permute-start.2) | collective-permute-done | bytes 1081376 | tf_op jit(solution)/shard_map/ppermute | solution.py:22
  62.2 3.8 %collective-permute-start.3 = (f32[66,16,256]{2,1,0:T(8,128)S(1)}, f32[66,16,256]{2,1,0:T(8,128)S(1)}, u32[]{:S(2)}, u32[]{:S(2)}) collective-permute-start(f32[66,16,256]{2,1,0:T(8,128)S(1)} %collective-permute-done.2.near1), channel_id=1, source_target_pairs={{0,4},{4,8},{6,2},{8,12},{10,6},{14,10},{1,5},{5,9},{7,3},{9,13},{... | collective-permute-start | bytes 3244040 | tf_op jit(solution)/shard_map/ppermute | solution.py:22
  66.0 0.1 collective-permute-done.7.beyond
  66.0 0.0 collective-permute-done.5.far1
  66.0 0.1 shard_map.66
  66.1 0.0 copy-start.3
  66.1 0.1 broadcast_select_fusion.2
  66.2 0.1 collective-permute-start.8
  66.2 1.7 %collective-permute-done.8 = f32[23,16,256]{2,1,0:T(8,128)S(1)} collective-permute-done((f32[23,16,256]{2,1,0:T(8,128)S(1)}, f32[23,16,256]{2,1,0:T(8,128)S(1)}, u32[]{:S(2)}, u32[]{:S(2)}) %collective-permute-start.8) | collective-permute-done | bytes 376864 | tf_op jit(solution)/shard_map/ppermute | solution.py:22
  67.9 0.1 broadcast_select_fusion
  68.0 0.0 copy-done.3
  68.0 10.8 %shard_map.67 = (f32[8,80,256]{2,1,0:T(8,128)S(1)}, f32[8,80,256]{2,1,0:T(8,128)S(1)}, f32[8,80,256]{2,1,0:T(8,128)S(1)}, f32[8,80,256]{2,1,0:T(8,128)S(1)}, f32...) custom-call(f32[76,16,256]{2,1,0:T(8,128)S(1)} %collective-permute-d, ...), custom_call_target="tpu_custom_call" | custom-call | tf_op jit(solution)/shard_map/pallas_call | solution.py:597
  78.8 9.0 %collective-permute-done.3.far2 = f32[66,16,256]{2,1,0:T(8,128)S(1)} collective-permute-done((f32[66,16,256]{2,1,0:T(8,128)S(1)}, f32[66,16,256]{2,1,0:T(8,128)S(1)}, u32[]{:S(2)}, u32[]{:S(2)}) %collective-permute-start.3) | collective-permute-done | bytes 1081376 | tf_op jit(solution)/shard_map/ppermute | solution.py:22
  87.8 0.0 copy-start.4
  87.8 6.1 %shard_map.68 = (f32[16,128]{1,0:T(8,128)S(1)}, bf16[2,64,64,256]{3,2,1,0:T(8,128)(2,1)S(1)}) custom-call(f32[66,16,256]{2,1,0:T(8,128)S(1)} %collective-permute-done.3.far2, f32[3,70,16,256]{3,2,1,0:T(8,128)S(1)} %get-tuple-element.30.u0_in, f32[2,70,16,256]{3,2,1,0:T(8,128)S(1)} %get-tuple-element.31.u1_in, ...), custom_call_target="tpu_custom_call" | custom-call | tf_op jit(solution)/shard_map/pallas_call | solution.py:610
  93.9 0.0 collective-permute-start.9
  93.9 1.2 %collective-permute-done.9 = f32[16,128]{1,0:T(8,128)S(1)} collective-permute-done((f32[16,128]{1,0:T(8,128)S(1)}, f32[16,128]{1,0:T(8,128)S(1)}, u32[]{:S(2)}, u32[]{:S(2)}) %collective-permute-start.9) | collective-permute-done | bytes 8224 | tf_op jit(solution)/shard_map/ppermute | solution.py:59
  95.1 2.6 %collective-permute-start.10 = (f32[16,128]{1,0:T(8,128)S(1)}, f32[16,128]{1,0:T(8,128)S(1)}, u32[]{:S(2)}, u32[]{:S(2)}) collective-permute-start(f32[16,128]{1,0:T(8,128)S(1)} %add.17), channel_id=1, source_target_pairs={{0,2},{2,0},{4,6},{6,4},{8,10},{10,8},{12,14},{14,12},{1,3},{3,1},... | collective-permute-start | bytes 24584 | tf_op jit(solution)/shard_map/ppermute | solution.py:59
  97.7 1.6 %collective-permute-done.10 = f32[16,128]{1,0:T(8,128)S(1)} collective-permute-done((f32[16,128]{1,0:T(8,128)S(1)}, f32[16,128]{1,0:T(8,128)S(1)}, u32[]{:S(2)}, u32[]{:S(2)}) %collective-permute-start.10) | collective-permute-done | bytes 8224 | tf_op jit(solution)/shard_map/ppermute | solution.py:59
  99.3 1.9 %collective-permute-start.11 = (f32[16,128]{1,0:T(8,128)S(1)}, f32[16,128]{1,0:T(8,128)S(1)}, u32[]{:S(2)}, u32[]{:S(2)}) collective-permute-start(f32[16,128]{1,0:T(8,128)S(1)} %add.18), channel_id=1, source_target_pairs={{0,4},{2,6},{4,0},{6,2},{8,12},{10,14},{12,8},{14,10},{1,5},{3,7},... | collective-permute-start | bytes 24584 | tf_op jit(solution)/shard_map/ppermute | solution.py:59
  101.2 1.8 %collective-permute-done.11 = f32[16,128]{1,0:T(8,128)S(1)} collective-permute-done((f32[16,128]{1,0:T(8,128)S(1)}, f32[16,128]{1,0:T(8,128)S(1)}, u32[]{:S(2)}, u32[]{:S(2)}) %collective-permute-start.11) | collective-permute-done | bytes 8224 | tf_op jit(solution)/shard_map/ppermute | solution.py:59
  103.0 2.9 %collective-permute-start.12 = (f32[16,128]{1,0:T(8,128)S(1)}, f32[16,128]{1,0:T(8,128)S(1)}, u32[]{:S(2)}, u32[]{:S(2)}) collective-permute-start(f32[16,128]{1,0:T(8,128)S(1)} %add.19), channel_id=1, source_target_pairs={{0,8},{2,10},{4,12},{6,14},{8,0},{10,2},{12,4},{14,6},{1,9},{3,11}... | collective-permute-start | bytes 24584 | tf_op jit(solution)/shard_map/ppermute | solution.py:59
  105.9 1.7 %collective-permute-done.12 = f32[16,128]{1,0:T(8,128)S(1)} collective-permute-done((f32[16,128]{1,0:T(8,128)S(1)}, f32[16,128]{1,0:T(8,128)S(1)}, u32[]{:S(2)}, u32[]{:S(2)}) %collective-permute-start.12) | collective-permute-done | bytes 8224 | tf_op jit(solution)/shard_map/ppermute | solution.py:59
  107.5 0.0 copy-done.4
  107.5 6.3 %shard_map.69 = (f32[16,2,64,256]{3,2,1,0:T(8,128)}, f32[16,2,64,256]{3,2,1,0:T(8,128)}) custom-call(s32[1]{0:T(128)} %bitcast.odd, f32[16,128]{1,0:T(8,128)S(1)} %add.20.moments, bf16[2,64,64,256]{3,2,1,0:T(8,128)(2,1)S(1)} %get-tuple-element.39.split01, bf16[2,64,64,256]{3,2,1,0:T(8,128)(2,1)S(1)} %get-tuple-element.40.split23, ...), custom_call_target="tpu_custom_call" | custom-call | tf_op jit(solution)/shard_map/pallas_call | solution.py:623
  (9 shorter events, 0.1 us)
Async XLA Ops:
  3.3 5.6 %copy-start.5 = (f32[3,16,256]{2,1,0:T(8,128)S(1)}, f32[3,16,256]{2,1,0:T(8,128)}, u32[]{:S(2)}) copy-start(f32[3,16,256]{2,1,0:T(8,128)} %get-tuple-element.24) | copy-start | bytes 147460
  3.3 5.6 %copy-start.6 = (f32[3,16,256]{2,1,0:T(8,128)S(1)}, f32[3,16,256]{2,1,0:T(8,128)}, u32[]{:S(2)}) copy-start(f32[3,16,256]{2,1,0:T(8,128)} %get-tuple-element.26) | copy-start | bytes 147460
  3.4 5.7 %copy-start = (f32[80,16,256]{2,1,0:T(8,128)S(1)}, f32[80,16,256]{2,1,0:T(8,128)}, u32[]{:S(2)}) copy-start(f32[80,16,256]{2,1,0:T(8,128)} %get-tuple-element.22.mine) | copy-start | bytes 3932164
  3.4 32.0 %collective-permute-start.1 = (f32[80,16,256]{2,1,0:T(8,128)}, f32[80,16,256]{2,1,0:T(8,128)S(1)}, u32[]{:S(2)}, u32[]{:S(2)}) collective-permute-start(f32[80,16,256]{2,1,0:T(8,128)} %get-tuple-element.22.mine), channel_id=1, source_target_pairs={{0,2},{2,0},{4,6},{6,4},{8,10},{10,8},{12,14},{14,12},{1,3},{3,1},... | collective-permute-start | bytes 3932168 | tf_op jit(solution)/shard_map/ppermute | solution.py:22
  7.9 1.0 copy-start.1
  9.0 6.0 %collective-permute-start = (f32[2,3,16,256]{3,2,1,0:T(8,128)S(1)}, f32[2,3,16,256]{3,2,1,0:T(8,128)S(1)}, u32[]{:S(2)}, u32[]{:S(2)}) collective-permute-start(f32[2,3,16,256]{3,2,1,0:T(8,128)S(1)} %maximum_select_fusion), channel_id=1, source_target_pairs={{0,1},{1,0},{2,3},{3,2},{4,5},{5,4},{6,7},{7,6},{8,9},{9,8},{10,11... | collective-permute-start | bytes 294920 | tf_op jit(solution)/shard_map/ppermute | solution.py:22
  9.1 33.9 %collective-permute-start.6 = (f32[80,16,256]{2,1,0:T(8,128)S(1)}, f32[80,16,256]{2,1,0:T(8,128)S(1)}, u32[]{:S(2)}, u32[]{:S(2)}) collective-permute-start(f32[80,16,256]{2,1,0:T(8,128)S(1)} %copy-done), channel_id=1, source_target_pairs={{4,0},{8,4},{2,6},{12,8},{6,10},{10,14},{5,1},{9,5},{3,7},{13,9},{... | collective-permute-start | bytes 3932168 | tf_op jit(solution)/shard_map/ppermute | solution.py:22
  10.4 32.6 %collective-permute-start.4 = (f32[76,16,256]{2,1,0:T(8,128)}, f32[76,16,256]{2,1,0:T(8,128)S(1)}, u32[]{:S(2)}, u32[]{:S(2)}) collective-permute-start(f32[76,16,256]{2,1,0:T(8,128)} %copy-done.1), channel_id=1, source_target_pairs={{0,4},{4,8},{6,2},{8,12},{10,6},{14,10},{1,5},{5,9},{7,3},{9,13},{... | collective-permute-start | bytes 3735560 | tf_op jit(solution)/shard_map/ppermute | solution.py:22
  15.1 1.3 %copy-start.2 = (f32[76,16,256]{2,1,0:T(8,128)S(1)}, f32[76,16,256]{2,1,0:T(8,128)}, u32[]{:S(2)}) copy-start(f32[76,16,256]{2,1,0:T(8,128)} %copy-done.1) | copy-start | bytes 3735556
  35.4 26.8 %collective-permute-start.2 = (f32[66,16,256]{2,1,0:T(8,128)S(1)}, f32[66,16,256]{2,1,0:T(8,128)S(1)}, u32[]{:S(2)}, u32[]{:S(2)}) collective-permute-start(f32[66,16,256]{2,1,0:T(8,128)S(1)} %shard_map.63), channel_id=1, source_target_pairs={{0,2},{2,0},{4,6},{6,4},{8,10},{10,8},{12,14},{14,12},{1,3},{3,1},... | collective-permute-start | bytes 3244040 | tf_op jit(solution)/shard_map/ppermute | solution.py:22
  37.2 28.8 %collective-permute-start.5 = (f32[64,16,256]{2,1,0:T(8,128)S(1)}, f32[64,16,256]{2,1,0:T(8,128)S(1)}, u32[]{:S(2)}, u32[]{:S(2)}) collective-permute-start(f32[64,16,256]{2,1,0:T(8,128)S(1)} %shard_map.64), channel_id=1, source_target_pairs={{0,4},{4,8},{6,2},{8,12},{10,6},{14,10},{1,5},{5,9},{7,3},{9,13},{... | collective-permute-start | bytes 3145736 | tf_op jit(solution)/shard_map/ppermute | solution.py:22
  43.0 23.0 %collective-permute-start.7 = (f32[16,16,256]{2,1,0:T(8,128)S(1)}, f32[16,16,256]{2,1,0:T(8,128)S(1)}, u32[]{:S(2)}, u32[]{:S(2)}) collective-permute-start(f32[16,16,256]{2,1,0:T(8,128)S(1)} %shard_map.65), channel_id=1, source_target_pairs={{0,2},{2,0},{4,6},{6,4},{8,10},{10,8},{12,14},{14,12},{1,3},{3,1},... | collective-permute-start | bytes 786440 | tf_op jit(solution)/shard_map/ppermute | solution.py:22
  62.2 25.6 %collective-permute-start.3 = (f32[66,16,256]{2,1,0:T(8,128)S(1)}, f32[66,16,256]{2,1,0:T(8,128)S(1)}, u32[]{:S(2)}, u32[]{:S(2)}) collective-permute-start(f32[66,16,256]{2,1,0:T(8,128)S(1)} %collective-permute-done.2.near1), channel_id=1, source_target_pairs={{0,4},{4,8},{6,2},{8,12},{10,6},{14,10},{1,5},{5,9},{7,3},{9,13},{... | collective-permute-start | bytes 3244040 | tf_op jit(solution)/shard_map/ppermute | solution.py:22
  66.1 1.9 %copy-start.3 = (f32[76,16,256]{2,1,0:T(8,128)S(1)}, f32[76,16,256]{2,1,0:T(8,128)}, u32[]{:S(2)}) copy-start(f32[76,16,256]{2,1,0:T(8,128)} %copy-done.1) | copy-start | bytes 3735556
  66.2 1.8 %collective-permute-start.8 = (f32[23,16,256]{2,1,0:T(8,128)S(1)}, f32[23,16,256]{2,1,0:T(8,128)S(1)}, u32[]{:S(2)}, u32[]{:S(2)}) collective-permute-start(f32[23,16,256]{2,1,0:T(8,128)S(1)} %broadcast_select_fusion.2), channel_id=1, source_target_pairs={{0,1},{1,0},{2,3},{3,2},{4,5},{5,4},{6,7},{7,6},{8,9},{9,8},{10,11... | collective-permute-start | bytes 1130504 | tf_op jit(solution)/shard_map/ppermute | solution.py:22
  87.8 19.8 %copy-start.4 = (f32[16,2,64,256]{3,2,1,0:T(8,128)S(1)}, f32[16,2,64,256]{3,2,1,0:T(8,128)}, u32[]{:S(2)}) copy-start(f32[16,2,64,256]{3,2,1,0:T(8,128)} %iterate.1) | copy-start | bytes 6291460
  93.9 1.2 %collective-permute-start.9 = (f32[16,128]{1,0:T(8,128)S(1)}, f32[16,128]{1,0:T(8,128)S(1)}, u32[]{:S(2)}, u32[]{:S(2)}) collective-permute-start(f32[16,128]{1,0:T(8,128)S(1)} %get-tuple-element.38), channel_id=1, source_target_pairs={{0,1},{1,0},{2,3},{3,2},{4,5},{5,4},{6,7},{7,6},{8,9},{9,8},{10,11... | collective-permute-start | bytes 24584 | tf_op jit(solution)/shard_map/ppermute | solution.py:59
  95.1 4.3 %collective-permute-start.10 = (f32[16,128]{1,0:T(8,128)S(1)}, f32[16,128]{1,0:T(8,128)S(1)}, u32[]{:S(2)}, u32[]{:S(2)}) collective-permute-start(f32[16,128]{1,0:T(8,128)S(1)} %add.17), channel_id=1, source_target_pairs={{0,2},{2,0},{4,6},{6,4},{8,10},{10,8},{12,14},{14,12},{1,3},{3,1},... | collective-permute-start | bytes 24584 | tf_op jit(solution)/shard_map/ppermute | solution.py:59
  99.3 3.7 %collective-permute-start.11 = (f32[16,128]{1,0:T(8,128)S(1)}, f32[16,128]{1,0:T(8,128)S(1)}, u32[]{:S(2)}, u32[]{:S(2)}) collective-permute-start(f32[16,128]{1,0:T(8,128)S(1)} %add.18), channel_id=1, source_target_pairs={{0,4},{2,6},{4,0},{6,2},{8,12},{10,14},{12,8},{14,10},{1,5},{3,7},... | collective-permute-start | bytes 24584 | tf_op jit(solution)/shard_map/ppermute | solution.py:59
  103.0 4.5 %collective-permute-start.12 = (f32[16,128]{1,0:T(8,128)S(1)}, f32[16,128]{1,0:T(8,128)S(1)}, u32[]{:S(2)}, u32[]{:S(2)}) collective-permute-start(f32[16,128]{1,0:T(8,128)S(1)} %add.19), channel_id=1, source_target_pairs={{0,8},{2,10},{4,12},{6,14},{8,0},{10,2},{12,4},{14,6},{1,9},{3,11}... | collective-permute-start | bytes 24584 | tf_op jit(solution)/shard_map/ppermute | solution.py:59

commit v15 on v14

--- a/solution.py
+++ b/solution.py
@@ -576,7 +576,7 @@
         )(source, *earlier)
 
     far1 = relayed(copied(rows, 0, near2))
-    beyond = swapped(copied(4 * count, rows, near3, far3))
+    beyond = swapped(handed_on(copied(4 * count, rows, near3, far3), near1))
     far2 = relayed(near1)
 
     edges = EDGES + sum(part is not None for _, *parts in FIELDS for part in parts)

time: 114 us -> 114 us (level)
  starting transfers between devices: 28.1 us -> 26.7 us
  waiting for transfers between devices: 54.7 us -> 56.1 us
    ppermute x9, starting transfers between devices: 20.7 us -> 19.3 us  [moved(): return lax.ppermute(block, axis, pairs)]
    ppermute x9, waiting for transfers between devices: 48.5 us -> 49.8 us  [moved(): return lax.ppermute(block, axis, pairs)]
where the time goes in v15:
time: 114 us
  waiting for transfers between devices  56.1 us (49%)
  Pallas kernels  27.9 us (24%)
  starting transfers between devices  26.7 us (23%)
  local copies, waits for them, and re-layouts  2.34 us (2%)
    ppermute x9, waiting for transfers between devices, moved(): return lax.ppermute(block, axis, pairs)  49.8 us
    ppermute x9, starting transfers between devices, moved(): return lax.ppermute(block, axis, pairs)  19.3 us
    pallas_call x1, Pallas kernels, on_device(): pl.pallas_call(partial(early_kernel, rows), out_shape=(array(*cells),) *...  10.8 us
    ppermute x4, starting transfers between devices, all_sum(): lax.ppermute(values, axis, [(i, i ^ step) for i in range(count)])  7.39 us
    pallas_call x1, Pallas kernels, on_device(): pl.pallas_call(outputs_kernel, out_shape=(array(*iterate.shape), array(*r...  6.31 us
    pallas_call x1, Pallas kernels, on_device(): pl.pallas_call(partial(late_kernel, rows), out_shape=(array(rhs, 128), ar...  6.28 us
    ppermute x4, waiting for transfers between devices, all_sum(): lax.ppermute(values, axis, [(i, i ^ step) for i in range(count)])  6.26 us
    pallas_call x1, Pallas kernels, on_device(): pl.pallas_call(far_kernel, out_shape=(array(rows + 4 * count, rhs, nx),)...  2.68 us
  transfers between devices with their start and end apart: 13, of which 10 were waited for; matrix products, arithmetic and copies ran while one was open for 0% of the time, Pallas kernels for 11%

profile of v15, /device:TPU:0, one launch (start us, length us, event | category | flops | bytes accessed | tf_op | source)
XLA Modules:
  0.0 114.0 jit_solution(7943891219908909585)
XLA Ops:
  0.6 2.7 %shard_map.59 = (f32[80,16,256]{2,1,0:T(8,128)}, f32[3,16,256]{2,1,0:T(8,128)}, f32[3,16,256]{2,1,0:T(8,128)}) custom-call(s32[1]{0:T(128)} %bitcast.odd, f32[16,2,64,256]{3,2,1,0:T(8,128)} %residual.3, s32[2,64,256]{2,1,0:T(8,128)} %labels.1, s32[2,64,256]{2,1,0:T(8,128)} %boundary.1), custom_call_target="tpu_custom_call" | custom-call | tf_op jit(solution)/shard_map/pallas_call | solution.py:523
  3.3 0.0 copy-start.5
  3.3 0.0 copy-start.6
  3.4 0.0 copy-start
  3.4 3.0 %collective-permute-start.1 = (f32[80,16,256]{2,1,0:T(8,128)}, f32[80,16,256]{2,1,0:T(8,128)S(1)}, u32[]{:S(2)}, u32[]{:S(2)}) collective-permute-start(f32[80,16,256]{2,1,0:T(8,128)} %get-tuple-element.22.mine), channel_id=1, source_target_pairs={{0,2},{2,0},{4,6},{6,4},{8,10},{10,8},{12,14},{14,12},{1,3},{3,1},... | collective-permute-start | bytes 3932168 | tf_op jit(solution)/shard_map/ppermute | solution.py:22
  6.4 1.6 %shard_map.60 = (f32[76,16,256]{2,1,0:T(8,128)S(1)}, f32[3,16,256]{2,1,0:T(8,128)S(1)}, f32[3,16,256]{2,1,0:T(8,128)S(1)}) custom-call(s32[1]{0:T(128)} %bitcast.odd, f32[16,2,64,256]{3,2,1,0:T(8,128)} %residual.3, f32[80,16,256]{2,1,0:T(8,128)} %get-tuple-element.22.mine), custom_call_target="tpu_custom_call" | custom-call | tf_op jit(solution)/shard_map/pallas_call | solution.py:536
  7.9 0.0 copy-start.1
  8.0 1.0 copy-done.1
  9.0 0.0 copy-done.5
  9.0 0.0 copy-done.6
  9.0 0.1 collective-permute-start
  9.1 0.0 copy-done
  9.1 1.3 %collective-permute-start.6 = (f32[80,16,256]{2,1,0:T(8,128)S(1)}, f32[80,16,256]{2,1,0:T(8,128)S(1)}, u32[]{:S(2)}, u32[]{:S(2)}) collective-permute-start(f32[80,16,256]{2,1,0:T(8,128)S(1)} %copy-done), channel_id=1, source_target_pairs={{4,0},{8,4},{2,6},{12,8},{6,10},{10,14},{5,1},{9,5},{3,7},{13,9},{... | collective-permute-start | bytes 3932168 | tf_op jit(solution)/shard_map/ppermute | solution.py:22
  10.4 4.6 %collective-permute-start.4 = (f32[76,16,256]{2,1,0:T(8,128)}, f32[76,16,256]{2,1,0:T(8,128)S(1)}, u32[]{:S(2)}, u32[]{:S(2)}) collective-permute-start(f32[76,16,256]{2,1,0:T(8,128)} %copy-done.1), channel_id=1, source_target_pairs={{0,4},{4,8},{6,2},{8,12},{10,6},{14,10},{1,5},{5,9},{7,3},{9,13},{... | collective-permute-start | bytes 3735560 | tf_op jit(solution)/shard_map/ppermute | solution.py:22
  15.0 0.0 collective-permute-done
  15.1 0.0 copy-start.2
  15.1 1.3 %copy-done.2 = f32[76,16,256]{2,1,0:T(8,128)S(1)} copy-done((f32[76,16,256]{2,1,0:T(8,128)S(1)}, f32[76,16,256]{2,1,0:T(8,128)}, u32[]{:S(2)}) %copy-start.2) | copy-done | bytes 1245208
  16.4 0.1 shard_map.61.earlier.message
  16.4 18.9 %collective-permute-done.1.message = f32[80,16,256]{2,1,0:T(8,128)S(1)} collective-permute-done((f32[80,16,256]{2,1,0:T(8,128)}, f32[80,16,256]{2,1,0:T(8,128)S(1)}, u32[]{:S(2)}, u32[]{:S(2)}) %collective-permute-start.1) | collective-permute-done | bytes 1310752 | tf_op jit(solution)/shard_map/ppermute | solution.py:22
  35.4 1.7 %collective-permute-start.2 = (f32[66,16,256]{2,1,0:T(8,128)S(1)}, f32[66,16,256]{2,1,0:T(8,128)S(1)}, u32[]{:S(2)}, u32[]{:S(2)}) collective-permute-start(f32[66,16,256]{2,1,0:T(8,128)S(1)} %shard_map.63), channel_id=1, source_target_pairs={{0,2},{2,0},{4,6},{6,4},{8,10},{10,8},{12,14},{14,12},{1,3},{3,1},... | collective-permute-start | bytes 3244040 | tf_op jit(solution)/shard_map/ppermute | solution.py:22
  37.1 0.1 shard_map.64
  37.2 3.5 %collective-permute-start.5 = (f32[64,16,256]{2,1,0:T(8,128)S(1)}, f32[64,16,256]{2,1,0:T(8,128)S(1)}, u32[]{:S(2)}, u32[]{:S(2)}) collective-permute-start(f32[64,16,256]{2,1,0:T(8,128)S(1)} %shard_map.64), channel_id=1, source_target_pairs={{0,4},{4,8},{6,2},{8,12},{10,6},{14,10},{1,5},{5,9},{7,3},{9,13},{... | collective-permute-start | bytes 3145736 | tf_op jit(solution)/shard_map/ppermute | solution.py:22
  40.7 2.2 %collective-permute-done.4.rest_0_.far3 = f32[76,16,256]{2,1,0:T(8,128)S(1)} collective-permute-done((f32[76,16,256]{2,1,0:T(8,128)}, f32[76,16,256]{2,1,0:T(8,128)S(1)}, u32[]{:S(2)}, u32[]{:S(2)}) %collective-permute-start.4) | collective-permute-done | bytes 1245216 | tf_op jit(solution)/shard_map/ppermute | solution.py:22
  43.0 0.0 collective-permute-done.6.source.near3
  43.0 17.4 %collective-permute-done.2.earlier.near1 = f32[66,16,256]{2,1,0:T(8,128)S(1)} collective-permute-done((f32[66,16,256]{2,1,0:T(8,128)S(1)}, f32[66,16,256]{2,1,0:T(8,128)S(1)}, u32[]{:S(2)}, u32[]{:S(2)}) %collective-permute-start.2) | collective-permute-done | bytes 1081376 | tf_op jit(solution)/shard_map/ppermute | solution.py:22
  60.4 1.4 %collective-permute-start.7 = (f32[16,16,256]{2,1,0:T(8,128)S(1)}, f32[16,16,256]{2,1,0:T(8,128)S(1)}, u32[]{:S(2)}, u32[]{:S(2)}) collective-permute-start(f32[16,16,256]{2,1,0:T(8,128)S(1)} %shard_map.66), channel_id=1, source_target_pairs={{0,2},{2,0},{4,6},{6,4},{8,10},{10,8},{12,14},{14,12},{1,3},{3,1},... | collective-permute-start | bytes 786440 | tf_op jit(solution)/shard_map/ppermute | solution.py:22
  61.8 3.5 %collective-permute-start.3 = (f32[66,16,256]{2,1,0:T(8,128)S(1)}, f32[66,16,256]{2,1,0:T(8,128)S(1)}, u32[]{:S(2)}, u32[]{:S(2)}) collective-permute-start(f32[66,16,256]{2,1,0:T(8,128)S(1)} %collective-permute-done.2.earlier.near1), channel_id=1, source_target_pairs={{0,4},{4,8},{6,2},{8,12},{10,6},{14,10},{1,5},{5,9},{7,3},{9,13},{... | collective-permute-start | bytes 3244040 | tf_op jit(solution)/shard_map/ppermute | solution.py:22
  65.4 0.0 collective-permute-done.5.far1
  65.4 1.6 %collective-permute-done.7.beyond = f32[16,16,256]{2,1,0:T(8,128)S(1)} collective-permute-done((f32[16,16,256]{2,1,0:T(8,128)S(1)}, f32[16,16,256]{2,1,0:T(8,128)S(1)}, u32[]{:S(2)}, u32[]{:S(2)}) %collective-permute-start.7) | collective-permute-done | bytes 262176 | tf_op jit(solution)/shard_map/ppermute | solution.py:22
  67.0 0.1 shard_map.67
  67.0 0.0 copy-start.3
  67.0 0.1 broadcast_select_fusion.2
  67.1 0.1 collective-permute-start.8
  67.2 1.7 %collective-permute-done.8 = f32[23,16,256]{2,1,0:T(8,128)S(1)} collective-permute-done((f32[23,16,256]{2,1,0:T(8,128)S(1)}, f32[23,16,256]{2,1,0:T(8,128)S(1)}, u32[]{:S(2)}, u32[]{:S(2)}) %collective-permute-start.8) | collective-permute-done | bytes 376864 | tf_op jit(solution)/shard_map/ppermute | solution.py:22
  68.9 0.1 broadcast_select_fusion
  69.0 0.0 copy-done.3
  69.0 10.8 %shard_map.68 = (f32[8,80,256]{2,1,0:T(8,128)S(1)}, f32[8,80,256]{2,1,0:T(8,128)S(1)}, f32[8,80,256]{2,1,0:T(8,128)S(1)}, f32[8,80,256]{2,1,0:T(8,128)S(1)}, f32...) custom-call(f32[76,16,256]{2,1,0:T(8,128)S(1)} %collective-permute-d, ...), custom_call_target="tpu_custom_call" | custom-call | tf_op jit(solution)/shard_map/pallas_call | solution.py:597
  79.8 8.0 %collective-permute-done.3.far2 = f32[66,16,256]{2,1,0:T(8,128)S(1)} collective-permute-done((f32[66,16,256]{2,1,0:T(8,128)S(1)}, f32[66,16,256]{2,1,0:T(8,128)S(1)}, u32[]{:S(2)}, u32[]{:S(2)}) %collective-permute-start.3) | collective-permute-done | bytes 1081376 | tf_op jit(solution)/shard_map/ppermute | solution.py:22
  87.8 0.0 copy-start.4
  87.8 6.3 %shard_map.69 = (f32[16,128]{1,0:T(8,128)S(1)}, bf16[2,64,64,256]{3,2,1,0:T(8,128)(2,1)S(1)}) custom-call(f32[66,16,256]{2,1,0:T(8,128)S(1)} %collective-permute-done.3.far2, f32[3,70,16,256]{3,2,1,0:T(8,128)S(1)} %get-tuple-element.30.u0_in, f32[2,70,16,256]{3,2,1,0:T(8,128)S(1)} %get-tuple-element.31.u1_in, ...), custom_call_target="tpu_custom_call" | custom-call | tf_op jit(solution)/shard_map/pallas_call | solution.py:610
  94.1 0.0 collective-permute-start.9
  94.1 1.2 %collective-permute-done.9 = f32[16,128]{1,0:T(8,128)S(1)} collective-permute-done((f32[16,128]{1,0:T(8,128)S(1)}, f32[16,128]{1,0:T(8,128)S(1)}, u32[]{:S(2)}, u32[]{:S(2)}) %collective-permute-start.9) | collective-permute-done | bytes 8224 | tf_op jit(solution)/shard_map/ppermute | solution.py:59
  95.2 2.6 %collective-permute-start.10 = (f32[16,128]{1,0:T(8,128)S(1)}, f32[16,128]{1,0:T(8,128)S(1)}, u32[]{:S(2)}, u32[]{:S(2)}) collective-permute-start(f32[16,128]{1,0:T(8,128)S(1)} %add.17), channel_id=1, source_target_pairs={{0,2},{2,0},{4,6},{6,4},{8,10},{10,8},{12,14},{14,12},{1,3},{3,1},... | collective-permute-start | bytes 24584 | tf_op jit(solution)/shard_map/ppermute | solution.py:59
  97.9 1.6 %collective-permute-done.10 = f32[16,128]{1,0:T(8,128)S(1)} collective-permute-done((f32[16,128]{1,0:T(8,128)S(1)}, f32[16,128]{1,0:T(8,128)S(1)}, u32[]{:S(2)}, u32[]{:S(2)}) %collective-permute-start.10) | collective-permute-done | bytes 8224 | tf_op jit(solution)/shard_map/ppermute | solution.py:59
  99.5 1.9 %collective-permute-start.11 = (f32[16,128]{1,0:T(8,128)S(1)}, f32[16,128]{1,0:T(8,128)S(1)}, u32[]{:S(2)}, u32[]{:S(2)}) collective-permute-start(f32[16,128]{1,0:T(8,128)S(1)} %add.18), channel_id=1, source_target_pairs={{0,4},{2,6},{4,0},{6,2},{8,12},{10,14},{12,8},{14,10},{1,5},{3,7},... | collective-permute-start | bytes 24584 | tf_op jit(solution)/shard_map/ppermute | solution.py:59
  101.4 1.8 %collective-permute-done.11 = f32[16,128]{1,0:T(8,128)S(1)} collective-permute-done((f32[16,128]{1,0:T(8,128)S(1)}, f32[16,128]{1,0:T(8,128)S(1)}, u32[]{:S(2)}, u32[]{:S(2)}) %collective-permute-start.11) | collective-permute-done | bytes 8224 | tf_op jit(solution)/shard_map/ppermute | solution.py:59
  103.2 2.9 %collective-permute-start.12 = (f32[16,128]{1,0:T(8,128)S(1)}, f32[16,128]{1,0:T(8,128)S(1)}, u32[]{:S(2)}, u32[]{:S(2)}) collective-permute-start(f32[16,128]{1,0:T(8,128)S(1)} %add.19), channel_id=1, source_target_pairs={{0,8},{2,10},{4,12},{6,14},{8,0},{10,2},{12,4},{14,6},{1,9},{3,11}... | collective-permute-start | bytes 24584 | tf_op jit(solution)/shard_map/ppermute | solution.py:59
  106.1 1.7 %collective-permute-done.12 = f32[16,128]{1,0:T(8,128)S(1)} collective-permute-done((f32[16,128]{1,0:T(8,128)S(1)}, f32[16,128]{1,0:T(8,128)S(1)}, u32[]{:S(2)}, u32[]{:S(2)}) %collective-permute-start.12) | collective-permute-done | bytes 8224 | tf_op jit(solution)/shard_map/ppermute | solution.py:59
  107.7 0.0 copy-done.4
  107.7 6.3 %shard_map.70 = (f32[16,2,64,256]{3,2,1,0:T(8,128)}, f32[16,2,64,256]{3,2,1,0:T(8,128)}) custom-call(s32[1]{0:T(128)} %bitcast.odd, f32[16,128]{1,0:T(8,128)S(1)} %add.20.moments, bf16[2,64,64,256]{3,2,1,0:T(8,128)(2,1)S(1)} %get-tuple-element.39.split01, bf16[2,64,64,256]{3,2,1,0:T(8,128)(2,1)S(1)} %get-tuple-element.40.split23, ...), custom_call_target="tpu_custom_call" | custom-call | tf_op jit(solution)/shard_map/pallas_call | solution.py:623
  (10 shorter events, 0.1 us)
Async XLA Ops:
  3.3 5.6 %copy-start.5 = (f32[3,16,256]{2,1,0:T(8,128)S(1)}, f32[3,16,256]{2,1,0:T(8,128)}, u32[]{:S(2)}) copy-start(f32[3,16,256]{2,1,0:T(8,128)} %get-tuple-element.24) | copy-start | bytes 147460
  3.3 5.6 %copy-start.6 = (f32[3,16,256]{2,1,0:T(8,128)S(1)}, f32[3,16,256]{2,1,0:T(8,128)}, u32[]{:S(2)}) copy-start(f32[3,16,256]{2,1,0:T(8,128)} %get-tuple-element.26) | copy-start | bytes 147460
  3.4 5.7 %copy-start = (f32[80,16,256]{2,1,0:T(8,128)S(1)}, f32[80,16,256]{2,1,0:T(8,128)}, u32[]{:S(2)}) copy-start(f32[80,16,256]{2,1,0:T(8,128)} %get-tuple-element.22.mine) | copy-start | bytes 3932164
  3.4 32.0 %collective-permute-start.1 = (f32[80,16,256]{2,1,0:T(8,128)}, f32[80,16,256]{2,1,0:T(8,128)S(1)}, u32[]{:S(2)}, u32[]{:S(2)}) collective-permute-start(f32[80,16,256]{2,1,0:T(8,128)} %get-tuple-element.22.mine), channel_id=1, source_target_pairs={{0,2},{2,0},{4,6},{6,4},{8,10},{10,8},{12,14},{14,12},{1,3},{3,1},... | collective-permute-start | bytes 3932168 | tf_op jit(solution)/shard_map/ppermute | solution.py:22
  7.9 1.0 copy-start.1
  9.0 6.0 %collective-permute-start = (f32[2,3,16,256]{3,2,1,0:T(8,128)S(1)}, f32[2,3,16,256]{3,2,1,0:T(8,128)S(1)}, u32[]{:S(2)}, u32[]{:S(2)}) collective-permute-start(f32[2,3,16,256]{3,2,1,0:T(8,128)S(1)} %maximum_select_fusion), channel_id=1, source_target_pairs={{0,1},{1,0},{2,3},{3,2},{4,5},{5,4},{6,7},{7,6},{8,9},{9,8},{10,11... | collective-permute-start | bytes 294920 | tf_op jit(solution)/shard_map/ppermute | solution.py:22
  9.1 33.9 %collective-permute-start.6 = (f32[80,16,256]{2,1,0:T(8,128)S(1)}, f32[80,16,256]{2,1,0:T(8,128)S(1)}, u32[]{:S(2)}, u32[]{:S(2)}) collective-permute-start(f32[80,16,256]{2,1,0:T(8,128)S(1)} %copy-done), channel_id=1, source_target_pairs={{4,0},{8,4},{2,6},{12,8},{6,10},{10,14},{5,1},{9,5},{3,7},{13,9},{... | collective-permute-start | bytes 3932168 | tf_op jit(solution)/shard_map/ppermute | solution.py:22
  10.4 32.6 %collective-permute-start.4 = (f32[76,16,256]{2,1,0:T(8,128)}, f32[76,16,256]{2,1,0:T(8,128)S(1)}, u32[]{:S(2)}, u32[]{:S(2)}) collective-permute-start(f32[76,16,256]{2,1,0:T(8,128)} %copy-done.1), channel_id=1, source_target_pairs={{0,4},{4,8},{6,2},{8,12},{10,6},{14,10},{1,5},{5,9},{7,3},{9,13},{... | collective-permute-start | bytes 3735560 | tf_op jit(solution)/shard_map/ppermute | solution.py:22
  15.1 1.3 %copy-start.2 = (f32[76,16,256]{2,1,0:T(8,128)S(1)}, f32[76,16,256]{2,1,0:T(8,128)}, u32[]{:S(2)}) copy-start(f32[76,16,256]{2,1,0:T(8,128)} %copy-done.1) | copy-start | bytes 3735556
  35.4 25.0 %collective-permute-start.2 = (f32[66,16,256]{2,1,0:T(8,128)S(1)}, f32[66,16,256]{2,1,0:T(8,128)S(1)}, u32[]{:S(2)}, u32[]{:S(2)}) collective-permute-start(f32[66,16,256]{2,1,0:T(8,128)S(1)} %shard_map.63), channel_id=1, source_target_pairs={{0,2},{2,0},{4,6},{6,4},{8,10},{10,8},{12,14},{14,12},{1,3},{3,1},... | collective-permute-start | bytes 3244040 | tf_op jit(solution)/shard_map/ppermute | solution.py:22
  37.2 28.2 %collective-permute-start.5 = (f32[64,16,256]{2,1,0:T(8,128)S(1)}, f32[64,16,256]{2,1,0:T(8,128)S(1)}, u32[]{:S(2)}, u32[]{:S(2)}) collective-permute-start(f32[64,16,256]{2,1,0:T(8,128)S(1)} %shard_map.64), channel_id=1, source_target_pairs={{0,4},{4,8},{6,2},{8,12},{10,6},{14,10},{1,5},{5,9},{7,3},{9,13},{... | collective-permute-start | bytes 3145736 | tf_op jit(solution)/shard_map/ppermute | solution.py:22
  60.4 6.6 %collective-permute-start.7 = (f32[16,16,256]{2,1,0:T(8,128)S(1)}, f32[16,16,256]{2,1,0:T(8,128)S(1)}, u32[]{:S(2)}, u32[]{:S(2)}) collective-permute-start(f32[16,16,256]{2,1,0:T(8,128)S(1)} %shard_map.66), channel_id=1, source_target_pairs={{0,2},{2,0},{4,6},{6,4},{8,10},{10,8},{12,14},{14,12},{1,3},{3,1},... | collective-permute-start | bytes 786440 | tf_op jit(solution)/shard_map/ppermute | solution.py:22
  61.8 25.9 %collective-permute-start.3 = (f32[66,16,256]{2,1,0:T(8,128)S(1)}, f32[66,16,256]{2,1,0:T(8,128)S(1)}, u32[]{:S(2)}, u32[]{:S(2)}) collective-permute-start(f32[66,16,256]{2,1,0:T(8,128)S(1)} %collective-permute-done.2.earlier.near1), channel_id=1, source_target_pairs={{0,4},{4,8},{6,2},{8,12},{10,6},{14,10},{1,5},{5,9},{7,3},{9,13},{... | collective-permute-start | bytes 3244040 | tf_op jit(solution)/shard_map/ppermute | solution.py:22
  67.0 1.9 %copy-start.3 = (f32[76,16,256]{2,1,0:T(8,128)S(1)}, f32[76,16,256]{2,1,0:T(8,128)}, u32[]{:S(2)}) copy-start(f32[76,16,256]{2,1,0:T(8,128)} %copy-done.1) | copy-start | bytes 3735556
  67.1 1.8 %collective-permute-start.8 = (f32[23,16,256]{2,1,0:T(8,128)S(1)}, f32[23,16,256]{2,1,0:T(8,128)S(1)}, u32[]{:S(2)}, u32[]{:S(2)}) collective-permute-start(f32[23,16,256]{2,1,0:T(8,128)S(1)} %broadcast_select_fusion.2), channel_id=1, source_target_pairs={{0,1},{1,0},{2,3},{3,2},{4,5},{5,4},{6,7},{7,6},{8,9},{9,8},{10,11... | collective-permute-start | bytes 1130504 | tf_op jit(solution)/shard_map/ppermute | solution.py:22
  87.8 20.0 %copy-start.4 = (f32[16,2,64,256]{3,2,1,0:T(8,128)S(1)}, f32[16,2,64,256]{3,2,1,0:T(8,128)}, u32[]{:S(2)}) copy-start(f32[16,2,64,256]{3,2,1,0:T(8,128)} %iterate.1) | copy-start | bytes 6291460
  94.1 1.2 %collective-permute-start.9 = (f32[16,128]{1,0:T(8,128)S(1)}, f32[16,128]{1,0:T(8,128)S(1)}, u32[]{:S(2)}, u32[]{:S(2)}) collective-permute-start(f32[16,128]{1,0:T(8,128)S(1)} %get-tuple-element.38), channel_id=1, source_target_pairs={{0,1},{1,0},{2,3},{3,2},{4,5},{5,4},{6,7},{7,6},{8,9},{9,8},{10,11... | collective-permute-start | bytes 24584 | tf_op jit(solution)/shard_map/ppermute | solution.py:59
  95.2 4.3 %collective-permute-start.10 = (f32[16,128]{1,0:T(8,128)S(1)}, f32[16,128]{1,0:T(8,128)S(1)}, u32[]{:S(2)}, u32[]{:S(2)}) collective-permute-start(f32[16,128]{1,0:T(8,128)S(1)} %add.17), channel_id=1, source_target_pairs={{0,2},{2,0},{4,6},{6,4},{8,10},{10,8},{12,14},{14,12},{1,3},{3,1},... | collective-permute-start | bytes 24584 | tf_op jit(solution)/shard_map/ppermute | solution.py:59
  99.5 3.7 %collective-permute-start.11 = (f32[16,128]{1,0:T(8,128)S(1)}, f32[16,128]{1,0:T(8,128)S(1)}, u32[]{:S(2)}, u32[]{:S(2)}) collective-permute-start(f32[16,128]{1,0:T(8,128)S(1)} %add.18), channel_id=1, source_target_pairs={{0,4},{2,6},{4,0},{6,2},{8,12},{10,14},{12,8},{14,10},{1,5},{3,7},... | collective-permute-start | bytes 24584 | tf_op jit(solution)/shard_map/ppermute | solution.py:59
  103.2 4.5 %collective-permute-start.12 = (f32[16,128]{1,0:T(8,128)S(1)}, f32[16,128]{1,0:T(8,128)S(1)}, u32[]{:S(2)}, u32[]{:S(2)}) collective-permute-start(f32[16,128]{1,0:T(8,128)S(1)} %add.19), channel_id=1, source_target_pairs={{0,8},{2,10},{4,12},{6,14},{8,0},{10,2},{12,4},{14,6},{1,9},{3,11}... | collective-permute-start | bytes 24584 | tf_op jit(solution)/shard_map/ppermute | solution.py:59
